TPU v7x, 256 devices: a whole 4x4x8 slice. The times are simulated.
256 devices in a mesh: lat: 16 (over x, z_lo), wave: 8 (over y, core), lev: 2 (over z_hi).
Axes of the slice: x: 4, y: 4, z: 8 (z_hi: 2, z_lo: 4; z = z_hi * 4 + z_lo), core: 2. Of those that a mesh axis runs over, the one named last changes fastest.
Arguments:
- out_grad: bfloat16 [64, 1280, 2560], P('lev', 'lat', 'wave'), may hold values from -6 to 6
- grid_state: bfloat16 [64, 1280, 2560], P('lev', 'lat', 'wave'), may hold values from -4 to 4
- tend_rate: float32 [64], P('lev'), may hold values from 0.5 to 2
- legendre_basis: bfloat16 [1280, 640, 640], P('lat', 'wave'), may hold values from -0.15625 to 0.15625
- wave_slot: int32 [640], replicated, may hold values from 0 to 639, each once
Outputs:
- spectral_grad: float32 [640, 2, 64, 640], P('lat', None, 'lev', 'wave')
Inputs may be any that keep to these rules, and one draw needn't show every extreme that they name: `wave_slot`: each wavenumber 0 to 639 occupies exactly one slot.
All inputs are finite; a program needn't handle non-finite values.
Results may differ from a plain program's by a relative error of at most 0.0051.
Values may be sent and summed in bfloat16 or wider, within the bound.
No kernel may reach another device: no remote copies, remote signals or barrier semaphores. Data moves between devices by JAX's collectives and lax.ppermute only.
A program may use at most 128 MiB of HBM per device.

v0:
```python
import math

import jax
import jax.numpy as jnp
from jax import lax
from jax.sharding import PartitionSpec as P


def wave_table(slots, lon_start, count, lon_total):
    lon = lon_start + jnp.arange(count, dtype=jnp.int32)
    index = slots[None, :] * lon[:, None] % lon_total
    angle = index.astype(jnp.float32) * (2.0 * math.pi / lon_total)
    scale = 1.0 / math.sqrt(lon_total)
    return (jnp.concatenate([jnp.cos(angle), -jnp.sin(angle)], 1) * scale).astype(jnp.bfloat16)


def local(out_grad, grid_state, tend_rate, legendre_basis, wave_slot):
    chan_dev, lat_dev, lon_dev = out_grad.shape
    slot_dev = legendre_basis.shape[1]
    lon_total = lon_dev * lax.axis_size("wave")
    slope = 1.0 - jnp.tanh(grid_state.astype(jnp.float32)) ** 2
    grid_grad = (out_grad.astype(jnp.float32) * (1.0 + tend_rate[:, None, None] * slope)).astype(
        jnp.bfloat16
    )
    flat = grid_grad.reshape(chan_dev * lat_dev, lon_dev)
    lon_start = lax.axis_index("wave") * lon_dev
    table = wave_table(wave_slot, lon_start, lon_dev, lon_total)
    term = jnp.dot(flat, table, preferred_element_type=jnp.float32)
    summed = lax.psum_scatter(
        term.reshape(-1, 2, slot_dev * lax.axis_size("wave")).transpose(2, 1, 0),
        "wave",
        scatter_dimension=0,
        tiled=True,
    )
    fourier = (
        summed.astype(jnp.bfloat16).reshape(slot_dev, 2, chan_dev, lat_dev).transpose(2, 3, 1, 0)
    )
    own_slots = lax.dynamic_slice_in_dim(wave_slot, lax.axis_index("wave") * slot_dev, slot_dev)
    deg_total = legendre_basis.shape[2]
    deg_dev = deg_total // lax.axis_size("lat")
    term = jnp.einsum("lsn,klps->npks", legendre_basis, fourier, preferred_element_type=jnp.float32)
    degree = jnp.arange(deg_dev * lax.axis_size("lat"), dtype=jnp.int32)
    keep = (degree[:, None] >= own_slots[None, :]).astype(jnp.float32)
    return lax.psum_scatter(term * keep[:, None, None, :], "lat", scatter_dimension=0, tiled=True)


def solution(mesh):
    in_specs = (
        P("lev", "lat", "wave"),
        P("lev", "lat", "wave"),
        P("lev"),
        P("lat", "wave", None),
        P(),
    )
    out_specs = P("lat", None, "lev", "wave")
    return jax.shard_map(local, mesh=mesh, in_specs=in_specs, out_specs=out_specs, check_vma=False)
```

profile of v0, /device:TPU:2, one launch (start us, length us, event | category | flops | bytes accessed | tf_op | source)
XLA Modules:
  0.0 657.3 jit_solution(9796702054225780561)
XLA Ops:
  6.5 0.0 copy-start.2
  6.5 0.0 copy-start
  6.5 0.0 reduce-scatter.2.cloned.1.call-start
  6.5 0.0 copy-start.1
  6.6 0.9 dynamic_slice.3
  7.5 0.1 fusion.11
  7.6 4.3 fusion.9
  11.8 0.1 fusion.1
  12.0 0.0 copy-done.2
  12.0 0.0 copy-done
  12.0 0.0 copy-done.1
  12.0 1.3 multiply_convert_fusion
  13.3 6.6 %convolution_bitcast_fusion = f32[640,2,2560]{0,2,1:T(8,128)} fusion(bf16[2560,320,1]{1,0,2:T(8,128)(2,1)S(1)} %bitcast.19, bf16[40,2,8,640]{3,2,1,0:T(8,128)(2,1)S(1)} %bitcast.20), kind=kOutput, calls=%fused_computation.2 | convolution fusion | flops 2097152000 | bytes 15564800 | tf_op jit(solution)/shard_map/dot_general | solution.py:28
  19.8 20.2 %copy.17 = f32[640,2,2560]{2,1,0:T(2,128)} copy(f32[640,2,2560]{0,2,1:T(8,128)} %convolution_bitcast_fusion) | data formatting | bytes 26214400 | tf_op jit(solution)/shard_map/transpose | solution.py:30
  40.1 0.0 copy-start.3
  40.1 138.8 %all-reduce.2 = bf16[640,2,2560]{2,1,0:T(2,128)(2,1)} all-reduce(f32[640,2,2560]{2,1,0:T(2,128)} %copy.17), channel_id=2, replica_groups=mesh['lat'=16,'wave'=8,'lev'=2] {'wave'}, use_global_device_ids=true, to_apply=%region_0.1.clone | all-reduce | flops 3276800 | bytes 19660800
  178.9 0.0 copy-done.3
  178.9 0.6 dynamic-slice
  180.1 1.7 dynamic-slice_convert_fusion
  181.8 1.6 reshape.33
  183.5 10.0 %bitcast_multiply_fusion = f32[640,2,32,80]{0,2,1,3:T(8,128)} fusion(bf16[80,80,640,1]{2,1,0,3:T(8,128)(2,1)} %bitcast.18, f32[640,80]{0,1:T(8,128)S(1)} %fusion.11, bf16[80,2,32,80]{3,2,1,0:T(8,128)(2,1)S(1)} %reshape.33), kind=kOutput, calls=%fused_computation | convolution fusion | flops 527564800 | bytes 22323200 | tf_op jit(solution)/shard_map/lsn,klps->npks/dot_general | solution.py:41
  193.5 19.1 %copy.19 = f32[640,2,32,80]{3,2,1,0:T(8,128)} copy(f32[640,2,32,80]{0,2,1,3:T(8,128)} %bitcast_multiply_fusion) | data formatting | bytes 26214400 | tf_op jit(solution)/shard_map/mul | solution.py:44
  212.6 0.0 reduce-scatter.2.cloned.1.call-update
  212.6 437.9 %reduce-scatter.2.cloned.1.call-done = f32[40,2,32,80]{3,2,1,0:T(8,128)} async-done(((f32[640,2,32,80]{3,2,1,0:T(8,128)}), f32[40,2,32,80]{3,2,1,0:T(8,128)}) %reduce-scatter.2.cloned.1.call-update) | async-done | bytes 819216 | tf_op jit(solution)/shard_map/reduce_scatter | solution.py:44
  (1 shorter events, 0.0 us)
Async XLA Ops:
  6.5 5.4 copy-start.2
  6.5 5.4 copy-start
  6.5 643.9 %reduce-scatter.2.cloned.1.call-start = ((), (), s32[]{:S(2)}) async-start(), calls=%async_computation.1 | async-start | bytes 22282240 | tf_op jit(solution)/shard_map/reduce_scatter | solution.py:44
  6.5 5.4 copy-start.1
  40.1 138.8 %copy-start.3 = (u32[256]{0:T(256)S(1)}, u32[256]{0:T(256)}, u32[]{:S(2)}) copy-start(u32[256]{0:T(256)} %constant.33) | copy-start | bytes 3076
Sparse Core Ops, SparseCore 0:
  212.7 437.6 reduce-scatter.1
where the time goes:
time: 661 us; the launch traced here: 657 us
  waiting for transfers between devices  438 us (66%)
  blocking collectives  139 us (21%)
  local copies, waits for them, and re-layouts  44.2 us (7%)
  matrix products  16.6 us (3%)
  between operations  14.1 us (2%)
    reduce_scatter x1, waiting for transfers between devices, local(): lax.psum_scatter(term * keep[:, None, None, :], 'lat', scatter_dimension=...  438 us
    unnamed x1, blocking collectives  139 us
    transpose x1, local copies, waits for them, and re-layouts, local(): term.reshape(-1, 2, slot_dev * lax.axis_size('wave')).transpose(2, 1, 0)  20.2 us
    mul x1, local copies, waits for them, and re-layouts, local(): term * keep[:, None, None, :]  19.1 us
  transfers between devices with their start and end apart: 1, of which 1 were waited for; matrix products, arithmetic and copies ran while one was open for 0% of the time, Pallas kernels for 0%

commit v1 on v0

v1 whole, which is shorter than its diff:
```python
import functools
import math

import jax
import jax.numpy as jnp
from jax import lax
from jax.experimental import pallas as pl
from jax.experimental.pallas import tpu as pltpu
from jax.sharding import Mesh, PartitionSpec as P

VMEM = 48 * 1024 * 1024


def params():
    return pltpu.CompilerParams(vmem_limit_bytes=VMEM)


def cost(flops, moved, trans=0):
    return pl.CostEstimate(flops=flops, bytes_accessed=moved, transcendentals=trans)


def basis_kernel(where_ref, basis_ref, *refs):
    outs, rows = refs[:-1], refs[-1]
    lats, _, degs = basis_ref.shape
    block = basis_ref[...].astype(jnp.float32)
    half = jnp.where(where_ref[8] == 0, block[:, :8], block[:, 8:])
    for t in range(degs // 128):
        lanes = slice(128 * t, 128 * t + 128)
        rows[t] = half[:, :, lanes].reshape(lats * 8, 128)
        for j, out in enumerate(outs):
            out[0, :, lanes] = rows[t, pl.ds(where_ref[j], lats, stride=8), :].astype(jnp.bfloat16)


def basis_blocks(where, basis):
    lats, slots, degs = basis.shape
    steps = slots // 16
    return pl.pallas_call(
        basis_kernel,
        grid_spec=pltpu.PrefetchScalarGridSpec(
            num_scalar_prefetch=1,
            grid=(steps,),
            in_specs=[pl.BlockSpec((lats, 16, degs), lambda b, w: (0, b, 0))],
            out_specs=[pl.BlockSpec((1, lats, degs), lambda b, w: (b, 0, 0))] * 8,
            scratch_shapes=[pltpu.VMEM((degs // 128, lats * 8, 128), jnp.float32)],
        ),
        out_shape=[jax.ShapeDtypeStruct((steps, lats, degs), jnp.bfloat16)] * 8,
        compiler_params=params(),
        cost_estimate=cost(0, 3 * lats * slots * degs),
        name="basis_blocks",
    )(where, basis)


def grad_kernel(rate_ref, grad_ref, state_ref, out_ref):
    w = pl.program_id(0)
    lons = grad_ref.shape[-1]
    for c in range(4):
        slope = 1.0 - jnp.tanh(state_ref[c, 0].astype(jnp.float32)) ** 2
        value = grad_ref[c, 0].astype(jnp.float32) * (1.0 + rate_ref[8 * c + w] * slope)
        out_ref[0, c // 2, :, pl.ds((c % 2) * lons, lons)] = value.astype(jnp.bfloat16)


def gradient(rate, grad, state):
    chans, lats, lons = grad.shape
    four = (4, chans // 4, lats, lons)
    spec = pl.BlockSpec((4, 1, lats, lons), lambda w: (0, w, 0, 0))
    return pl.pallas_call(
        grad_kernel,
        grid=(8,),
        in_specs=[pl.BlockSpec(memory_space=pltpu.SMEM), spec, spec],
        out_specs=pl.BlockSpec((1, 2, lats, 2 * lons), lambda w: (w, 0, 0, 0)),
        out_shape=jax.ShapeDtypeStruct((8, 2, lats, 2 * lons), jnp.bfloat16),
        compiler_params=params(),
        cost_estimate=cost(6 * grad.size, 6 * grad.size, grad.size),
        name="gradient",
    )(rate, grad.reshape(four), state.reshape(four))


def table_kernel(coarse_cos, coarse_sin, fine_cos, fine_sin, out_ref):
    fine = fine_cos.shape[1]
    for j in range(coarse_cos.shape[1]):
        cos, sin = coarse_cos[:, j : j + 1], coarse_sin[:, j : j + 1]
        lanes = slice(j * fine, (j + 1) * fine)
        out_ref[0, :, lanes] = (cos * fine_cos[...] - sin * fine_sin[...]).astype(jnp.bfloat16)
        out_ref[1, :, lanes] = (-sin * fine_cos[...] - cos * fine_sin[...]).astype(jnp.bfloat16)


def wave_table(slots, lon_total, fine):
    def trig(lon):
        index = slots[:, None] * lon[None, :] % lon_total
        angle = index.astype(jnp.float32) * (2.0 * math.pi / lon_total)
        return jnp.cos(angle), jnp.sin(angle)

    coarse_cos, coarse_sin = trig(fine * jnp.arange(lon_total // fine, dtype=jnp.int32))
    fine_cos, fine_sin = trig(jnp.arange(fine, dtype=jnp.int32))
    scale = 1.0 / math.sqrt(lon_total)
    count, block = slots.shape[0], 128
    coarse_spec = pl.BlockSpec((block, lon_total // fine), lambda s: (s, 0))
    fine_spec = pl.BlockSpec((block, fine), lambda s: (s, 0))
    return pl.pallas_call(
        table_kernel,
        grid=(count // block,),
        in_specs=[coarse_spec, coarse_spec, fine_spec, fine_spec],
        out_specs=pl.BlockSpec((2, block, lon_total), lambda s: (0, s, 0)),
        out_shape=jax.ShapeDtypeStruct((2, count, lon_total), jnp.bfloat16),
        compiler_params=params(),
        cost_estimate=cost(6 * count * lon_total, 4 * count * lon_total),
        name="wave_table",
    )(coarse_cos * scale, coarse_sin * scale, fine_cos, fine_sin)


def fourier_kernel(grad_ref, table_ref, out_ref, rows):
    lats, lons = grad_ref.shape[2], grad_ref.shape[3] // 2

    @pl.when(pl.program_id(0) == 0)
    def _():
        for w in range(8):
            for c in range(4):
                rows[pl.ds(c * lats, lats), pl.ds(w * lons, lons)] = grad_ref[
                    w, c // 2, :, pl.ds((c % 2) * lons, lons)
                ]

    width = 4 * lats
    for p in range(2):
        value = lax.dot_general(
            table_ref[p], rows[...], (((1,), (1,)), ((), ())), preferred_element_type=jnp.float32
        )
        out_ref[:, pl.ds(p * width, width)] = value.astype(jnp.bfloat16)


def fourier_rows(grad, table):
    _, _, lats, lons2 = grad.shape
    slots, lon_total = table.shape[1:]
    block = 128
    return pl.pallas_call(
        fourier_kernel,
        grid=(slots // block,),
        in_specs=[
            pl.BlockSpec(grad.shape, lambda s: (0, 0, 0, 0)),
            pl.BlockSpec((2, block, lon_total), lambda s: (0, s, 0)),
        ],
        out_specs=pl.BlockSpec((block, 8 * lats), lambda s: (s, 0)),
        out_shape=jax.ShapeDtypeStruct((slots, 8 * lats), jnp.bfloat16),
        scratch_shapes=[pltpu.VMEM((4 * lats, lon_total), jnp.bfloat16)],
        compiler_params=params(),
        cost_estimate=cost(2 * 2 * slots * lon_total * 4 * lats, 2 * (grad.size + table.size)),
        name="fourier_rows",
    )(grad, table)


def turn_kernel(in_ref, out_ref, rows):
    waves, slots, width = in_ref.shape
    for t in range(width // 128):
        lanes = slice(128 * t, 128 * t + 128)
        rows[t] = in_ref[:, :, lanes].astype(jnp.float32).reshape(waves * slots, 128)
        for s in range(slots):
            b, lev, r = s // 16, s // 8 % 2, s % 8
            out_ref[2 * r + lev, b, :, lanes] = rows[t, pl.ds(s, waves, stride=slots), :].astype(
                jnp.bfloat16
            )


def turn(fourier):
    waves, slots, width = fourier.shape
    return pl.pallas_call(
        turn_kernel,
        out_shape=jax.ShapeDtypeStruct((16, slots // 16, waves, width), jnp.bfloat16),
        scratch_shapes=[pltpu.VMEM((width // 128, waves * slots, 128), jnp.float32)],
        compiler_params=params(),
        cost_estimate=cost(0, 4 * fourier.size),
        name="turn",
    )(fourier)


def spectral_kernel(where_ref, slot_ref, four_ref, *refs):
    bases, out_ref, left, total = refs[:8], refs[8], refs[9], refs[10]
    lats, degs = bases[0].shape[1:]
    deg_dev = degs // 16
    degree = lax.broadcasted_iota(jnp.int32, (128, degs), 1)

    def summed(b):
        for j in range(8):
            source = where_ref[8 + j]
            for lev in range(2):
                block = four_ref[2 * source + lev, b].astype(jnp.float32)
                for seg in range(8):
                    left[pl.ds(64 * lev + 8 * seg, 8), pl.ds(j * lats, lats)] = block[
                        :, seg * lats : (seg + 1) * lats
                    ]
        basis = jnp.concatenate([ref[b] for ref in bases], 0)
        value = jnp.dot(
            left[...].astype(jnp.bfloat16), basis, preferred_element_type=jnp.float32
        )
        return jnp.where(degree >= slot_ref[b], value, 0.0)

    for k in range(2):
        even, odd = summed(2 * k), summed(2 * k + 1)
        for lev in range(2):
            both = jnp.concatenate([even[64 * lev :][:64], odd[64 * lev :][:64]], 0).T
            for a in range(16):
                out_ref[2 * a + lev, pl.ds(k * deg_dev, deg_dev)] = both[
                    a * deg_dev : (a + 1) * deg_dev
                ].astype(jnp.bfloat16)
    total[...] = summed(4).T
    even = total[pl.ds(0, degs // 2, stride=2), :]
    odd = total[pl.ds(1, degs // 2, stride=2), :]
    low = lax.broadcasted_iota(jnp.int32, even.shape, 1) < 64
    for lev in range(2):
        if lev == 0:
            both = jnp.where(low, even, pltpu.roll(odd, 64, 1))
        else:
            both = jnp.where(low, pltpu.roll(even, 64, 1), odd)
        for a in range(16):
            out_ref[2 * a + lev, pl.ds(2 * deg_dev, deg_dev // 2)] = both[
                a * (deg_dev // 2) : (a + 1) * (deg_dev // 2)
            ].astype(jnp.bfloat16)
    rows = 5 * deg_dev // 2
    if out_ref.shape[1] > rows:
        for a in range(32):
            out_ref[a, pl.ds(rows, out_ref.shape[1] - rows)] = jnp.zeros(
                (out_ref.shape[1] - rows, 128), jnp.bfloat16
            )


def spectral_parts(where, slots, fourier, bases):
    _, lats, degs = bases[0].shape
    smem = pl.BlockSpec(memory_space=pltpu.SMEM)
    return pl.pallas_call(
        spectral_kernel,
        in_specs=[smem, smem] + [pl.BlockSpec(memory_space=pltpu.VMEM)] * 9,
        out_shape=jax.ShapeDtypeStruct((32, 104, 128), jnp.bfloat16),
        scratch_shapes=[
            pltpu.VMEM((128, 8 * lats), jnp.float32),
            pltpu.VMEM((degs, 128), jnp.float32),
        ],
        compiler_params=params(),
        cost_estimate=cost(5 * 2 * 128 * 8 * lats * degs, 16 * bases[0].size + 2 * fourier.size),
        name="spectral_parts",
    )(where, slots, fourier, *bases)


def finish_kernel(in_ref, out_ref, rows):
    depth = in_ref.shape[1]
    for x in range(4):
        for zq in range(2):
            for lev in range(2):
                first = in_ref[8 * x + 2 * zq + lev].astype(jnp.float32)
                second = in_ref[8 * x + 4 + 2 * zq + lev].astype(jnp.float32)
                rows[pl.ds((8 * lev + 2 * x + zq) * depth, depth), :] = first + second
    low = lax.broadcasted_iota(jnp.int32, (16, 128), 1) < 64
    for n in range(0, 40, 2):
        parts = []
        for k in range(2):
            one = rows[pl.ds(40 * k + n, 16, stride=depth), :]
            two = rows[pl.ds(40 * k + n + 1, 16, stride=depth), :]
            parts.append(jnp.where(low, one, pltpu.roll(two, 64, 1)))
            parts.append(jnp.where(low, pltpu.roll(one, 64, 1), two))
        parts.append(rows[pl.ds(80 + n // 2, 16, stride=depth), :])
        out_ref[pl.ds(64 * n, 128), :] = jnp.concatenate(parts, 0).T


def finish(received):
    return pl.pallas_call(
        finish_kernel,
        out_shape=jax.ShapeDtypeStruct((40 * 64, 80), jnp.float32),
        scratch_shapes=[pltpu.VMEM((16 * received.shape[1], 128), jnp.float32)],
        compiler_params=params(),
        cost_estimate=cost(received.size, 2 * received.size + 4 * 40 * 64 * 128),
        name="finish",
    )(received)


def local(out_grad, grid_state, tend_rate, legendre_basis, wave_slot):
    lats, lons = out_grad.shape[1:]
    slot_dev, degs = legendre_basis.shape[1:]
    x, zq = lax.axis_index("x"), lax.axis_index("zq")
    wave, lev = lax.axis_index("wave"), lax.axis_index("lev")
    offsets = [(dx, dz) for dx in range(4) for dz in range(2)]
    to = [(x + dx) % 4 * 2 + (zq + dz) % 2 for dx, dz in offsets]
    source = [(x - dx) % 4 * 2 + (zq - dz) % 2 for dx, dz in offsets]
    where = jnp.stack(to + [lev]).astype(jnp.int32)
    sources = jnp.stack(to + source).astype(jnp.int32)

    grad = gradient(tend_rate, out_grad, grid_state)
    grad = lax.all_to_all(grad, "wave", 0, 0)

    blocks = basis_blocks(where, legendre_basis)
    bases = [blocks[0]]
    for (dx, dz), block in list(zip(offsets, blocks))[1:]:
        pairs = [
            (2 * a + b, 2 * ((a + dx) % 4) + (b + dz) % 2) for a in range(4) for b in range(2)
        ]
        bases.append(lax.ppermute(block, ("x", "zq"), pairs))

    table = wave_table(wave_slot, lons * 8, 128)
    fourier = fourier_rows(grad, table)
    fourier = lax.all_to_all(fourier.reshape(8, slot_dev, 8 * lats), "wave", 0, 0)
    fourier = lax.all_to_all(turn(fourier), ("x", "zq", "lev"), 0, 0, tiled=True)

    first = wave * slot_dev + 8 * lev + 2 * x + zq
    slots = jnp.take(wave_slot, first + 16 * jnp.arange(slot_dev // 16, dtype=jnp.int32))
    parts = spectral_parts(sources, slots, fourier, bases)
    parts = lax.all_to_all(parts, ("x", "zp", "zq", "lev"), 0, 0, tiled=True)
    return finish(parts).reshape(degs // 16, 2, 32, slot_dev)


def solution(mesh):
    fine = Mesh(
        mesh.devices.reshape(4, 2, 2, *mesh.devices.shape[1:]), ("x", "zp", "zq", "wave", "lev")
    )
    lat = ("x", "zp", "zq")
    in_specs = (P("lev", lat, "wave"), P("lev", lat, "wave"), P("lev"), P(lat, "wave", None), P())
    out_specs = P(lat, None, "lev", "wave")
    return jax.shard_map(local, mesh=fine, in_specs=in_specs, out_specs=out_specs, check_vma=False)
```

time: 661 us -> 173 us (0.26)
  waiting for transfers between devices: 438 us -> 56.4 us
  blocking collectives: 139 us -> 45.7 us
  local copies, waits for them, and re-layouts: 44.2 us -> 4.73 us
  Pallas kernels: 0 us -> 33.9 us
  starting transfers between devices: 0.01 us -> 29.1 us
  matrix products: 16.6 us -> 0 us
  between operations: 14.1 us -> 0.08 us
    reduce_scatter x1 -> x0, waiting for transfers between devices: 438 us -> none  [local(): lax.psum_scatter(term * keep[:, None, None, :], 'lat', scatter_dimension=...]
    unnamed x1 -> x0, blocking collectives: 139 us -> none
    all_to_all x0 -> x2, blocking collectives: none -> 45.7 us  [the longest x1 29.8 us: local(): parts = lax.all_to_all(parts, ('x', 'zp', 'zq', 'lev'), 0, 0, tiled=True)]
    ppermute x0 -> x7, waiting for transfers between devices: none -> 43.8 us  [local(): bases.append(lax.ppermute(block, ('x', 'zq'), pairs))]
    pallas_call x0 -> x7, Pallas kernels: none -> 33.9 us  [the longest x1 8.6 us: basis_blocks(): pl.pallas_call(basis_kernel, grid_spec=pltpu.PrefetchScalarGridSpec(num_s...]
    transpose x1 -> x0, local copies, waits for them, and re-layouts: 20.2 us -> none  [local(): term.reshape(-1, 2, slot_dev * lax.axis_size('wave')).transpose(2, 1, 0)]
    mul x1 -> x0, local copies, waits for them, and re-layouts: 19.1 us -> none  [local(): term * keep[:, None, None, :]]
    dot_general x2 -> x0, matrix products: 16.6 us -> none  [the longest x1 10 us: local(): jnp.einsum('lsn,klps->npks', legendre_basis, fourier, preferred_element_t...]
  transfers between devices with their start and end apart: 1 -> 9, of which waited for: 1 -> 5; matrix products, arithmetic and copies ran while one was open for 0% -> 2% of each run, Pallas kernels for 0% -> 9%
where the time goes in v1:
time: 173 us
  waiting for transfers between devices  56.4 us (33%)
  blocking collectives  45.7 us (26%)
  Pallas kernels  33.9 us (20%)
  starting transfers between devices  29.1 us (17%)
  local copies, waits for them, and re-layouts  4.73 us (3%)
  other arithmetic  2.76 us (2%)
    ppermute x7, waiting for transfers between devices, local(): bases.append(lax.ppermute(block, ('x', 'zq'), pairs))  43.8 us
    all_to_all x1, blocking collectives, local(): parts = lax.all_to_all(parts, ('x', 'zp', 'zq', 'lev'), 0, 0, tiled=True)  29.8 us
    all_to_all x1, blocking collectives, local(): lax.all_to_all(fourier.reshape(8, slot_dev, 8 * lats), 'wave', 0, 0)  16 us
    ppermute x7, starting transfers between devices, local(): bases.append(lax.ppermute(block, ('x', 'zq'), pairs))  13 us
    all_to_all x1, waiting for transfers between devices, local(): grad = lax.all_to_all(grad, 'wave', 0, 0)  12.6 us
    all_to_all x1, starting transfers between devices, local(): lax.all_to_all(turn(fourier), ('x', 'zq', 'lev'), 0, 0, tiled=True)  11.5 us
    pallas_call x1, Pallas kernels, basis_blocks(): pl.pallas_call(basis_kernel, grid_spec=pltpu.PrefetchScalarGridSpec(num_s...  8.6 us
    pallas_call x1, Pallas kernels, fourier_rows(): pl.pallas_call(fourier_kernel, grid=(slots // block,), in_specs=[pl.Block...  8.28 us
  transfers between devices with their start and end apart: 9, of which 5 were waited for; matrix products, arithmetic and copies ran while one was open for 2% of the time, Pallas kernels for 9%

profile of v1, /device:TPU:2, one launch (start us, length us, event | category | flops | bytes accessed | tf_op | source)
XLA Modules:
  0.0 172.7 jit_solution(10475409889589140163)
XLA Ops:
  0.0 0.0 copy-start
  0.0 1.5 copy-done
  1.5 0.0 copy-start.1
  1.5 1.5 copy-done.1
  3.1 0.0 copy-start.2
  3.1 0.7 copy-done.2
  3.7 4.4 %gradient.1 = bf16[8,2,80,640]{3,2,1,0:T(8,128)(2,1)} custom-call(f32[32]{0:T(128)S(1)} %copy-done.2, bf16[4,8,80,320]{3,2,1,0:T(8,128)(2,1)S(1)} %bitcast.23, bf16[4,8,80,320]{3,2,1,0:T(8,128)(2,1)S(1)} %bitcast.24), custom_call_target="tpu_custom_call" | custom-call | flops 4915200 | bytes 4915200 | tf_op jit(solution)/shard_map/gradient/pallas_call | solution.py:66
  8.1 0.0 copy-start.3
  8.1 4.6 %all-to-all-start = ((bf16[8,2,80,640]{3,2,1,0:T(8,128)(2,1)}), bf16[8,2,80,640]{3,2,1,0:T(8,128)(2,1)S(1)}, u32[]{:S(2)}, u32[]{:S(2)}) async-start(bf16[8,2,80,640]{3,2,1,0:T(8,128)(2,1)} %gradient.1), calls=%async_computation | async-start | bytes 3276800 | tf_op jit(solution)/shard_map/all_to_all | solution.py:284
  12.7 0.0 copy-done.3
  12.7 0.1 fusion.7
  12.8 0.2 copy.6
  13.0 1.4 fusion.4
  14.4 1.2 sine_multiply_fusion
  15.7 6.7 %wave_table.1.table_ref = bf16[2,640,2560]{2,1,0:T(8,128)(2,1)} custom-call(f32[640,20]{1,0:T(8,128)S(1)} %get-tuple-element.22.coarse_cos, f32[640,20]{1,0:T(8,128)S(1)} %get-tuple-element.21.coarse_sin, f32[640,128]{1,0:T(8,128)S(1)} %get-tuple-element.24.fine_cos, f32[640,128]{1,0:T(8,128)S(1)} %get-tuple-element.23.fine_sin), custom_call_target="tpu_custom_call" | custom-call | flops 9830400 | bytes 6553600 | tf_op jit(solution)/shard_map/wave_table/pallas_call | solution.py:99
  22.4 12.6 %all-to-all-done.grad_ref = bf16[8,2,80,640]{3,2,1,0:T(8,128)(2,1)S(1)} async-done(((bf16[8,2,80,640]{3,2,1,0:T(8,128)(2,1)}), bf16[8,2,80,640]{3,2,1,0:T(8,128)(2,1)S(1)}, u32[]{:S(2)}, u32[]{:S(2)}) %all-to-all-start) | async-done | bytes 1638432 | tf_op jit(solution)/shard_map/all_to_all | solution.py:284
  35.0 8.3 %fourier_rows.1 = bf16[640,640]{1,0:T(8,128)(2,1)S(1)} custom-call(bf16[8,2,80,640]{3,2,1,0:T(8,128)(2,1)S(1)} %all-to-all-done.grad_ref, bf16[2,640,2560]{2,1,0:T(8,128)(2,1)} %wave_table.1.table_ref), custom_call_target="tpu_custom_call" | custom-call | flops 2097152000 | bytes 8192000 | tf_op jit(solution)/shard_map/fourier_rows/pallas_call | solution.py:134
  43.3 16.0 %all_to_all.20.in_ref = bf16[8,80,640]{2,1,0:T(8,128)(2,1)S(1)} all-to-all(bf16[8,80,640]{2,1,0:T(8,128)(2,1)S(1)} %bitcast.22), channel_id=1, replica_groups=mesh['x'=4,'zp'=2,'zq'=2,'wave'=8,'lev'=2] {'wave'}, dimensions={0} | all-to-all | bytes 1638400 | tf_op jit(solution)/shard_map/all_to_all | solution.py:296
  59.3 1.5 turn.1
  60.8 11.5 %all-to-all-start.2 = ((bf16[16,5,8,640]{3,2,1,0:T(8,128)(2,1)}), bf16[16,5,8,640]{3,2,1,0:T(8,128)(2,1)S(1)}, u32[]{:S(2)}, u32[]{:S(2)}) async-start(bf16[16,5,8,640]{3,2,1,0:T(8,128)(2,1)} %turn.1), calls=%async_computation.2 | async-start | bytes 1638400 | tf_op jit(solution)/shard_map/all_to_all | solution.py:297
  72.3 0.1 stack.80.where_ref
  72.3 8.6 %basis_blocks.1 = (bf16[5,80,640]{2,1,0:T(8,128)(2,1)S(1)}, bf16[5,80,640]{2,1,0:T(8,128)(2,1)S(1)}, bf16[5,80,640]{2,1,0:T(8,128)(2,1)S(1)}, bf16[5,80,640]{2,1...) custom-call(s32[9]{0:T(128)S(1)} %stack.80.where_ref, ...), custom_call_target="tpu_custom_call" | custom-call | bytes 12288000 | tf_op jit(solution)/shard_map/basis_blocks/pallas_call | solution.py:37
  80.9 1.5 collective-permute-start
  82.4 1.5 collective-permute-start.1
  83.9 1.2 collective-permute-start.2
  85.1 1.5 collective-permute-start.3
  86.5 3.0 %collective-permute-start.4 = (bf16[5,80,640]{2,1,0:T(8,128)(2,1)}, bf16[5,80,640]{2,1,0:T(8,128)(2,1)}, u32[]{:S(2)}, u32[]{:S(2)}) collective-permute-start(bf16[5,80,640]{2,1,0:T(8,128)(2,1)} %get-tuple-element.18), channel_id=1, source_target_pairs={{0,144},{16,128},{64,208},{80,192},{128,16},{144,0},{192,80},{208,... | collective-permute-start | bytes 1536008 | tf_op jit(solution)/shard_map/ppermute | solution.py:292
  89.5 13.3 %collective-permute-done.refs_1_ = bf16[5,80,640]{2,1,0:T(8,128)(2,1)S(1)} collective-permute-done((bf16[5,80,640]{2,1,0:T(8,128)(2,1)S(1)}, bf16[5,80,640]{2,1,0:T(8,128)(2,1)S(1)}, u32[]{:S(2)}, u32[]{:S(2)}) %collective-permute-start) | collective-permute-done | bytes 512032 | tf_op jit(solution)/shard_map/ppermute | solution.py:292
  102.8 0.3 collective-permute-start.5
  103.1 0.0 collective-permute-done.1.refs_2_
  103.1 4.2 %collective-permute-start.6 = (bf16[5,80,640]{2,1,0:T(8,128)(2,1)}, bf16[5,80,640]{2,1,0:T(8,128)(2,1)}, u32[]{:S(2)}, u32[]{:S(2)}) collective-permute-start(bf16[5,80,640]{2,1,0:T(8,128)(2,1)} %get-tuple-element.20), channel_id=1, source_target_pairs={{0,208},{16,192},{64,16},{80,0},{128,80},{144,64},{192,144},{208,1... | collective-permute-start | bytes 1536008 | tf_op jit(solution)/shard_map/ppermute | solution.py:292
  107.3 0.6 gather_fusion
  107.9 0.1 stack.78.where_ref
  108.0 5.6 %collective-permute-done.2.refs_3_ = bf16[5,80,640]{2,1,0:T(8,128)(2,1)S(1)} collective-permute-done((bf16[5,80,640]{2,1,0:T(8,128)(2,1)}, bf16[5,80,640]{2,1,0:T(8,128)(2,1)S(1)}, u32[]{:S(2)}, u32[]{:S(2)}) %collective-permute-start.2) | collective-permute-done | bytes 512032 | tf_op jit(solution)/shard_map/ppermute | solution.py:292
  113.6 0.0 collective-permute-done.3.refs_4_
  113.6 14.1 %collective-permute-done.4.refs_5_ = bf16[5,80,640]{2,1,0:T(8,128)(2,1)} collective-permute-done((bf16[5,80,640]{2,1,0:T(8,128)(2,1)}, bf16[5,80,640]{2,1,0:T(8,128)(2,1)}, u32[]{:S(2)}, u32[]{:S(2)}) %collective-permute-start.4) | collective-permute-done | bytes 512032 | tf_op jit(solution)/shard_map/ppermute | solution.py:292
  127.8 10.7 %collective-permute-done.5.refs_6_ = bf16[5,80,640]{2,1,0:T(8,128)(2,1)} collective-permute-done((bf16[5,80,640]{2,1,0:T(8,128)(2,1)}, bf16[5,80,640]{2,1,0:T(8,128)(2,1)}, u32[]{:S(2)}, u32[]{:S(2)}) %collective-permute-start.5) | collective-permute-done | bytes 512032 | tf_op jit(solution)/shard_map/ppermute | solution.py:292
  138.5 0.0 collective-permute-done.6.refs_7_
  138.5 0.0 all-to-all-done.2.four_ref
  138.5 2.8 %spectral_parts.1 = bf16[32,104,128]{2,1,0:T(8,128)(2,1)S(1)} custom-call(s32[16]{0:T(128)S(1)} %stack.78.where_ref, s32[5]{0:T(128)S(1)} %and_select_fusion.slot_ref, bf16[16,5,8,640]{3,2,1,0:T(8,128)(2,1)S(1)} %all-to-all-done.2.four_ref, bf16[5,80,640]{2,1,0:T(8,128)(2,1)S(1)} %get-tuple-element.13.refs_0_, ...), custom_call_target="tpu_custom_call" | custom-call | flops 524288000 | bytes 4915200 | tf_op jit(solution)/shard_map/spectral_parts/pallas_call | solution.py:227
  141.3 29.8 %all_to_all.21.in_ref = bf16[32,104,128]{2,1,0:T(8,128)(2,1)S(1)} all-to-all(bf16[32,104,128]{2,1,0:T(8,128)(2,1)S(1)} %spectral_parts.1), channel_id=1, replica_groups=mesh['x'=4,'zp'=2,'zq'=2,'wave'=8,'lev'=2] {'x','zp','zq','lev'}, dimensions={0} | all-to-all | bytes 1703936 | tf_op jit(solution)/shard_map/all_to_all | solution.py:302
  171.0 1.7 finish.1
  (4 shorter events, 0.0 us)
Async XLA Ops:
  0.0 1.5 copy-start
  1.5 1.5 copy-start.1
  3.1 0.7 copy-start.2
  8.1 4.6 %copy-start.3 = (s32[640]{0:T(1024)S(1)}, s32[640]{0:T(1024)}, u32[]{:S(2)}) copy-start(s32[640]{0:T(1024)} %param.9) | copy-start | bytes 7684
  8.1 26.9 %all-to-all-start = ((bf16[8,2,80,640]{3,2,1,0:T(8,128)(2,1)}), bf16[8,2,80,640]{3,2,1,0:T(8,128)(2,1)S(1)}, u32[]{:S(2)}, u32[]{:S(2)}) async-start(bf16[8,2,80,640]{3,2,1,0:T(8,128)(2,1)} %gradient.1), calls=%async_computation | async-start | bytes 3276800 | tf_op jit(solution)/shard_map/all_to_all | solution.py:284
  60.8 77.7 %all-to-all-start.2 = ((bf16[16,5,8,640]{3,2,1,0:T(8,128)(2,1)}), bf16[16,5,8,640]{3,2,1,0:T(8,128)(2,1)S(1)}, u32[]{:S(2)}, u32[]{:S(2)}) async-start(bf16[16,5,8,640]{3,2,1,0:T(8,128)(2,1)} %turn.1), calls=%async_computation.2 | async-start | bytes 1638400 | tf_op jit(solution)/shard_map/all_to_all | solution.py:297
  80.9 21.8 %collective-permute-start = (bf16[5,80,640]{2,1,0:T(8,128)(2,1)S(1)}, bf16[5,80,640]{2,1,0:T(8,128)(2,1)S(1)}, u32[]{:S(2)}, u32[]{:S(2)}) collective-permute-start(bf16[5,80,640]{2,1,0:T(8,128)(2,1)S(1)} %get-tuple-element.14), channel_id=1, source_target_pairs={{0,16},{16,0},{64,80},{80,64},{128,144},{144,128},{192,208},{208,1... | collective-permute-start | bytes 1536008 | tf_op jit(solution)/shard_map/ppermute | solution.py:292
  82.4 20.7 %collective-permute-start.1 = (bf16[5,80,640]{2,1,0:T(8,128)(2,1)S(1)}, bf16[5,80,640]{2,1,0:T(8,128)(2,1)S(1)}, u32[]{:S(2)}, u32[]{:S(2)}) collective-permute-start(bf16[5,80,640]{2,1,0:T(8,128)(2,1)S(1)} %get-tuple-element.15), channel_id=1, source_target_pairs={{0,64},{16,80},{64,128},{80,144},{128,192},{144,208},{192,0},{208,... | collective-permute-start | bytes 1536008 | tf_op jit(solution)/shard_map/ppermute | solution.py:292
  83.9 29.7 %collective-permute-start.2 = (bf16[5,80,640]{2,1,0:T(8,128)(2,1)}, bf16[5,80,640]{2,1,0:T(8,128)(2,1)S(1)}, u32[]{:S(2)}, u32[]{:S(2)}) collective-permute-start(bf16[5,80,640]{2,1,0:T(8,128)(2,1)} %get-tuple-element.16), channel_id=1, source_target_pairs={{0,80},{16,64},{64,144},{80,128},{128,208},{144,192},{192,16},{208... | collective-permute-start | bytes 1536008 | tf_op jit(solution)/shard_map/ppermute | solution.py:292
  85.1 28.6 %collective-permute-start.3 = (bf16[5,80,640]{2,1,0:T(8,128)(2,1)}, bf16[5,80,640]{2,1,0:T(8,128)(2,1)S(1)}, u32[]{:S(2)}, u32[]{:S(2)}) collective-permute-start(bf16[5,80,640]{2,1,0:T(8,128)(2,1)} %get-tuple-element.17), channel_id=1, source_target_pairs={{0,128},{16,144},{64,192},{80,208},{128,0},{144,16},{192,64},{208,... | collective-permute-start | bytes 1536008 | tf_op jit(solution)/shard_map/ppermute | solution.py:292
  86.5 41.2 %collective-permute-start.4 = (bf16[5,80,640]{2,1,0:T(8,128)(2,1)}, bf16[5,80,640]{2,1,0:T(8,128)(2,1)}, u32[]{:S(2)}, u32[]{:S(2)}) collective-permute-start(bf16[5,80,640]{2,1,0:T(8,128)(2,1)} %get-tuple-element.18), channel_id=1, source_target_pairs={{0,144},{16,128},{64,208},{80,192},{128,16},{144,0},{192,80},{208,... | collective-permute-start | bytes 1536008 | tf_op jit(solution)/shard_map/ppermute | solution.py:292
  102.8 35.7 %collective-permute-start.5 = (bf16[5,80,640]{2,1,0:T(8,128)(2,1)}, bf16[5,80,640]{2,1,0:T(8,128)(2,1)}, u32[]{:S(2)}, u32[]{:S(2)}) collective-permute-start(bf16[5,80,640]{2,1,0:T(8,128)(2,1)} %get-tuple-element.19), channel_id=1, source_target_pairs={{0,192},{16,208},{64,0},{80,16},{128,64},{144,80},{192,128},{208,1... | collective-permute-start | bytes 1536008 | tf_op jit(solution)/shard_map/ppermute | solution.py:292
  103.1 35.4 %collective-permute-start.6 = (bf16[5,80,640]{2,1,0:T(8,128)(2,1)}, bf16[5,80,640]{2,1,0:T(8,128)(2,1)}, u32[]{:S(2)}, u32[]{:S(2)}) collective-permute-start(bf16[5,80,640]{2,1,0:T(8,128)(2,1)} %get-tuple-element.20), channel_id=1, source_target_pairs={{0,208},{16,192},{64,16},{80,0},{128,80},{144,64},{192,144},{208,1... | collective-permute-start | bytes 1536008 | tf_op jit(solution)/shard_map/ppermute | solution.py:292

commit v2 on v1

--- a/solution.py
+++ b/solution.py
@@ -51,103 +51,103 @@
 
 
 def grad_kernel(rate_ref, grad_ref, state_ref, out_ref):
-    w = pl.program_id(0)
-    lons = grad_ref.shape[-1]
-    for c in range(4):
-        slope = 1.0 - jnp.tanh(state_ref[c, 0].astype(jnp.float32)) ** 2
-        value = grad_ref[c, 0].astype(jnp.float32) * (1.0 + rate_ref[8 * c + w] * slope)
-        out_ref[0, c // 2, :, pl.ds((c % 2) * lons, lons)] = value.astype(jnp.bfloat16)
+    lons, waves = grad_ref.shape[-1], grad_ref.shape[1]
+    for v in range(waves):
+        w = pl.program_id(0) * waves + v
+        for c in range(4):
+            slope = 1.0 - jnp.tanh(state_ref[c, v].astype(jnp.float32)) ** 2
+            value = grad_ref[c, v].astype(jnp.float32) * (1.0 + rate_ref[8 * c + w] * slope)
+            out_ref[v, c // 2, :, pl.ds((c % 2) * lons, lons)] = value.astype(jnp.bfloat16)
 
 
 def gradient(rate, grad, state):
     chans, lats, lons = grad.shape
     four = (4, chans // 4, lats, lons)
-    spec = pl.BlockSpec((4, 1, lats, lons), lambda w: (0, w, 0, 0))
+    spec = pl.BlockSpec((4, 2, lats, lons), lambda w: (0, w, 0, 0))
     return pl.pallas_call(
         grad_kernel,
-        grid=(8,),
+        grid=(4,),
         in_specs=[pl.BlockSpec(memory_space=pltpu.SMEM), spec, spec],
-        out_specs=pl.BlockSpec((1, 2, lats, 2 * lons), lambda w: (w, 0, 0, 0)),
+        out_specs=pl.BlockSpec((2, 2, lats, 2 * lons), lambda w: (w, 0, 0, 0)),
         out_shape=jax.ShapeDtypeStruct((8, 2, lats, 2 * lons), jnp.bfloat16),
-        compiler_params=params(),
+        compiler_params=pltpu.CompilerParams(vmem_limit_bytes=60 * 1024 * 1024),
         cost_estimate=cost(6 * grad.size, 6 * grad.size, grad.size),
         name="gradient",
     )(rate, grad.reshape(four), state.reshape(four))
 
 
 def table_kernel(coarse_cos, coarse_sin, fine_cos, fine_sin, out_ref):
-    fine = fine_cos.shape[1]
-    for j in range(coarse_cos.shape[1]):
-        cos, sin = coarse_cos[:, j : j + 1], coarse_sin[:, j : j + 1]
-        lanes = slice(j * fine, (j + 1) * fine)
-        out_ref[0, :, lanes] = (cos * fine_cos[...] - sin * fine_sin[...]).astype(jnp.bfloat16)
-        out_ref[1, :, lanes] = (-sin * fine_cos[...] - cos * fine_sin[...]).astype(jnp.bfloat16)
+    fine = fine_cos.shape[0]
+    count = fine_cos.shape[1]
+    step = out_ref.shape[0] // fine
+    for v in range(step):
+        j = pl.program_id(0) * step + v
+        cos, sin = coarse_cos[pl.ds(j, 1), :], coarse_sin[pl.ds(j, 1), :]
+        rows = slice(v * fine, (v + 1) * fine)
+        out_ref[rows, :count] = (cos * fine_cos[...] - sin * fine_sin[...]).astype(jnp.bfloat16)
+        out_ref[rows, count:] = (-sin * fine_cos[...] - cos * fine_sin[...]).astype(jnp.bfloat16)
 
 
 def wave_table(slots, lon_total, fine):
     def trig(lon):
-        index = slots[:, None] * lon[None, :] % lon_total
+        index = slots[None, :] * lon[:, None] % lon_total
         angle = index.astype(jnp.float32) * (2.0 * math.pi / lon_total)
         return jnp.cos(angle), jnp.sin(angle)
 
     coarse_cos, coarse_sin = trig(fine * jnp.arange(lon_total // fine, dtype=jnp.int32))
     fine_cos, fine_sin = trig(jnp.arange(fine, dtype=jnp.int32))
     scale = 1.0 / math.sqrt(lon_total)
-    count, block = slots.shape[0], 128
-    coarse_spec = pl.BlockSpec((block, lon_total // fine), lambda s: (s, 0))
-    fine_spec = pl.BlockSpec((block, fine), lambda s: (s, 0))
+    count, steps = slots.shape[0], 5
+    whole = lambda a: pl.BlockSpec(a.shape, lambda j: (0, 0))
     return pl.pallas_call(
         table_kernel,
-        grid=(count // block,),
-        in_specs=[coarse_spec, coarse_spec, fine_spec, fine_spec],
-        out_specs=pl.BlockSpec((2, block, lon_total), lambda s: (0, s, 0)),
-        out_shape=jax.ShapeDtypeStruct((2, count, lon_total), jnp.bfloat16),
+        grid=(steps,),
+        in_specs=[whole(a) for a in (coarse_cos, coarse_sin, fine_cos, fine_sin)],
+        out_specs=pl.BlockSpec((lon_total // steps, 2 * count), lambda j: (j, 0)),
+        out_shape=jax.ShapeDtypeStruct((lon_total, 2 * count), jnp.bfloat16),
         compiler_params=params(),
         cost_estimate=cost(6 * count * lon_total, 4 * count * lon_total),
         name="wave_table",
     )(coarse_cos * scale, coarse_sin * scale, fine_cos, fine_sin)
 
 
-def fourier_kernel(grad_ref, table_ref, out_ref, rows):
+def fourier_kernel(grad_ref, table_ref, *refs):
+    out_ref, rows = refs[-2:]
     lats, lons = grad_ref.shape[2], grad_ref.shape[3] // 2
-
-    @pl.when(pl.program_id(0) == 0)
-    def _():
-        for w in range(8):
-            for c in range(4):
-                rows[pl.ds(c * lats, lats), pl.ds(w * lons, lons)] = grad_ref[
-                    w, c // 2, :, pl.ds((c % 2) * lons, lons)
-                ]
-
-    width = 4 * lats
-    for p in range(2):
-        value = lax.dot_general(
-            table_ref[p], rows[...], (((1,), (1,)), ((), ())), preferred_element_type=jnp.float32
-        )
-        out_ref[:, pl.ds(p * width, width)] = value.astype(jnp.bfloat16)
-
-
-def fourier_rows(grad, table):
+    for w in range(8):
+        for c in range(4):
+            rows[pl.ds(c * lats, lats), pl.ds(w * lons, lons)] = grad_ref[
+                w, c // 2, :, pl.ds((c % 2) * lons, lons)
+            ]
+    width, slots = 4 * lats, out_ref.shape[0]
+    for t in range(2 * slots // 256):
+        value = jnp.dot(
+            rows[...], table_ref[:, 256 * t : 256 * t + 256], preferred_element_type=jnp.float32
+        ).T
+        for part in range(2):
+            p, first = divmod(256 * t + 128 * part, slots)
+            out_ref[pl.ds(first, 128), pl.ds(p * width, width)] = value[
+                128 * part : 128 * part + 128
+            ].astype(jnp.bfloat16)
+
+
+def fourier_rows(grad, table, early):
     _, _, lats, lons2 = grad.shape
-    slots, lon_total = table.shape[1:]
-    block = 128
+    lon_total, slots = table.shape[0], table.shape[1] // 2
+    vmem = pl.BlockSpec(memory_space=pltpu.VMEM)
     return pl.pallas_call(
         fourier_kernel,
-        grid=(slots // block,),
-        in_specs=[
-            pl.BlockSpec(grad.shape, lambda s: (0, 0, 0, 0)),
-            pl.BlockSpec((2, block, lon_total), lambda s: (0, s, 0)),
-        ],
-        out_specs=pl.BlockSpec((block, 8 * lats), lambda s: (s, 0)),
+        in_specs=[vmem, vmem] + [pl.BlockSpec(memory_space=pl.ANY)] * len(early),
         out_shape=jax.ShapeDtypeStruct((slots, 8 * lats), jnp.bfloat16),
         scratch_shapes=[pltpu.VMEM((4 * lats, lon_total), jnp.bfloat16)],
         compiler_params=params(),
         cost_estimate=cost(2 * 2 * slots * lon_total * 4 * lats, 2 * (grad.size + table.size)),
         name="fourier_rows",
-    )(grad, table)
-
-
-def turn_kernel(in_ref, out_ref, rows):
+    )(grad, table, *early)
+
+
+def turn_kernel(in_ref, *refs):
+    out_ref, rows = refs[-2:]
     waves, slots, width = in_ref.shape
     for t in range(width // 128):
         lanes = slice(128 * t, 128 * t + 128)
@@ -159,16 +159,18 @@
             )
 
 
-def turn(fourier):
+def turn(fourier, early):
     waves, slots, width = fourier.shape
     return pl.pallas_call(
         turn_kernel,
+        in_specs=[pl.BlockSpec(memory_space=pltpu.VMEM)]
+        + [pl.BlockSpec(memory_space=pl.ANY)] * len(early),
         out_shape=jax.ShapeDtypeStruct((16, slots // 16, waves, width), jnp.bfloat16),
         scratch_shapes=[pltpu.VMEM((width // 128, waves * slots, 128), jnp.float32)],
         compiler_params=params(),
         cost_estimate=cost(0, 4 * fourier.size),
         name="turn",
-    )(fourier)
+    )(fourier, *early)
 
 
 def spectral_kernel(where_ref, slot_ref, four_ref, *refs):
@@ -291,10 +293,11 @@
         ]
         bases.append(lax.ppermute(block, ("x", "zq"), pairs))
 
+    by = dict(zip(offsets, bases))
     table = wave_table(wave_slot, lons * 8, 128)
-    fourier = fourier_rows(grad, table)
+    fourier = fourier_rows(grad, table, [by[0, 1], by[1, 0], by[3, 0]])
     fourier = lax.all_to_all(fourier.reshape(8, slot_dev, 8 * lats), "wave", 0, 0)
-    fourier = lax.all_to_all(turn(fourier), ("x", "zq", "lev"), 0, 0, tiled=True)
+    fourier = lax.all_to_all(turn(fourier, [by[1, 1], by[2, 0], by[3, 1], by[2, 1]]), ("x", "zq", "lev"), 0, 0, tiled=True)
 
     first = wave * slot_dev + 8 * lev + 2 * x + zq
     slots = jnp.take(wave_slot, first + 16 * jnp.arange(slot_dev // 16, dtype=jnp.int32))

time: 173 us -> 160 us (0.925)
  blocking collectives: 45.7 us -> 32.4 us
  local copies, waits for them, and re-layouts: 4.73 us -> 11.3 us
  Pallas kernels: 33.9 us -> 27.8 us
    all_to_all x1 -> x2, waiting for transfers between devices: 0.01 us -> 17.4 us  [the longest x1 17.4 us: local(): lax.all_to_all(turn(fourier, [by[1, 1], by[2, 0], by[3, 1], by[2, 1]]), (...]
    all_to_all x1 -> x0, blocking collectives: 16 us -> none  [local(): lax.all_to_all(fourier.reshape(8, slot_dev, 8 * lats), 'wave', 0, 0)]
    all_to_all x1, waiting for transfers between devices: 12.6 us -> 0.01 us  [local(): grad = lax.all_to_all(grad, 'wave', 0, 0)]
    unnamed x8 -> x32, local copies, waits for them, and re-layouts: 3.75 us -> 10.5 us
    ppermute x7, waiting for transfers between devices: 43.8 us -> 39.5 us  [local(): bases.append(lax.ppermute(block, ('x', 'zq'), pairs))]
    pallas_call x4, Pallas kernels: 20.9 us -> 16.9 us  [the longest x1 6.39 us: fourier_rows(): pl.pallas_call(fourier_kernel, in_specs=[vmem, vmem] + [pl.BlockSpec(memo...]
    all_to_all x1 -> x2, starting transfers between devices: 11.5 us -> 14.7 us  [the longest x1 10.2 us: local(): lax.all_to_all(turn(fourier, [by[1, 1], by[2, 0], by[3, 1], by[2, 1]]), (...]
    ppermute x7, starting transfers between devices: 13 us -> 9.88 us  [local(): bases.append(lax.ppermute(block, ('x', 'zq'), pairs))]
  transfers between devices with their start and end apart: 9 -> 10, of which waited for: 5 -> 6; matrix products, arithmetic and copies ran while one was open for 2% -> 2% of each run, Pallas kernels for 9% -> 7%
where the time goes in v2:
time: 160 us; the launch traced here: 159 us
  waiting for transfers between devices  56.9 us (36%)
  blocking collectives  32.4 us (20%)
  starting transfers between devices  29 us (18%)
  Pallas kernels  27.8 us (17%)
  local copies, waits for them, and re-layouts  11.3 us (7%)
  other arithmetic  1.69 us (1%)
    ppermute x7, waiting for transfers between devices, local(): bases.append(lax.ppermute(block, ('x', 'zq'), pairs))  39.5 us
    all_to_all x1, blocking collectives, local(): parts = lax.all_to_all(parts, ('x', 'zp', 'zq', 'lev'), 0, 0, tiled=True)  32.4 us
    all_to_all x1, waiting for transfers between devices, local(): lax.all_to_all(turn(fourier, [by[1, 1], by[2, 0], by[3, 1], by[2, 1]]), (...  17.4 us
    unnamed x32, local copies, waits for them, and re-layouts  10.5 us
    all_to_all x1, starting transfers between devices, local(): lax.all_to_all(turn(fourier, [by[1, 1], by[2, 0], by[3, 1], by[2, 1]]), (...  10.2 us
    ppermute x7, starting transfers between devices, local(): bases.append(lax.ppermute(block, ('x', 'zq'), pairs))  9.88 us
    pallas_call x1, Pallas kernels, basis_blocks(): pl.pallas_call(basis_kernel, grid_spec=pltpu.PrefetchScalarGridSpec(num_s...  7.24 us
    pallas_call x1, Pallas kernels, fourier_rows(): pl.pallas_call(fourier_kernel, in_specs=[vmem, vmem] + [pl.BlockSpec(memo...  6.39 us
  transfers between devices with their start and end apart: 10, of which 6 were waited for; matrix products, arithmetic and copies ran while one was open for 2% of the time, Pallas kernels for 7%

profile of v2, /device:TPU:2, one launch (start us, length us, event | category | flops | bytes accessed | tf_op | source)
XLA Modules:
  0.0 159.3 jit_solution(12978804244652425425)
XLA Ops:
  0.0 4.6 %gradient.1 = bf16[8,2,80,640]{3,2,1,0:T(8,128)(2,1)} custom-call(f32[32]{0:T(128)} %rate_ref.1, bf16[4,8,80,320]{3,2,1,0:T(8,128)(2,1)} %bitcast.22, bf16[4,8,80,320]{3,2,1,0:T(8,128)(2,1)} %bitcast.23), custom_call_target="tpu_custom_call" | custom-call | flops 4915200 | bytes 4915200 | tf_op jit(solution)/shard_map/gradient/pallas_call | solution.py:67
  4.6 4.5 %all-to-all-start = ((bf16[8,2,80,640]{3,2,1,0:T(8,128)(2,1)}), bf16[8,2,80,640]{3,2,1,0:T(8,128)(2,1)S(1)}, u32[]{:S(2)}, u32[]{:S(2)}) async-start(bf16[8,2,80,640]{3,2,1,0:T(8,128)(2,1)} %gradient.1), calls=%async_computation | async-start | bytes 3276800 | tf_op jit(solution)/shard_map/all_to_all | solution.py:286
  9.1 0.1 stack.80.where_ref
  9.2 7.2 %basis_blocks.1 = (bf16[5,80,640]{2,1,0:T(8,128)(2,1)S(1)}, bf16[5,80,640]{2,1,0:T(8,128)(2,1)S(1)}, bf16[5,80,640]{2,1,0:T(8,128)(2,1)S(1)}, bf16[5,80,640]{2,1...) custom-call(s32[9]{0:T(128)S(1)} %stack.80.where_ref, ...), custom_call_target="tpu_custom_call" | custom-call | bytes 12288000 | tf_op jit(solution)/shard_map/basis_blocks/pallas_call | solution.py:37
  16.4 0.0 copy-start.9
  16.4 0.8 copy-done.9
  17.3 2.0 %collective-permute-start = (bf16[5,80,640]{2,1,0:T(8,128)(2,1)S(1)}, bf16[5,80,640]{2,1,0:T(8,128)(2,1)S(1)}, u32[]{:S(2)}, u32[]{:S(2)}) collective-permute-start(bf16[5,80,640]{2,1,0:T(8,128)(2,1)S(1)} %get-tuple-element.13), channel_id=1, source_target_pairs={{0,16},{16,0},{64,80},{80,64},{128,144},{144,128},{192,208},{208,1... | collective-permute-start | bytes 1536008 | tf_op jit(solution)/shard_map/ppermute | solution.py:294
  19.3 1.5 collective-permute-start.1
  20.8 0.5 collective-permute-start.2
  21.3 0.0 copy-done.15
  21.3 0.3 sine_multiply_fusion
  21.6 1.3 fusion.4
  23.0 4.4 %wave_table.1.table_ref = bf16[2560,1280]{1,0:T(8,128)(2,1)} custom-call(f32[20,640]{1,0:T(8,128)S(1)} %get-tuple-element.22.coarse_cos, f32[20,640]{1,0:T(8,128)S(1)} %get-tuple-element.21.coarse_sin, f32[128,640]{1,0:T(8,128)S(1)} %get-tuple-element.24.fine_cos, f32[128,640]{1,0:T(8,128)S(1)} %get-tuple-element.23.fine_sin), custom_call_target="tpu_custom_call" | custom-call | flops 9830400 | bytes 6553600 | tf_op jit(solution)/shard_map/wave_table/pallas_call | solution.py:102
  27.3 0.0 copy-done.13
  27.3 0.0 copy-done.14
  27.3 4.3 %collective-permute-done.refs_0_.refs_1_ = bf16[5,80,640]{2,1,0:T(8,128)(2,1)S(1)} collective-permute-done((bf16[5,80,640]{2,1,0:T(8,128)(2,1)S(1)}, bf16[5,80,640]{2,1,0:T(8,128)(2,1)S(1)}, u32[]{:S(2)}, u32[]{:S(2)}) %collective-permute-start) | collective-permute-done | bytes 512032 | tf_op jit(solution)/shard_map/ppermute | solution.py:294
  31.6 1.5 collective-permute-done.1.refs_1_.refs_2_
  33.1 1.2 collective-permute-done.2.refs_2_.refs_6_
  34.3 0.0 all-to-all-done.grad_ref
  34.3 6.4 %fourier_rows.1 = bf16[640,640]{1,0:T(8,128)(2,1)} custom-call(bf16[8,2,80,640]{3,2,1,0:T(8,128)(2,1)S(1)} %all-to-all-done.grad_ref, bf16[2560,1280]{1,0:T(8,128)(2,1)} %wave_table.1.table_ref, bf16[5,80,640]{2,1,0:T(8,128)(2,1)S(1)} %collective-permute-done.refs_0_.refs_1_, bf16[5,80,640]{2,1,0:T(8,128)(2,1)S(1)} %collective-permute-done.1.refs_1_.refs_2_, ...), custom_call_target="tpu_custom_call" | custom-call | flops 2097152000 | bytes 8192000 | tf_op jit(solution)/shard_map/fourier_rows/pallas_call | solution.py:138
  40.7 4.4 %all-to-all-start.1 = ((bf16[8,80,640]{2,1,0:T(8,128)(2,1)}), bf16[8,80,640]{2,1,0:T(8,128)(2,1)S(1)}, u32[]{:S(2)}, u32[]{:S(2)}) async-start(bf16[8,80,640]{2,1,0:T(8,128)(2,1)} %bitcast.19), calls=%async_computation.1 | async-start | bytes 1638400 | tf_op jit(solution)/shard_map/all_to_all | solution.py:299
  45.1 1.0 collective-permute-start.3
  46.1 1.9 %collective-permute-start.4 = (bf16[5,80,640]{2,1,0:T(8,128)(2,1)}, bf16[5,80,640]{2,1,0:T(8,128)(2,1)S(1)}, u32[]{:S(2)}, u32[]{:S(2)}) collective-permute-start(bf16[5,80,640]{2,1,0:T(8,128)(2,1)} %copy-done.13), channel_id=1, source_target_pairs={{0,128},{16,144},{64,192},{80,208},{128,0},{144,16},{192,64},{208,... | collective-permute-start | bytes 1536008 | tf_op jit(solution)/shard_map/ppermute | solution.py:294
  48.0 2.9 %collective-permute-start.5 = (bf16[5,80,640]{2,1,0:T(8,128)(2,1)}, bf16[5,80,640]{2,1,0:T(8,128)(2,1)S(1)}, u32[]{:S(2)}, u32[]{:S(2)}) collective-permute-start(bf16[5,80,640]{2,1,0:T(8,128)(2,1)} %copy-done.12), channel_id=1, source_target_pairs={{0,208},{16,192},{64,16},{80,0},{128,80},{144,64},{192,144},{208,1... | collective-permute-start | bytes 1536008 | tf_op jit(solution)/shard_map/ppermute | solution.py:294
  51.0 0.0 collective-permute-start.6
  51.0 9.8 %collective-permute-done.3.refs_0_.refs_3_ = bf16[5,80,640]{2,1,0:T(8,128)(2,1)S(1)} collective-permute-done((bf16[5,80,640]{2,1,0:T(8,128)(2,1)}, bf16[5,80,640]{2,1,0:T(8,128)(2,1)S(1)}, u32[]{:S(2)}, u32[]{:S(2)}) %collective-permute-start.3) | collective-permute-done | bytes 512032 | tf_op jit(solution)/shard_map/ppermute | solution.py:294
  60.7 22.8 %collective-permute-done.4.refs_1_.refs_4_ = bf16[5,80,640]{2,1,0:T(8,128)(2,1)S(1)} collective-permute-done((bf16[5,80,640]{2,1,0:T(8,128)(2,1)}, bf16[5,80,640]{2,1,0:T(8,128)(2,1)S(1)}, u32[]{:S(2)}, u32[]{:S(2)}) %collective-permute-start.4) | collective-permute-done | bytes 512032 | tf_op jit(solution)/shard_map/ppermute | solution.py:294
  83.6 0.8 copy-done
  84.4 0.0 collective-permute-done.5.refs_2_.refs_7_
  84.4 0.8 copy-done.3
  85.2 0.0 collective-permute-done.6.refs_3_.refs_5_
  85.2 0.8 copy-done.6
  86.0 0.0 all-to-all-done.1.in_ref
  86.0 1.0 copy-done.1
  87.0 1.0 copy-done.4
  88.1 1.0 copy-done.7
  89.1 1.5 turn.1
  90.6 10.2 %all-to-all-start.2 = ((bf16[16,5,8,640]{3,2,1,0:T(8,128)(2,1)}), bf16[16,5,8,640]{3,2,1,0:T(8,128)(2,1)S(1)}, u32[]{:S(2)}, u32[]{:S(2)}) async-start(bf16[16,5,8,640]{3,2,1,0:T(8,128)(2,1)} %turn.1), calls=%async_computation.2 | async-start | bytes 1638400 | tf_op jit(solution)/shard_map/all_to_all | solution.py:300
  100.9 0.6 gather_fusion
  101.5 0.1 stack.78.where_ref
  101.6 17.4 %all-to-all-done.2.four_ref = bf16[16,5,8,640]{3,2,1,0:T(8,128)(2,1)S(1)} async-done(((bf16[16,5,8,640]{3,2,1,0:T(8,128)(2,1)}), bf16[16,5,8,640]{3,2,1,0:T(8,128)(2,1)S(1)}, u32[]{:S(2)}, u32[]{:S(2)}) %all-to-all-start.2) | async-done | bytes 819232 | tf_op jit(solution)/shard_map/all_to_all | solution.py:300
  119.0 1.0 copy-done.2
  120.1 1.0 copy-done.5
  121.1 1.0 copy-done.8
  122.1 1.0 copy-done.10
  123.2 2.0 %spectral_parts.1 = bf16[32,104,128]{2,1,0:T(8,128)(2,1)S(1)} custom-call(s32[16]{0:T(128)S(1)} %stack.78.where_ref, s32[5]{0:T(128)S(1)} %and_select_fusion.slot_ref, bf16[16,5,8,640]{3,2,1,0:T(8,128)(2,1)S(1)} %all-to-all-done.2.four_ref, bf16[5,80,640]{2,1,0:T(8,128)(2,1)S(1)} %copy-done.10, bf16[5,80,640]{2,1,0:T(8,128)(2,1)S(1)} %collective-permute-done.refs_0_.refs_1_, ...), custom_call_target="tpu_custom_call" | custom-call | flops 524288000 | bytes 4915200 | tf_op jit(solution)/shard_map/spectral_parts/pallas_call | solution.py:229
  125.2 32.4 %all_to_all.20.in_ref = bf16[32,104,128]{2,1,0:T(8,128)(2,1)S(1)} all-to-all(bf16[32,104,128]{2,1,0:T(8,128)(2,1)S(1)} %spectral_parts.1), channel_id=1, replica_groups=mesh['x'=4,'zp'=2,'zq'=2,'wave'=8,'lev'=2] {'x','zp','zq','lev'}, dimensions={0} | all-to-all | bytes 1703936 | tf_op jit(solution)/shard_map/all_to_all | solution.py:305
  157.6 1.7 %finish.1 = f32[2560,80]{1,0:T(8,128)} custom-call(bf16[32,104,128]{2,1,0:T(8,128)(2,1)S(1)} %all_to_all.20.in_ref), custom_call_target="tpu_custom_call" | custom-call | flops 425984 | bytes 2162688 | tf_op jit(solution)/shard_map/finish/pallas_call | solution.py:264
  (21 shorter events, 0.1 us)
Async XLA Ops:
  4.6 29.7 %all-to-all-start = ((bf16[8,2,80,640]{3,2,1,0:T(8,128)(2,1)}), bf16[8,2,80,640]{3,2,1,0:T(8,128)(2,1)S(1)}, u32[]{:S(2)}, u32[]{:S(2)}) async-start(bf16[8,2,80,640]{3,2,1,0:T(8,128)(2,1)} %gradient.1), calls=%async_computation | async-start | bytes 3276800 | tf_op jit(solution)/shard_map/all_to_all | solution.py:286
  9.2 12.1 %copy-start.15 = (s32[640]{0:T(1024)S(1)}, s32[640]{0:T(1024)}, u32[]{:S(2)}) copy-start(s32[640]{0:T(1024)} %param.9) | copy-start | bytes 7684
  16.4 0.8 copy-start.9
  17.3 10.1 %copy-start.11 = (bf16[5,80,640]{2,1,0:T(8,128)(2,1)}, bf16[5,80,640]{2,1,0:T(8,128)(2,1)S(1)}, u32[]{:S(2)}) copy-start(bf16[5,80,640]{2,1,0:T(8,128)(2,1)S(1)} %get-tuple-element.19) | copy-start | bytes 1536004
  17.3 10.1 %copy-start.12 = (bf16[5,80,640]{2,1,0:T(8,128)(2,1)}, bf16[5,80,640]{2,1,0:T(8,128)(2,1)S(1)}, u32[]{:S(2)}) copy-start(bf16[5,80,640]{2,1,0:T(8,128)(2,1)S(1)} %get-tuple-element.18) | copy-start | bytes 1536004
  17.3 10.1 %copy-start.13 = (bf16[5,80,640]{2,1,0:T(8,128)(2,1)}, bf16[5,80,640]{2,1,0:T(8,128)(2,1)S(1)}, u32[]{:S(2)}) copy-start(bf16[5,80,640]{2,1,0:T(8,128)(2,1)S(1)} %get-tuple-element.17) | copy-start | bytes 1536004
  17.3 10.1 %copy-start.14 = (bf16[5,80,640]{2,1,0:T(8,128)(2,1)}, bf16[5,80,640]{2,1,0:T(8,128)(2,1)S(1)}, u32[]{:S(2)}) copy-start(bf16[5,80,640]{2,1,0:T(8,128)(2,1)S(1)} %get-tuple-element.16) | copy-start | bytes 1536004
  17.3 14.3 %collective-permute-start = (bf16[5,80,640]{2,1,0:T(8,128)(2,1)S(1)}, bf16[5,80,640]{2,1,0:T(8,128)(2,1)S(1)}, u32[]{:S(2)}, u32[]{:S(2)}) collective-permute-start(bf16[5,80,640]{2,1,0:T(8,128)(2,1)S(1)} %get-tuple-element.13), channel_id=1, source_target_pairs={{0,16},{16,0},{64,80},{80,64},{128,144},{144,128},{192,208},{208,1... | collective-permute-start | bytes 1536008 | tf_op jit(solution)/shard_map/ppermute | solution.py:294
  19.3 13.8 %collective-permute-start.1 = (bf16[5,80,640]{2,1,0:T(8,128)(2,1)S(1)}, bf16[5,80,640]{2,1,0:T(8,128)(2,1)S(1)}, u32[]{:S(2)}, u32[]{:S(2)}) collective-permute-start(bf16[5,80,640]{2,1,0:T(8,128)(2,1)S(1)} %get-tuple-element.14), channel_id=1, source_target_pairs={{0,64},{16,80},{64,128},{80,144},{128,192},{144,208},{192,0},{208,... | collective-permute-start | bytes 1536008 | tf_op jit(solution)/shard_map/ppermute | solution.py:294
  20.8 13.5 %collective-permute-start.2 = (bf16[5,80,640]{2,1,0:T(8,128)(2,1)S(1)}, bf16[5,80,640]{2,1,0:T(8,128)(2,1)S(1)}, u32[]{:S(2)}, u32[]{:S(2)}) collective-permute-start(bf16[5,80,640]{2,1,0:T(8,128)(2,1)S(1)} %get-tuple-element.15), channel_id=1, source_target_pairs={{0,192},{16,208},{64,0},{80,16},{128,64},{144,80},{192,128},{208,1... | collective-permute-start | bytes 1536008 | tf_op jit(solution)/shard_map/ppermute | solution.py:294
  40.7 45.3 %all-to-all-start.1 = ((bf16[8,80,640]{2,1,0:T(8,128)(2,1)}), bf16[8,80,640]{2,1,0:T(8,128)(2,1)S(1)}, u32[]{:S(2)}, u32[]{:S(2)}) async-start(bf16[8,80,640]{2,1,0:T(8,128)(2,1)} %bitcast.19), calls=%async_computation.1 | async-start | bytes 1638400 | tf_op jit(solution)/shard_map/all_to_all | solution.py:299
  45.1 15.6 %collective-permute-start.3 = (bf16[5,80,640]{2,1,0:T(8,128)(2,1)}, bf16[5,80,640]{2,1,0:T(8,128)(2,1)S(1)}, u32[]{:S(2)}, u32[]{:S(2)}) collective-permute-start(bf16[5,80,640]{2,1,0:T(8,128)(2,1)} %copy-done.14), channel_id=1, source_target_pairs={{0,80},{16,64},{64,144},{80,128},{128,208},{144,192},{192,16},{208... | collective-permute-start | bytes 1536008 | tf_op jit(solution)/shard_map/ppermute | solution.py:294
  46.1 37.4 %collective-permute-start.4 = (bf16[5,80,640]{2,1,0:T(8,128)(2,1)}, bf16[5,80,640]{2,1,0:T(8,128)(2,1)S(1)}, u32[]{:S(2)}, u32[]{:S(2)}) collective-permute-start(bf16[5,80,640]{2,1,0:T(8,128)(2,1)} %copy-done.13), channel_id=1, source_target_pairs={{0,128},{16,144},{64,192},{80,208},{128,0},{144,16},{192,64},{208,... | collective-permute-start | bytes 1536008 | tf_op jit(solution)/shard_map/ppermute | solution.py:294
  48.0 36.3 %collective-permute-start.5 = (bf16[5,80,640]{2,1,0:T(8,128)(2,1)}, bf16[5,80,640]{2,1,0:T(8,128)(2,1)S(1)}, u32[]{:S(2)}, u32[]{:S(2)}) collective-permute-start(bf16[5,80,640]{2,1,0:T(8,128)(2,1)} %copy-done.12), channel_id=1, source_target_pairs={{0,208},{16,192},{64,16},{80,0},{128,80},{144,64},{192,144},{208,1... | collective-permute-start | bytes 1536008 | tf_op jit(solution)/shard_map/ppermute | solution.py:294
  51.0 34.2 %collective-permute-start.6 = (bf16[5,80,640]{2,1,0:T(8,128)(2,1)}, bf16[5,80,640]{2,1,0:T(8,128)(2,1)S(1)}, u32[]{:S(2)}, u32[]{:S(2)}) collective-permute-start(bf16[5,80,640]{2,1,0:T(8,128)(2,1)} %copy-done.11), channel_id=1, source_target_pairs={{0,144},{16,128},{64,208},{80,192},{128,16},{144,0},{192,80},{208,... | collective-permute-start | bytes 1536008 | tf_op jit(solution)/shard_map/ppermute | solution.py:294
  83.6 0.8 copy-start
  84.4 0.8 copy-start.3
  85.2 0.8 copy-start.6
  86.0 1.0 copy-start.1
  87.0 1.0 copy-start.4
  88.1 1.0 copy-start.7
  90.6 28.4 %all-to-all-start.2 = ((bf16[16,5,8,640]{3,2,1,0:T(8,128)(2,1)}), bf16[16,5,8,640]{3,2,1,0:T(8,128)(2,1)S(1)}, u32[]{:S(2)}, u32[]{:S(2)}) async-start(bf16[16,5,8,640]{3,2,1,0:T(8,128)(2,1)} %turn.1), calls=%async_computation.2 | async-start | bytes 1638400 | tf_op jit(solution)/shard_map/all_to_all | solution.py:300
  119.0 1.0 copy-start.2
  120.1 1.0 copy-start.5
  121.1 1.0 copy-start.8
  122.1 1.0 copy-start.10

commit v3 on v2

v3 whole, which is shorter than its diff:
```python
import math

import jax
import jax.numpy as jnp
from jax import lax
from jax.experimental import pallas as pl
from jax.experimental.pallas import tpu as pltpu
from jax.sharding import Mesh, PartitionSpec as P

def params(mib):
    return pltpu.CompilerParams(vmem_limit_bytes=mib * 1024 * 1024)


def cost(flops, moved, trans=0):
    return pl.CostEstimate(flops=flops, bytes_accessed=moved, transcendentals=trans)


def basis_kernel(lev_ref, basis_ref, out_ref):
    lats, _, degs = basis_ref.shape
    row = lax.broadcasted_iota(jnp.int32, (128, 128), 0)
    col = lax.broadcasted_iota(jnp.int32, (128, 128), 1)
    swap = (col == row % 16 * 8 + row // 16).astype(jnp.bfloat16)
    for g in range(lats // 16):
        block = basis_ref[16 * g : 16 * g + 16].astype(jnp.float32).reshape(128, degs)
        turned = jnp.dot(swap, block.astype(jnp.bfloat16), preferred_element_type=jnp.float32)
        out_ref[:, 0, 16 * g : 16 * g + 16, :] = turned.astype(jnp.bfloat16).reshape(8, 16, degs)


def basis_blocks(lev, basis):
    lats, slots, degs = basis.shape
    steps = slots // 16
    return pl.pallas_call(
        basis_kernel,
        grid_spec=pltpu.PrefetchScalarGridSpec(
            num_scalar_prefetch=1,
            grid=(steps,),
            in_specs=[pl.BlockSpec((lats, 8, degs), lambda b, lev: (0, 2 * b + lev[0], 0))],
            out_specs=pl.BlockSpec((8, 1, lats, degs), lambda b, lev: (0, b, 0, 0)),
        ),
        out_shape=jax.ShapeDtypeStruct((8, steps, lats, degs), jnp.bfloat16),
        compiler_params=params(60),
        cost_estimate=cost(0, 2 * lats * slots * degs),
        name="basis_blocks",
    )(lev, basis)


def grad_kernel(wave_ref, rate_ref, grad_hbm, state_hbm, _, *refs):
    outs, (grad_buf, state_buf, sems) = refs[:8], refs[8:]
    lons = grad_hbm.shape[-1]
    copies = []
    for k in range(8):
        to = wave_ref[k]
        copies.append(pltpu.make_async_copy(grad_hbm.at[:, to], grad_buf.at[k], sems.at[0, k]))
        copies.append(pltpu.make_async_copy(state_hbm.at[:, to], state_buf.at[k], sems.at[1, k]))
    for copy in copies:
        copy.start()
    for k in range(8):
        copies[2 * k].wait()
        copies[2 * k + 1].wait()
        for c in range(4):
            slope = 1.0 - jnp.tanh(state_buf[k, c].astype(jnp.float32)) ** 2
            rate = rate_ref[8 * c + wave_ref[k]]
            value = grad_buf[k, c].astype(jnp.float32) * (1.0 + rate * slope)
            outs[k][c // 2, :, pl.ds((c % 2) * lons, lons)] = value.astype(jnp.bfloat16)


def gradient(to, rate, grad, state, after):
    chans, lats, lons = grad.shape
    four = (4, chans // 4, lats, lons)
    smem, hbm = pl.BlockSpec(memory_space=pltpu.SMEM), pl.BlockSpec(memory_space=pltpu.HBM)
    buffer = pltpu.VMEM((8, 4, lats, lons), jnp.bfloat16)
    return pl.pallas_call(
        grad_kernel,
        in_specs=[smem, smem, hbm, hbm, pl.BlockSpec(memory_space=pl.ANY)],
        out_shape=[jax.ShapeDtypeStruct((2, lats, 2 * lons), jnp.bfloat16)] * 8,
        scratch_shapes=[buffer, buffer, pltpu.SemaphoreType.DMA((2, 8))],
        compiler_params=params(12),
        cost_estimate=cost(6 * grad.size, 6 * grad.size, grad.size),
        name="gradient",
    )(to, rate, grad.reshape(four), state.reshape(four), after)


def table_kernel(coarse_cos, coarse_sin, fine_cos, fine_sin, out_ref):
    fine = fine_cos.shape[0]
    for j in range(coarse_cos.shape[0]):
        cos, sin = coarse_cos[j : j + 1, :], coarse_sin[j : j + 1, :]
        out_ref[0, j * fine : (j + 1) * fine, :] = (
            cos * fine_cos[...] - sin * fine_sin[...]
        ).astype(jnp.bfloat16)


def wave_table(slots, blocks, lons, fine):
    lon_total = 8 * lons
    quarter = jnp.array([0, lon_total // 4], jnp.int32)[None, :, None]
    phase = jnp.broadcast_to(quarter, (8, 2, slots.shape[1])).reshape(1, -1)
    slot = jnp.broadcast_to(slots[:, None, :], (8, 2, slots.shape[1])).reshape(1, -1)

    def trig(lon, shift):
        index = (slot * lon[:, None] + shift) % lon_total
        angle = index.astype(jnp.float32) * (2.0 * math.pi / lon_total)
        return jnp.cos(angle), jnp.sin(angle)

    starts = blocks[:, None] * lons + fine * jnp.arange(lons // fine, dtype=jnp.int32)[None, :]
    coarse_cos, coarse_sin = trig(starts.reshape(-1), 0)
    fine_cos, fine_sin = trig(jnp.arange(fine, dtype=jnp.int32), phase)
    scale = 1.0 / math.sqrt(lon_total)
    columns = slot.shape[1]
    part = lambda a: pl.BlockSpec((a.shape[0], 256), lambda j: (0, j))
    return pl.pallas_call(
        table_kernel,
        grid=(columns // 256,),
        in_specs=[part(a) for a in (coarse_cos, coarse_sin, fine_cos, fine_sin)],
        out_specs=pl.BlockSpec((1, lon_total, 256), lambda j: (j, 0, 0)),
        out_shape=jax.ShapeDtypeStruct((columns // 256, lon_total, 256), jnp.bfloat16),
        compiler_params=params(12),
        cost_estimate=cost(3 * columns * lon_total, 2 * columns * lon_total),
        name="wave_table",
    )(coarse_cos * scale, coarse_sin * scale, fine_cos, fine_sin)


def fourier_kernel(table_ref, *refs):
    grads, outs, rows = refs[:8], refs[8:16], refs[16]
    lats, lons = grads[0].shape[1], grads[0].shape[2] // 2
    for k in range(8):
        for c in range(4):
            rows[pl.ds(c * lats, lats), pl.ds(k * lons, lons)] = grads[k][
                c // 2, :, pl.ds((c % 2) * lons, lons)
            ]
    width, slots = 4 * lats, outs[0].shape[0]
    for step in range(16 * slots // 256):
        value = jnp.dot(rows[...], table_ref[step], preferred_element_type=jnp.float32).T
        first, stop = 256 * step, 256 * step + 256
        for kp in range(first // slots, -(-stop // slots)):
            low, high = max(first, kp * slots), min(stop, (kp + 1) * slots)
            outs[kp // 2][low - kp * slots : high - kp * slots, pl.ds(kp % 2 * width, width)] = (
                value[low - first : high - first].astype(jnp.bfloat16)
            )


def fourier_rows(table, grads):
    _, lats, lons2 = grads[0].shape
    steps, lon_total, _ = table.shape
    slots = steps * 256 // 16
    return pl.pallas_call(
        fourier_kernel,
        in_specs=[pl.BlockSpec(memory_space=pltpu.VMEM)] * 9,
        out_shape=[jax.ShapeDtypeStruct((slots, 8 * lats), jnp.bfloat16)] * 8,
        scratch_shapes=[pltpu.VMEM((4 * lats, lon_total), jnp.bfloat16)],
        compiler_params=params(24),
        cost_estimate=cost(2 * steps * 256 * lon_total * 4 * lats, 2 * table.size),
        name="fourier_rows",
    )(table, *grads)


def turn_kernel(wave_ref, _, *refs):
    blocks, (out_ref, rows) = refs[:8], refs[8:]
    slots, width = blocks[0].shape
    for t in range(width // 128):
        lanes = slice(128 * t, 128 * t + 128)
        for k in range(8):
            start = pl.multiple_of(wave_ref[k] * slots, 8)
            rows[t, pl.ds(start, slots), :] = blocks[k][:, lanes].astype(jnp.float32)
        for s in range(slots):
            b, lev, r = s // 16, s // 8 % 2, s % 8
            out_ref[2 * r + lev, b, :, lanes] = rows[t, pl.ds(s, 8, stride=slots), :].astype(
                jnp.bfloat16
            )


def turn(waves, after, blocks):
    slots, width = blocks[0].shape
    vmem = pl.BlockSpec(memory_space=pltpu.VMEM)
    return pl.pallas_call(
        turn_kernel,
        in_specs=[pl.BlockSpec(memory_space=pltpu.SMEM), pl.BlockSpec(memory_space=pl.ANY)]
        + [vmem] * 8,
        out_shape=jax.ShapeDtypeStruct((16, slots // 16, 8, width), jnp.bfloat16),
        scratch_shapes=[pltpu.VMEM((width // 128, 8 * slots, 128), jnp.float32)],
        compiler_params=params(12),
        cost_estimate=cost(0, 32 * blocks[0].size),
        name="turn",
    )(waves, after, *blocks)


def spectral_kernel(slot_ref, four_hbm, basis_hbm, out_ref, four_ref, basis, left, total, sems):
    steps, _, lats, degs = basis.shape
    deg_dev = degs // 16
    copies = [
        pltpu.make_async_copy(basis_hbm.at[:, b], basis.at[b], sems.at[b]) for b in range(steps)
    ]
    fetch = pltpu.make_async_copy(four_hbm, four_ref, sems.at[steps])
    fetch.start()
    for copy in copies:
        copy.start()
    fetch.wait()

    def summed(b):
        for q in range(8):
            for lev in range(2):
                block = four_ref[2 * q + lev, b].astype(jnp.float32)
                for seg in range(8):
                    left[pl.ds(64 * lev + 8 * seg, 8), pl.ds(q * lats, lats)] = block[
                        :, seg * lats : (seg + 1) * lats
                    ]
        copies[b].wait()
        value = jnp.dot(
            left[...].astype(jnp.bfloat16),
            basis[b].reshape(8 * lats, degs),
            preferred_element_type=jnp.float32,
        )
        degree = lax.broadcasted_iota(jnp.int32, value.shape, 1)
        return jnp.where(degree >= slot_ref[b], value, 0.0)

    for k in range(2):
        even, odd = summed(2 * k), summed(2 * k + 1)
        for lev in range(2):
            rows = slice(64 * lev, 64 * lev + 64)
            both = jnp.concatenate([even[rows], odd[rows]], 0).T
            for a in range(16):
                out_ref[2 * a + lev, pl.ds(k * deg_dev, deg_dev)] = both[
                    a * deg_dev : (a + 1) * deg_dev
                ].astype(jnp.bfloat16)
    total[...] = summed(4).T
    half = deg_dev // 2
    even = total[pl.ds(0, degs // 2, stride=2), :]
    odd = total[pl.ds(1, degs // 2, stride=2), :]
    low = lax.broadcasted_iota(jnp.int32, even.shape, 1) < 64
    pair = (
        jnp.where(low, even, pltpu.roll(odd, 64, 1)),
        jnp.where(low, pltpu.roll(even, 64, 1), odd),
    )
    for a in range(16):
        for lev in range(2):
            out_ref[2 * a + lev, pl.ds(2 * deg_dev, half)] = pair[lev][
                a * half : (a + 1) * half
            ].astype(jnp.bfloat16)
    rows = 5 * half
    for a in range(32):
        out_ref[a, pl.ds(rows, out_ref.shape[1] - rows)] = jnp.zeros(
            (out_ref.shape[1] - rows, 128), jnp.bfloat16
        )


def spectral_parts(slots, fourier, basis):
    _, steps, lats, degs = basis.shape
    hbm = pl.BlockSpec(memory_space=pl.ANY)
    return pl.pallas_call(
        spectral_kernel,
        in_specs=[pl.BlockSpec(memory_space=pltpu.SMEM), hbm, hbm],
        out_shape=jax.ShapeDtypeStruct((32, 104, 128), jnp.bfloat16),
        scratch_shapes=[
            pltpu.VMEM(fourier.shape, jnp.bfloat16),
            pltpu.VMEM((steps, 8, lats, degs), jnp.bfloat16),
            pltpu.VMEM((128, 8 * lats), jnp.float32),
            pltpu.VMEM((degs, 128), jnp.float32),
            pltpu.SemaphoreType.DMA((steps + 1,)),
        ],
        compiler_params=params(16),
        cost_estimate=cost(5 * 2 * 128 * 8 * lats * degs, 2 * basis.size + 2 * fourier.size),
        name="spectral_parts",
    )(slots, fourier, basis)


def finish_kernel(in_ref, out_ref, rows):
    depth = in_ref.shape[1]
    for x in range(4):
        for zq in range(2):
            for lev in range(2):
                first = in_ref[8 * x + 2 * zq + lev].astype(jnp.float32)
                second = in_ref[8 * x + 4 + 2 * zq + lev].astype(jnp.float32)
                rows[pl.ds((8 * lev + 2 * x + zq) * depth, depth), :] = first + second
    low = lax.broadcasted_iota(jnp.int32, (16, 128), 1) < 64
    for n in range(0, 40, 2):
        parts = []
        for k in range(2):
            one = rows[pl.ds(40 * k + n, 16, stride=depth), :]
            two = rows[pl.ds(40 * k + n + 1, 16, stride=depth), :]
            parts.append(jnp.where(low, one, pltpu.roll(two, 64, 1)))
            parts.append(jnp.where(low, pltpu.roll(one, 64, 1), two))
        parts.append(rows[pl.ds(80 + n // 2, 16, stride=depth), :])
        out_ref[pl.ds(64 * n, 128), :] = jnp.concatenate(parts, 0).T


def finish(received):
    return pl.pallas_call(
        finish_kernel,
        out_shape=jax.ShapeDtypeStruct((40 * 64, 80), jnp.float32),
        scratch_shapes=[pltpu.VMEM((16 * received.shape[1], 128), jnp.float32)],
        compiler_params=params(12),
        cost_estimate=cost(received.size, 2 * received.size + 4 * 40 * 64 * 128),
        name="finish",
    )(received)


def local(out_grad, grid_state, tend_rate, legendre_basis, wave_slot):
    lats, lons = out_grad.shape[1:]
    slot_dev, degs = legendre_basis.shape[1:]
    x, zq = lax.axis_index("x"), lax.axis_index("zq")
    wave, lev = lax.axis_index("wave"), lax.axis_index("lev")

    partner = wave ^ jnp.arange(8, dtype=jnp.int32)

    def swapped(blocks):
        return [blocks[0]] + [
            lax.ppermute(blocks[k], "wave", [(w, w ^ k) for w in range(8)]) for k in range(1, 8)
        ]

    basis = basis_blocks(lev.astype(jnp.int32)[None], legendre_basis)
    grads = gradient(partner, tend_rate, out_grad, grid_state, basis)
    basis = lax.all_to_all(basis, ("x", "zq"), 0, 0, tiled=True)
    grads = swapped(grads)
    table = wave_table(wave_slot.reshape(8, slot_dev)[partner], partner, lons, 64)
    blocks = swapped(fourier_rows(table, grads))
    fourier = lax.all_to_all(turn(partner, basis, blocks), ("x", "zq", "lev"), 0, 0, tiled=True)

    first = wave * slot_dev + 8 * lev + 2 * x + zq
    slots = jnp.take(wave_slot, first + 16 * jnp.arange(slot_dev // 16, dtype=jnp.int32))
    parts = spectral_parts(slots, fourier, basis)
    parts = lax.all_to_all(parts, ("x", "zp", "zq", "lev"), 0, 0, tiled=True)
    return finish(parts).reshape(degs // 16, 2, 32, slot_dev)


def solution(mesh):
    fine = Mesh(
        mesh.devices.reshape(4, 2, 2, *mesh.devices.shape[1:]), ("x", "zp", "zq", "wave", "lev")
    )
    lat = ("x", "zp", "zq")
    in_specs = (P("lev", lat, "wave"), P("lev", lat, "wave"), P("lev"), P(lat, "wave", None), P())
    out_specs = P(lat, None, "lev", "wave")
    return jax.shard_map(local, mesh=fine, in_specs=in_specs, out_specs=out_specs, check_vma=False)
```

time: 160 us -> 137 us (0.86)
  waiting for transfers between devices: 56.9 us -> 40.6 us
  local copies, waits for them, and re-layouts: 11.3 us -> 5.28 us
  Pallas kernels: 27.8 us -> 22.6 us
  starting transfers between devices: 29 us -> 32.9 us
    ppermute x7 -> x14, waiting for transfers between devices: 39.5 us -> 21.8 us  [swapped(): lax.ppermute(blocks[k], 'wave', [(w, w ^ k) for w in range(8)])]
    unnamed x32 -> x10, local copies, waits for them, and re-layouts: 10.5 us -> 3.71 us
    ppermute x7 -> x14, starting transfers between devices: 9.88 us -> 16 us  [swapped(): lax.ppermute(blocks[k], 'wave', [(w, w ^ k) for w in range(8)])]
    pallas_call x5, Pallas kernels: 18.8 us -> 14.2 us  [the longest x1 4.03 us: spectral_parts(): pl.pallas_call(spectral_kernel, in_specs=[pl.BlockSpec(memory_space=pltpu...]
    all_to_all x3 -> x2, starting transfers between devices: 19.1 us -> 17 us  [the longest x1 10.1 us: local(): lax.all_to_all(turn(partner, basis, blocks), ('x', 'zq', 'lev'), 0, 0, ti...]
    all_to_all x3 -> x2, waiting for transfers between devices: 17.4 us -> 18.7 us  [the longest x1 18.7 us: local(): lax.all_to_all(turn(partner, basis, blocks), ('x', 'zq', 'lev'), 0, 0, ti...]
  transfers between devices with their start and end apart: 10 -> 16, of which waited for: 6 -> 10; matrix products, arithmetic and copies ran while one was open for 2% -> 3% of each run, Pallas kernels for 7% -> 6%
where the time goes in v3:
time: 137 us; the launch traced here: 136 us
  waiting for transfers between devices  40.6 us (30%)
  starting transfers between devices  32.9 us (24%)
  blocking collectives  32.5 us (24%)
  Pallas kernels  22.6 us (16%)
  local copies, waits for them, and re-layouts  5.28 us (4%)
  other arithmetic  2.38 us (2%)
    all_to_all x1, blocking collectives, local(): parts = lax.all_to_all(parts, ('x', 'zp', 'zq', 'lev'), 0, 0, tiled=True)  32.5 us
    ppermute x14, waiting for transfers between devices, swapped(): lax.ppermute(blocks[k], 'wave', [(w, w ^ k) for w in range(8)])  21.8 us
    all_to_all x1, waiting for transfers between devices, local(): lax.all_to_all(turn(partner, basis, blocks), ('x', 'zq', 'lev'), 0, 0, ti...  18.7 us
    ppermute x14, starting transfers between devices, swapped(): lax.ppermute(blocks[k], 'wave', [(w, w ^ k) for w in range(8)])  16 us
    all_to_all x1, starting transfers between devices, local(): lax.all_to_all(turn(partner, basis, blocks), ('x', 'zq', 'lev'), 0, 0, ti...  10.1 us
    all_to_all x1, starting transfers between devices, local(): basis = lax.all_to_all(basis, ('x', 'zq'), 0, 0, tiled=True)  6.84 us
    pallas_call x1, Pallas kernels, basis_blocks(): pl.pallas_call(basis_kernel, grid_spec=pltpu.PrefetchScalarGridSpec(num_s...  6.68 us
    pallas_call x1, Pallas kernels, spectral_parts(): pl.pallas_call(spectral_kernel, in_specs=[pl.BlockSpec(memory_space=pltpu...  4.03 us
  transfers between devices with their start and end apart: 16, of which 10 were waited for; matrix products, arithmetic and copies ran while one was open for 3% of the time, Pallas kernels for 6%

profile of v3, /device:TPU:2, one launch (start us, length us, event | category | flops | bytes accessed | tf_op | source)
XLA Modules:
  0.0 136.4 jit_solution(4514996314944277328)
XLA Ops:
  0.0 6.7 %basis_blocks.1._ = bf16[8,5,80,640]{3,2,1,0:T(8,128)(2,1)} custom-call(s32[1]{0:T(128)} %bitcast.1.lev_ref, bf16[80,80,640]{2,1,0:T(8,128)(2,1)} %basis_ref.1), custom_call_target="tpu_custom_call" | custom-call | bytes 8192000 | tf_op jit(solution)/shard_map/basis_blocks/pallas_call | solution.py:32
  6.7 6.8 %all-to-all-start = ((bf16[8,5,80,640]{3,2,1,0:T(8,128)(2,1)}), bf16[8,5,80,640]{3,2,1,0:T(8,128)(2,1)}, u32[]{:S(2)}, u32[]{:S(2)}) async-start(bf16[8,5,80,640]{3,2,1,0:T(8,128)(2,1)} %basis_blocks.1._), calls=%async_computation | async-start | bytes 8192000 | tf_op jit(solution)/shard_map/all_to_all | solution.py:310
  13.6 2.2 %copy-done = bf16[8,5,80,640]{3,2,1,0:T(8,128)(2,1)S(1)} copy-done((bf16[8,5,80,640]{3,2,1,0:T(8,128)(2,1)S(1)}, bf16[8,5,80,640]{3,2,1,0:T(8,128)(2,1)}, u32[]{:S(2)}) %copy-start) | copy-done | bytes 4096024
  15.7 1.5 %copy-done.2 = bf16[32,80,320]{2,1,0:T(8,128)(2,1)S(1)} copy-done((bf16[32,80,320]{2,1,0:T(8,128)(2,1)S(1)}, bf16[32,80,320]{2,1,0:T(8,128)(2,1)}, u32[]{:S(2)}) %copy-start.2) | copy-done | bytes 1638424
  17.3 3.8 %gradient.1 = (bf16[2,80,640]{2,1,0:T(8,128)(2,1)S(1)}, bf16[2,80,640]{2,1,0:T(8,128)(2,1)}, bf16[2,80,640]{2,1,0:T(8,128)(2,1)S(1)}, bf16[2,80,640]{2,1,0:T(8,1...) custom-call(s32[8]{0:T(128)S(1)} %iota_xor_fusion.wave_ref, ...), custom_call_target="tpu_custom_call" | custom-call | flops 4915200 | bytes 4915200 | tf_op jit(solution)/shard_map/gradient/pallas_call | solution.py:72
  21.1 0.1 collective-permute-start
  21.2 1.1 collective-permute-start.1
  22.3 0.7 collective-permute-start.2
  23.1 2.7 %collective-permute-start.3 = (bf16[2,80,640]{2,1,0:T(8,128)(2,1)S(1)}, bf16[2,80,640]{2,1,0:T(8,128)(2,1)S(1)}, u32[]{:S(2)}, u32[]{:S(2)}) collective-permute-start(bf16[2,80,640]{2,1,0:T(8,128)(2,1)S(1)} %get-tuple-element.25), channel_id=1, source_target_pairs={{0,8},{2,10},{4,12},{6,14},{8,0},{10,2},{12,4},{14,6},{1,9},{3,11}... | collective-permute-start | bytes 614408 | tf_op jit(solution)/shard_map/ppermute | solution.py:305
  25.7 0.5 collective-permute-start.4
  26.3 0.1 reshape.81
  26.4 0.6 gather_fusion.1
  26.9 0.1 mul.86
  27.0 0.1 broadcast_in_dim.9
  27.1 0.1 add.110
  27.2 1.3 fusion.4
  28.6 0.1 broadcast_add_fusion
  28.6 0.1 add.108
  28.7 0.0 collective-permute-done.refs_1_
  28.7 2.6 %collective-permute-start.5 = (bf16[2,80,640]{2,1,0:T(8,128)(2,1)S(1)}, bf16[2,80,640]{2,1,0:T(8,128)(2,1)S(1)}, u32[]{:S(2)}, u32[]{:S(2)}) collective-permute-start(bf16[2,80,640]{2,1,0:T(8,128)(2,1)S(1)} %get-tuple-element.27), channel_id=1, source_target_pairs={{0,12},{2,14},{4,8},{6,10},{8,4},{10,6},{12,0},{14,2},{1,13},{3,15... | collective-permute-start | bytes 614408 | tf_op jit(solution)/shard_map/ppermute | solution.py:305
  31.3 0.0 collective-permute-done.1.refs_2_
  31.3 0.5 collective-permute-start.6
  31.8 0.9 sine_multiply_fusion
  32.7 1.7 %wave_table.1.table_ref = bf16[5,2560,256]{2,1,0:T(8,128)(2,1)S(1)} custom-call(f32[40,1280]{1,0:T(8,128)S(1)} %get-tuple-element.40.coarse_cos, f32[40,1280]{1,0:T(8,128)S(1)} %get-tuple-element.39.coarse_sin, f32[64,1280]{1,0:T(8,128)S(1)} %get-tuple-element.38.fine_cos, f32[64,1280]{1,0:T(8,128)S(1)} %get-tuple-element.37.fine_sin), custom_call_target="tpu_custom_call" | custom-call | flops 9830400 | bytes 6553600 | tf_op jit(solution)/shard_map/wave_table/pallas_call | solution.py:109
  34.4 0.0 collective-permute-done.2.refs_3_
  34.4 5.5 %collective-permute-done.3.refs_4_ = bf16[2,80,640]{2,1,0:T(8,128)(2,1)S(1)} collective-permute-done((bf16[2,80,640]{2,1,0:T(8,128)(2,1)S(1)}, bf16[2,80,640]{2,1,0:T(8,128)(2,1)S(1)}, u32[]{:S(2)}, u32[]{:S(2)}) %collective-permute-start.3) | collective-permute-done | bytes 204832 | tf_op jit(solution)/shard_map/ppermute | solution.py:305
  40.0 3.4 %collective-permute-done.4.refs_5_ = bf16[2,80,640]{2,1,0:T(8,128)(2,1)S(1)} collective-permute-done((bf16[2,80,640]{2,1,0:T(8,128)(2,1)S(1)}, bf16[2,80,640]{2,1,0:T(8,128)(2,1)S(1)}, u32[]{:S(2)}, u32[]{:S(2)}) %collective-permute-start.4) | collective-permute-done | bytes 204832 | tf_op jit(solution)/shard_map/ppermute | solution.py:305
  43.4 3.3 %collective-permute-done.5.refs_6_ = bf16[2,80,640]{2,1,0:T(8,128)(2,1)S(1)} collective-permute-done((bf16[2,80,640]{2,1,0:T(8,128)(2,1)S(1)}, bf16[2,80,640]{2,1,0:T(8,128)(2,1)S(1)}, u32[]{:S(2)}, u32[]{:S(2)}) %collective-permute-start.5) | collective-permute-done | bytes 204832 | tf_op jit(solution)/shard_map/ppermute | solution.py:305
  46.7 3.5 %collective-permute-done.6.refs_7_ = bf16[2,80,640]{2,1,0:T(8,128)(2,1)S(1)} collective-permute-done((bf16[2,80,640]{2,1,0:T(8,128)(2,1)S(1)}, bf16[2,80,640]{2,1,0:T(8,128)(2,1)S(1)}, u32[]{:S(2)}, u32[]{:S(2)}) %collective-permute-start.6) | collective-permute-done | bytes 204832 | tf_op jit(solution)/shard_map/ppermute | solution.py:305
  50.1 2.6 %fourier_rows.1 = (bf16[80,640]{1,0:T(8,128)(2,1)S(1)}, bf16[80,640]{1,0:T(8,128)(2,1)S(1)}, bf16[80,640]{1,0:T(8,128)(2,1)S(1)}, bf16[80,640]{1,0:T(8,128)(2,1)...) custom-call(bf16[5,2560,256]{2,1,0:T(8,128)(2,1)S(1)} %wave_table.1., ...), custom_call_target="tpu_custom_call" | custom-call | flops 2097152000 | bytes 6553600 | tf_op jit(solution)/shard_map/fourier_rows/pallas_call | solution.py:144
  52.7 1.5 %collective-permute-start.10 = (bf16[80,640]{1,0:T(8,128)(2,1)S(1)}, bf16[80,640]{1,0:T(8,128)(2,1)S(1)}, u32[]{:S(2)}, u32[]{:S(2)}) collective-permute-start(bf16[80,640]{1,0:T(8,128)(2,1)S(1)} %get-tuple-element.33), channel_id=1, source_target_pairs={{0,8},{2,10},{4,12},{6,14},{8,0},{10,2},{12,4},{14,6},{1,9},{3,11}... | collective-permute-start | bytes 307208 | tf_op jit(solution)/shard_map/ppermute | solution.py:305
  54.3 1.9 %collective-permute-start.11 = (bf16[80,640]{1,0:T(8,128)(2,1)S(1)}, bf16[80,640]{1,0:T(8,128)(2,1)S(1)}, u32[]{:S(2)}, u32[]{:S(2)}) collective-permute-start(bf16[80,640]{1,0:T(8,128)(2,1)S(1)} %get-tuple-element.34), channel_id=1, source_target_pairs={{0,10},{2,8},{4,14},{6,12},{8,2},{10,0},{12,6},{14,4},{1,11},{3,9}... | collective-permute-start | bytes 307208 | tf_op jit(solution)/shard_map/ppermute | solution.py:305
  56.2 2.4 %collective-permute-start.12 = (bf16[80,640]{1,0:T(8,128)(2,1)S(1)}, bf16[80,640]{1,0:T(8,128)(2,1)S(1)}, u32[]{:S(2)}, u32[]{:S(2)}) collective-permute-start(bf16[80,640]{1,0:T(8,128)(2,1)S(1)} %get-tuple-element.35), channel_id=1, source_target_pairs={{0,12},{2,14},{4,8},{6,10},{8,4},{10,6},{12,0},{14,2},{1,13},{3,15... | collective-permute-start | bytes 307208 | tf_op jit(solution)/shard_map/ppermute | solution.py:305
  58.6 0.5 collective-permute-start.13
  59.0 0.5 collective-permute-start.7
  59.6 0.4 collective-permute-done.10.refs_4_
  60.0 1.6 %collective-permute-done.11.refs_5_ = bf16[80,640]{1,0:T(8,128)(2,1)S(1)} collective-permute-done((bf16[80,640]{1,0:T(8,128)(2,1)S(1)}, bf16[80,640]{1,0:T(8,128)(2,1)S(1)}, u32[]{:S(2)}, u32[]{:S(2)}) %collective-permute-start.11) | collective-permute-done | bytes 102432 | tf_op jit(solution)/shard_map/ppermute | solution.py:305
  61.6 0.9 collective-permute-start.9
  62.5 1.6 %collective-permute-done.12.refs_6_ = bf16[80,640]{1,0:T(8,128)(2,1)S(1)} collective-permute-done((bf16[80,640]{1,0:T(8,128)(2,1)S(1)}, bf16[80,640]{1,0:T(8,128)(2,1)S(1)}, u32[]{:S(2)}, u32[]{:S(2)}) %collective-permute-start.12) | collective-permute-done | bytes 102432 | tf_op jit(solution)/shard_map/ppermute | solution.py:305
  64.1 2.1 %collective-permute-done.13.refs_7_ = bf16[80,640]{1,0:T(8,128)(2,1)S(1)} collective-permute-done((bf16[80,640]{1,0:T(8,128)(2,1)S(1)}, bf16[80,640]{1,0:T(8,128)(2,1)S(1)}, u32[]{:S(2)}, u32[]{:S(2)}) %collective-permute-start.13) | collective-permute-done | bytes 102432 | tf_op jit(solution)/shard_map/ppermute | solution.py:305
  66.2 0.4 collective-permute-done.9.refs_3_
  66.6 2.1 %turn.1 = bf16[16,5,8,640]{3,2,1,0:T(8,128)(2,1)} custom-call(s32[8]{0:T(128)S(1)} %iota_xor_fusion.wave_ref, bf16[8,5,80,640]{3,2,1,0:T(8,128)(2,1)} %all-to-all-done._.basis_hbm, bf16[80,640]{1,0:T(8,128)(2,1)S(1)} %get-tuple-element.29.refs_0_, bf16[80,640]{1,0:T(8,128)(2,1)S(1)} %collective-permute-done.7.refs_1_, ...), custom_call_target="tpu_custom_call" | custom-call | bytes 1638400 | tf_op jit(solution)/shard_map/turn/pallas_call | solution.py:173
  68.7 10.1 %all-to-all-start.1 = ((bf16[16,5,8,640]{3,2,1,0:T(8,128)(2,1)}), bf16[16,5,8,640]{3,2,1,0:T(8,128)(2,1)S(1)}, u32[]{:S(2)}, u32[]{:S(2)}) async-start(bf16[16,5,8,640]{3,2,1,0:T(8,128)(2,1)} %turn.1), calls=%async_computation.1 | async-start | bytes 1638400 | tf_op jit(solution)/shard_map/all_to_all | solution.py:314
  78.8 0.6 gather_fusion
  79.5 18.7 %all-to-all-done.1.four_hbm = bf16[16,5,8,640]{3,2,1,0:T(8,128)(2,1)S(1)} async-done(((bf16[16,5,8,640]{3,2,1,0:T(8,128)(2,1)}), bf16[16,5,8,640]{3,2,1,0:T(8,128)(2,1)S(1)}, u32[]{:S(2)}, u32[]{:S(2)}) %all-to-all-start.1) | async-done | bytes 819232 | tf_op jit(solution)/shard_map/all_to_all | solution.py:314
  98.2 4.0 %spectral_parts.1 = bf16[32,104,128]{2,1,0:T(8,128)(2,1)S(1)} custom-call(s32[5]{0:T(128)S(1)} %and_select_fusion.slot_ref, bf16[16,5,8,640]{3,2,1,0:T(8,128)(2,1)S(1)} %all-to-all-done.1.four_hbm, bf16[8,5,80,640]{3,2,1,0:T(8,128)(2,1)} %all-to-all-done._.basis_hbm), custom_call_target="tpu_custom_call" | custom-call | flops 524288000 | bytes 4915200 | tf_op jit(solution)/shard_map/spectral_parts/pallas_call | solution.py:247
  102.2 32.5 %all_to_all.15.in_ref = bf16[32,104,128]{2,1,0:T(8,128)(2,1)S(1)} all-to-all(bf16[32,104,128]{2,1,0:T(8,128)(2,1)S(1)} %spectral_parts.1), channel_id=1, replica_groups=mesh['x'=4,'zp'=2,'zq'=2,'wave'=8,'lev'=2] {'x','zp','zq','lev'}, dimensions={0} | all-to-all | bytes 1703936 | tf_op jit(solution)/shard_map/all_to_all | solution.py:319
  134.7 1.7 %finish.1 = f32[2560,80]{1,0:T(8,128)} custom-call(bf16[32,104,128]{2,1,0:T(8,128)(2,1)S(1)} %all_to_all.15.in_ref), custom_call_target="tpu_custom_call" | custom-call | flops 425984 | bytes 2162688 | tf_op jit(solution)/shard_map/finish/pallas_call | solution.py:285
  (22 shorter events, 0.1 us)
Async XLA Ops:
  6.7 6.9 %copy-start.1 = (bf16[32,80,320]{2,1,0:T(8,128)(2,1)S(1)}, bf16[32,80,320]{2,1,0:T(8,128)(2,1)}, u32[]{:S(2)}) copy-start(bf16[32,80,320]{2,1,0:T(8,128)(2,1)} %param.6) | copy-start | bytes 4915204
  6.7 6.9 %copy-start.3 = (f32[32]{0:T(128)S(1)}, f32[32]{0:T(128)}, u32[]{:S(2)}) copy-start(f32[32]{0:T(128)} %rate_ref.1) | copy-start | bytes 388
  6.7 59.9 %all-to-all-start = ((bf16[8,5,80,640]{3,2,1,0:T(8,128)(2,1)}), bf16[8,5,80,640]{3,2,1,0:T(8,128)(2,1)}, u32[]{:S(2)}, u32[]{:S(2)}) async-start(bf16[8,5,80,640]{3,2,1,0:T(8,128)(2,1)} %basis_blocks.1._), calls=%async_computation | async-start | bytes 8192000 | tf_op jit(solution)/shard_map/all_to_all | solution.py:310
  13.5 12.7 %copy-start.4 = (s32[640]{0:T(1024)S(1)}, s32[640]{0:T(1024)}, u32[]{:S(2)}) copy-start(s32[640]{0:T(1024)} %param.10) | copy-start | bytes 7684
  13.6 2.2 %copy-start = (bf16[8,5,80,640]{3,2,1,0:T(8,128)(2,1)S(1)}, bf16[8,5,80,640]{3,2,1,0:T(8,128)(2,1)}, u32[]{:S(2)}) copy-start(bf16[8,5,80,640]{3,2,1,0:T(8,128)(2,1)} %basis_blocks.1._) | copy-start | bytes 12288004
  15.7 1.5 %copy-start.2 = (bf16[32,80,320]{2,1,0:T(8,128)(2,1)S(1)}, bf16[32,80,320]{2,1,0:T(8,128)(2,1)}, u32[]{:S(2)}) copy-start(bf16[32,80,320]{2,1,0:T(8,128)(2,1)} %param.7) | copy-start | bytes 4915204
  21.1 7.6 %collective-permute-start = (bf16[2,80,640]{2,1,0:T(8,128)(2,1)}, bf16[2,80,640]{2,1,0:T(8,128)(2,1)S(1)}, u32[]{:S(2)}, u32[]{:S(2)}) collective-permute-start(bf16[2,80,640]{2,1,0:T(8,128)(2,1)} %get-tuple-element.22), channel_id=1, source_target_pairs={{0,2},{2,0},{4,6},{6,4},{8,10},{10,8},{12,14},{14,12},{1,3},{3,1},... | collective-permute-start | bytes 614408 | tf_op jit(solution)/shard_map/ppermute | solution.py:305
  21.2 10.1 %collective-permute-start.1 = (bf16[2,80,640]{2,1,0:T(8,128)(2,1)S(1)}, bf16[2,80,640]{2,1,0:T(8,128)(2,1)S(1)}, u32[]{:S(2)}, u32[]{:S(2)}) collective-permute-start(bf16[2,80,640]{2,1,0:T(8,128)(2,1)S(1)} %get-tuple-element.23), channel_id=1, source_target_pairs={{0,4},{2,6},{4,0},{6,2},{8,12},{10,14},{12,8},{14,10},{1,5},{3,7},... | collective-permute-start | bytes 614408 | tf_op jit(solution)/shard_map/ppermute | solution.py:305
  22.3 12.1 %collective-permute-start.2 = (bf16[2,80,640]{2,1,0:T(8,128)(2,1)S(1)}, bf16[2,80,640]{2,1,0:T(8,128)(2,1)S(1)}, u32[]{:S(2)}, u32[]{:S(2)}) collective-permute-start(bf16[2,80,640]{2,1,0:T(8,128)(2,1)S(1)} %get-tuple-element.24), channel_id=1, source_target_pairs={{0,6},{2,4},{4,2},{6,0},{8,14},{10,12},{12,10},{14,8},{1,7},{3,5},... | collective-permute-start | bytes 614408 | tf_op jit(solution)/shard_map/ppermute | solution.py:305
  23.1 16.9 %collective-permute-start.3 = (bf16[2,80,640]{2,1,0:T(8,128)(2,1)S(1)}, bf16[2,80,640]{2,1,0:T(8,128)(2,1)S(1)}, u32[]{:S(2)}, u32[]{:S(2)}) collective-permute-start(bf16[2,80,640]{2,1,0:T(8,128)(2,1)S(1)} %get-tuple-element.25), channel_id=1, source_target_pairs={{0,8},{2,10},{4,12},{6,14},{8,0},{10,2},{12,4},{14,6},{1,9},{3,11}... | collective-permute-start | bytes 614408 | tf_op jit(solution)/shard_map/ppermute | solution.py:305
  25.7 17.7 %collective-permute-start.4 = (bf16[2,80,640]{2,1,0:T(8,128)(2,1)S(1)}, bf16[2,80,640]{2,1,0:T(8,128)(2,1)S(1)}, u32[]{:S(2)}, u32[]{:S(2)}) collective-permute-start(bf16[2,80,640]{2,1,0:T(8,128)(2,1)S(1)} %get-tuple-element.26), channel_id=1, source_target_pairs={{0,10},{2,8},{4,14},{6,12},{8,2},{10,0},{12,6},{14,4},{1,11},{3,9}... | collective-permute-start | bytes 614408 | tf_op jit(solution)/shard_map/ppermute | solution.py:305
  28.7 18.0 %collective-permute-start.5 = (bf16[2,80,640]{2,1,0:T(8,128)(2,1)S(1)}, bf16[2,80,640]{2,1,0:T(8,128)(2,1)S(1)}, u32[]{:S(2)}, u32[]{:S(2)}) collective-permute-start(bf16[2,80,640]{2,1,0:T(8,128)(2,1)S(1)} %get-tuple-element.27), channel_id=1, source_target_pairs={{0,12},{2,14},{4,8},{6,10},{8,4},{10,6},{12,0},{14,2},{1,13},{3,15... | collective-permute-start | bytes 614408 | tf_op jit(solution)/shard_map/ppermute | solution.py:305
  31.3 18.9 %collective-permute-start.6 = (bf16[2,80,640]{2,1,0:T(8,128)(2,1)S(1)}, bf16[2,80,640]{2,1,0:T(8,128)(2,1)S(1)}, u32[]{:S(2)}, u32[]{:S(2)}) collective-permute-start(bf16[2,80,640]{2,1,0:T(8,128)(2,1)S(1)} %get-tuple-element.28), channel_id=1, source_target_pairs={{0,14},{2,12},{4,10},{6,8},{8,6},{10,4},{12,2},{14,0},{1,15},{3,13... | collective-permute-start | bytes 614408 | tf_op jit(solution)/shard_map/ppermute | solution.py:305
  52.7 7.3 %collective-permute-start.10 = (bf16[80,640]{1,0:T(8,128)(2,1)S(1)}, bf16[80,640]{1,0:T(8,128)(2,1)S(1)}, u32[]{:S(2)}, u32[]{:S(2)}) collective-permute-start(bf16[80,640]{1,0:T(8,128)(2,1)S(1)} %get-tuple-element.33), channel_id=1, source_target_pairs={{0,8},{2,10},{4,12},{6,14},{8,0},{10,2},{12,4},{14,6},{1,9},{3,11}... | collective-permute-start | bytes 307208 | tf_op jit(solution)/shard_map/ppermute | solution.py:305
  54.3 7.3 %collective-permute-start.11 = (bf16[80,640]{1,0:T(8,128)(2,1)S(1)}, bf16[80,640]{1,0:T(8,128)(2,1)S(1)}, u32[]{:S(2)}, u32[]{:S(2)}) collective-permute-start(bf16[80,640]{1,0:T(8,128)(2,1)S(1)} %get-tuple-element.34), channel_id=1, source_target_pairs={{0,10},{2,8},{4,14},{6,12},{8,2},{10,0},{12,6},{14,4},{1,11},{3,9}... | collective-permute-start | bytes 307208 | tf_op jit(solution)/shard_map/ppermute | solution.py:305
  56.2 7.9 %collective-permute-start.12 = (bf16[80,640]{1,0:T(8,128)(2,1)S(1)}, bf16[80,640]{1,0:T(8,128)(2,1)S(1)}, u32[]{:S(2)}, u32[]{:S(2)}) collective-permute-start(bf16[80,640]{1,0:T(8,128)(2,1)S(1)} %get-tuple-element.35), channel_id=1, source_target_pairs={{0,12},{2,14},{4,8},{6,10},{8,4},{10,6},{12,0},{14,2},{1,13},{3,15... | collective-permute-start | bytes 307208 | tf_op jit(solution)/shard_map/ppermute | solution.py:305
  58.6 7.6 %collective-permute-start.13 = (bf16[80,640]{1,0:T(8,128)(2,1)S(1)}, bf16[80,640]{1,0:T(8,128)(2,1)S(1)}, u32[]{:S(2)}, u32[]{:S(2)}) collective-permute-start(bf16[80,640]{1,0:T(8,128)(2,1)S(1)} %get-tuple-element.36), channel_id=1, source_target_pairs={{0,14},{2,12},{4,10},{6,8},{8,6},{10,4},{12,2},{14,0},{1,15},{3,13... | collective-permute-start | bytes 307208 | tf_op jit(solution)/shard_map/ppermute | solution.py:305
  59.0 7.1 %collective-permute-start.7 = (bf16[80,640]{1,0:T(8,128)(2,1)S(1)}, bf16[80,640]{1,0:T(8,128)(2,1)S(1)}, u32[]{:S(2)}, u32[]{:S(2)}) collective-permute-start(bf16[80,640]{1,0:T(8,128)(2,1)S(1)} %get-tuple-element.30), channel_id=1, source_target_pairs={{0,2},{2,0},{4,6},{6,4},{8,10},{10,8},{12,14},{14,12},{1,3},{3,1},... | collective-permute-start | bytes 307208 | tf_op jit(solution)/shard_map/ppermute | solution.py:305
  60.0 6.2 %collective-permute-start.8 = (bf16[80,640]{1,0:T(8,128)(2,1)S(1)}, bf16[80,640]{1,0:T(8,128)(2,1)S(1)}, u32[]{:S(2)}, u32[]{:S(2)}) collective-permute-start(bf16[80,640]{1,0:T(8,128)(2,1)S(1)} %get-tuple-element.31), channel_id=1, source_target_pairs={{0,4},{2,6},{4,0},{6,2},{8,12},{10,14},{12,8},{14,10},{1,5},{3,7},... | collective-permute-start | bytes 307208 | tf_op jit(solution)/shard_map/ppermute | solution.py:305
  61.6 5.0 %collective-permute-start.9 = (bf16[80,640]{1,0:T(8,128)(2,1)S(1)}, bf16[80,640]{1,0:T(8,128)(2,1)S(1)}, u32[]{:S(2)}, u32[]{:S(2)}) collective-permute-start(bf16[80,640]{1,0:T(8,128)(2,1)S(1)} %get-tuple-element.32), channel_id=1, source_target_pairs={{0,6},{2,4},{4,2},{6,0},{8,14},{10,12},{12,10},{14,8},{1,7},{3,5},... | collective-permute-start | bytes 307208 | tf_op jit(solution)/shard_map/ppermute | solution.py:305
  68.7 29.5 %all-to-all-start.1 = ((bf16[16,5,8,640]{3,2,1,0:T(8,128)(2,1)}), bf16[16,5,8,640]{3,2,1,0:T(8,128)(2,1)S(1)}, u32[]{:S(2)}, u32[]{:S(2)}) async-start(bf16[16,5,8,640]{3,2,1,0:T(8,128)(2,1)} %turn.1), calls=%async_computation.1 | async-start | bytes 1638400 | tf_op jit(solution)/shard_map/all_to_all | solution.py:314

commit v4 on v3

--- a/solution.py
+++ b/solution.py
@@ -15,66 +15,77 @@
     return pl.CostEstimate(flops=flops, bytes_accessed=moved, transcendentals=trans)
 
 
-def basis_kernel(lev_ref, basis_ref, out_ref):
-    lats, _, degs = basis_ref.shape
+def basis_kernel(lev_ref, basis_hbm, out_hbm, token_ref, in_buf, out_buf, in_sems, out_sems):
+    steps, lats, _, degs = in_buf.shape
+    lev = lev_ref[0]
+    reads = [
+        pltpu.make_async_copy(basis_hbm.at[:, 2 * b + lev], in_buf.at[b], in_sems.at[b])
+        for b in range(steps)
+    ]
+    for read in reads:
+        read.start()
     row = lax.broadcasted_iota(jnp.int32, (128, 128), 0)
     col = lax.broadcasted_iota(jnp.int32, (128, 128), 1)
     swap = (col == row % 16 * 8 + row // 16).astype(jnp.bfloat16)
-    for g in range(lats // 16):
-        block = basis_ref[16 * g : 16 * g + 16].astype(jnp.float32).reshape(128, degs)
-        turned = jnp.dot(swap, block.astype(jnp.bfloat16), preferred_element_type=jnp.float32)
-        out_ref[:, 0, 16 * g : 16 * g + 16, :] = turned.astype(jnp.bfloat16).reshape(8, 16, degs)
+    token_ref[...] = jnp.zeros_like(token_ref)
+    writes = []
+    for b in range(steps):
+        reads[b].wait()
+        for g in range(lats // 16):
+            block = in_buf[b, 16 * g : 16 * g + 16].astype(jnp.float32).reshape(128, degs)
+            turned = jnp.dot(swap, block.astype(jnp.bfloat16), preferred_element_type=jnp.float32)
+            out_buf[b, :, 16 * g : 16 * g + 16, :] = turned.astype(jnp.bfloat16).reshape(
+                8, 16, degs
+            )
+        writes.append(pltpu.make_async_copy(out_buf.at[b], out_hbm.at[:, b], out_sems.at[b]))
+        writes[b].start()
+    for write in writes:
+        write.wait()
 
 
 def basis_blocks(lev, basis):
     lats, slots, degs = basis.shape
     steps = slots // 16
+    hbm = pl.BlockSpec(memory_space=pltpu.HBM)
     return pl.pallas_call(
         basis_kernel,
-        grid_spec=pltpu.PrefetchScalarGridSpec(
-            num_scalar_prefetch=1,
-            grid=(steps,),
-            in_specs=[pl.BlockSpec((lats, 8, degs), lambda b, lev: (0, 2 * b + lev[0], 0))],
-            out_specs=pl.BlockSpec((8, 1, lats, degs), lambda b, lev: (0, b, 0, 0)),
-        ),
-        out_shape=jax.ShapeDtypeStruct((8, steps, lats, degs), jnp.bfloat16),
+        in_specs=[pl.BlockSpec(memory_space=pltpu.SMEM), hbm],
+        out_specs=[hbm, pl.BlockSpec(memory_space=pltpu.VMEM)],
+        out_shape=[
+            jax.ShapeDtypeStruct((8, steps, lats, degs), jnp.bfloat16),
+            jax.ShapeDtypeStruct((8, 128), jnp.float32),
+        ],
+        scratch_shapes=[
+            pltpu.VMEM((steps, lats, 8, degs), jnp.bfloat16),
+            pltpu.VMEM((steps, 8, lats, degs), jnp.bfloat16),
+            pltpu.SemaphoreType.DMA((steps,)),
+            pltpu.SemaphoreType.DMA((steps,)),
+        ],
         compiler_params=params(60),
         cost_estimate=cost(0, 2 * lats * slots * degs),
         name="basis_blocks",
-    )(lev, basis)
-
-
-def grad_kernel(wave_ref, rate_ref, grad_hbm, state_hbm, _, *refs):
-    outs, (grad_buf, state_buf, sems) = refs[:8], refs[8:]
-    lons = grad_hbm.shape[-1]
-    copies = []
+    )(lev, basis.reshape(lats, slots // 8, 8, degs))
+
+
+def grad_kernel(wave_ref, rate_ref, grad_ref, state_ref, _, *outs):
+    lons = grad_ref.shape[-1]
     for k in range(8):
         to = wave_ref[k]
-        copies.append(pltpu.make_async_copy(grad_hbm.at[:, to], grad_buf.at[k], sems.at[0, k]))
-        copies.append(pltpu.make_async_copy(state_hbm.at[:, to], state_buf.at[k], sems.at[1, k]))
-    for copy in copies:
-        copy.start()
-    for k in range(8):
-        copies[2 * k].wait()
-        copies[2 * k + 1].wait()
         for c in range(4):
-            slope = 1.0 - jnp.tanh(state_buf[k, c].astype(jnp.float32)) ** 2
-            rate = rate_ref[8 * c + wave_ref[k]]
-            value = grad_buf[k, c].astype(jnp.float32) * (1.0 + rate * slope)
+            slope = 1.0 - jnp.tanh(state_ref[c, to].astype(jnp.float32)) ** 2
+            value = grad_ref[c, to].astype(jnp.float32) * (1.0 + rate_ref[8 * c + to] * slope)
             outs[k][c // 2, :, pl.ds((c % 2) * lons, lons)] = value.astype(jnp.bfloat16)
 
 
 def gradient(to, rate, grad, state, after):
     chans, lats, lons = grad.shape
     four = (4, chans // 4, lats, lons)
-    smem, hbm = pl.BlockSpec(memory_space=pltpu.SMEM), pl.BlockSpec(memory_space=pltpu.HBM)
-    buffer = pltpu.VMEM((8, 4, lats, lons), jnp.bfloat16)
+    smem, vmem = pl.BlockSpec(memory_space=pltpu.SMEM), pl.BlockSpec(memory_space=pltpu.VMEM)
     return pl.pallas_call(
         grad_kernel,
-        in_specs=[smem, smem, hbm, hbm, pl.BlockSpec(memory_space=pl.ANY)],
+        in_specs=[smem, smem, vmem, vmem, vmem],
         out_shape=[jax.ShapeDtypeStruct((2, lats, 2 * lons), jnp.bfloat16)] * 8,
-        scratch_shapes=[buffer, buffer, pltpu.SemaphoreType.DMA((2, 8))],
-        compiler_params=params(12),
+        compiler_params=params(16),
         cost_estimate=cost(6 * grad.size, 6 * grad.size, grad.size),
         name="gradient",
     )(to, rate, grad.reshape(four), state.reshape(four), after)
@@ -301,12 +312,13 @@
     partner = wave ^ jnp.arange(8, dtype=jnp.int32)
 
     def swapped(blocks):
-        return [blocks[0]] + [
-            lax.ppermute(blocks[k], "wave", [(w, w ^ k) for w in range(8)]) for k in range(1, 8)
-        ]
-
-    basis = basis_blocks(lev.astype(jnp.int32)[None], legendre_basis)
-    grads = gradient(partner, tend_rate, out_grad, grid_state, basis)
+        blocks = list(blocks)
+        for k in (4, 5, 2, 6, 3, 7, 1):
+            blocks[k] = lax.ppermute(blocks[k], "wave", [(w, w ^ k) for w in range(8)])
+        return blocks
+
+    basis, token = basis_blocks(lev.astype(jnp.int32)[None], legendre_basis)
+    grads = gradient(partner, tend_rate, out_grad, grid_state, token)
     basis = lax.all_to_all(basis, ("x", "zq"), 0, 0, tiled=True)
     grads = swapped(grads)
     table = wave_table(wave_slot.reshape(8, slot_dev)[partner], partner, lons, 64)

time: 137 us -> 135 us (0.985)
  waiting for transfers between devices: 40.6 us -> 47.3 us
  Pallas kernels: 22.6 us -> 19.2 us
  blocking collectives: 32.5 us -> 29.1 us
  local copies, waits for them, and re-layouts: 5.28 us -> 3.14 us
    all_to_all x1, waiting for transfers between devices: 18.7 us -> 22.2 us  [local(): lax.all_to_all(turn(partner, basis, blocks), ('x', 'zq', 'lev'), 0, 0, ti...]
    pallas_call x2, Pallas kernels: 10.5 us -> 7.09 us  [the longest x1 4.65 us: basis_blocks(): pl.pallas_call(basis_kernel, in_specs=[pl.BlockSpec(memory_space=pltpu.SM...]
    all_to_all x1, blocking collectives: 32.5 us -> 29.1 us  [local(): parts = lax.all_to_all(parts, ('x', 'zp', 'zq', 'lev'), 0, 0, tiled=True)]
    ppermute x14, waiting for transfers between devices: 21.8 us -> 25.1 us  [swapped(): blocks[k] = lax.ppermute(blocks[k], 'wave', [(w, w ^ k) for w in range(8)])]
    unnamed x10, local copies, waits for them, and re-layouts: 3.71 us -> 1.57 us
  transfers between devices with their start and end apart: 16 -> 16, of which waited for: 10 -> 9; matrix products, arithmetic and copies ran while one was open for 3% -> 3% of each run, Pallas kernels for 6% -> 5%
where the time goes in v4:
time: 135 us
  waiting for transfers between devices  47.3 us (35%)
  starting transfers between devices  33.5 us (25%)
  blocking collectives  29.1 us (22%)
  Pallas kernels  19.2 us (14%)
  local copies, waits for them, and re-layouts  3.14 us (2%)
  other arithmetic  2.38 us (2%)
    all_to_all x1, blocking collectives, local(): parts = lax.all_to_all(parts, ('x', 'zp', 'zq', 'lev'), 0, 0, tiled=True)  29.1 us
    ppermute x14, waiting for transfers between devices, swapped(): blocks[k] = lax.ppermute(blocks[k], 'wave', [(w, w ^ k) for w in range(8)])  25.1 us
    all_to_all x1, waiting for transfers between devices, local(): lax.all_to_all(turn(partner, basis, blocks), ('x', 'zq', 'lev'), 0, 0, ti...  22.2 us
    ppermute x14, starting transfers between devices, swapped(): blocks[k] = lax.ppermute(blocks[k], 'wave', [(w, w ^ k) for w in range(8)])  16.4 us
    all_to_all x1, starting transfers between devices, local(): lax.all_to_all(turn(partner, basis, blocks), ('x', 'zq', 'lev'), 0, 0, ti...  10.3 us
    all_to_all x1, starting transfers between devices, local(): basis = lax.all_to_all(basis, ('x', 'zq'), 0, 0, tiled=True)  6.86 us
    pallas_call x1, Pallas kernels, basis_blocks(): pl.pallas_call(basis_kernel, in_specs=[pl.BlockSpec(memory_space=pltpu.SM...  4.65 us
    pallas_call x1, Pallas kernels, spectral_parts(): pl.pallas_call(spectral_kernel, in_specs=[pl.BlockSpec(memory_space=pltpu...  4.03 us
  transfers between devices with their start and end apart: 16, of which 9 were waited for; matrix products, arithmetic and copies ran while one was open for 3% of the time, Pallas kernels for 5%

profile of v4, /device:TPU:2, one launch (start us, length us, event | category | flops | bytes accessed | tf_op | source)
XLA Modules:
  0.0 134.8 jit_solution(10141776702010661361)
XLA Ops:
  0.0 4.6 %basis_blocks.1 = (bf16[8,5,80,640]{3,2,1,0:T(8,128)(2,1)}, f32[8,128]{1,0:T(8,128)}) custom-call(s32[1]{0:T(128)} %bitcast.1.lev_ref, bf16[80,10,8,640]{3,2,1,0:T(8,128)(2,1)} %bitcast.11), custom_call_target="tpu_custom_call" | custom-call | bytes 8192000 | tf_op jit(solution)/shard_map/basis_blocks/pallas_call | solution.py:50
  4.7 0.0 copy-start
  4.7 0.0 copy-start.2
  4.7 0.0 copy-start.3
  4.7 0.0 copy-start.4
  4.7 6.9 %all-to-all-start = ((bf16[8,5,80,640]{3,2,1,0:T(8,128)(2,1)}), bf16[8,5,80,640]{3,2,1,0:T(8,128)(2,1)}, u32[]{:S(2)}, u32[]{:S(2)}) async-start(bf16[8,5,80,640]{3,2,1,0:T(8,128)(2,1)} %get-tuple-element.23), calls=%async_computation | async-start | bytes 8192000 | tf_op jit(solution)/shard_map/all_to_all | solution.py:322
  11.6 0.0 copy-start.1
  11.6 1.5 %copy-done.1 = bf16[32,80,320]{2,1,0:T(8,128)(2,1)S(1)} copy-done((bf16[32,80,320]{2,1,0:T(8,128)(2,1)S(1)}, bf16[32,80,320]{2,1,0:T(8,128)(2,1)}, u32[]{:S(2)}) %copy-start.1) | copy-done | bytes 1638424
  13.1 2.4 %gradient.1 = (bf16[2,80,640]{2,1,0:T(8,128)(2,1)S(1)}, bf16[2,80,640]{2,1,0:T(8,128)(2,1)}, bf16[2,80,640]{2,1,0:T(8,128)(2,1)S(1)}, bf16[2,80,640]{2,1,0:T(8,1...) custom-call(s32[8]{0:T(128)S(1)} %iota_xor_fusion.wave_ref, ...), custom_call_target="tpu_custom_call" | custom-call | flops 4915200 | bytes 4915200 | tf_op jit(solution)/shard_map/gradient/pallas_call | solution.py:84
  15.6 0.0 collective-permute-start
  15.6 1.1 collective-permute-start.1
  16.6 0.8 collective-permute-start.2
  17.4 2.7 %collective-permute-start.3 = (bf16[2,80,640]{2,1,0:T(8,128)(2,1)S(1)}, bf16[2,80,640]{2,1,0:T(8,128)(2,1)S(1)}, u32[]{:S(2)}, u32[]{:S(2)}) collective-permute-start(bf16[2,80,640]{2,1,0:T(8,128)(2,1)S(1)} %get-tuple-element.29), channel_id=1, source_target_pairs={{0,8},{2,10},{4,12},{6,14},{8,0},{10,2},{12,4},{14,6},{1,9},{3,11}... | collective-permute-start | bytes 614408 | tf_op jit(solution)/shard_map/ppermute | solution.py:317
  20.1 0.5 collective-permute-start.4
  20.6 0.1 reshape.85
  20.7 0.6 gather_fusion.1
  21.3 0.1 mul.86
  21.4 0.1 broadcast_in_dim.9
  21.4 0.1 add.110
  21.5 1.3 fusion.4
  22.9 0.1 broadcast_add_fusion
  22.9 0.1 add.108
  23.0 2.6 %collective-permute-start.5 = (bf16[2,80,640]{2,1,0:T(8,128)(2,1)S(1)}, bf16[2,80,640]{2,1,0:T(8,128)(2,1)S(1)}, u32[]{:S(2)}, u32[]{:S(2)}) collective-permute-start(bf16[2,80,640]{2,1,0:T(8,128)(2,1)S(1)} %get-tuple-element.31), channel_id=1, source_target_pairs={{0,12},{2,14},{4,8},{6,10},{8,4},{10,6},{12,0},{14,2},{1,13},{3,15... | collective-permute-start | bytes 614408 | tf_op jit(solution)/shard_map/ppermute | solution.py:317
  25.6 0.6 collective-permute-start.6
  26.2 0.9 sine_multiply_fusion
  27.1 1.7 %wave_table.1.table_ref = bf16[5,2560,256]{2,1,0:T(8,128)(2,1)S(1)} custom-call(f32[40,1280]{1,0:T(8,128)S(1)} %get-tuple-element.44.coarse_cos, f32[40,1280]{1,0:T(8,128)S(1)} %get-tuple-element.43.coarse_sin, f32[64,1280]{1,0:T(8,128)S(1)} %get-tuple-element.42.fine_cos, f32[64,1280]{1,0:T(8,128)S(1)} %get-tuple-element.41.fine_sin), custom_call_target="tpu_custom_call" | custom-call | flops 9830400 | bytes 6553600 | tf_op jit(solution)/shard_map/wave_table/pallas_call | solution.py:120
  28.8 5.4 %collective-permute-done.3.refs_4_ = bf16[2,80,640]{2,1,0:T(8,128)(2,1)S(1)} collective-permute-done((bf16[2,80,640]{2,1,0:T(8,128)(2,1)S(1)}, bf16[2,80,640]{2,1,0:T(8,128)(2,1)S(1)}, u32[]{:S(2)}, u32[]{:S(2)}) %collective-permute-start.3) | collective-permute-done | bytes 204832 | tf_op jit(solution)/shard_map/ppermute | solution.py:317
  34.3 3.6 %collective-permute-done.4.refs_5_ = bf16[2,80,640]{2,1,0:T(8,128)(2,1)S(1)} collective-permute-done((bf16[2,80,640]{2,1,0:T(8,128)(2,1)S(1)}, bf16[2,80,640]{2,1,0:T(8,128)(2,1)S(1)}, u32[]{:S(2)}, u32[]{:S(2)}) %collective-permute-start.4) | collective-permute-done | bytes 204832 | tf_op jit(solution)/shard_map/ppermute | solution.py:317
  37.9 3.1 %collective-permute-done.5.refs_6_ = bf16[2,80,640]{2,1,0:T(8,128)(2,1)S(1)} collective-permute-done((bf16[2,80,640]{2,1,0:T(8,128)(2,1)S(1)}, bf16[2,80,640]{2,1,0:T(8,128)(2,1)S(1)}, u32[]{:S(2)}, u32[]{:S(2)}) %collective-permute-start.5) | collective-permute-done | bytes 204832 | tf_op jit(solution)/shard_map/ppermute | solution.py:317
  41.0 3.6 %collective-permute-done.6.refs_7_ = bf16[2,80,640]{2,1,0:T(8,128)(2,1)S(1)} collective-permute-done((bf16[2,80,640]{2,1,0:T(8,128)(2,1)S(1)}, bf16[2,80,640]{2,1,0:T(8,128)(2,1)S(1)}, u32[]{:S(2)}, u32[]{:S(2)}) %collective-permute-start.6) | collective-permute-done | bytes 204832 | tf_op jit(solution)/shard_map/ppermute | solution.py:317
  44.6 2.6 %fourier_rows.1 = (bf16[80,640]{1,0:T(8,128)(2,1)S(1)}, bf16[80,640]{1,0:T(8,128)(2,1)S(1)}, bf16[80,640]{1,0:T(8,128)(2,1)S(1)}, bf16[80,640]{1,0:T(8,128)(2,1)...) custom-call(bf16[5,2560,256]{2,1,0:T(8,128)(2,1)S(1)} %wave_table.1., ...), custom_call_target="tpu_custom_call" | custom-call | flops 2097152000 | bytes 6553600 | tf_op jit(solution)/shard_map/fourier_rows/pallas_call | solution.py:155
  47.2 0.5 collective-permute-start.7
  47.7 1.4 %collective-permute-start.9 = (bf16[80,640]{1,0:T(8,128)(2,1)S(1)}, bf16[80,640]{1,0:T(8,128)(2,1)S(1)}, u32[]{:S(2)}, u32[]{:S(2)}) collective-permute-start(bf16[80,640]{1,0:T(8,128)(2,1)S(1)} %get-tuple-element.36), channel_id=1, source_target_pairs={{0,6},{2,4},{4,2},{6,0},{8,14},{10,12},{12,10},{14,8},{1,7},{3,5},... | collective-permute-start | bytes 307208 | tf_op jit(solution)/shard_map/ppermute | solution.py:317
  49.2 2.4 %collective-permute-start.10 = (bf16[80,640]{1,0:T(8,128)(2,1)S(1)}, bf16[80,640]{1,0:T(8,128)(2,1)S(1)}, u32[]{:S(2)}, u32[]{:S(2)}) collective-permute-start(bf16[80,640]{1,0:T(8,128)(2,1)S(1)} %get-tuple-element.37), channel_id=1, source_target_pairs={{0,8},{2,10},{4,12},{6,14},{8,0},{10,2},{12,4},{14,6},{1,9},{3,11}... | collective-permute-start | bytes 307208 | tf_op jit(solution)/shard_map/ppermute | solution.py:317
  51.6 1.1 collective-permute-start.11
  52.8 2.4 %collective-permute-start.12 = (bf16[80,640]{1,0:T(8,128)(2,1)S(1)}, bf16[80,640]{1,0:T(8,128)(2,1)S(1)}, u32[]{:S(2)}, u32[]{:S(2)}) collective-permute-start(bf16[80,640]{1,0:T(8,128)(2,1)S(1)} %get-tuple-element.39), channel_id=1, source_target_pairs={{0,12},{2,14},{4,8},{6,10},{8,4},{10,6},{12,0},{14,2},{1,13},{3,15... | collective-permute-start | bytes 307208 | tf_op jit(solution)/shard_map/ppermute | solution.py:317
  55.2 0.3 collective-permute-start.13
  55.4 4.4 %collective-permute-done.10.refs_4_ = bf16[80,640]{1,0:T(8,128)(2,1)S(1)} collective-permute-done((bf16[80,640]{1,0:T(8,128)(2,1)S(1)}, bf16[80,640]{1,0:T(8,128)(2,1)S(1)}, u32[]{:S(2)}, u32[]{:S(2)}) %collective-permute-start.10) | collective-permute-done | bytes 102432 | tf_op jit(solution)/shard_map/ppermute | solution.py:317
  59.8 0.8 collective-permute-done.11.refs_5_
  60.5 2.8 %collective-permute-done.12.refs_6_ = bf16[80,640]{1,0:T(8,128)(2,1)S(1)} collective-permute-done((bf16[80,640]{1,0:T(8,128)(2,1)S(1)}, bf16[80,640]{1,0:T(8,128)(2,1)S(1)}, u32[]{:S(2)}, u32[]{:S(2)}) %collective-permute-start.12) | collective-permute-done | bytes 102432 | tf_op jit(solution)/shard_map/ppermute | solution.py:317
  63.4 1.3 collective-permute-done.13.refs_7_
  64.7 2.1 %turn.1 = bf16[16,5,8,640]{3,2,1,0:T(8,128)(2,1)} custom-call(s32[8]{0:T(128)S(1)} %iota_xor_fusion.wave_ref, bf16[8,5,80,640]{3,2,1,0:T(8,128)(2,1)} %all-to-all-done._.basis_hbm, bf16[80,640]{1,0:T(8,128)(2,1)S(1)} %get-tuple-element.33.refs_0_, bf16[80,640]{1,0:T(8,128)(2,1)S(1)} %collective-permute-done.7.refs_1_, ...), custom_call_target="tpu_custom_call" | custom-call | bytes 1638400 | tf_op jit(solution)/shard_map/turn/pallas_call | solution.py:184
  66.8 10.3 %all-to-all-start.1 = ((bf16[16,5,8,640]{3,2,1,0:T(8,128)(2,1)}), bf16[16,5,8,640]{3,2,1,0:T(8,128)(2,1)S(1)}, u32[]{:S(2)}, u32[]{:S(2)}) async-start(bf16[16,5,8,640]{3,2,1,0:T(8,128)(2,1)} %turn.1), calls=%async_computation.1 | async-start | bytes 1638400 | tf_op jit(solution)/shard_map/all_to_all | solution.py:326
  77.1 0.6 gather_fusion
  77.7 22.2 %all-to-all-done.1.four_hbm = bf16[16,5,8,640]{3,2,1,0:T(8,128)(2,1)S(1)} async-done(((bf16[16,5,8,640]{3,2,1,0:T(8,128)(2,1)}), bf16[16,5,8,640]{3,2,1,0:T(8,128)(2,1)S(1)}, u32[]{:S(2)}, u32[]{:S(2)}) %all-to-all-start.1) | async-done | bytes 819232 | tf_op jit(solution)/shard_map/all_to_all | solution.py:326
  100.0 4.0 %spectral_parts.1 = bf16[32,104,128]{2,1,0:T(8,128)(2,1)S(1)} custom-call(s32[5]{0:T(128)S(1)} %and_select_fusion.slot_ref, bf16[16,5,8,640]{3,2,1,0:T(8,128)(2,1)S(1)} %all-to-all-done.1.four_hbm, bf16[8,5,80,640]{3,2,1,0:T(8,128)(2,1)} %all-to-all-done._.basis_hbm), custom_call_target="tpu_custom_call" | custom-call | flops 524288000 | bytes 4915200 | tf_op jit(solution)/shard_map/spectral_parts/pallas_call | solution.py:258
  104.0 29.1 %all_to_all.15.in_ref = bf16[32,104,128]{2,1,0:T(8,128)(2,1)S(1)} all-to-all(bf16[32,104,128]{2,1,0:T(8,128)(2,1)S(1)} %spectral_parts.1), channel_id=1, replica_groups=mesh['x'=4,'zp'=2,'zq'=2,'wave'=8,'lev'=2] {'x','zp','zq','lev'}, dimensions={0} | all-to-all | bytes 1703936 | tf_op jit(solution)/shard_map/all_to_all | solution.py:331
  133.1 1.7 %finish.1 = f32[2560,80]{1,0:T(8,128)} custom-call(bf16[32,104,128]{2,1,0:T(8,128)(2,1)S(1)} %all_to_all.15.in_ref), custom_call_target="tpu_custom_call" | custom-call | flops 425984 | bytes 2162688 | tf_op jit(solution)/shard_map/finish/pallas_call | solution.py:296
  (22 shorter events, 0.1 us)
Async XLA Ops:
  4.7 6.9 %copy-start = (bf16[32,80,320]{2,1,0:T(8,128)(2,1)S(1)}, bf16[32,80,320]{2,1,0:T(8,128)(2,1)}, u32[]{:S(2)}) copy-start(bf16[32,80,320]{2,1,0:T(8,128)(2,1)} %param.6) | copy-start | bytes 4915204
  4.7 6.9 %copy-start.2 = (f32[8,128]{1,0:T(8,128)S(1)}, f32[8,128]{1,0:T(8,128)}, u32[]{:S(2)}) copy-start(f32[8,128]{1,0:T(8,128)} %get-tuple-element.24._) | copy-start | bytes 12292
  4.7 6.9 %copy-start.3 = (f32[32]{0:T(128)S(1)}, f32[32]{0:T(128)}, u32[]{:S(2)}) copy-start(f32[32]{0:T(128)} %rate_ref.1) | copy-start | bytes 388
  4.7 15.9 %copy-start.4 = (s32[640]{0:T(1024)S(1)}, s32[640]{0:T(1024)}, u32[]{:S(2)}) copy-start(s32[640]{0:T(1024)} %param.10) | copy-start | bytes 7684
  4.7 60.0 %all-to-all-start = ((bf16[8,5,80,640]{3,2,1,0:T(8,128)(2,1)}), bf16[8,5,80,640]{3,2,1,0:T(8,128)(2,1)}, u32[]{:S(2)}, u32[]{:S(2)}) async-start(bf16[8,5,80,640]{3,2,1,0:T(8,128)(2,1)} %get-tuple-element.23), calls=%async_computation | async-start | bytes 8192000 | tf_op jit(solution)/shard_map/all_to_all | solution.py:322
  11.6 1.5 %copy-start.1 = (bf16[32,80,320]{2,1,0:T(8,128)(2,1)S(1)}, bf16[32,80,320]{2,1,0:T(8,128)(2,1)}, u32[]{:S(2)}) copy-start(bf16[32,80,320]{2,1,0:T(8,128)(2,1)} %param.7) | copy-start | bytes 4915204
  15.6 7.4 %collective-permute-start = (bf16[2,80,640]{2,1,0:T(8,128)(2,1)}, bf16[2,80,640]{2,1,0:T(8,128)(2,1)S(1)}, u32[]{:S(2)}, u32[]{:S(2)}) collective-permute-start(bf16[2,80,640]{2,1,0:T(8,128)(2,1)} %get-tuple-element.26), channel_id=1, source_target_pairs={{0,2},{2,0},{4,6},{6,4},{8,10},{10,8},{12,14},{14,12},{1,3},{3,1},... | collective-permute-start | bytes 614408 | tf_op jit(solution)/shard_map/ppermute | solution.py:317
  15.6 10.0 %collective-permute-start.1 = (bf16[2,80,640]{2,1,0:T(8,128)(2,1)S(1)}, bf16[2,80,640]{2,1,0:T(8,128)(2,1)S(1)}, u32[]{:S(2)}, u32[]{:S(2)}) collective-permute-start(bf16[2,80,640]{2,1,0:T(8,128)(2,1)S(1)} %get-tuple-element.27), channel_id=1, source_target_pairs={{0,4},{2,6},{4,0},{6,2},{8,12},{10,14},{12,8},{14,10},{1,5},{3,7},... | collective-permute-start | bytes 614408 | tf_op jit(solution)/shard_map/ppermute | solution.py:317
  16.6 12.2 %collective-permute-start.2 = (bf16[2,80,640]{2,1,0:T(8,128)(2,1)S(1)}, bf16[2,80,640]{2,1,0:T(8,128)(2,1)S(1)}, u32[]{:S(2)}, u32[]{:S(2)}) collective-permute-start(bf16[2,80,640]{2,1,0:T(8,128)(2,1)S(1)} %get-tuple-element.28), channel_id=1, source_target_pairs={{0,6},{2,4},{4,2},{6,0},{8,14},{10,12},{12,10},{14,8},{1,7},{3,5},... | collective-permute-start | bytes 614408 | tf_op jit(solution)/shard_map/ppermute | solution.py:317
  17.4 16.8 %collective-permute-start.3 = (bf16[2,80,640]{2,1,0:T(8,128)(2,1)S(1)}, bf16[2,80,640]{2,1,0:T(8,128)(2,1)S(1)}, u32[]{:S(2)}, u32[]{:S(2)}) collective-permute-start(bf16[2,80,640]{2,1,0:T(8,128)(2,1)S(1)} %get-tuple-element.29), channel_id=1, source_target_pairs={{0,8},{2,10},{4,12},{6,14},{8,0},{10,2},{12,4},{14,6},{1,9},{3,11}... | collective-permute-start | bytes 614408 | tf_op jit(solution)/shard_map/ppermute | solution.py:317
  20.1 17.8 %collective-permute-start.4 = (bf16[2,80,640]{2,1,0:T(8,128)(2,1)S(1)}, bf16[2,80,640]{2,1,0:T(8,128)(2,1)S(1)}, u32[]{:S(2)}, u32[]{:S(2)}) collective-permute-start(bf16[2,80,640]{2,1,0:T(8,128)(2,1)S(1)} %get-tuple-element.30), channel_id=1, source_target_pairs={{0,10},{2,8},{4,14},{6,12},{8,2},{10,0},{12,6},{14,4},{1,11},{3,9}... | collective-permute-start | bytes 614408 | tf_op jit(solution)/shard_map/ppermute | solution.py:317
  23.0 17.9 %collective-permute-start.5 = (bf16[2,80,640]{2,1,0:T(8,128)(2,1)S(1)}, bf16[2,80,640]{2,1,0:T(8,128)(2,1)S(1)}, u32[]{:S(2)}, u32[]{:S(2)}) collective-permute-start(bf16[2,80,640]{2,1,0:T(8,128)(2,1)S(1)} %get-tuple-element.31), channel_id=1, source_target_pairs={{0,12},{2,14},{4,8},{6,10},{8,4},{10,6},{12,0},{14,2},{1,13},{3,15... | collective-permute-start | bytes 614408 | tf_op jit(solution)/shard_map/ppermute | solution.py:317
  25.6 19.0 %collective-permute-start.6 = (bf16[2,80,640]{2,1,0:T(8,128)(2,1)S(1)}, bf16[2,80,640]{2,1,0:T(8,128)(2,1)S(1)}, u32[]{:S(2)}, u32[]{:S(2)}) collective-permute-start(bf16[2,80,640]{2,1,0:T(8,128)(2,1)S(1)} %get-tuple-element.32), channel_id=1, source_target_pairs={{0,14},{2,12},{4,10},{6,8},{8,6},{10,4},{12,2},{14,0},{1,15},{3,13... | collective-permute-start | bytes 614408 | tf_op jit(solution)/shard_map/ppermute | solution.py:317
  47.2 5.6 %collective-permute-start.7 = (bf16[80,640]{1,0:T(8,128)(2,1)S(1)}, bf16[80,640]{1,0:T(8,128)(2,1)S(1)}, u32[]{:S(2)}, u32[]{:S(2)}) collective-permute-start(bf16[80,640]{1,0:T(8,128)(2,1)S(1)} %get-tuple-element.34), channel_id=1, source_target_pairs={{0,2},{2,0},{4,6},{6,4},{8,10},{10,8},{12,14},{14,12},{1,3},{3,1},... | collective-permute-start | bytes 307208 | tf_op jit(solution)/shard_map/ppermute | solution.py:317
  47.7 7.4 %collective-permute-start.8 = (bf16[80,640]{1,0:T(8,128)(2,1)S(1)}, bf16[80,640]{1,0:T(8,128)(2,1)S(1)}, u32[]{:S(2)}, u32[]{:S(2)}) collective-permute-start(bf16[80,640]{1,0:T(8,128)(2,1)S(1)} %get-tuple-element.35), channel_id=1, source_target_pairs={{0,4},{2,6},{4,0},{6,2},{8,12},{10,14},{12,8},{14,10},{1,5},{3,7},... | collective-permute-start | bytes 307208 | tf_op jit(solution)/shard_map/ppermute | solution.py:317
  47.7 7.7 %collective-permute-start.9 = (bf16[80,640]{1,0:T(8,128)(2,1)S(1)}, bf16[80,640]{1,0:T(8,128)(2,1)S(1)}, u32[]{:S(2)}, u32[]{:S(2)}) collective-permute-start(bf16[80,640]{1,0:T(8,128)(2,1)S(1)} %get-tuple-element.36), channel_id=1, source_target_pairs={{0,6},{2,4},{4,2},{6,0},{8,14},{10,12},{12,10},{14,8},{1,7},{3,5},... | collective-permute-start | bytes 307208 | tf_op jit(solution)/shard_map/ppermute | solution.py:317
  49.2 10.6 %collective-permute-start.10 = (bf16[80,640]{1,0:T(8,128)(2,1)S(1)}, bf16[80,640]{1,0:T(8,128)(2,1)S(1)}, u32[]{:S(2)}, u32[]{:S(2)}) collective-permute-start(bf16[80,640]{1,0:T(8,128)(2,1)S(1)} %get-tuple-element.37), channel_id=1, source_target_pairs={{0,8},{2,10},{4,12},{6,14},{8,0},{10,2},{12,4},{14,6},{1,9},{3,11}... | collective-permute-start | bytes 307208 | tf_op jit(solution)/shard_map/ppermute | solution.py:317
  51.6 8.9 %collective-permute-start.11 = (bf16[80,640]{1,0:T(8,128)(2,1)S(1)}, bf16[80,640]{1,0:T(8,128)(2,1)S(1)}, u32[]{:S(2)}, u32[]{:S(2)}) collective-permute-start(bf16[80,640]{1,0:T(8,128)(2,1)S(1)} %get-tuple-element.38), channel_id=1, source_target_pairs={{0,10},{2,8},{4,14},{6,12},{8,2},{10,0},{12,6},{14,4},{1,11},{3,9}... | collective-permute-start | bytes 307208 | tf_op jit(solution)/shard_map/ppermute | solution.py:317
  52.8 10.6 %collective-permute-start.12 = (bf16[80,640]{1,0:T(8,128)(2,1)S(1)}, bf16[80,640]{1,0:T(8,128)(2,1)S(1)}, u32[]{:S(2)}, u32[]{:S(2)}) collective-permute-start(bf16[80,640]{1,0:T(8,128)(2,1)S(1)} %get-tuple-element.39), channel_id=1, source_target_pairs={{0,12},{2,14},{4,8},{6,10},{8,4},{10,6},{12,0},{14,2},{1,13},{3,15... | collective-permute-start | bytes 307208 | tf_op jit(solution)/shard_map/ppermute | solution.py:317
  55.2 9.5 %collective-permute-start.13 = (bf16[80,640]{1,0:T(8,128)(2,1)S(1)}, bf16[80,640]{1,0:T(8,128)(2,1)S(1)}, u32[]{:S(2)}, u32[]{:S(2)}) collective-permute-start(bf16[80,640]{1,0:T(8,128)(2,1)S(1)} %get-tuple-element.40), channel_id=1, source_target_pairs={{0,14},{2,12},{4,10},{6,8},{8,6},{10,4},{12,2},{14,0},{1,15},{3,13... | collective-permute-start | bytes 307208 | tf_op jit(solution)/shard_map/ppermute | solution.py:317
  66.8 33.2 %all-to-all-start.1 = ((bf16[16,5,8,640]{3,2,1,0:T(8,128)(2,1)}), bf16[16,5,8,640]{3,2,1,0:T(8,128)(2,1)S(1)}, u32[]{:S(2)}, u32[]{:S(2)}) async-start(bf16[16,5,8,640]{3,2,1,0:T(8,128)(2,1)} %turn.1), calls=%async_computation.1 | async-start | bytes 1638400 | tf_op jit(solution)/shard_map/all_to_all | solution.py:326

commit v5 on v4

--- a/solution.py
+++ b/solution.py
@@ -6,6 +6,10 @@
 from jax.experimental import pallas as pl
 from jax.experimental.pallas import tpu as pltpu
 from jax.sharding import Mesh, PartitionSpec as P
+
+TO = ((0, 1, 2, 6, 4, 3, 7, 5), (0, 1, 6, 2, 4, 7, 3, 5))
+FROM = ((0, 1, 2, 6, 4, 7, 3, 5), (0, 1, 6, 2, 4, 3, 7, 5))
+
 
 def params(mib):
     return pltpu.CompilerParams(vmem_limit_bytes=mib * 1024 * 1024)
@@ -196,12 +200,16 @@
 def spectral_kernel(slot_ref, four_hbm, basis_hbm, out_ref, four_ref, basis, left, total, sems):
     steps, _, lats, degs = basis.shape
     deg_dev = degs // 16
+    fetch = pltpu.make_async_copy(four_hbm, four_ref, sems.at[steps, 0])
+    fetch.start()
     copies = [
-        pltpu.make_async_copy(basis_hbm.at[:, b], basis.at[b], sems.at[b]) for b in range(steps)
+        [
+            pltpu.make_async_copy(basis_hbm.at[q, b], basis.at[b, q], sems.at[b, q])
+            for q in range(8)
+        ]
+        for b in range(steps)
     ]
-    fetch = pltpu.make_async_copy(four_hbm, four_ref, sems.at[steps])
-    fetch.start()
-    for copy in copies:
+    for copy in sum(copies, []):
         copy.start()
     fetch.wait()
 
@@ -213,7 +221,8 @@
                     left[pl.ds(64 * lev + 8 * seg, 8), pl.ds(q * lats, lats)] = block[
                         :, seg * lats : (seg + 1) * lats
                     ]
-        copies[b].wait()
+        for copy in copies[b]:
+            copy.wait()
         value = jnp.dot(
             left[...].astype(jnp.bfloat16),
             basis[b].reshape(8 * lats, degs),
@@ -264,7 +273,7 @@
             pltpu.VMEM((steps, 8, lats, degs), jnp.bfloat16),
             pltpu.VMEM((128, 8 * lats), jnp.float32),
             pltpu.VMEM((degs, 128), jnp.float32),
-            pltpu.SemaphoreType.DMA((steps + 1,)),
+            pltpu.SemaphoreType.DMA((steps + 1, 8)),
         ],
         compiler_params=params(16),
         cost_estimate=cost(5 * 2 * 128 * 8 * lats * degs, 2 * basis.size + 2 * fourier.size),
@@ -309,21 +318,24 @@
     x, zq = lax.axis_index("x"), lax.axis_index("zq")
     wave, lev = lax.axis_index("wave"), lax.axis_index("lev")
 
-    partner = wave ^ jnp.arange(8, dtype=jnp.int32)
+    to, source = (
+        wave ^ jnp.where(wave % 2 == 0, *(jnp.array(row, jnp.int32) for row in table))
+        for table in (TO, FROM)
+    )
 
     def swapped(blocks):
-        blocks = list(blocks)
-        for k in (4, 5, 2, 6, 3, 7, 1):
-            blocks[k] = lax.ppermute(blocks[k], "wave", [(w, w ^ k) for w in range(8)])
-        return blocks
+        return [blocks[0]] + [
+            lax.ppermute(blocks[k], "wave", [(w, w ^ TO[w % 2][k]) for w in range(8)])
+            for k in range(1, 8)
+        ]
 
     basis, token = basis_blocks(lev.astype(jnp.int32)[None], legendre_basis)
-    grads = gradient(partner, tend_rate, out_grad, grid_state, token)
+    grads = gradient(to, tend_rate, out_grad, grid_state, token)
     basis = lax.all_to_all(basis, ("x", "zq"), 0, 0, tiled=True)
     grads = swapped(grads)
-    table = wave_table(wave_slot.reshape(8, slot_dev)[partner], partner, lons, 64)
+    table = wave_table(wave_slot.reshape(8, slot_dev)[to], source, lons, 64)
     blocks = swapped(fourier_rows(table, grads))
-    fourier = lax.all_to_all(turn(partner, basis, blocks), ("x", "zq", "lev"), 0, 0, tiled=True)
+    fourier = lax.all_to_all(turn(source, basis, blocks), ("x", "zq", "lev"), 0, 0, tiled=True)
 
     first = wave * slot_dev + 8 * lev + 2 * x + zq
     slots = jnp.take(wave_slot, first + 16 * jnp.arange(slot_dev // 16, dtype=jnp.int32))

time: 135 us -> 128 us (0.948)
  waiting for transfers between devices: 47.3 us -> 40.4 us
    ppermute x14, waiting for transfers between devices: 25.1 us -> 16.4 us  [swapped(): lax.ppermute(blocks[k], 'wave', [(w, w ^ TO[w % 2][k]) for w in range(8)])]
    all_to_all x1, waiting for transfers between devices: 0.01 us -> 2.97 us  [local(): basis = lax.all_to_all(basis, ('x', 'zq'), 0, 0, tiled=True)]
  transfers between devices with their start and end apart: 16 -> 16, of which waited for: 9 -> 10; matrix products, arithmetic and copies ran while one was open for 3% -> 3% of each run, Pallas kernels for 5% -> 5%
where the time goes in v5:
time: 128 us; the launch traced here: 127 us
  waiting for transfers between devices  40.4 us (32%)
  starting transfers between devices  32.2 us (25%)
  blocking collectives  29.1 us (23%)
  Pallas kernels  19.7 us (15%)
  local copies, waits for them, and re-layouts  3.16 us (2%)
  other arithmetic  2.39 us (2%)
    all_to_all x1, blocking collectives, local(): parts = lax.all_to_all(parts, ('x', 'zp', 'zq', 'lev'), 0, 0, tiled=True)  29.1 us
    all_to_all x1, waiting for transfers between devices, local(): lax.all_to_all(turn(source, basis, blocks), ('x', 'zq', 'lev'), 0, 0, til...  21.1 us
    ppermute x14, waiting for transfers between devices, swapped(): lax.ppermute(blocks[k], 'wave', [(w, w ^ TO[w % 2][k]) for w in range(8)])  16.4 us
    ppermute x14, starting transfers between devices, swapped(): lax.ppermute(blocks[k], 'wave', [(w, w ^ TO[w % 2][k]) for w in range(8)])  15.1 us
    all_to_all x1, starting transfers between devices, local(): lax.all_to_all(turn(source, basis, blocks), ('x', 'zq', 'lev'), 0, 0, til...  10.3 us
    all_to_all x1, starting transfers between devices, local(): basis = lax.all_to_all(basis, ('x', 'zq'), 0, 0, tiled=True)  6.84 us
    pallas_call x1, Pallas kernels, basis_blocks(): pl.pallas_call(basis_kernel, in_specs=[pl.BlockSpec(memory_space=pltpu.SM...  4.65 us
    pallas_call x1, Pallas kernels, spectral_parts(): pl.pallas_call(spectral_kernel, in_specs=[pl.BlockSpec(memory_space=pltpu...  4.52 us
  transfers between devices with their start and end apart: 16, of which 10 were waited for; matrix products, arithmetic and copies ran while one was open for 3% of the time, Pallas kernels for 5%

profile of v5, /device:TPU:2, one launch (start us, length us, event | category | flops | bytes accessed | tf_op | source)
XLA Modules:
  0.0 127.2 jit_solution(12156285510435138960)
XLA Ops:
  0.0 4.7 %basis_blocks.1 = (bf16[8,5,80,640]{3,2,1,0:T(8,128)(2,1)}, f32[8,128]{1,0:T(8,128)}) custom-call(s32[1]{0:T(128)} %bitcast.1.lev_ref, bf16[80,10,8,640]{3,2,1,0:T(8,128)(2,1)} %bitcast.9), custom_call_target="tpu_custom_call" | custom-call | bytes 8192000 | tf_op jit(solution)/shard_map/basis_blocks/pallas_call | solution.py:54
  4.7 0.0 copy-start.7
  4.7 0.0 copy-start.8
  4.7 0.0 copy-start
  4.7 0.0 copy-start.2
  4.7 0.0 copy-start.3
  4.7 0.0 copy-start.4
  4.7 6.8 %all-to-all-start = ((bf16[8,5,80,640]{3,2,1,0:T(8,128)(2,1)}), bf16[8,5,80,640]{3,2,1,0:T(8,128)(2,1)}, u32[]{:S(2)}, u32[]{:S(2)}) async-start(bf16[8,5,80,640]{3,2,1,0:T(8,128)(2,1)} %get-tuple-element.23), calls=%async_computation | async-start | bytes 8192000 | tf_op jit(solution)/shard_map/all_to_all | solution.py:334
  11.6 0.0 copy-start.1
  11.6 1.5 %copy-done.1 = bf16[32,80,320]{2,1,0:T(8,128)(2,1)S(1)} copy-done((bf16[32,80,320]{2,1,0:T(8,128)(2,1)S(1)}, bf16[32,80,320]{2,1,0:T(8,128)(2,1)}, u32[]{:S(2)}) %copy-start.1) | copy-done | bytes 1638424
  13.2 2.4 %gradient.1 = (bf16[2,80,640]{2,1,0:T(8,128)(2,1)S(1)}, bf16[2,80,640]{2,1,0:T(8,128)(2,1)}, bf16[2,80,640]{2,1,0:T(8,128)(2,1)S(1)}, bf16[2,80,640]{2,1,0:T(8,1...) custom-call(s32[8]{0:T(128)S(1)} %get-tuple-element.42.wave_ref, ...), custom_call_target="tpu_custom_call" | custom-call | flops 4915200 | bytes 4915200 | tf_op jit(solution)/shard_map/gradient/pallas_call | solution.py:88
  15.6 0.0 collective-permute-start
  15.6 1.1 collective-permute-start.1
  16.7 2.2 %collective-permute-start.2 = (bf16[2,80,640]{2,1,0:T(8,128)(2,1)S(1)}, bf16[2,80,640]{2,1,0:T(8,128)(2,1)S(1)}, u32[]{:S(2)}, u32[]{:S(2)}) collective-permute-start(bf16[2,80,640]{2,1,0:T(8,128)(2,1)S(1)} %get-tuple-element.28), channel_id=1, source_target_pairs={{0,12},{2,6},{4,8},{6,2},{8,4},{10,14},{12,0},{14,10},{1,13},{3,7}... | collective-permute-start | bytes 614408 | tf_op jit(solution)/shard_map/ppermute | solution.py:328
  18.9 0.8 collective-permute-start.3
  19.7 0.1 reshape.67
  19.8 0.6 gather_fusion.1
  20.4 0.1 mul.86
  20.5 0.1 broadcast_in_dim.12
  20.6 0.1 add.109
  20.7 1.3 %fusion.4 = (f32[64,1280]{1,0:T(8,128)S(1)}, f32[64,1280]{1,0:T(8,128)S(1)}) fusion(s32[1280]{0:T(1024)S(1)} %add.109, s32[1280]{0:T(1024)S(1)} %mul.86), kind=kLoop, calls=%fused_computation.8 | loop fusion | flops 819200 | bytes 665600 | tf_op jit(solution)/shard_map/sin | solution.py:116
  22.0 0.1 broadcast_add_fusion
  22.1 0.1 add.107
  22.2 3.0 %collective-permute-start.5 = (bf16[2,80,640]{2,1,0:T(8,128)(2,1)S(1)}, bf16[2,80,640]{2,1,0:T(8,128)(2,1)S(1)}, u32[]{:S(2)}, u32[]{:S(2)}) collective-permute-start(bf16[2,80,640]{2,1,0:T(8,128)(2,1)S(1)} %get-tuple-element.31), channel_id=1, source_target_pairs={{0,14},{2,4},{4,10},{6,0},{8,6},{10,12},{12,2},{14,8},{1,15},{3,5}... | collective-permute-start | bytes 614408 | tf_op jit(solution)/shard_map/ppermute | solution.py:328
  25.2 0.7 collective-permute-start.6
  26.0 0.9 sine_multiply_fusion
  26.9 1.7 %wave_table.1.table_ref = bf16[5,2560,256]{2,1,0:T(8,128)(2,1)S(1)} custom-call(f32[40,1280]{1,0:T(8,128)S(1)} %get-tuple-element.48.coarse_cos, f32[40,1280]{1,0:T(8,128)S(1)} %get-tuple-element.47.coarse_sin, f32[64,1280]{1,0:T(8,128)S(1)} %get-tuple-element.46.fine_cos, f32[64,1280]{1,0:T(8,128)S(1)} %get-tuple-element.45.fine_sin), custom_call_target="tpu_custom_call" | custom-call | flops 9830400 | bytes 6553600 | tf_op jit(solution)/shard_map/wave_table/pallas_call | solution.py:124
  28.6 1.4 %collective-permute-done.3.refs_4_ = bf16[2,80,640]{2,1,0:T(8,128)(2,1)S(1)} collective-permute-done((bf16[2,80,640]{2,1,0:T(8,128)(2,1)S(1)}, bf16[2,80,640]{2,1,0:T(8,128)(2,1)S(1)}, u32[]{:S(2)}, u32[]{:S(2)}) %collective-permute-start.3) | collective-permute-done | bytes 204832 | tf_op jit(solution)/shard_map/ppermute | solution.py:328
  30.0 1.7 %collective-permute-done.4.refs_5_ = bf16[2,80,640]{2,1,0:T(8,128)(2,1)S(1)} collective-permute-done((bf16[2,80,640]{2,1,0:T(8,128)(2,1)S(1)}, bf16[2,80,640]{2,1,0:T(8,128)(2,1)S(1)}, u32[]{:S(2)}, u32[]{:S(2)}) %collective-permute-start.4) | collective-permute-done | bytes 204832 | tf_op jit(solution)/shard_map/ppermute | solution.py:328
  31.8 4.6 %collective-permute-done.5.refs_6_ = bf16[2,80,640]{2,1,0:T(8,128)(2,1)S(1)} collective-permute-done((bf16[2,80,640]{2,1,0:T(8,128)(2,1)S(1)}, bf16[2,80,640]{2,1,0:T(8,128)(2,1)S(1)}, u32[]{:S(2)}, u32[]{:S(2)}) %collective-permute-start.5) | collective-permute-done | bytes 204832 | tf_op jit(solution)/shard_map/ppermute | solution.py:328
  36.3 2.4 %collective-permute-done.6.refs_7_ = bf16[2,80,640]{2,1,0:T(8,128)(2,1)S(1)} collective-permute-done((bf16[2,80,640]{2,1,0:T(8,128)(2,1)S(1)}, bf16[2,80,640]{2,1,0:T(8,128)(2,1)S(1)}, u32[]{:S(2)}, u32[]{:S(2)}) %collective-permute-start.6) | collective-permute-done | bytes 204832 | tf_op jit(solution)/shard_map/ppermute | solution.py:328
  38.7 2.6 %fourier_rows.1 = (bf16[80,640]{1,0:T(8,128)(2,1)S(1)}, bf16[80,640]{1,0:T(8,128)(2,1)S(1)}, bf16[80,640]{1,0:T(8,128)(2,1)S(1)}, bf16[80,640]{1,0:T(8,128)(2,1)...) custom-call(bf16[5,2560,256]{2,1,0:T(8,128)(2,1)S(1)} %wave_table.1., ...), custom_call_target="tpu_custom_call" | custom-call | flops 2097152000 | bytes 6553600 | tf_op jit(solution)/shard_map/fourier_rows/pallas_call | solution.py:159
  41.3 0.2 collective-permute-start.7
  41.5 1.4 %collective-permute-start.9 = (bf16[80,640]{1,0:T(8,128)(2,1)S(1)}, bf16[80,640]{1,0:T(8,128)(2,1)S(1)}, u32[]{:S(2)}, u32[]{:S(2)}) collective-permute-start(bf16[80,640]{1,0:T(8,128)(2,1)S(1)} %get-tuple-element.36), channel_id=1, source_target_pairs={{0,12},{2,6},{4,8},{6,2},{8,4},{10,14},{12,0},{14,10},{1,13},{3,7}... | collective-permute-start | bytes 307208 | tf_op jit(solution)/shard_map/ppermute | solution.py:328
  42.9 2.7 %collective-permute-start.10 = (bf16[80,640]{1,0:T(8,128)(2,1)S(1)}, bf16[80,640]{1,0:T(8,128)(2,1)S(1)}, u32[]{:S(2)}, u32[]{:S(2)}) collective-permute-start(bf16[80,640]{1,0:T(8,128)(2,1)S(1)} %get-tuple-element.37), channel_id=1, source_target_pairs={{0,8},{2,10},{4,12},{6,14},{8,0},{10,2},{12,4},{14,6},{1,9},{3,11}... | collective-permute-start | bytes 307208 | tf_op jit(solution)/shard_map/ppermute | solution.py:328
  45.6 3.0 %collective-permute-start.12 = (bf16[80,640]{1,0:T(8,128)(2,1)S(1)}, bf16[80,640]{1,0:T(8,128)(2,1)S(1)}, u32[]{:S(2)}, u32[]{:S(2)}) collective-permute-start(bf16[80,640]{1,0:T(8,128)(2,1)S(1)} %get-tuple-element.39), channel_id=1, source_target_pairs={{0,14},{2,4},{4,10},{6,0},{8,6},{10,12},{12,2},{14,8},{1,15},{3,5}... | collective-permute-start | bytes 307208 | tf_op jit(solution)/shard_map/ppermute | solution.py:328
  48.6 1.6 %collective-permute-done.10.refs_4_ = bf16[80,640]{1,0:T(8,128)(2,1)S(1)} collective-permute-done((bf16[80,640]{1,0:T(8,128)(2,1)S(1)}, bf16[80,640]{1,0:T(8,128)(2,1)S(1)}, u32[]{:S(2)}, u32[]{:S(2)}) %collective-permute-start.10) | collective-permute-done | bytes 102432 | tf_op jit(solution)/shard_map/ppermute | solution.py:328
  50.2 1.2 collective-permute-done.11.refs_5_
  51.4 0.2 collective-permute-done.12.refs_6_
  51.7 3.2 %collective-permute-done.13.refs_7_ = bf16[80,640]{1,0:T(8,128)(2,1)S(1)} collective-permute-done((bf16[80,640]{1,0:T(8,128)(2,1)S(1)}, bf16[80,640]{1,0:T(8,128)(2,1)S(1)}, u32[]{:S(2)}, u32[]{:S(2)}) %collective-permute-start.13) | collective-permute-done | bytes 102432 | tf_op jit(solution)/shard_map/ppermute | solution.py:328
  54.8 3.0 %all-to-all-done._.basis_hbm = bf16[8,5,80,640]{3,2,1,0:T(8,128)(2,1)} async-done(((bf16[8,5,80,640]{3,2,1,0:T(8,128)(2,1)}), bf16[8,5,80,640]{3,2,1,0:T(8,128)(2,1)}, u32[]{:S(2)}, u32[]{:S(2)}) %all-to-all-start) | async-done | bytes 4096032 | tf_op jit(solution)/shard_map/all_to_all | solution.py:334
  57.8 2.1 %turn.1 = bf16[16,5,8,640]{3,2,1,0:T(8,128)(2,1)} custom-call(s32[8]{0:T(128)S(1)} %get-tuple-element.44.wave_ref, bf16[8,5,80,640]{3,2,1,0:T(8,128)(2,1)} %all-to-all-done._.basis_hbm, bf16[80,640]{1,0:T(8,128)(2,1)S(1)} %get-tuple-element.33.refs_0_, bf16[80,640]{1,0:T(8,128)(2,1)S(1)} %collective-permute-done.7.refs_1_, ...), custom_call_target="tpu_custom_call" | custom-call | bytes 1638400 | tf_op jit(solution)/shard_map/turn/pallas_call | solution.py:188
  59.9 10.3 %all-to-all-start.1 = ((bf16[16,5,8,640]{3,2,1,0:T(8,128)(2,1)}), bf16[16,5,8,640]{3,2,1,0:T(8,128)(2,1)S(1)}, u32[]{:S(2)}, u32[]{:S(2)}) async-start(bf16[16,5,8,640]{3,2,1,0:T(8,128)(2,1)} %turn.1), calls=%async_computation.1 | async-start | bytes 1638400 | tf_op jit(solution)/shard_map/all_to_all | solution.py:338
  70.2 0.6 gather_fusion
  70.8 21.1 %all-to-all-done.1.four_hbm = bf16[16,5,8,640]{3,2,1,0:T(8,128)(2,1)S(1)} async-done(((bf16[16,5,8,640]{3,2,1,0:T(8,128)(2,1)}), bf16[16,5,8,640]{3,2,1,0:T(8,128)(2,1)S(1)}, u32[]{:S(2)}, u32[]{:S(2)}) %all-to-all-start.1) | async-done | bytes 819232 | tf_op jit(solution)/shard_map/all_to_all | solution.py:338
  91.9 4.5 %spectral_parts.1 = bf16[32,104,128]{2,1,0:T(8,128)(2,1)S(1)} custom-call(s32[5]{0:T(128)S(1)} %and_select_fusion.slot_ref, bf16[16,5,8,640]{3,2,1,0:T(8,128)(2,1)S(1)} %all-to-all-done.1.four_hbm, bf16[8,5,80,640]{3,2,1,0:T(8,128)(2,1)} %all-to-all-done._.basis_hbm), custom_call_target="tpu_custom_call" | custom-call | flops 524288000 | bytes 4915200 | tf_op jit(solution)/shard_map/spectral_parts/pallas_call | solution.py:267
  96.4 29.1 %all_to_all.15.in_ref = bf16[32,104,128]{2,1,0:T(8,128)(2,1)S(1)} all-to-all(bf16[32,104,128]{2,1,0:T(8,128)(2,1)S(1)} %spectral_parts.1), channel_id=1, replica_groups=mesh['x'=4,'zp'=2,'zq'=2,'wave'=8,'lev'=2] {'x','zp','zq','lev'}, dimensions={0} | all-to-all | bytes 1703936 | tf_op jit(solution)/shard_map/all_to_all | solution.py:343
  125.5 1.7 %finish.1 = f32[2560,80]{1,0:T(8,128)} custom-call(bf16[32,104,128]{2,1,0:T(8,128)(2,1)S(1)} %all_to_all.15.in_ref), custom_call_target="tpu_custom_call" | custom-call | flops 425984 | bytes 2162688 | tf_op jit(solution)/shard_map/finish/pallas_call | solution.py:305
  (29 shorter events, 0.1 us)
Async XLA Ops:
  4.7 6.9 %copy-start.7 = (s32[8]{0:T(128)S(1)}, s32[8]{0:T(128)}, u32[]{:S(2)}) copy-start(s32[8]{0:T(128)} %constant.94.clone) | copy-start | bytes 100
  4.7 6.9 %copy-start.8 = (s32[8]{0:T(128)S(1)}, s32[8]{0:T(128)}, u32[]{:S(2)}) copy-start(s32[8]{0:T(128)} %constant.95.clone) | copy-start | bytes 100
  4.7 6.9 %copy-start = (bf16[32,80,320]{2,1,0:T(8,128)(2,1)S(1)}, bf16[32,80,320]{2,1,0:T(8,128)(2,1)}, u32[]{:S(2)}) copy-start(bf16[32,80,320]{2,1,0:T(8,128)(2,1)} %param.10) | copy-start | bytes 4915204
  4.7 6.9 %copy-start.2 = (f32[8,128]{1,0:T(8,128)S(1)}, f32[8,128]{1,0:T(8,128)}, u32[]{:S(2)}) copy-start(f32[8,128]{1,0:T(8,128)} %get-tuple-element.24._) | copy-start | bytes 12292
  4.7 6.9 %copy-start.3 = (f32[32]{0:T(128)S(1)}, f32[32]{0:T(128)}, u32[]{:S(2)}) copy-start(f32[32]{0:T(128)} %rate_ref.1) | copy-start | bytes 388
  4.7 15.0 %copy-start.4 = (s32[640]{0:T(1024)S(1)}, s32[640]{0:T(1024)}, u32[]{:S(2)}) copy-start(s32[640]{0:T(1024)} %param.14) | copy-start | bytes 7684
  4.7 53.1 %all-to-all-start = ((bf16[8,5,80,640]{3,2,1,0:T(8,128)(2,1)}), bf16[8,5,80,640]{3,2,1,0:T(8,128)(2,1)}, u32[]{:S(2)}, u32[]{:S(2)}) async-start(bf16[8,5,80,640]{3,2,1,0:T(8,128)(2,1)} %get-tuple-element.23), calls=%async_computation | async-start | bytes 8192000 | tf_op jit(solution)/shard_map/all_to_all | solution.py:334
  11.6 9.1 %copy-start.5 = (s32[8]{0:T(128)S(1)}, s32[8]{0:T(128)}, u32[]{:S(2)}) copy-start(s32[8]{0:T(128)} %constant.96.clone) | copy-start | bytes 100
  11.6 9.1 %copy-start.6 = (s32[8]{0:T(128)S(1)}, s32[8]{0:T(128)}, u32[]{:S(2)}) copy-start(s32[8]{0:T(128)} %constant.97.clone) | copy-start | bytes 100
  11.6 1.5 %copy-start.1 = (bf16[32,80,320]{2,1,0:T(8,128)(2,1)S(1)}, bf16[32,80,320]{2,1,0:T(8,128)(2,1)}, u32[]{:S(2)}) copy-start(bf16[32,80,320]{2,1,0:T(8,128)(2,1)} %param.11) | copy-start | bytes 4915204
  15.6 6.6 %collective-permute-start = (bf16[2,80,640]{2,1,0:T(8,128)(2,1)}, bf16[2,80,640]{2,1,0:T(8,128)(2,1)S(1)}, u32[]{:S(2)}, u32[]{:S(2)}) collective-permute-start(bf16[2,80,640]{2,1,0:T(8,128)(2,1)} %get-tuple-element.26), channel_id=1, source_target_pairs={{0,2},{2,0},{4,6},{6,4},{8,10},{10,8},{12,14},{14,12},{1,3},{3,1},... | collective-permute-start | bytes 614408 | tf_op jit(solution)/shard_map/ppermute | solution.py:328
  15.6 9.6 %collective-permute-start.1 = (bf16[2,80,640]{2,1,0:T(8,128)(2,1)S(1)}, bf16[2,80,640]{2,1,0:T(8,128)(2,1)S(1)}, u32[]{:S(2)}, u32[]{:S(2)}) collective-permute-start(bf16[2,80,640]{2,1,0:T(8,128)(2,1)S(1)} %get-tuple-element.27), channel_id=1, source_target_pairs={{0,4},{2,14},{4,0},{6,10},{8,12},{10,6},{12,8},{14,2},{1,5},{3,15}... | collective-permute-start | bytes 614408 | tf_op jit(solution)/shard_map/ppermute | solution.py:328
  16.7 11.9 %collective-permute-start.2 = (bf16[2,80,640]{2,1,0:T(8,128)(2,1)S(1)}, bf16[2,80,640]{2,1,0:T(8,128)(2,1)S(1)}, u32[]{:S(2)}, u32[]{:S(2)}) collective-permute-start(bf16[2,80,640]{2,1,0:T(8,128)(2,1)S(1)} %get-tuple-element.28), channel_id=1, source_target_pairs={{0,12},{2,6},{4,8},{6,2},{8,4},{10,14},{12,0},{14,10},{1,13},{3,7}... | collective-permute-start | bytes 614408 | tf_op jit(solution)/shard_map/ppermute | solution.py:328
  18.9 11.1 %collective-permute-start.3 = (bf16[2,80,640]{2,1,0:T(8,128)(2,1)S(1)}, bf16[2,80,640]{2,1,0:T(8,128)(2,1)S(1)}, u32[]{:S(2)}, u32[]{:S(2)}) collective-permute-start(bf16[2,80,640]{2,1,0:T(8,128)(2,1)S(1)} %get-tuple-element.29), channel_id=1, source_target_pairs={{0,8},{2,10},{4,12},{6,14},{8,0},{10,2},{12,4},{14,6},{1,9},{3,11}... | collective-permute-start | bytes 614408 | tf_op jit(solution)/shard_map/ppermute | solution.py:328
  19.7 12.0 %collective-permute-start.4 = (bf16[2,80,640]{2,1,0:T(8,128)(2,1)S(1)}, bf16[2,80,640]{2,1,0:T(8,128)(2,1)S(1)}, u32[]{:S(2)}, u32[]{:S(2)}) collective-permute-start(bf16[2,80,640]{2,1,0:T(8,128)(2,1)S(1)} %get-tuple-element.30), channel_id=1, source_target_pairs={{0,6},{2,12},{4,2},{6,8},{8,14},{10,4},{12,10},{14,0},{1,7},{3,13}... | collective-permute-start | bytes 614408 | tf_op jit(solution)/shard_map/ppermute | solution.py:328
  22.2 14.2 %collective-permute-start.5 = (bf16[2,80,640]{2,1,0:T(8,128)(2,1)S(1)}, bf16[2,80,640]{2,1,0:T(8,128)(2,1)S(1)}, u32[]{:S(2)}, u32[]{:S(2)}) collective-permute-start(bf16[2,80,640]{2,1,0:T(8,128)(2,1)S(1)} %get-tuple-element.31), channel_id=1, source_target_pairs={{0,14},{2,4},{4,10},{6,0},{8,6},{10,12},{12,2},{14,8},{1,15},{3,5}... | collective-permute-start | bytes 614408 | tf_op jit(solution)/shard_map/ppermute | solution.py:328
  25.2 13.5 %collective-permute-start.6 = (bf16[2,80,640]{2,1,0:T(8,128)(2,1)S(1)}, bf16[2,80,640]{2,1,0:T(8,128)(2,1)S(1)}, u32[]{:S(2)}, u32[]{:S(2)}) collective-permute-start(bf16[2,80,640]{2,1,0:T(8,128)(2,1)S(1)} %get-tuple-element.32), channel_id=1, source_target_pairs={{0,10},{2,8},{4,14},{6,12},{8,2},{10,0},{12,6},{14,4},{1,11},{3,9}... | collective-permute-start | bytes 614408 | tf_op jit(solution)/shard_map/ppermute | solution.py:328
  41.3 4.3 %collective-permute-start.7 = (bf16[80,640]{1,0:T(8,128)(2,1)S(1)}, bf16[80,640]{1,0:T(8,128)(2,1)S(1)}, u32[]{:S(2)}, u32[]{:S(2)}) collective-permute-start(bf16[80,640]{1,0:T(8,128)(2,1)S(1)} %get-tuple-element.34), channel_id=1, source_target_pairs={{0,2},{2,0},{4,6},{6,4},{8,10},{10,8},{12,14},{14,12},{1,3},{3,1},... | collective-permute-start | bytes 307208 | tf_op jit(solution)/shard_map/ppermute | solution.py:328
  41.5 7.1 %collective-permute-start.8 = (bf16[80,640]{1,0:T(8,128)(2,1)S(1)}, bf16[80,640]{1,0:T(8,128)(2,1)S(1)}, u32[]{:S(2)}, u32[]{:S(2)}) collective-permute-start(bf16[80,640]{1,0:T(8,128)(2,1)S(1)} %get-tuple-element.35), channel_id=1, source_target_pairs={{0,4},{2,14},{4,0},{6,10},{8,12},{10,6},{12,8},{14,2},{1,5},{3,15}... | collective-permute-start | bytes 307208 | tf_op jit(solution)/shard_map/ppermute | solution.py:328
  41.5 7.1 %collective-permute-start.9 = (bf16[80,640]{1,0:T(8,128)(2,1)S(1)}, bf16[80,640]{1,0:T(8,128)(2,1)S(1)}, u32[]{:S(2)}, u32[]{:S(2)}) collective-permute-start(bf16[80,640]{1,0:T(8,128)(2,1)S(1)} %get-tuple-element.36), channel_id=1, source_target_pairs={{0,12},{2,6},{4,8},{6,2},{8,4},{10,14},{12,0},{14,10},{1,13},{3,7}... | collective-permute-start | bytes 307208 | tf_op jit(solution)/shard_map/ppermute | solution.py:328
  42.9 7.3 %collective-permute-start.10 = (bf16[80,640]{1,0:T(8,128)(2,1)S(1)}, bf16[80,640]{1,0:T(8,128)(2,1)S(1)}, u32[]{:S(2)}, u32[]{:S(2)}) collective-permute-start(bf16[80,640]{1,0:T(8,128)(2,1)S(1)} %get-tuple-element.37), channel_id=1, source_target_pairs={{0,8},{2,10},{4,12},{6,14},{8,0},{10,2},{12,4},{14,6},{1,9},{3,11}... | collective-permute-start | bytes 307208 | tf_op jit(solution)/shard_map/ppermute | solution.py:328
  45.6 5.8 %collective-permute-start.11 = (bf16[80,640]{1,0:T(8,128)(2,1)S(1)}, bf16[80,640]{1,0:T(8,128)(2,1)S(1)}, u32[]{:S(2)}, u32[]{:S(2)}) collective-permute-start(bf16[80,640]{1,0:T(8,128)(2,1)S(1)} %get-tuple-element.38), channel_id=1, source_target_pairs={{0,6},{2,12},{4,2},{6,8},{8,14},{10,4},{12,10},{14,0},{1,7},{3,13}... | collective-permute-start | bytes 307208 | tf_op jit(solution)/shard_map/ppermute | solution.py:328
  45.6 6.0 %collective-permute-start.12 = (bf16[80,640]{1,0:T(8,128)(2,1)S(1)}, bf16[80,640]{1,0:T(8,128)(2,1)S(1)}, u32[]{:S(2)}, u32[]{:S(2)}) collective-permute-start(bf16[80,640]{1,0:T(8,128)(2,1)S(1)} %get-tuple-element.39), channel_id=1, source_target_pairs={{0,14},{2,4},{4,10},{6,0},{8,6},{10,12},{12,2},{14,8},{1,15},{3,5}... | collective-permute-start | bytes 307208 | tf_op jit(solution)/shard_map/ppermute | solution.py:328
  48.6 6.2 %collective-permute-start.13 = (bf16[80,640]{1,0:T(8,128)(2,1)S(1)}, bf16[80,640]{1,0:T(8,128)(2,1)S(1)}, u32[]{:S(2)}, u32[]{:S(2)}) collective-permute-start(bf16[80,640]{1,0:T(8,128)(2,1)S(1)} %get-tuple-element.40), channel_id=1, source_target_pairs={{0,10},{2,8},{4,14},{6,12},{8,2},{10,0},{12,6},{14,4},{1,11},{3,9}... | collective-permute-start | bytes 307208 | tf_op jit(solution)/shard_map/ppermute | solution.py:328
  59.9 32.0 %all-to-all-start.1 = ((bf16[16,5,8,640]{3,2,1,0:T(8,128)(2,1)}), bf16[16,5,8,640]{3,2,1,0:T(8,128)(2,1)S(1)}, u32[]{:S(2)}, u32[]{:S(2)}) async-start(bf16[16,5,8,640]{3,2,1,0:T(8,128)(2,1)} %turn.1), calls=%async_computation.1 | async-start | bytes 1638400 | tf_op jit(solution)/shard_map/all_to_all | solution.py:338

commit v6 on v5

--- a/solution.py
+++ b/solution.py
@@ -11,6 +11,34 @@
 FROM = ((0, 1, 2, 6, 4, 7, 3, 5), (0, 1, 6, 2, 4, 3, 7, 5))
 
 
+AXES = ("x", "zp", "zq", "wave", "lev")
+BASIS_AT = ([m for m in range(8)], [m % 2 * 4 + -(m // 2) % 4 for m in range(8)])
+FOUR_AT = (
+    [m for m in range(16)],
+    [m % 2 * 8 + m // 2 % 2 * 4 + -(m // 4) % 4 for m in range(16)],
+)
+LAST_AT = (
+    [m for m in range(32)],
+    [-(m % 2 * 4 + m // 2 % 4) % 8 * 4 + -(m // 8) % 4 for m in range(32)],
+)
+
+
+def exchange(blocks, at, axes):
+    sizes = dict(x=4, zp=2, zq=2, wave=8, lev=2)
+    coordinates = [dict()]
+    for axis in AXES:
+        coordinates = [{**c, axis: i} for c in coordinates for i in range(sizes[axis])]
+    groups = {}
+    for index, c in enumerate(coordinates):
+        member = 0
+        for axis in axes:
+            member = member * sizes[axis] + c[axis]
+        key = tuple(c[axis] for axis in AXES if axis not in axes)
+        groups.setdefault(key, {})[at[c["wave"] % 2][member]] = index
+    lists = [[group[i] for i in range(len(group))] for group in groups.values()]
+    return lax.all_to_all(blocks, AXES, 0, 0, tiled=True, axis_index_groups=lists)
+
+
 def params(mib):
     return pltpu.CompilerParams(vmem_limit_bytes=mib * 1024 * 1024)
 
@@ -19,7 +47,7 @@
     return pl.CostEstimate(flops=flops, bytes_accessed=moved, transcendentals=trans)
 
 
-def basis_kernel(lev_ref, basis_hbm, out_hbm, token_ref, in_buf, out_buf, in_sems, out_sems):
+def basis_kernel(lev_ref, at_ref, basis_hbm, out_hbm, token_ref, in_buf, out_buf, in_sems, out_sems):
     steps, lats, _, degs = in_buf.shape
     lev = lev_ref[0]
     reads = [
@@ -41,19 +69,23 @@
             out_buf[b, :, 16 * g : 16 * g + 16, :] = turned.astype(jnp.bfloat16).reshape(
                 8, 16, degs
             )
-        writes.append(pltpu.make_async_copy(out_buf.at[b], out_hbm.at[:, b], out_sems.at[b]))
-        writes[b].start()
+        for r in range(8):
+            write = pltpu.make_async_copy(
+                out_buf.at[b, r], out_hbm.at[at_ref[r], b], out_sems.at[b, r]
+            )
+            write.start()
+            writes.append(write)
     for write in writes:
         write.wait()
 
 
-def basis_blocks(lev, basis):
+def basis_blocks(lev, at, basis):
     lats, slots, degs = basis.shape
     steps = slots // 16
-    hbm = pl.BlockSpec(memory_space=pltpu.HBM)
+    hbm, smem = pl.BlockSpec(memory_space=pltpu.HBM), pl.BlockSpec(memory_space=pltpu.SMEM)
     return pl.pallas_call(
         basis_kernel,
-        in_specs=[pl.BlockSpec(memory_space=pltpu.SMEM), hbm],
+        in_specs=[smem, smem, hbm],
         out_specs=[hbm, pl.BlockSpec(memory_space=pltpu.VMEM)],
         out_shape=[
             jax.ShapeDtypeStruct((8, steps, lats, degs), jnp.bfloat16),
@@ -63,12 +95,12 @@
             pltpu.VMEM((steps, lats, 8, degs), jnp.bfloat16),
             pltpu.VMEM((steps, 8, lats, degs), jnp.bfloat16),
             pltpu.SemaphoreType.DMA((steps,)),
-            pltpu.SemaphoreType.DMA((steps,)),
+            pltpu.SemaphoreType.DMA((steps, 8)),
         ],
         compiler_params=params(60),
         cost_estimate=cost(0, 2 * lats * slots * degs),
         name="basis_blocks",
-    )(lev, basis.reshape(lats, slots // 8, 8, degs))
+    )(lev, at, basis.reshape(lats, slots // 8, 8, degs))
 
 
 def grad_kernel(wave_ref, rate_ref, grad_ref, state_ref, _, *outs):
@@ -167,7 +199,7 @@
     )(table, *grads)
 
 
-def turn_kernel(wave_ref, _, *refs):
+def turn_kernel(wave_ref, at_ref, _, *refs):
     blocks, (out_ref, rows) = refs[:8], refs[8:]
     slots, width = blocks[0].shape
     for t in range(width // 128):
@@ -177,52 +209,44 @@
             rows[t, pl.ds(start, slots), :] = blocks[k][:, lanes].astype(jnp.float32)
         for s in range(slots):
             b, lev, r = s // 16, s // 8 % 2, s % 8
-            out_ref[2 * r + lev, b, :, lanes] = rows[t, pl.ds(s, 8, stride=slots), :].astype(
+            out_ref[at_ref[2 * r + lev], b, :, lanes] = rows[t, pl.ds(s, 8, stride=slots), :].astype(
                 jnp.bfloat16
             )
 
 
-def turn(waves, after, blocks):
+def turn(waves, at, after, blocks):
     slots, width = blocks[0].shape
-    vmem = pl.BlockSpec(memory_space=pltpu.VMEM)
+    vmem, smem = pl.BlockSpec(memory_space=pltpu.VMEM), pl.BlockSpec(memory_space=pltpu.SMEM)
     return pl.pallas_call(
         turn_kernel,
-        in_specs=[pl.BlockSpec(memory_space=pltpu.SMEM), pl.BlockSpec(memory_space=pl.ANY)]
-        + [vmem] * 8,
+        in_specs=[smem, smem, pl.BlockSpec(memory_space=pl.ANY)] + [vmem] * 8,
         out_shape=jax.ShapeDtypeStruct((16, slots // 16, 8, width), jnp.bfloat16),
         scratch_shapes=[pltpu.VMEM((width // 128, 8 * slots, 128), jnp.float32)],
         compiler_params=params(12),
         cost_estimate=cost(0, 32 * blocks[0].size),
         name="turn",
-    )(waves, after, *blocks)
-
-
-def spectral_kernel(slot_ref, four_hbm, basis_hbm, out_ref, four_ref, basis, left, total, sems):
+    )(waves, at, after, *blocks)
+
+
+def spectral_kernel(slot_ref, four_at, last_at, four_ref, basis_hbm, out_ref, *scratch):
+    basis, left, total, sems = scratch
     steps, _, lats, degs = basis.shape
     deg_dev = degs // 16
-    fetch = pltpu.make_async_copy(four_hbm, four_ref, sems.at[steps, 0])
-    fetch.start()
     copies = [
-        [
-            pltpu.make_async_copy(basis_hbm.at[q, b], basis.at[b, q], sems.at[b, q])
-            for q in range(8)
-        ]
-        for b in range(steps)
+        pltpu.make_async_copy(basis_hbm.at[:, b], basis.at[b], sems.at[b]) for b in range(steps)
     ]
-    for copy in sum(copies, []):
+    for copy in copies:
         copy.start()
-    fetch.wait()
 
     def summed(b):
-        for q in range(8):
+        for j in range(8):
             for lev in range(2):
-                block = four_ref[2 * q + lev, b].astype(jnp.float32)
+                block = four_ref[four_at[2 * j + lev], b].astype(jnp.float32)
                 for seg in range(8):
-                    left[pl.ds(64 * lev + 8 * seg, 8), pl.ds(q * lats, lats)] = block[
+                    left[pl.ds(64 * lev + 8 * seg, 8), pl.ds(j * lats, lats)] = block[
                         :, seg * lats : (seg + 1) * lats
                     ]
-        for copy in copies[b]:
-            copy.wait()
+        copies[b].wait()
         value = jnp.dot(
             left[...].astype(jnp.bfloat16),
             basis[b].reshape(8 * lats, degs),
@@ -237,7 +261,7 @@
             rows = slice(64 * lev, 64 * lev + 64)
             both = jnp.concatenate([even[rows], odd[rows]], 0).T
             for a in range(16):
-                out_ref[2 * a + lev, pl.ds(k * deg_dev, deg_dev)] = both[
+                out_ref[last_at[2 * a + lev], pl.ds(k * deg_dev, deg_dev)] = both[
                     a * deg_dev : (a + 1) * deg_dev
                 ].astype(jnp.bfloat16)
     total[...] = summed(4).T
@@ -251,7 +275,7 @@
     )
     for a in range(16):
         for lev in range(2):
-            out_ref[2 * a + lev, pl.ds(2 * deg_dev, half)] = pair[lev][
+            out_ref[last_at[2 * a + lev], pl.ds(2 * deg_dev, half)] = pair[lev][
                 a * half : (a + 1) * half
             ].astype(jnp.bfloat16)
     rows = 5 * half
@@ -261,33 +285,32 @@
         )
 
 
-def spectral_parts(slots, fourier, basis):
+def spectral_parts(slots, four_at, last_at, fourier, basis):
     _, steps, lats, degs = basis.shape
-    hbm = pl.BlockSpec(memory_space=pl.ANY)
+    vmem, smem = pl.BlockSpec(memory_space=pltpu.VMEM), pl.BlockSpec(memory_space=pltpu.SMEM)
     return pl.pallas_call(
         spectral_kernel,
-        in_specs=[pl.BlockSpec(memory_space=pltpu.SMEM), hbm, hbm],
+        in_specs=[smem, smem, smem, vmem, pl.BlockSpec(memory_space=pl.ANY)],
         out_shape=jax.ShapeDtypeStruct((32, 104, 128), jnp.bfloat16),
         scratch_shapes=[
-            pltpu.VMEM(fourier.shape, jnp.bfloat16),
             pltpu.VMEM((steps, 8, lats, degs), jnp.bfloat16),
             pltpu.VMEM((128, 8 * lats), jnp.float32),
             pltpu.VMEM((degs, 128), jnp.float32),
-            pltpu.SemaphoreType.DMA((steps + 1, 8)),
+            pltpu.SemaphoreType.DMA((steps,)),
         ],
         compiler_params=params(16),
         cost_estimate=cost(5 * 2 * 128 * 8 * lats * degs, 2 * basis.size + 2 * fourier.size),
         name="spectral_parts",
-    )(slots, fourier, basis)
-
-
-def finish_kernel(in_ref, out_ref, rows):
+    )(slots, four_at, last_at, fourier, basis)
+
+
+def finish_kernel(at_ref, in_ref, out_ref, rows):
     depth = in_ref.shape[1]
     for x in range(4):
         for zq in range(2):
             for lev in range(2):
-                first = in_ref[8 * x + 2 * zq + lev].astype(jnp.float32)
-                second = in_ref[8 * x + 4 + 2 * zq + lev].astype(jnp.float32)
+                first = in_ref[at_ref[8 * x + 2 * zq + lev]].astype(jnp.float32)
+                second = in_ref[at_ref[8 * x + 4 + 2 * zq + lev]].astype(jnp.float32)
                 rows[pl.ds((8 * lev + 2 * x + zq) * depth, depth), :] = first + second
     low = lax.broadcasted_iota(jnp.int32, (16, 128), 1) < 64
     for n in range(0, 40, 2):
@@ -301,15 +324,16 @@
         out_ref[pl.ds(64 * n, 128), :] = jnp.concatenate(parts, 0).T
 
 
-def finish(received):
+def finish(at, received):
     return pl.pallas_call(
         finish_kernel,
+        in_specs=[pl.BlockSpec(memory_space=pltpu.SMEM), pl.BlockSpec(memory_space=pltpu.VMEM)],
         out_shape=jax.ShapeDtypeStruct((40 * 64, 80), jnp.float32),
         scratch_shapes=[pltpu.VMEM((16 * received.shape[1], 128), jnp.float32)],
         compiler_params=params(12),
         cost_estimate=cost(received.size, 2 * received.size + 4 * 40 * 64 * 128),
         name="finish",
-    )(received)
+    )(at, received)
 
 
 def local(out_grad, grid_state, tend_rate, legendre_basis, wave_slot):
@@ -329,25 +353,32 @@
             for k in range(1, 8)
         ]
 
-    basis, token = basis_blocks(lev.astype(jnp.int32)[None], legendre_basis)
+    def own(table):
+        return jnp.where(wave % 2 == 0, *(jnp.array(row, jnp.int32) for row in table))
+
+    basis_at, four_at, last_at = own(BASIS_AT), own(FOUR_AT), own(LAST_AT)
+    beside = tuple(
+        [four[2 * basis.index(j) + lev] for j in range(8) for lev in range(2)]
+        for basis, four in zip(BASIS_AT, FOUR_AT)
+    )
+
+    basis, token = basis_blocks(lev.astype(jnp.int32)[None], basis_at, legendre_basis)
     grads = gradient(to, tend_rate, out_grad, grid_state, token)
-    basis = lax.all_to_all(basis, ("x", "zq"), 0, 0, tiled=True)
+    basis = exchange(basis, BASIS_AT, ("x", "zq"))
     grads = swapped(grads)
     table = wave_table(wave_slot.reshape(8, slot_dev)[to], source, lons, 64)
     blocks = swapped(fourier_rows(table, grads))
-    fourier = lax.all_to_all(turn(source, basis, blocks), ("x", "zq", "lev"), 0, 0, tiled=True)
+    fourier = exchange(turn(source, four_at, basis, blocks), FOUR_AT, ("x", "zq", "lev"))
 
     first = wave * slot_dev + 8 * lev + 2 * x + zq
     slots = jnp.take(wave_slot, first + 16 * jnp.arange(slot_dev // 16, dtype=jnp.int32))
-    parts = spectral_parts(slots, fourier, basis)
-    parts = lax.all_to_all(parts, ("x", "zp", "zq", "lev"), 0, 0, tiled=True)
-    return finish(parts).reshape(degs // 16, 2, 32, slot_dev)
+    parts = spectral_parts(slots, own(beside), last_at, fourier, basis)
+    parts = exchange(parts, LAST_AT, ("x", "zp", "zq", "lev"))
+    return finish(last_at, parts).reshape(degs // 16, 2, 32, slot_dev)
 
 
 def solution(mesh):
-    fine = Mesh(
-        mesh.devices.reshape(4, 2, 2, *mesh.devices.shape[1:]), ("x", "zp", "zq", "wave", "lev")
-    )
+    fine = Mesh(mesh.devices.reshape(4, 2, 2, *mesh.devices.shape[1:]), AXES)
     lat = ("x", "zp", "zq")
     in_specs = (P("lev", lat, "wave"), P("lev", lat, "wave"), P("lev"), P(lat, "wave", None), P())
     out_specs = P(lat, None, "lev", "wave")

time: 128 us -> 131 us (1.023)
  no operation moved by 1% of the time
where the time goes in v6:
time: 131 us; the launch traced here: 130 us
  waiting for transfers between devices  40.1 us (31%)
  starting transfers between devices  32.2 us (25%)
  blocking collectives  30.2 us (23%)
  Pallas kernels  20.8 us (16%)
  other arithmetic  3.59 us (3%)
  local copies, waits for them, and re-layouts  3.17 us (2%)
    all_to_all x1, blocking collectives, exchange(): lax.all_to_all(blocks, AXES, 0, 0, tiled=True, axis_index_groups=lists)  30.2 us
    all_to_all x2, waiting for transfers between devices, exchange(): lax.all_to_all(blocks, AXES, 0, 0, tiled=True, axis_index_groups=lists)  23.7 us
    all_to_all x2, starting transfers between devices, exchange(): lax.all_to_all(blocks, AXES, 0, 0, tiled=True, axis_index_groups=lists)  17.1 us
    ppermute x14, waiting for transfers between devices, swapped(): lax.ppermute(blocks[k], 'wave', [(w, w ^ TO[w % 2][k]) for w in range(8)])  16.3 us
    ppermute x14, starting transfers between devices, swapped(): lax.ppermute(blocks[k], 'wave', [(w, w ^ TO[w % 2][k]) for w in range(8)])  15.1 us
    pallas_call x1, Pallas kernels, basis_blocks(): pl.pallas_call(basis_kernel, in_specs=[smem, smem, hbm], out_specs=[hbm,...  5.68 us
    pallas_call x1, Pallas kernels, spectral_parts(): pl.pallas_call(spectral_kernel, in_specs=[smem, smem, smem, vmem, pl.Bloc...  3.94 us
  transfers between devices with their start and end apart: 16, of which 10 were waited for; matrix products, arithmetic and copies ran while one was open for 3% of the time, Pallas kernels for 5%

profile of v6, /device:TPU:2, one launch (start us, length us, event | category | flops | bytes accessed | tf_op | source)
XLA Modules:
  0.0 130.3 jit_solution(13273645624079716045)
XLA Ops:
  0.0 1.2 compare_select_fusion
  1.2 5.7 %basis_blocks.1 = (bf16[8,5,80,640]{3,2,1,0:T(8,128)(2,1)}, f32[8,128]{1,0:T(8,128)}) custom-call(s32[1]{0:T(128)} %bitcast.1.lev_ref, s32[8]{0:T(128)} %get-tuple-element.49.at_ref, bf16[80,10,8,640]{3,2,1,0:T(8,128)(2,1)} %bitcast.9), custom_call_target="tpu_custom_call" | custom-call | bytes 8192000 | tf_op jit(solution)/shard_map/basis_blocks/pallas_call | solution.py:86
  6.9 0.0 copy-start.2
  6.9 0.0 copy-start.3
  6.9 0.0 copy-start.5
  7.0 0.0 copy-start.6
  7.0 6.8 %all-to-all-start = ((bf16[8,5,80,640]{3,2,1,0:T(8,128)(2,1)}), bf16[8,5,80,640]{3,2,1,0:T(8,128)(2,1)}, u32[]{:S(2)}, u32[]{:S(2)}) async-start(bf16[8,5,80,640]{3,2,1,0:T(8,128)(2,1)} %get-tuple-element.23), calls=%async_computation | async-start | bytes 8192000 | tf_op jit(solution)/shard_map/all_to_all | solution.py:39
  13.8 1.5 %copy-done.1 = bf16[32,80,320]{2,1,0:T(8,128)(2,1)S(1)} copy-done((bf16[32,80,320]{2,1,0:T(8,128)(2,1)S(1)}, bf16[32,80,320]{2,1,0:T(8,128)(2,1)}, u32[]{:S(2)}) %copy-start.1) | copy-done | bytes 1638424
  15.4 2.4 %gradient.1 = (bf16[2,80,640]{2,1,0:T(8,128)(2,1)S(1)}, bf16[2,80,640]{2,1,0:T(8,128)(2,1)}, bf16[2,80,640]{2,1,0:T(8,128)(2,1)S(1)}, bf16[2,80,640]{2,1,0:T(8,1...) custom-call(s32[8]{0:T(128)S(1)} %get-tuple-element.42.wave_ref, ...), custom_call_target="tpu_custom_call" | custom-call | flops 4915200 | bytes 4915200 | tf_op jit(solution)/shard_map/gradient/pallas_call | solution.py:120
  17.8 1.1 collective-permute-start.1
  18.9 2.2 %collective-permute-start.2 = (bf16[2,80,640]{2,1,0:T(8,128)(2,1)S(1)}, bf16[2,80,640]{2,1,0:T(8,128)(2,1)S(1)}, u32[]{:S(2)}, u32[]{:S(2)}) collective-permute-start(bf16[2,80,640]{2,1,0:T(8,128)(2,1)S(1)} %get-tuple-element.28), channel_id=1, source_target_pairs={{0,12},{2,6},{4,8},{6,2},{8,4},{10,14},{12,0},{14,10},{1,13},{3,7}... | collective-permute-start | bytes 614408 | tf_op jit(solution)/shard_map/ppermute | solution.py:352
  21.1 0.8 collective-permute-start.3
  21.9 0.0 collective-permute-start.4
  21.9 0.1 reshape.67
  22.0 0.6 gather_fusion.1
  22.6 0.1 mul.86
  22.7 0.1 broadcast_in_dim.12
  22.7 0.1 add.113
  22.9 1.3 %fusion.4 = (f32[64,1280]{1,0:T(8,128)S(1)}, f32[64,1280]{1,0:T(8,128)S(1)}) fusion(s32[1280]{0:T(1024)S(1)} %add.113, s32[1280]{0:T(1024)S(1)} %mul.86), kind=kLoop, calls=%fused_computation.8 | loop fusion | flops 819200 | bytes 665600 | tf_op jit(solution)/shard_map/sin | solution.py:148
  24.2 0.1 broadcast_add_fusion
  24.3 0.1 add.111
  24.4 3.0 %collective-permute-start.5 = (bf16[2,80,640]{2,1,0:T(8,128)(2,1)S(1)}, bf16[2,80,640]{2,1,0:T(8,128)(2,1)S(1)}, u32[]{:S(2)}, u32[]{:S(2)}) collective-permute-start(bf16[2,80,640]{2,1,0:T(8,128)(2,1)S(1)} %get-tuple-element.31), channel_id=1, source_target_pairs={{0,14},{2,4},{4,10},{6,0},{8,6},{10,12},{12,2},{14,8},{1,15},{3,5}... | collective-permute-start | bytes 614408 | tf_op jit(solution)/shard_map/ppermute | solution.py:352
  27.4 0.8 collective-permute-start.6
  28.1 0.9 sine_multiply_fusion
  29.1 1.7 %wave_table.1.table_ref = bf16[5,2560,256]{2,1,0:T(8,128)(2,1)S(1)} custom-call(f32[40,1280]{1,0:T(8,128)S(1)} %get-tuple-element.48.coarse_cos, f32[40,1280]{1,0:T(8,128)S(1)} %get-tuple-element.47.coarse_sin, f32[64,1280]{1,0:T(8,128)S(1)} %get-tuple-element.46.fine_cos, f32[64,1280]{1,0:T(8,128)S(1)} %get-tuple-element.45.fine_sin), custom_call_target="tpu_custom_call" | custom-call | flops 9830400 | bytes 6553600 | tf_op jit(solution)/shard_map/wave_table/pallas_call | solution.py:156
  30.8 1.4 %collective-permute-done.3.refs_4_ = bf16[2,80,640]{2,1,0:T(8,128)(2,1)S(1)} collective-permute-done((bf16[2,80,640]{2,1,0:T(8,128)(2,1)S(1)}, bf16[2,80,640]{2,1,0:T(8,128)(2,1)S(1)}, u32[]{:S(2)}, u32[]{:S(2)}) %collective-permute-start.3) | collective-permute-done | bytes 204832 | tf_op jit(solution)/shard_map/ppermute | solution.py:352
  32.2 1.7 %collective-permute-done.4.refs_5_ = bf16[2,80,640]{2,1,0:T(8,128)(2,1)S(1)} collective-permute-done((bf16[2,80,640]{2,1,0:T(8,128)(2,1)S(1)}, bf16[2,80,640]{2,1,0:T(8,128)(2,1)S(1)}, u32[]{:S(2)}, u32[]{:S(2)}) %collective-permute-start.4) | collective-permute-done | bytes 204832 | tf_op jit(solution)/shard_map/ppermute | solution.py:352
  33.9 4.6 %collective-permute-done.5.refs_6_ = bf16[2,80,640]{2,1,0:T(8,128)(2,1)S(1)} collective-permute-done((bf16[2,80,640]{2,1,0:T(8,128)(2,1)S(1)}, bf16[2,80,640]{2,1,0:T(8,128)(2,1)S(1)}, u32[]{:S(2)}, u32[]{:S(2)}) %collective-permute-start.5) | collective-permute-done | bytes 204832 | tf_op jit(solution)/shard_map/ppermute | solution.py:352
  38.5 2.3 %collective-permute-done.6.refs_7_ = bf16[2,80,640]{2,1,0:T(8,128)(2,1)S(1)} collective-permute-done((bf16[2,80,640]{2,1,0:T(8,128)(2,1)S(1)}, bf16[2,80,640]{2,1,0:T(8,128)(2,1)S(1)}, u32[]{:S(2)}, u32[]{:S(2)}) %collective-permute-start.6) | collective-permute-done | bytes 204832 | tf_op jit(solution)/shard_map/ppermute | solution.py:352
  40.9 2.6 %fourier_rows.1 = (bf16[80,640]{1,0:T(8,128)(2,1)S(1)}, bf16[80,640]{1,0:T(8,128)(2,1)S(1)}, bf16[80,640]{1,0:T(8,128)(2,1)S(1)}, bf16[80,640]{1,0:T(8,128)(2,1)...) custom-call(bf16[5,2560,256]{2,1,0:T(8,128)(2,1)S(1)} %wave_table.1., ...), custom_call_target="tpu_custom_call" | custom-call | flops 2097152000 | bytes 6553600 | tf_op jit(solution)/shard_map/fourier_rows/pallas_call | solution.py:191
  43.5 0.0 copy-start.8
  43.5 0.0 copy-start.7
  43.5 0.2 collective-permute-start.7
  43.7 1.4 %collective-permute-start.9 = (bf16[80,640]{1,0:T(8,128)(2,1)S(1)}, bf16[80,640]{1,0:T(8,128)(2,1)S(1)}, u32[]{:S(2)}, u32[]{:S(2)}) collective-permute-start(bf16[80,640]{1,0:T(8,128)(2,1)S(1)} %get-tuple-element.36), channel_id=1, source_target_pairs={{0,12},{2,6},{4,8},{6,2},{8,4},{10,14},{12,0},{14,10},{1,13},{3,7}... | collective-permute-start | bytes 307208 | tf_op jit(solution)/shard_map/ppermute | solution.py:352
  45.1 2.7 %collective-permute-start.10 = (bf16[80,640]{1,0:T(8,128)(2,1)S(1)}, bf16[80,640]{1,0:T(8,128)(2,1)S(1)}, u32[]{:S(2)}, u32[]{:S(2)}) collective-permute-start(bf16[80,640]{1,0:T(8,128)(2,1)S(1)} %get-tuple-element.37), channel_id=1, source_target_pairs={{0,8},{2,10},{4,12},{6,14},{8,0},{10,2},{12,4},{14,6},{1,9},{3,11}... | collective-permute-start | bytes 307208 | tf_op jit(solution)/shard_map/ppermute | solution.py:352
  47.8 3.0 %collective-permute-start.12 = (bf16[80,640]{1,0:T(8,128)(2,1)S(1)}, bf16[80,640]{1,0:T(8,128)(2,1)S(1)}, u32[]{:S(2)}, u32[]{:S(2)}) collective-permute-start(bf16[80,640]{1,0:T(8,128)(2,1)S(1)} %get-tuple-element.39), channel_id=1, source_target_pairs={{0,14},{2,4},{4,10},{6,0},{8,6},{10,12},{12,2},{14,8},{1,15},{3,5}... | collective-permute-start | bytes 307208 | tf_op jit(solution)/shard_map/ppermute | solution.py:352
  50.8 1.7 %collective-permute-done.10.refs_4_ = bf16[80,640]{1,0:T(8,128)(2,1)S(1)} collective-permute-done((bf16[80,640]{1,0:T(8,128)(2,1)S(1)}, bf16[80,640]{1,0:T(8,128)(2,1)S(1)}, u32[]{:S(2)}, u32[]{:S(2)}) %collective-permute-start.10) | collective-permute-done | bytes 102432 | tf_op jit(solution)/shard_map/ppermute | solution.py:352
  52.5 1.2 collective-permute-done.11.refs_5_
  53.6 0.2 collective-permute-done.12.refs_6_
  53.8 3.2 %collective-permute-done.13.refs_7_ = bf16[80,640]{1,0:T(8,128)(2,1)S(1)} collective-permute-done((bf16[80,640]{1,0:T(8,128)(2,1)S(1)}, bf16[80,640]{1,0:T(8,128)(2,1)S(1)}, u32[]{:S(2)}, u32[]{:S(2)}) %collective-permute-start.13) | collective-permute-done | bytes 102432 | tf_op jit(solution)/shard_map/ppermute | solution.py:352
  57.0 3.1 %all-to-all-done._.basis_hbm = bf16[8,5,80,640]{3,2,1,0:T(8,128)(2,1)} async-done(((bf16[8,5,80,640]{3,2,1,0:T(8,128)(2,1)}), bf16[8,5,80,640]{3,2,1,0:T(8,128)(2,1)}, u32[]{:S(2)}, u32[]{:S(2)}) %all-to-all-start) | async-done | bytes 4096032 | tf_op jit(solution)/shard_map/all_to_all | solution.py:39
  60.1 2.1 %turn.1 = bf16[16,5,8,640]{3,2,1,0:T(8,128)(2,1)} custom-call(s32[8]{0:T(128)S(1)} %get-tuple-element.44.wave_ref, s32[16]{0:T(128)S(1)} %broadcast_select_fusion.3.at_ref, bf16[8,5,80,640]{3,2,1,0:T(8,128)(2,1)} %all-to-all-done._.basis_hbm, bf16[80,640]{1,0:T(8,128)(2,1)S(1)} %get-tuple-element.33.refs_0_, ...), custom_call_target="tpu_custom_call" | custom-call | bytes 1638400 | tf_op jit(solution)/shard_map/turn/pallas_call | solution.py:220
  62.2 10.2 %all-to-all-start.1 = ((bf16[16,5,8,640]{3,2,1,0:T(8,128)(2,1)}), bf16[16,5,8,640]{3,2,1,0:T(8,128)(2,1)S(1)}, u32[]{:S(2)}, u32[]{:S(2)}) async-start(bf16[16,5,8,640]{3,2,1,0:T(8,128)(2,1)} %turn.1), calls=%async_computation.1 | async-start | bytes 1638400 | tf_op jit(solution)/shard_map/all_to_all | solution.py:39
  72.5 0.6 gather_fusion
  73.2 20.6 %all-to-all-done.1.four_ref = bf16[16,5,8,640]{3,2,1,0:T(8,128)(2,1)S(1)} async-done(((bf16[16,5,8,640]{3,2,1,0:T(8,128)(2,1)}), bf16[16,5,8,640]{3,2,1,0:T(8,128)(2,1)S(1)}, u32[]{:S(2)}, u32[]{:S(2)}) %all-to-all-start.1) | async-done | bytes 819232 | tf_op jit(solution)/shard_map/all_to_all | solution.py:39
  93.8 3.9 %spectral_parts.1 = bf16[32,104,128]{2,1,0:T(8,128)(2,1)S(1)} custom-call(s32[5]{0:T(128)S(1)} %and_select_fusion.slot_ref, s32[16]{0:T(128)S(1)} %broadcast_select_fusion.4.four_at, s32[32]{0:T(128)S(1)} %broadcast_select_fusion.5.last_at.at_ref, bf16[16,5,8,640]{3,2,1,0:T(8,128)(2,1)S(1)} %all-to-all-done.1.four_ref, ...), custom_call_target="tpu_custom_call" | custom-call | flops 524288000 | bytes 4915200 | tf_op jit(solution)/shard_map/spectral_parts/pallas_call | solution.py:291
  97.8 30.2 %all_to_all.15.in_ref = bf16[32,104,128]{2,1,0:T(8,128)(2,1)S(1)} all-to-all(bf16[32,104,128]{2,1,0:T(8,128)(2,1)S(1)} %spectral_parts.1), channel_id=1, replica_groups={{0,1,16,17,32,33,48,49,64,65,80,81,96,97,112,113,128,129,144,145,160,16..., dimensions={0} | all-to-all | bytes 1703936 | tf_op jit(solution)/shard_map/all_to_all | solution.py:39
  128.0 2.3 %finish.1 = f32[2560,80]{1,0:T(8,128)} custom-call(s32[32]{0:T(128)S(1)} %broadcast_select_fusion.5.last_at.at_ref, bf16[32,104,128]{2,1,0:T(8,128)(2,1)S(1)} %all_to_all.15.in_ref), custom_call_target="tpu_custom_call" | custom-call | flops 425984 | bytes 2162688 | tf_op jit(solution)/shard_map/finish/pallas_call | solution.py:328
  (34 shorter events, 0.1 us)
Async XLA Ops:
  6.9 6.9 %copy-start = (bf16[32,80,320]{2,1,0:T(8,128)(2,1)S(1)}, bf16[32,80,320]{2,1,0:T(8,128)(2,1)}, u32[]{:S(2)}) copy-start(bf16[32,80,320]{2,1,0:T(8,128)(2,1)} %param.18) | copy-start | bytes 4915204
  6.9 6.9 %copy-start.2 = (f32[8,128]{1,0:T(8,128)S(1)}, f32[8,128]{1,0:T(8,128)}, u32[]{:S(2)}) copy-start(f32[8,128]{1,0:T(8,128)} %get-tuple-element.24._) | copy-start | bytes 12292
  6.9 6.9 %copy-start.3 = (f32[32]{0:T(128)S(1)}, f32[32]{0:T(128)}, u32[]{:S(2)}) copy-start(f32[32]{0:T(128)} %rate_ref.1) | copy-start | bytes 388
  6.9 15.0 %copy-start.4 = (s32[640]{0:T(1024)S(1)}, s32[640]{0:T(1024)}, u32[]{:S(2)}) copy-start(s32[640]{0:T(1024)} %param.22) | copy-start | bytes 7684
  6.9 15.9 %copy-start.5 = (s32[8]{0:T(128)S(1)}, s32[8]{0:T(128)}, u32[]{:S(2)}) copy-start(s32[8]{0:T(128)} %constant.118.clone) | copy-start | bytes 100
  7.0 15.9 %copy-start.6 = (s32[8]{0:T(128)S(1)}, s32[8]{0:T(128)}, u32[]{:S(2)}) copy-start(s32[8]{0:T(128)} %constant.119.clone) | copy-start | bytes 100
  7.0 53.2 %all-to-all-start = ((bf16[8,5,80,640]{3,2,1,0:T(8,128)(2,1)}), bf16[8,5,80,640]{3,2,1,0:T(8,128)(2,1)}, u32[]{:S(2)}, u32[]{:S(2)}) async-start(bf16[8,5,80,640]{3,2,1,0:T(8,128)(2,1)} %get-tuple-element.23), calls=%async_computation | async-start | bytes 8192000 | tf_op jit(solution)/shard_map/all_to_all | solution.py:39
  13.8 1.5 %copy-start.1 = (bf16[32,80,320]{2,1,0:T(8,128)(2,1)S(1)}, bf16[32,80,320]{2,1,0:T(8,128)(2,1)}, u32[]{:S(2)}) copy-start(bf16[32,80,320]{2,1,0:T(8,128)(2,1)} %param.19) | copy-start | bytes 4915204
  17.8 6.6 %collective-permute-start = (bf16[2,80,640]{2,1,0:T(8,128)(2,1)}, bf16[2,80,640]{2,1,0:T(8,128)(2,1)S(1)}, u32[]{:S(2)}, u32[]{:S(2)}) collective-permute-start(bf16[2,80,640]{2,1,0:T(8,128)(2,1)} %get-tuple-element.26), channel_id=1, source_target_pairs={{0,2},{2,0},{4,6},{6,4},{8,10},{10,8},{12,14},{14,12},{1,3},{3,1},... | collective-permute-start | bytes 614408 | tf_op jit(solution)/shard_map/ppermute | solution.py:352
  17.8 9.6 %collective-permute-start.1 = (bf16[2,80,640]{2,1,0:T(8,128)(2,1)S(1)}, bf16[2,80,640]{2,1,0:T(8,128)(2,1)S(1)}, u32[]{:S(2)}, u32[]{:S(2)}) collective-permute-start(bf16[2,80,640]{2,1,0:T(8,128)(2,1)S(1)} %get-tuple-element.27), channel_id=1, source_target_pairs={{0,4},{2,14},{4,0},{6,10},{8,12},{10,6},{12,8},{14,2},{1,5},{3,15}... | collective-permute-start | bytes 614408 | tf_op jit(solution)/shard_map/ppermute | solution.py:352
  18.9 11.9 %collective-permute-start.2 = (bf16[2,80,640]{2,1,0:T(8,128)(2,1)S(1)}, bf16[2,80,640]{2,1,0:T(8,128)(2,1)S(1)}, u32[]{:S(2)}, u32[]{:S(2)}) collective-permute-start(bf16[2,80,640]{2,1,0:T(8,128)(2,1)S(1)} %get-tuple-element.28), channel_id=1, source_target_pairs={{0,12},{2,6},{4,8},{6,2},{8,4},{10,14},{12,0},{14,10},{1,13},{3,7}... | collective-permute-start | bytes 614408 | tf_op jit(solution)/shard_map/ppermute | solution.py:352
  21.1 11.1 %collective-permute-start.3 = (bf16[2,80,640]{2,1,0:T(8,128)(2,1)S(1)}, bf16[2,80,640]{2,1,0:T(8,128)(2,1)S(1)}, u32[]{:S(2)}, u32[]{:S(2)}) collective-permute-start(bf16[2,80,640]{2,1,0:T(8,128)(2,1)S(1)} %get-tuple-element.29), channel_id=1, source_target_pairs={{0,8},{2,10},{4,12},{6,14},{8,0},{10,2},{12,4},{14,6},{1,9},{3,11}... | collective-permute-start | bytes 614408 | tf_op jit(solution)/shard_map/ppermute | solution.py:352
  21.9 12.0 %collective-permute-start.4 = (bf16[2,80,640]{2,1,0:T(8,128)(2,1)S(1)}, bf16[2,80,640]{2,1,0:T(8,128)(2,1)S(1)}, u32[]{:S(2)}, u32[]{:S(2)}) collective-permute-start(bf16[2,80,640]{2,1,0:T(8,128)(2,1)S(1)} %get-tuple-element.30), channel_id=1, source_target_pairs={{0,6},{2,12},{4,2},{6,8},{8,14},{10,4},{12,10},{14,0},{1,7},{3,13}... | collective-permute-start | bytes 614408 | tf_op jit(solution)/shard_map/ppermute | solution.py:352
  24.4 14.2 %collective-permute-start.5 = (bf16[2,80,640]{2,1,0:T(8,128)(2,1)S(1)}, bf16[2,80,640]{2,1,0:T(8,128)(2,1)S(1)}, u32[]{:S(2)}, u32[]{:S(2)}) collective-permute-start(bf16[2,80,640]{2,1,0:T(8,128)(2,1)S(1)} %get-tuple-element.31), channel_id=1, source_target_pairs={{0,14},{2,4},{4,10},{6,0},{8,6},{10,12},{12,2},{14,8},{1,15},{3,5}... | collective-permute-start | bytes 614408 | tf_op jit(solution)/shard_map/ppermute | solution.py:352
  27.4 13.5 %collective-permute-start.6 = (bf16[2,80,640]{2,1,0:T(8,128)(2,1)S(1)}, bf16[2,80,640]{2,1,0:T(8,128)(2,1)S(1)}, u32[]{:S(2)}, u32[]{:S(2)}) collective-permute-start(bf16[2,80,640]{2,1,0:T(8,128)(2,1)S(1)} %get-tuple-element.32), channel_id=1, source_target_pairs={{0,10},{2,8},{4,14},{6,12},{8,2},{10,0},{12,6},{14,4},{1,11},{3,9}... | collective-permute-start | bytes 614408 | tf_op jit(solution)/shard_map/ppermute | solution.py:352
  40.9 9.9 %copy-start.9 = (s32[16]{0:T(128)S(1)}, s32[16]{0:T(128)}, u32[]{:S(2)}) copy-start(s32[16]{0:T(128)} %constant.121.clone) | copy-start | bytes 196
  43.5 29.6 %copy-start.8 = (s32[32]{0:T(128)S(1)}, s32[32]{0:T(128)}, u32[]{:S(2)}) copy-start(s32[32]{0:T(128)} %constant.122.clone) | copy-start | bytes 388
  43.5 29.7 %copy-start.7 = (s32[16]{0:T(128)S(1)}, s32[16]{0:T(128)}, u32[]{:S(2)}) copy-start(s32[16]{0:T(128)} %constant.124.clone) | copy-start | bytes 196
  43.5 4.3 %collective-permute-start.7 = (bf16[80,640]{1,0:T(8,128)(2,1)S(1)}, bf16[80,640]{1,0:T(8,128)(2,1)S(1)}, u32[]{:S(2)}, u32[]{:S(2)}) collective-permute-start(bf16[80,640]{1,0:T(8,128)(2,1)S(1)} %get-tuple-element.34), channel_id=1, source_target_pairs={{0,2},{2,0},{4,6},{6,4},{8,10},{10,8},{12,14},{14,12},{1,3},{3,1},... | collective-permute-start | bytes 307208 | tf_op jit(solution)/shard_map/ppermute | solution.py:352
  43.7 7.1 %collective-permute-start.8 = (bf16[80,640]{1,0:T(8,128)(2,1)S(1)}, bf16[80,640]{1,0:T(8,128)(2,1)S(1)}, u32[]{:S(2)}, u32[]{:S(2)}) collective-permute-start(bf16[80,640]{1,0:T(8,128)(2,1)S(1)} %get-tuple-element.35), channel_id=1, source_target_pairs={{0,4},{2,14},{4,0},{6,10},{8,12},{10,6},{12,8},{14,2},{1,5},{3,15}... | collective-permute-start | bytes 307208 | tf_op jit(solution)/shard_map/ppermute | solution.py:352
  43.7 7.1 %collective-permute-start.9 = (bf16[80,640]{1,0:T(8,128)(2,1)S(1)}, bf16[80,640]{1,0:T(8,128)(2,1)S(1)}, u32[]{:S(2)}, u32[]{:S(2)}) collective-permute-start(bf16[80,640]{1,0:T(8,128)(2,1)S(1)} %get-tuple-element.36), channel_id=1, source_target_pairs={{0,12},{2,6},{4,8},{6,2},{8,4},{10,14},{12,0},{14,10},{1,13},{3,7}... | collective-permute-start | bytes 307208 | tf_op jit(solution)/shard_map/ppermute | solution.py:352
  45.1 7.3 %collective-permute-start.10 = (bf16[80,640]{1,0:T(8,128)(2,1)S(1)}, bf16[80,640]{1,0:T(8,128)(2,1)S(1)}, u32[]{:S(2)}, u32[]{:S(2)}) collective-permute-start(bf16[80,640]{1,0:T(8,128)(2,1)S(1)} %get-tuple-element.37), channel_id=1, source_target_pairs={{0,8},{2,10},{4,12},{6,14},{8,0},{10,2},{12,4},{14,6},{1,9},{3,11}... | collective-permute-start | bytes 307208 | tf_op jit(solution)/shard_map/ppermute | solution.py:352
  47.8 5.8 %collective-permute-start.11 = (bf16[80,640]{1,0:T(8,128)(2,1)S(1)}, bf16[80,640]{1,0:T(8,128)(2,1)S(1)}, u32[]{:S(2)}, u32[]{:S(2)}) collective-permute-start(bf16[80,640]{1,0:T(8,128)(2,1)S(1)} %get-tuple-element.38), channel_id=1, source_target_pairs={{0,6},{2,12},{4,2},{6,8},{8,14},{10,4},{12,10},{14,0},{1,7},{3,13}... | collective-permute-start | bytes 307208 | tf_op jit(solution)/shard_map/ppermute | solution.py:352
  47.8 6.0 %collective-permute-start.12 = (bf16[80,640]{1,0:T(8,128)(2,1)S(1)}, bf16[80,640]{1,0:T(8,128)(2,1)S(1)}, u32[]{:S(2)}, u32[]{:S(2)}) collective-permute-start(bf16[80,640]{1,0:T(8,128)(2,1)S(1)} %get-tuple-element.39), channel_id=1, source_target_pairs={{0,14},{2,4},{4,10},{6,0},{8,6},{10,12},{12,2},{14,8},{1,15},{3,5}... | collective-permute-start | bytes 307208 | tf_op jit(solution)/shard_map/ppermute | solution.py:352
  50.8 6.3 %collective-permute-start.13 = (bf16[80,640]{1,0:T(8,128)(2,1)S(1)}, bf16[80,640]{1,0:T(8,128)(2,1)S(1)}, u32[]{:S(2)}, u32[]{:S(2)}) collective-permute-start(bf16[80,640]{1,0:T(8,128)(2,1)S(1)} %get-tuple-element.40), channel_id=1, source_target_pairs={{0,10},{2,8},{4,14},{6,12},{8,2},{10,0},{12,6},{14,4},{1,11},{3,9}... | collective-permute-start | bytes 307208 | tf_op jit(solution)/shard_map/ppermute | solution.py:352
  62.2 31.6 %all-to-all-start.1 = ((bf16[16,5,8,640]{3,2,1,0:T(8,128)(2,1)}), bf16[16,5,8,640]{3,2,1,0:T(8,128)(2,1)S(1)}, u32[]{:S(2)}, u32[]{:S(2)}) async-start(bf16[16,5,8,640]{3,2,1,0:T(8,128)(2,1)} %turn.1), calls=%async_computation.1 | async-start | bytes 1638400 | tf_op jit(solution)/shard_map/all_to_all | solution.py:39

commit v7 on v5

--- a/solution.py
+++ b/solution.py
@@ -167,7 +167,7 @@
     )(table, *grads)
 
 
-def turn_kernel(wave_ref, _, *refs):
+def turn_kernel(wave_ref, *refs):
     blocks, (out_ref, rows) = refs[:8], refs[8:]
     slots, width = blocks[0].shape
     for t in range(width // 128):
@@ -182,36 +182,30 @@
             )
 
 
-def turn(waves, after, blocks):
+def turn(waves, blocks):
     slots, width = blocks[0].shape
     vmem = pl.BlockSpec(memory_space=pltpu.VMEM)
     return pl.pallas_call(
         turn_kernel,
-        in_specs=[pl.BlockSpec(memory_space=pltpu.SMEM), pl.BlockSpec(memory_space=pl.ANY)]
-        + [vmem] * 8,
+        in_specs=[pl.BlockSpec(memory_space=pltpu.SMEM)] + [vmem] * 8,
         out_shape=jax.ShapeDtypeStruct((16, slots // 16, 8, width), jnp.bfloat16),
         scratch_shapes=[pltpu.VMEM((width // 128, 8 * slots, 128), jnp.float32)],
         compiler_params=params(12),
         cost_estimate=cost(0, 32 * blocks[0].size),
         name="turn",
-    )(waves, after, *blocks)
-
-
-def spectral_kernel(slot_ref, four_hbm, basis_hbm, out_ref, four_ref, basis, left, total, sems):
+    )(waves, *blocks)
+
+
+def spectral_kernel(slot_ref, four_ref, head_ref, basis_any, out_ref, basis, left, total, sems):
     steps, _, lats, degs = basis.shape
     deg_dev = degs // 16
-    fetch = pltpu.make_async_copy(four_hbm, four_ref, sems.at[steps, 0])
-    fetch.start()
+    head = head_ref.shape[1]
     copies = [
-        [
-            pltpu.make_async_copy(basis_hbm.at[q, b], basis.at[b, q], sems.at[b, q])
-            for q in range(8)
-        ]
-        for b in range(steps)
+        pltpu.make_async_copy(basis_any.at[:, b], basis.at[b], sems.at[b])
+        for b in range(head, steps)
     ]
-    for copy in sum(copies, []):
+    for copy in copies:
         copy.start()
-    fetch.wait()
 
     def summed(b):
         for q in range(8):
@@ -221,11 +215,14 @@
                     left[pl.ds(64 * lev + 8 * seg, 8), pl.ds(q * lats, lats)] = block[
                         :, seg * lats : (seg + 1) * lats
                     ]
-        for copy in copies[b]:
-            copy.wait()
+        if b >= head:
+            copies[b - head].wait()
+            blocks = basis[b]
+        else:
+            blocks = head_ref[:, b]
         value = jnp.dot(
             left[...].astype(jnp.bfloat16),
-            basis[b].reshape(8 * lats, degs),
+            blocks.reshape(8 * lats, degs),
             preferred_element_type=jnp.float32,
         )
         degree = lax.broadcasted_iota(jnp.int32, value.shape, 1)
@@ -261,24 +258,23 @@
         )
 
 
-def spectral_parts(slots, fourier, basis):
+def spectral_parts(slots, fourier, head, basis):
     _, steps, lats, degs = basis.shape
-    hbm = pl.BlockSpec(memory_space=pl.ANY)
+    vmem, smem = pl.BlockSpec(memory_space=pltpu.VMEM), pl.BlockSpec(memory_space=pltpu.SMEM)
     return pl.pallas_call(
         spectral_kernel,
-        in_specs=[pl.BlockSpec(memory_space=pltpu.SMEM), hbm, hbm],
+        in_specs=[smem, vmem, vmem, pl.BlockSpec(memory_space=pl.ANY)],
         out_shape=jax.ShapeDtypeStruct((32, 104, 128), jnp.bfloat16),
         scratch_shapes=[
-            pltpu.VMEM(fourier.shape, jnp.bfloat16),
             pltpu.VMEM((steps, 8, lats, degs), jnp.bfloat16),
             pltpu.VMEM((128, 8 * lats), jnp.float32),
             pltpu.VMEM((degs, 128), jnp.float32),
-            pltpu.SemaphoreType.DMA((steps + 1, 8)),
+            pltpu.SemaphoreType.DMA((steps,)),
         ],
         compiler_params=params(16),
         cost_estimate=cost(5 * 2 * 128 * 8 * lats * degs, 2 * basis.size + 2 * fourier.size),
         name="spectral_parts",
-    )(slots, fourier, basis)
+    )(slots, fourier, head, basis)
 
 
 def finish_kernel(in_ref, out_ref, rows):
@@ -335,11 +331,12 @@
     grads = swapped(grads)
     table = wave_table(wave_slot.reshape(8, slot_dev)[to], source, lons, 64)
     blocks = swapped(fourier_rows(table, grads))
-    fourier = lax.all_to_all(turn(source, basis, blocks), ("x", "zq", "lev"), 0, 0, tiled=True)
+    fourier, basis = lax.optimization_barrier((turn(source, blocks), basis))
+    fourier = lax.all_to_all(fourier, ("x", "zq", "lev"), 0, 0, tiled=True)
 
     first = wave * slot_dev + 8 * lev + 2 * x + zq
     slots = jnp.take(wave_slot, first + 16 * jnp.arange(slot_dev // 16, dtype=jnp.int32))
-    parts = spectral_parts(slots, fourier, basis)
+    parts = spectral_parts(slots, fourier, basis[:, :2], basis)
     parts = lax.all_to_all(parts, ("x", "zp", "zq", "lev"), 0, 0, tiled=True)
     return finish(parts).reshape(degs // 16, 2, 32, slot_dev)
 

time: 128 us -> 125 us (0.977)
  waiting for transfers between devices: 40.4 us -> 33.7 us
  blocking collectives: 29.1 us -> 32.5 us
  local copies, waits for them, and re-layouts: 3.16 us -> 4.74 us
    all_to_all x1, waiting for transfers between devices: 21.1 us -> 16.5 us  [local(): fourier = lax.all_to_all(fourier, ('x', 'zq', 'lev'), 0, 0, tiled=True)]
    all_to_all x1, blocking collectives: 29.1 us -> 32.5 us  [local(): parts = lax.all_to_all(parts, ('x', 'zp', 'zq', 'lev'), 0, 0, tiled=True)]
    all_to_all x1, waiting for transfers between devices: 2.97 us -> 0.88 us  [local(): basis = lax.all_to_all(basis, ('x', 'zq'), 0, 0, tiled=True)]
    slice x0 -> x1, local copies, waits for them, and re-layouts: none -> 1.58 us  [local(): parts = spectral_parts(slots, fourier, basis[:, :2], basis)]
  transfers between devices with their start and end apart: 16 -> 16, of which waited for: 10 -> 10; matrix products, arithmetic and copies ran while one was open for 3% -> 4% of each run, Pallas kernels for 5% -> 7%
where the time goes in v7:
time: 125 us; the launch traced here: 124 us
  waiting for transfers between devices  33.7 us (27%)
  blocking collectives  32.5 us (26%)
  starting transfers between devices  32.2 us (26%)
  Pallas kernels  18.5 us (15%)
  local copies, waits for them, and re-layouts  4.74 us (4%)
  other arithmetic  2.39 us (2%)
    all_to_all x1, blocking collectives, local(): parts = lax.all_to_all(parts, ('x', 'zp', 'zq', 'lev'), 0, 0, tiled=True)  32.5 us
    all_to_all x1, waiting for transfers between devices, local(): fourier = lax.all_to_all(fourier, ('x', 'zq', 'lev'), 0, 0, tiled=True)  16.5 us
    ppermute x14, waiting for transfers between devices, swapped(): lax.ppermute(blocks[k], 'wave', [(w, w ^ TO[w % 2][k]) for w in range(8)])  16.4 us
    ppermute x14, starting transfers between devices, swapped(): lax.ppermute(blocks[k], 'wave', [(w, w ^ TO[w % 2][k]) for w in range(8)])  15.1 us
    all_to_all x1, starting transfers between devices, local(): fourier = lax.all_to_all(fourier, ('x', 'zq', 'lev'), 0, 0, tiled=True)  10.3 us
    all_to_all x1, starting transfers between devices, local(): basis = lax.all_to_all(basis, ('x', 'zq'), 0, 0, tiled=True)  6.84 us
    pallas_call x1, Pallas kernels, basis_blocks(): pl.pallas_call(basis_kernel, in_specs=[pl.BlockSpec(memory_space=pltpu.SM...  4.65 us
    pallas_call x1, Pallas kernels, spectral_parts(): pl.pallas_call(spectral_kernel, in_specs=[smem, vmem, vmem, pl.BlockSpec(...  3.31 us
  transfers between devices with their start and end apart: 16, of which 10 were waited for; matrix products, arithmetic and copies ran while one was open for 4% of the time, Pallas kernels for 7%

profile of v7, /device:TPU:2, one launch (start us, length us, event | category | flops | bytes accessed | tf_op | source)
XLA Modules:
  0.0 124.3 jit_solution(9152279716977016682)
XLA Ops:
  0.0 4.7 %basis_blocks.1 = (bf16[8,5,80,640]{3,2,1,0:T(8,128)(2,1)}, f32[8,128]{1,0:T(8,128)}) custom-call(s32[1]{0:T(128)} %bitcast.3.lev_ref, bf16[80,10,8,640]{3,2,1,0:T(8,128)(2,1)} %bitcast.9), custom_call_target="tpu_custom_call" | custom-call | bytes 8192000 | tf_op jit(solution)/shard_map/basis_blocks/pallas_call | solution.py:54
  4.7 0.0 copy-start.7
  4.7 0.0 copy-start.8
  4.7 0.0 copy-start
  4.7 0.0 copy-start.2
  4.7 0.0 copy-start.3
  4.7 0.0 copy-start.4
  4.7 6.8 %all-to-all-start = ((bf16[8,5,80,640]{3,2,1,0:T(8,128)(2,1)}), bf16[8,5,80,640]{3,2,1,0:T(8,128)(2,1)}, u32[]{:S(2)}, u32[]{:S(2)}) async-start(bf16[8,5,80,640]{3,2,1,0:T(8,128)(2,1)} %get-tuple-element.42), calls=%async_computation | async-start | bytes 8192000 | tf_op jit(solution)/shard_map/all_to_all | solution.py:330
  11.6 0.0 copy-start.1
  11.6 1.5 %copy-done.1 = bf16[32,80,320]{2,1,0:T(8,128)(2,1)S(1)} copy-done((bf16[32,80,320]{2,1,0:T(8,128)(2,1)S(1)}, bf16[32,80,320]{2,1,0:T(8,128)(2,1)}, u32[]{:S(2)}) %copy-start.1) | copy-done | bytes 1638424
  13.2 2.4 %gradient.1 = (bf16[2,80,640]{2,1,0:T(8,128)(2,1)S(1)}, bf16[2,80,640]{2,1,0:T(8,128)(2,1)}, bf16[2,80,640]{2,1,0:T(8,128)(2,1)S(1)}, bf16[2,80,640]{2,1,0:T(8,1...) custom-call(s32[8]{0:T(128)S(1)} %get-tuple-element.46.wave_ref, ...), custom_call_target="tpu_custom_call" | custom-call | flops 4915200 | bytes 4915200 | tf_op jit(solution)/shard_map/gradient/pallas_call | solution.py:88
  15.6 1.1 collective-permute-start.1
  16.7 2.2 %collective-permute-start.2 = (bf16[2,80,640]{2,1,0:T(8,128)(2,1)S(1)}, bf16[2,80,640]{2,1,0:T(8,128)(2,1)S(1)}, u32[]{:S(2)}, u32[]{:S(2)}) collective-permute-start(bf16[2,80,640]{2,1,0:T(8,128)(2,1)S(1)} %get-tuple-element.29), channel_id=1, source_target_pairs={{0,12},{2,6},{4,8},{6,2},{8,4},{10,14},{12,0},{14,10},{1,13},{3,7}... | collective-permute-start | bytes 614408 | tf_op jit(solution)/shard_map/ppermute | solution.py:324
  18.9 0.8 collective-permute-start.3
  19.7 0.1 reshape.66
  19.8 0.6 gather_fusion.1
  20.4 0.1 mul.86
  20.5 0.1 broadcast_in_dim.11
  20.6 0.1 add.109
  20.7 1.3 %fusion.4 = (f32[64,1280]{1,0:T(8,128)S(1)}, f32[64,1280]{1,0:T(8,128)S(1)}) fusion(s32[1280]{0:T(1024)S(1)} %add.109, s32[1280]{0:T(1024)S(1)} %mul.86), kind=kLoop, calls=%fused_computation.8 | loop fusion | flops 819200 | bytes 665600 | tf_op jit(solution)/shard_map/sin | solution.py:116
  22.0 0.1 broadcast_add_fusion
  22.1 0.1 add.107
  22.2 3.0 %collective-permute-start.5 = (bf16[2,80,640]{2,1,0:T(8,128)(2,1)S(1)}, bf16[2,80,640]{2,1,0:T(8,128)(2,1)S(1)}, u32[]{:S(2)}, u32[]{:S(2)}) collective-permute-start(bf16[2,80,640]{2,1,0:T(8,128)(2,1)S(1)} %get-tuple-element.32), channel_id=1, source_target_pairs={{0,14},{2,4},{4,10},{6,0},{8,6},{10,12},{12,2},{14,8},{1,15},{3,5}... | collective-permute-start | bytes 614408 | tf_op jit(solution)/shard_map/ppermute | solution.py:324
  25.2 0.7 collective-permute-start.6
  26.0 0.9 sine_multiply_fusion
  26.9 1.7 %wave_table.1.table_ref = bf16[5,2560,256]{2,1,0:T(8,128)(2,1)S(1)} custom-call(f32[40,1280]{1,0:T(8,128)S(1)} %get-tuple-element.52.coarse_cos, f32[40,1280]{1,0:T(8,128)S(1)} %get-tuple-element.51.coarse_sin, f32[64,1280]{1,0:T(8,128)S(1)} %get-tuple-element.50.fine_cos, f32[64,1280]{1,0:T(8,128)S(1)} %get-tuple-element.49.fine_sin), custom_call_target="tpu_custom_call" | custom-call | flops 9830400 | bytes 6553600 | tf_op jit(solution)/shard_map/wave_table/pallas_call | solution.py:124
  28.6 1.4 %collective-permute-done.3.refs_4_ = bf16[2,80,640]{2,1,0:T(8,128)(2,1)S(1)} collective-permute-done((bf16[2,80,640]{2,1,0:T(8,128)(2,1)S(1)}, bf16[2,80,640]{2,1,0:T(8,128)(2,1)S(1)}, u32[]{:S(2)}, u32[]{:S(2)}) %collective-permute-start.3) | collective-permute-done | bytes 204832 | tf_op jit(solution)/shard_map/ppermute | solution.py:324
  30.0 1.7 %collective-permute-done.4.refs_5_ = bf16[2,80,640]{2,1,0:T(8,128)(2,1)S(1)} collective-permute-done((bf16[2,80,640]{2,1,0:T(8,128)(2,1)S(1)}, bf16[2,80,640]{2,1,0:T(8,128)(2,1)S(1)}, u32[]{:S(2)}, u32[]{:S(2)}) %collective-permute-start.4) | collective-permute-done | bytes 204832 | tf_op jit(solution)/shard_map/ppermute | solution.py:324
  31.8 4.6 %collective-permute-done.5.refs_6_ = bf16[2,80,640]{2,1,0:T(8,128)(2,1)S(1)} collective-permute-done((bf16[2,80,640]{2,1,0:T(8,128)(2,1)S(1)}, bf16[2,80,640]{2,1,0:T(8,128)(2,1)S(1)}, u32[]{:S(2)}, u32[]{:S(2)}) %collective-permute-start.5) | collective-permute-done | bytes 204832 | tf_op jit(solution)/shard_map/ppermute | solution.py:324
  36.3 2.4 %collective-permute-done.6.refs_7_ = bf16[2,80,640]{2,1,0:T(8,128)(2,1)S(1)} collective-permute-done((bf16[2,80,640]{2,1,0:T(8,128)(2,1)S(1)}, bf16[2,80,640]{2,1,0:T(8,128)(2,1)S(1)}, u32[]{:S(2)}, u32[]{:S(2)}) %collective-permute-start.6) | collective-permute-done | bytes 204832 | tf_op jit(solution)/shard_map/ppermute | solution.py:324
  38.7 2.6 %fourier_rows.1 = (bf16[80,640]{1,0:T(8,128)(2,1)S(1)}, bf16[80,640]{1,0:T(8,128)(2,1)S(1)}, bf16[80,640]{1,0:T(8,128)(2,1)S(1)}, bf16[80,640]{1,0:T(8,128)(2,1)...) custom-call(bf16[5,2560,256]{2,1,0:T(8,128)(2,1)S(1)} %wave_table.1., ...), custom_call_target="tpu_custom_call" | custom-call | flops 2097152000 | bytes 6553600 | tf_op jit(solution)/shard_map/fourier_rows/pallas_call | solution.py:159
  41.3 0.2 collective-permute-start.7
  41.5 1.4 %collective-permute-start.9 = (bf16[80,640]{1,0:T(8,128)(2,1)S(1)}, bf16[80,640]{1,0:T(8,128)(2,1)S(1)}, u32[]{:S(2)}, u32[]{:S(2)}) collective-permute-start(bf16[80,640]{1,0:T(8,128)(2,1)S(1)} %get-tuple-element.37), channel_id=1, source_target_pairs={{0,12},{2,6},{4,8},{6,2},{8,4},{10,14},{12,0},{14,10},{1,13},{3,7}... | collective-permute-start | bytes 307208 | tf_op jit(solution)/shard_map/ppermute | solution.py:324
  42.9 2.7 %collective-permute-start.10 = (bf16[80,640]{1,0:T(8,128)(2,1)S(1)}, bf16[80,640]{1,0:T(8,128)(2,1)S(1)}, u32[]{:S(2)}, u32[]{:S(2)}) collective-permute-start(bf16[80,640]{1,0:T(8,128)(2,1)S(1)} %get-tuple-element.38), channel_id=1, source_target_pairs={{0,8},{2,10},{4,12},{6,14},{8,0},{10,2},{12,4},{14,6},{1,9},{3,11}... | collective-permute-start | bytes 307208 | tf_op jit(solution)/shard_map/ppermute | solution.py:324
  45.6 3.0 %collective-permute-start.12 = (bf16[80,640]{1,0:T(8,128)(2,1)S(1)}, bf16[80,640]{1,0:T(8,128)(2,1)S(1)}, u32[]{:S(2)}, u32[]{:S(2)}) collective-permute-start(bf16[80,640]{1,0:T(8,128)(2,1)S(1)} %get-tuple-element.40), channel_id=1, source_target_pairs={{0,14},{2,4},{4,10},{6,0},{8,6},{10,12},{12,2},{14,8},{1,15},{3,5}... | collective-permute-start | bytes 307208 | tf_op jit(solution)/shard_map/ppermute | solution.py:324
  48.6 1.6 %collective-permute-done.10.refs_4_ = bf16[80,640]{1,0:T(8,128)(2,1)S(1)} collective-permute-done((bf16[80,640]{1,0:T(8,128)(2,1)S(1)}, bf16[80,640]{1,0:T(8,128)(2,1)S(1)}, u32[]{:S(2)}, u32[]{:S(2)}) %collective-permute-start.10) | collective-permute-done | bytes 102432 | tf_op jit(solution)/shard_map/ppermute | solution.py:324
  50.2 1.2 collective-permute-done.11.refs_5_
  51.4 0.2 collective-permute-done.12.refs_6_
  51.7 3.2 %collective-permute-done.13.refs_7_ = bf16[80,640]{1,0:T(8,128)(2,1)S(1)} collective-permute-done((bf16[80,640]{1,0:T(8,128)(2,1)S(1)}, bf16[80,640]{1,0:T(8,128)(2,1)S(1)}, u32[]{:S(2)}, u32[]{:S(2)}) %collective-permute-start.13) | collective-permute-done | bytes 102432 | tf_op jit(solution)/shard_map/ppermute | solution.py:324
  54.8 2.1 %turn.1 = bf16[16,5,8,640]{3,2,1,0:T(8,128)(2,1)} custom-call(s32[8]{0:T(128)S(1)} %get-tuple-element.48.wave_ref, bf16[80,640]{1,0:T(8,128)(2,1)S(1)} %get-tuple-element.34.refs_0_, bf16[80,640]{1,0:T(8,128)(2,1)S(1)} %collective-permute-done.7.refs_1_, bf16[80,640]{1,0:T(8,128)(2,1)S(1)} %collective-permute-done.8.refs_2_, ...), custom_call_target="tpu_custom_call" | custom-call | bytes 1638400 | tf_op jit(solution)/shard_map/turn/pallas_call | solution.py:188
  56.9 0.9 all-to-all-done.basis_any
  57.8 10.3 %all-to-all-start.1 = ((bf16[16,5,8,640]{3,2,1,0:T(8,128)(2,1)}), bf16[16,5,8,640]{3,2,1,0:T(8,128)(2,1)S(1)}, u32[]{:S(2)}, u32[]{:S(2)}) async-start(bf16[16,5,8,640]{3,2,1,0:T(8,128)(2,1)} %turn.1), calls=%async_computation.1 | async-start | bytes 1638400 | tf_op jit(solution)/shard_map/all_to_all | solution.py:335
  68.1 0.6 gather_fusion
  68.7 1.6 %slice.3.head_ref = bf16[8,2,80,640]{3,2,1,0:T(8,128)(2,1)S(1)} slice(bf16[8,5,80,640]{3,2,1,0:T(8,128)(2,1)} %all-to-all-done.basis_any), slice={[0:8], [0:2], [0:80], [0:640]} | slice | bytes 3276800 | tf_op jit(solution)/shard_map/slice | solution.py:339
  70.3 16.5 %all-to-all-done.1.four_ref = bf16[16,5,8,640]{3,2,1,0:T(8,128)(2,1)S(1)} async-done(((bf16[16,5,8,640]{3,2,1,0:T(8,128)(2,1)}), bf16[16,5,8,640]{3,2,1,0:T(8,128)(2,1)S(1)}, u32[]{:S(2)}, u32[]{:S(2)}) %all-to-all-start.1) | async-done | bytes 819232 | tf_op jit(solution)/shard_map/all_to_all | solution.py:335
  86.8 3.3 %spectral_parts.1 = bf16[32,104,128]{2,1,0:T(8,128)(2,1)S(1)} custom-call(s32[5]{0:T(128)S(1)} %and_select_fusion.slot_ref, bf16[16,5,8,640]{3,2,1,0:T(8,128)(2,1)S(1)} %all-to-all-done.1.four_ref, bf16[8,2,80,640]{3,2,1,0:T(8,128)(2,1)S(1)} %slice.3.head_ref, bf16[8,5,80,640]{3,2,1,0:T(8,128)(2,1)} %all-to-all-done.basis_any), custom_call_target="tpu_custom_call" | custom-call | flops 524288000 | bytes 4915200 | tf_op jit(solution)/shard_map/spectral_parts/pallas_call | solution.py:264
  90.1 32.5 %all_to_all.15.in_ref = bf16[32,104,128]{2,1,0:T(8,128)(2,1)S(1)} all-to-all(bf16[32,104,128]{2,1,0:T(8,128)(2,1)S(1)} %spectral_parts.1), channel_id=1, replica_groups=mesh['x'=4,'zp'=2,'zq'=2,'wave'=8,'lev'=2] {'x','zp','zq','lev'}, dimensions={0} | all-to-all | bytes 1703936 | tf_op jit(solution)/shard_map/all_to_all | solution.py:340
  122.6 1.7 %finish.1 = f32[2560,80]{1,0:T(8,128)} custom-call(bf16[32,104,128]{2,1,0:T(8,128)(2,1)S(1)} %all_to_all.15.in_ref), custom_call_target="tpu_custom_call" | custom-call | flops 425984 | bytes 2162688 | tf_op jit(solution)/shard_map/finish/pallas_call | solution.py:301
  (30 shorter events, 0.1 us)
Async XLA Ops:
  4.7 6.9 %copy-start.7 = (s32[8]{0:T(128)S(1)}, s32[8]{0:T(128)}, u32[]{:S(2)}) copy-start(s32[8]{0:T(128)} %constant.94.clone) | copy-start | bytes 100
  4.7 6.9 %copy-start.8 = (s32[8]{0:T(128)S(1)}, s32[8]{0:T(128)}, u32[]{:S(2)}) copy-start(s32[8]{0:T(128)} %constant.95.clone) | copy-start | bytes 100
  4.7 6.9 %copy-start = (bf16[32,80,320]{2,1,0:T(8,128)(2,1)S(1)}, bf16[32,80,320]{2,1,0:T(8,128)(2,1)}, u32[]{:S(2)}) copy-start(bf16[32,80,320]{2,1,0:T(8,128)(2,1)} %param.10) | copy-start | bytes 4915204
  4.7 6.9 %copy-start.2 = (f32[8,128]{1,0:T(8,128)S(1)}, f32[8,128]{1,0:T(8,128)}, u32[]{:S(2)}) copy-start(f32[8,128]{1,0:T(8,128)} %get-tuple-element.25._) | copy-start | bytes 12292
  4.7 6.9 %copy-start.3 = (f32[32]{0:T(128)S(1)}, f32[32]{0:T(128)}, u32[]{:S(2)}) copy-start(f32[32]{0:T(128)} %rate_ref.1) | copy-start | bytes 388
  4.7 15.0 %copy-start.4 = (s32[640]{0:T(1024)S(1)}, s32[640]{0:T(1024)}, u32[]{:S(2)}) copy-start(s32[640]{0:T(1024)} %param.14) | copy-start | bytes 7684
  4.7 53.1 %all-to-all-start = ((bf16[8,5,80,640]{3,2,1,0:T(8,128)(2,1)}), bf16[8,5,80,640]{3,2,1,0:T(8,128)(2,1)}, u32[]{:S(2)}, u32[]{:S(2)}) async-start(bf16[8,5,80,640]{3,2,1,0:T(8,128)(2,1)} %get-tuple-element.42), calls=%async_computation | async-start | bytes 8192000 | tf_op jit(solution)/shard_map/all_to_all | solution.py:330
  11.6 9.1 %copy-start.5 = (s32[8]{0:T(128)S(1)}, s32[8]{0:T(128)}, u32[]{:S(2)}) copy-start(s32[8]{0:T(128)} %constant.96.clone) | copy-start | bytes 100
  11.6 9.1 %copy-start.6 = (s32[8]{0:T(128)S(1)}, s32[8]{0:T(128)}, u32[]{:S(2)}) copy-start(s32[8]{0:T(128)} %constant.97.clone) | copy-start | bytes 100
  11.6 1.5 %copy-start.1 = (bf16[32,80,320]{2,1,0:T(8,128)(2,1)S(1)}, bf16[32,80,320]{2,1,0:T(8,128)(2,1)}, u32[]{:S(2)}) copy-start(bf16[32,80,320]{2,1,0:T(8,128)(2,1)} %param.11) | copy-start | bytes 4915204
  15.6 6.6 %collective-permute-start = (bf16[2,80,640]{2,1,0:T(8,128)(2,1)}, bf16[2,80,640]{2,1,0:T(8,128)(2,1)S(1)}, u32[]{:S(2)}, u32[]{:S(2)}) collective-permute-start(bf16[2,80,640]{2,1,0:T(8,128)(2,1)} %get-tuple-element.27), channel_id=1, source_target_pairs={{0,2},{2,0},{4,6},{6,4},{8,10},{10,8},{12,14},{14,12},{1,3},{3,1},... | collective-permute-start | bytes 614408 | tf_op jit(solution)/shard_map/ppermute | solution.py:324
  15.6 9.6 %collective-permute-start.1 = (bf16[2,80,640]{2,1,0:T(8,128)(2,1)S(1)}, bf16[2,80,640]{2,1,0:T(8,128)(2,1)S(1)}, u32[]{:S(2)}, u32[]{:S(2)}) collective-permute-start(bf16[2,80,640]{2,1,0:T(8,128)(2,1)S(1)} %get-tuple-element.28), channel_id=1, source_target_pairs={{0,4},{2,14},{4,0},{6,10},{8,12},{10,6},{12,8},{14,2},{1,5},{3,15}... | collective-permute-start | bytes 614408 | tf_op jit(solution)/shard_map/ppermute | solution.py:324
  16.7 11.9 %collective-permute-start.2 = (bf16[2,80,640]{2,1,0:T(8,128)(2,1)S(1)}, bf16[2,80,640]{2,1,0:T(8,128)(2,1)S(1)}, u32[]{:S(2)}, u32[]{:S(2)}) collective-permute-start(bf16[2,80,640]{2,1,0:T(8,128)(2,1)S(1)} %get-tuple-element.29), channel_id=1, source_target_pairs={{0,12},{2,6},{4,8},{6,2},{8,4},{10,14},{12,0},{14,10},{1,13},{3,7}... | collective-permute-start | bytes 614408 | tf_op jit(solution)/shard_map/ppermute | solution.py:324
  18.9 11.1 %collective-permute-start.3 = (bf16[2,80,640]{2,1,0:T(8,128)(2,1)S(1)}, bf16[2,80,640]{2,1,0:T(8,128)(2,1)S(1)}, u32[]{:S(2)}, u32[]{:S(2)}) collective-permute-start(bf16[2,80,640]{2,1,0:T(8,128)(2,1)S(1)} %get-tuple-element.30), channel_id=1, source_target_pairs={{0,8},{2,10},{4,12},{6,14},{8,0},{10,2},{12,4},{14,6},{1,9},{3,11}... | collective-permute-start | bytes 614408 | tf_op jit(solution)/shard_map/ppermute | solution.py:324
  19.7 12.0 %collective-permute-start.4 = (bf16[2,80,640]{2,1,0:T(8,128)(2,1)S(1)}, bf16[2,80,640]{2,1,0:T(8,128)(2,1)S(1)}, u32[]{:S(2)}, u32[]{:S(2)}) collective-permute-start(bf16[2,80,640]{2,1,0:T(8,128)(2,1)S(1)} %get-tuple-element.31), channel_id=1, source_target_pairs={{0,6},{2,12},{4,2},{6,8},{8,14},{10,4},{12,10},{14,0},{1,7},{3,13}... | collective-permute-start | bytes 614408 | tf_op jit(solution)/shard_map/ppermute | solution.py:324
  22.2 14.2 %collective-permute-start.5 = (bf16[2,80,640]{2,1,0:T(8,128)(2,1)S(1)}, bf16[2,80,640]{2,1,0:T(8,128)(2,1)S(1)}, u32[]{:S(2)}, u32[]{:S(2)}) collective-permute-start(bf16[2,80,640]{2,1,0:T(8,128)(2,1)S(1)} %get-tuple-element.32), channel_id=1, source_target_pairs={{0,14},{2,4},{4,10},{6,0},{8,6},{10,12},{12,2},{14,8},{1,15},{3,5}... | collective-permute-start | bytes 614408 | tf_op jit(solution)/shard_map/ppermute | solution.py:324
  25.2 13.5 %collective-permute-start.6 = (bf16[2,80,640]{2,1,0:T(8,128)(2,1)S(1)}, bf16[2,80,640]{2,1,0:T(8,128)(2,1)S(1)}, u32[]{:S(2)}, u32[]{:S(2)}) collective-permute-start(bf16[2,80,640]{2,1,0:T(8,128)(2,1)S(1)} %get-tuple-element.33), channel_id=1, source_target_pairs={{0,10},{2,8},{4,14},{6,12},{8,2},{10,0},{12,6},{14,4},{1,11},{3,9}... | collective-permute-start | bytes 614408 | tf_op jit(solution)/shard_map/ppermute | solution.py:324
  41.3 4.3 %collective-permute-start.7 = (bf16[80,640]{1,0:T(8,128)(2,1)S(1)}, bf16[80,640]{1,0:T(8,128)(2,1)S(1)}, u32[]{:S(2)}, u32[]{:S(2)}) collective-permute-start(bf16[80,640]{1,0:T(8,128)(2,1)S(1)} %get-tuple-element.35), channel_id=1, source_target_pairs={{0,2},{2,0},{4,6},{6,4},{8,10},{10,8},{12,14},{14,12},{1,3},{3,1},... | collective-permute-start | bytes 307208 | tf_op jit(solution)/shard_map/ppermute | solution.py:324
  41.5 7.1 %collective-permute-start.8 = (bf16[80,640]{1,0:T(8,128)(2,1)S(1)}, bf16[80,640]{1,0:T(8,128)(2,1)S(1)}, u32[]{:S(2)}, u32[]{:S(2)}) collective-permute-start(bf16[80,640]{1,0:T(8,128)(2,1)S(1)} %get-tuple-element.36), channel_id=1, source_target_pairs={{0,4},{2,14},{4,0},{6,10},{8,12},{10,6},{12,8},{14,2},{1,5},{3,15}... | collective-permute-start | bytes 307208 | tf_op jit(solution)/shard_map/ppermute | solution.py:324
  41.5 7.1 %collective-permute-start.9 = (bf16[80,640]{1,0:T(8,128)(2,1)S(1)}, bf16[80,640]{1,0:T(8,128)(2,1)S(1)}, u32[]{:S(2)}, u32[]{:S(2)}) collective-permute-start(bf16[80,640]{1,0:T(8,128)(2,1)S(1)} %get-tuple-element.37), channel_id=1, source_target_pairs={{0,12},{2,6},{4,8},{6,2},{8,4},{10,14},{12,0},{14,10},{1,13},{3,7}... | collective-permute-start | bytes 307208 | tf_op jit(solution)/shard_map/ppermute | solution.py:324
  42.9 7.3 %collective-permute-start.10 = (bf16[80,640]{1,0:T(8,128)(2,1)S(1)}, bf16[80,640]{1,0:T(8,128)(2,1)S(1)}, u32[]{:S(2)}, u32[]{:S(2)}) collective-permute-start(bf16[80,640]{1,0:T(8,128)(2,1)S(1)} %get-tuple-element.38), channel_id=1, source_target_pairs={{0,8},{2,10},{4,12},{6,14},{8,0},{10,2},{12,4},{14,6},{1,9},{3,11}... | collective-permute-start | bytes 307208 | tf_op jit(solution)/shard_map/ppermute | solution.py:324
  45.6 5.8 %collective-permute-start.11 = (bf16[80,640]{1,0:T(8,128)(2,1)S(1)}, bf16[80,640]{1,0:T(8,128)(2,1)S(1)}, u32[]{:S(2)}, u32[]{:S(2)}) collective-permute-start(bf16[80,640]{1,0:T(8,128)(2,1)S(1)} %get-tuple-element.39), channel_id=1, source_target_pairs={{0,6},{2,12},{4,2},{6,8},{8,14},{10,4},{12,10},{14,0},{1,7},{3,13}... | collective-permute-start | bytes 307208 | tf_op jit(solution)/shard_map/ppermute | solution.py:324
  45.6 6.0 %collective-permute-start.12 = (bf16[80,640]{1,0:T(8,128)(2,1)S(1)}, bf16[80,640]{1,0:T(8,128)(2,1)S(1)}, u32[]{:S(2)}, u32[]{:S(2)}) collective-permute-start(bf16[80,640]{1,0:T(8,128)(2,1)S(1)} %get-tuple-element.40), channel_id=1, source_target_pairs={{0,14},{2,4},{4,10},{6,0},{8,6},{10,12},{12,2},{14,8},{1,15},{3,5}... | collective-permute-start | bytes 307208 | tf_op jit(solution)/shard_map/ppermute | solution.py:324
  48.6 6.2 %collective-permute-start.13 = (bf16[80,640]{1,0:T(8,128)(2,1)S(1)}, bf16[80,640]{1,0:T(8,128)(2,1)S(1)}, u32[]{:S(2)}, u32[]{:S(2)}) collective-permute-start(bf16[80,640]{1,0:T(8,128)(2,1)S(1)} %get-tuple-element.41), channel_id=1, source_target_pairs={{0,10},{2,8},{4,14},{6,12},{8,2},{10,0},{12,6},{14,4},{1,11},{3,9}... | collective-permute-start | bytes 307208 | tf_op jit(solution)/shard_map/ppermute | solution.py:324
  57.8 29.0 %all-to-all-start.1 = ((bf16[16,5,8,640]{3,2,1,0:T(8,128)(2,1)}), bf16[16,5,8,640]{3,2,1,0:T(8,128)(2,1)S(1)}, u32[]{:S(2)}, u32[]{:S(2)}) async-start(bf16[16,5,8,640]{3,2,1,0:T(8,128)(2,1)} %turn.1), calls=%async_computation.1 | async-start | bytes 1638400 | tf_op jit(solution)/shard_map/all_to_all | solution.py:335

commit v8 on v7

--- a/solution.py
+++ b/solution.py
@@ -35,12 +35,14 @@
     writes = []
     for b in range(steps):
         reads[b].wait()
+        lanes = 384
         for g in range(lats // 16):
-            block = in_buf[b, 16 * g : 16 * g + 16].astype(jnp.float32).reshape(128, degs)
+            part = slice(16 * g, 16 * g + 16)
+            block = in_buf[b, part, :, :lanes].astype(jnp.float32).reshape(128, lanes)
             turned = jnp.dot(swap, block.astype(jnp.bfloat16), preferred_element_type=jnp.float32)
-            out_buf[b, :, 16 * g : 16 * g + 16, :] = turned.astype(jnp.bfloat16).reshape(
-                8, 16, degs
-            )
+            out_buf[b, :, part, :lanes] = turned.astype(jnp.bfloat16).reshape(8, 16, lanes)
+            other = jnp.swapaxes(in_buf[b, part, :, lanes:].astype(jnp.float32), 0, 1)
+            out_buf[b, :, part, lanes:] = other.astype(jnp.bfloat16)
         writes.append(pltpu.make_async_copy(out_buf.at[b], out_hbm.at[:, b], out_sems.at[b]))
         writes[b].start()
     for write in writes:
@@ -200,11 +202,15 @@
     steps, _, lats, degs = basis.shape
     deg_dev = degs // 16
     head = head_ref.shape[1]
+    halves = (pl.ds(0, 4), pl.ds(4, 4))
     copies = [
-        pltpu.make_async_copy(basis_any.at[:, b], basis.at[b], sems.at[b])
+        [
+            pltpu.make_async_copy(basis_any.at[part, b], basis.at[b, part], sems.at[b, i])
+            for i, part in enumerate(halves)
+        ]
         for b in range(head, steps)
     ]
-    for copy in copies:
+    for copy in sum(copies, []):
         copy.start()
 
     def summed(b):
@@ -216,7 +222,8 @@
                         :, seg * lats : (seg + 1) * lats
                     ]
         if b >= head:
-            copies[b - head].wait()
+            for copy in copies[b - head]:
+                copy.wait()
             blocks = basis[b]
         else:
             blocks = head_ref[:, b]
@@ -269,7 +276,7 @@
             pltpu.VMEM((steps, 8, lats, degs), jnp.bfloat16),
             pltpu.VMEM((128, 8 * lats), jnp.float32),
             pltpu.VMEM((degs, 128), jnp.float32),
-            pltpu.SemaphoreType.DMA((steps,)),
+            pltpu.SemaphoreType.DMA((steps, 2)),
         ],
         compiler_params=params(16),
         cost_estimate=cost(5 * 2 * 128 * 8 * lats * degs, 2 * basis.size + 2 * fourier.size),
@@ -277,7 +284,7 @@
     )(slots, fourier, head, basis)
 
 
-def finish_kernel(in_ref, out_ref, rows):
+def finish_kernel(in_ref, out_hbm, rows, out_ref, sems):
     depth = in_ref.shape[1]
     for x in range(4):
         for zq in range(2):
@@ -286,6 +293,7 @@
                 second = in_ref[8 * x + 4 + 2 * zq + lev].astype(jnp.float32)
                 rows[pl.ds((8 * lev + 2 * x + zq) * depth, depth), :] = first + second
     low = lax.broadcasted_iota(jnp.int32, (16, 128), 1) < 64
+    copies = []
     for n in range(0, 40, 2):
         parts = []
         for k in range(2):
@@ -295,13 +303,27 @@
             parts.append(jnp.where(low, pltpu.roll(one, 64, 1), two))
         parts.append(rows[pl.ds(80 + n // 2, 16, stride=depth), :])
         out_ref[pl.ds(64 * n, 128), :] = jnp.concatenate(parts, 0).T
+        if n % 10 == 8:
+            piece = pl.ds(64 * (n - 8), 640)
+            copies.append(
+                pltpu.make_async_copy(out_ref.at[piece], out_hbm.at[piece], sems.at[n // 10])
+            )
+            copies[-1].start()
+    for copy in copies:
+        copy.wait()
 
 
 def finish(received):
     return pl.pallas_call(
         finish_kernel,
+        in_specs=[pl.BlockSpec(memory_space=pltpu.VMEM)],
+        out_specs=pl.BlockSpec(memory_space=pltpu.HBM),
         out_shape=jax.ShapeDtypeStruct((40 * 64, 80), jnp.float32),
-        scratch_shapes=[pltpu.VMEM((16 * received.shape[1], 128), jnp.float32)],
+        scratch_shapes=[
+            pltpu.VMEM((16 * received.shape[1], 128), jnp.float32),
+            pltpu.VMEM((40 * 64, 80), jnp.float32),
+            pltpu.SemaphoreType.DMA((4,)),
+        ],
         compiler_params=params(12),
         cost_estimate=cost(received.size, 2 * received.size + 4 * 40 * 64 * 128),
         name="finish",

time: 125 us -> 125 us (level)
  no operation moved by 1% of the time
where the time goes in v8:
time: 125 us; the launch traced here: 124 us
  waiting for transfers between devices  33.7 us (27%)
  blocking collectives  32.5 us (26%)
  starting transfers between devices  32.2 us (26%)
  Pallas kernels  18.2 us (15%)
  local copies, waits for them, and re-layouts  4.74 us (4%)
  other arithmetic  2.39 us (2%)
    all_to_all x1, blocking collectives, local(): parts = lax.all_to_all(parts, ('x', 'zp', 'zq', 'lev'), 0, 0, tiled=True)  32.5 us
    all_to_all x1, waiting for transfers between devices, local(): fourier = lax.all_to_all(fourier, ('x', 'zq', 'lev'), 0, 0, tiled=True)  16.5 us
    ppermute x14, waiting for transfers between devices, swapped(): lax.ppermute(blocks[k], 'wave', [(w, w ^ TO[w % 2][k]) for w in range(8)])  16.4 us
    ppermute x14, starting transfers between devices, swapped(): lax.ppermute(blocks[k], 'wave', [(w, w ^ TO[w % 2][k]) for w in range(8)])  15.1 us
    all_to_all x1, starting transfers between devices, local(): fourier = lax.all_to_all(fourier, ('x', 'zq', 'lev'), 0, 0, tiled=True)  10.3 us
    all_to_all x1, starting transfers between devices, local(): basis = lax.all_to_all(basis, ('x', 'zq'), 0, 0, tiled=True)  6.84 us
    pallas_call x1, Pallas kernels, basis_blocks(): pl.pallas_call(basis_kernel, in_specs=[pl.BlockSpec(memory_space=pltpu.SM...  4.63 us
    pallas_call x1, Pallas kernels, spectral_parts(): pl.pallas_call(spectral_kernel, in_specs=[smem, vmem, vmem, pl.BlockSpec(...  3.25 us
  transfers between devices with their start and end apart: 16, of which 10 were waited for; matrix products, arithmetic and copies ran while one was open for 4% of the time, Pallas kernels for 7%

profile of v8, /device:TPU:2, one launch (start us, length us, event | category | flops | bytes accessed | tf_op | source)
XLA Modules:
  0.0 124.1 jit_solution(15920523258014167716)
XLA Ops:
  0.0 4.6 %basis_blocks.1 = (bf16[8,5,80,640]{3,2,1,0:T(8,128)(2,1)}, f32[8,128]{1,0:T(8,128)}) custom-call(s32[1]{0:T(128)} %bitcast.3.lev_ref, bf16[80,10,8,640]{3,2,1,0:T(8,128)(2,1)} %bitcast.9), custom_call_target="tpu_custom_call" | custom-call | bytes 8192000 | tf_op jit(solution)/shard_map/basis_blocks/pallas_call | solution.py:56
  4.6 0.0 copy-start.7
  4.6 0.0 copy-start.8
  4.7 0.0 copy-start
  4.7 0.0 copy-start.2
  4.7 0.0 copy-start.3
  4.7 0.0 copy-start.4
  4.7 6.8 %all-to-all-start = ((bf16[8,5,80,640]{3,2,1,0:T(8,128)(2,1)}), bf16[8,5,80,640]{3,2,1,0:T(8,128)(2,1)}, u32[]{:S(2)}, u32[]{:S(2)}) async-start(bf16[8,5,80,640]{3,2,1,0:T(8,128)(2,1)} %get-tuple-element.42), calls=%async_computation | async-start | bytes 8192000 | tf_op jit(solution)/shard_map/all_to_all | solution.py:352
  11.6 0.0 copy-start.1
  11.6 1.5 %copy-done.1 = bf16[32,80,320]{2,1,0:T(8,128)(2,1)S(1)} copy-done((bf16[32,80,320]{2,1,0:T(8,128)(2,1)S(1)}, bf16[32,80,320]{2,1,0:T(8,128)(2,1)}, u32[]{:S(2)}) %copy-start.1) | copy-done | bytes 1638424
  13.2 2.4 %gradient.1 = (bf16[2,80,640]{2,1,0:T(8,128)(2,1)S(1)}, bf16[2,80,640]{2,1,0:T(8,128)(2,1)}, bf16[2,80,640]{2,1,0:T(8,128)(2,1)S(1)}, bf16[2,80,640]{2,1,0:T(8,1...) custom-call(s32[8]{0:T(128)S(1)} %get-tuple-element.46.wave_ref, ...), custom_call_target="tpu_custom_call" | custom-call | flops 4915200 | bytes 4915200 | tf_op jit(solution)/shard_map/gradient/pallas_call | solution.py:90
  15.6 1.1 collective-permute-start.1
  16.7 2.2 %collective-permute-start.2 = (bf16[2,80,640]{2,1,0:T(8,128)(2,1)S(1)}, bf16[2,80,640]{2,1,0:T(8,128)(2,1)S(1)}, u32[]{:S(2)}, u32[]{:S(2)}) collective-permute-start(bf16[2,80,640]{2,1,0:T(8,128)(2,1)S(1)} %get-tuple-element.29), channel_id=1, source_target_pairs={{0,12},{2,6},{4,8},{6,2},{8,4},{10,14},{12,0},{14,10},{1,13},{3,7}... | collective-permute-start | bytes 614408 | tf_op jit(solution)/shard_map/ppermute | solution.py:346
  18.9 0.9 collective-permute-start.3
  19.7 0.1 reshape.66
  19.8 0.6 gather_fusion.1
  20.4 0.1 mul.86
  20.5 0.1 broadcast_in_dim.11
  20.5 0.1 add.109
  20.7 1.3 %fusion.4 = (f32[64,1280]{1,0:T(8,128)S(1)}, f32[64,1280]{1,0:T(8,128)S(1)}) fusion(s32[1280]{0:T(1024)S(1)} %add.109, s32[1280]{0:T(1024)S(1)} %mul.86), kind=kLoop, calls=%fused_computation.8 | loop fusion | flops 819200 | bytes 665600 | tf_op jit(solution)/shard_map/sin | solution.py:118
  22.0 0.1 broadcast_add_fusion
  22.1 0.1 add.107
  22.2 3.0 %collective-permute-start.5 = (bf16[2,80,640]{2,1,0:T(8,128)(2,1)S(1)}, bf16[2,80,640]{2,1,0:T(8,128)(2,1)S(1)}, u32[]{:S(2)}, u32[]{:S(2)}) collective-permute-start(bf16[2,80,640]{2,1,0:T(8,128)(2,1)S(1)} %get-tuple-element.32), channel_id=1, source_target_pairs={{0,14},{2,4},{4,10},{6,0},{8,6},{10,12},{12,2},{14,8},{1,15},{3,5}... | collective-permute-start | bytes 614408 | tf_op jit(solution)/shard_map/ppermute | solution.py:346
  25.2 0.7 collective-permute-start.6
  25.9 0.9 sine_multiply_fusion
  26.8 1.7 %wave_table.1.table_ref = bf16[5,2560,256]{2,1,0:T(8,128)(2,1)S(1)} custom-call(f32[40,1280]{1,0:T(8,128)S(1)} %get-tuple-element.52.coarse_cos, f32[40,1280]{1,0:T(8,128)S(1)} %get-tuple-element.51.coarse_sin, f32[64,1280]{1,0:T(8,128)S(1)} %get-tuple-element.50.fine_cos, f32[64,1280]{1,0:T(8,128)S(1)} %get-tuple-element.49.fine_sin), custom_call_target="tpu_custom_call" | custom-call | flops 9830400 | bytes 6553600 | tf_op jit(solution)/shard_map/wave_table/pallas_call | solution.py:126
  28.6 1.4 %collective-permute-done.3.refs_4_ = bf16[2,80,640]{2,1,0:T(8,128)(2,1)S(1)} collective-permute-done((bf16[2,80,640]{2,1,0:T(8,128)(2,1)S(1)}, bf16[2,80,640]{2,1,0:T(8,128)(2,1)S(1)}, u32[]{:S(2)}, u32[]{:S(2)}) %collective-permute-start.3) | collective-permute-done | bytes 204832 | tf_op jit(solution)/shard_map/ppermute | solution.py:346
  30.0 1.7 %collective-permute-done.4.refs_5_ = bf16[2,80,640]{2,1,0:T(8,128)(2,1)S(1)} collective-permute-done((bf16[2,80,640]{2,1,0:T(8,128)(2,1)S(1)}, bf16[2,80,640]{2,1,0:T(8,128)(2,1)S(1)}, u32[]{:S(2)}, u32[]{:S(2)}) %collective-permute-start.4) | collective-permute-done | bytes 204832 | tf_op jit(solution)/shard_map/ppermute | solution.py:346
  31.7 4.6 %collective-permute-done.5.refs_6_ = bf16[2,80,640]{2,1,0:T(8,128)(2,1)S(1)} collective-permute-done((bf16[2,80,640]{2,1,0:T(8,128)(2,1)S(1)}, bf16[2,80,640]{2,1,0:T(8,128)(2,1)S(1)}, u32[]{:S(2)}, u32[]{:S(2)}) %collective-permute-start.5) | collective-permute-done | bytes 204832 | tf_op jit(solution)/shard_map/ppermute | solution.py:346
  36.3 2.4 %collective-permute-done.6.refs_7_ = bf16[2,80,640]{2,1,0:T(8,128)(2,1)S(1)} collective-permute-done((bf16[2,80,640]{2,1,0:T(8,128)(2,1)S(1)}, bf16[2,80,640]{2,1,0:T(8,128)(2,1)S(1)}, u32[]{:S(2)}, u32[]{:S(2)}) %collective-permute-start.6) | collective-permute-done | bytes 204832 | tf_op jit(solution)/shard_map/ppermute | solution.py:346
  38.7 2.6 %fourier_rows.1 = (bf16[80,640]{1,0:T(8,128)(2,1)S(1)}, bf16[80,640]{1,0:T(8,128)(2,1)S(1)}, bf16[80,640]{1,0:T(8,128)(2,1)S(1)}, bf16[80,640]{1,0:T(8,128)(2,1)...) custom-call(bf16[5,2560,256]{2,1,0:T(8,128)(2,1)S(1)} %wave_table.1., ...), custom_call_target="tpu_custom_call" | custom-call | flops 2097152000 | bytes 6553600 | tf_op jit(solution)/shard_map/fourier_rows/pallas_call | solution.py:161
  41.3 0.2 collective-permute-start.7
  41.5 1.4 %collective-permute-start.9 = (bf16[80,640]{1,0:T(8,128)(2,1)S(1)}, bf16[80,640]{1,0:T(8,128)(2,1)S(1)}, u32[]{:S(2)}, u32[]{:S(2)}) collective-permute-start(bf16[80,640]{1,0:T(8,128)(2,1)S(1)} %get-tuple-element.37), channel_id=1, source_target_pairs={{0,12},{2,6},{4,8},{6,2},{8,4},{10,14},{12,0},{14,10},{1,13},{3,7}... | collective-permute-start | bytes 307208 | tf_op jit(solution)/shard_map/ppermute | solution.py:346
  42.9 2.7 %collective-permute-start.10 = (bf16[80,640]{1,0:T(8,128)(2,1)S(1)}, bf16[80,640]{1,0:T(8,128)(2,1)S(1)}, u32[]{:S(2)}, u32[]{:S(2)}) collective-permute-start(bf16[80,640]{1,0:T(8,128)(2,1)S(1)} %get-tuple-element.38), channel_id=1, source_target_pairs={{0,8},{2,10},{4,12},{6,14},{8,0},{10,2},{12,4},{14,6},{1,9},{3,11}... | collective-permute-start | bytes 307208 | tf_op jit(solution)/shard_map/ppermute | solution.py:346
  45.6 3.0 %collective-permute-start.12 = (bf16[80,640]{1,0:T(8,128)(2,1)S(1)}, bf16[80,640]{1,0:T(8,128)(2,1)S(1)}, u32[]{:S(2)}, u32[]{:S(2)}) collective-permute-start(bf16[80,640]{1,0:T(8,128)(2,1)S(1)} %get-tuple-element.40), channel_id=1, source_target_pairs={{0,14},{2,4},{4,10},{6,0},{8,6},{10,12},{12,2},{14,8},{1,15},{3,5}... | collective-permute-start | bytes 307208 | tf_op jit(solution)/shard_map/ppermute | solution.py:346
  48.6 1.6 %collective-permute-done.10.refs_4_ = bf16[80,640]{1,0:T(8,128)(2,1)S(1)} collective-permute-done((bf16[80,640]{1,0:T(8,128)(2,1)S(1)}, bf16[80,640]{1,0:T(8,128)(2,1)S(1)}, u32[]{:S(2)}, u32[]{:S(2)}) %collective-permute-start.10) | collective-permute-done | bytes 102432 | tf_op jit(solution)/shard_map/ppermute | solution.py:346
  50.2 1.2 collective-permute-done.11.refs_5_
  51.4 0.2 collective-permute-done.12.refs_6_
  51.6 3.1 %collective-permute-done.13.refs_7_ = bf16[80,640]{1,0:T(8,128)(2,1)S(1)} collective-permute-done((bf16[80,640]{1,0:T(8,128)(2,1)S(1)}, bf16[80,640]{1,0:T(8,128)(2,1)S(1)}, u32[]{:S(2)}, u32[]{:S(2)}) %collective-permute-start.13) | collective-permute-done | bytes 102432 | tf_op jit(solution)/shard_map/ppermute | solution.py:346
  54.8 2.1 %turn.1 = bf16[16,5,8,640]{3,2,1,0:T(8,128)(2,1)} custom-call(s32[8]{0:T(128)S(1)} %get-tuple-element.48.wave_ref, bf16[80,640]{1,0:T(8,128)(2,1)S(1)} %get-tuple-element.34.refs_0_, bf16[80,640]{1,0:T(8,128)(2,1)S(1)} %collective-permute-done.7.refs_1_, bf16[80,640]{1,0:T(8,128)(2,1)S(1)} %collective-permute-done.8.refs_2_, ...), custom_call_target="tpu_custom_call" | custom-call | bytes 1638400 | tf_op jit(solution)/shard_map/turn/pallas_call | solution.py:190
  56.9 0.9 all-to-all-done.basis_any
  57.8 10.3 %all-to-all-start.1 = ((bf16[16,5,8,640]{3,2,1,0:T(8,128)(2,1)}), bf16[16,5,8,640]{3,2,1,0:T(8,128)(2,1)S(1)}, u32[]{:S(2)}, u32[]{:S(2)}) async-start(bf16[16,5,8,640]{3,2,1,0:T(8,128)(2,1)} %turn.1), calls=%async_computation.1 | async-start | bytes 1638400 | tf_op jit(solution)/shard_map/all_to_all | solution.py:357
  68.0 0.6 gather_fusion
  68.7 1.6 %slice.3.head_ref = bf16[8,2,80,640]{3,2,1,0:T(8,128)(2,1)S(1)} slice(bf16[8,5,80,640]{3,2,1,0:T(8,128)(2,1)} %all-to-all-done.basis_any), slice={[0:8], [0:2], [0:80], [0:640]} | slice | bytes 3276800 | tf_op jit(solution)/shard_map/slice | solution.py:361
  70.3 16.5 %all-to-all-done.1.four_ref = bf16[16,5,8,640]{3,2,1,0:T(8,128)(2,1)S(1)} async-done(((bf16[16,5,8,640]{3,2,1,0:T(8,128)(2,1)}), bf16[16,5,8,640]{3,2,1,0:T(8,128)(2,1)S(1)}, u32[]{:S(2)}, u32[]{:S(2)}) %all-to-all-start.1) | async-done | bytes 819232 | tf_op jit(solution)/shard_map/all_to_all | solution.py:357
  86.8 3.2 %spectral_parts.1 = bf16[32,104,128]{2,1,0:T(8,128)(2,1)S(1)} custom-call(s32[5]{0:T(128)S(1)} %and_select_fusion.slot_ref, bf16[16,5,8,640]{3,2,1,0:T(8,128)(2,1)S(1)} %all-to-all-done.1.four_ref, bf16[8,2,80,640]{3,2,1,0:T(8,128)(2,1)S(1)} %slice.3.head_ref, bf16[8,5,80,640]{3,2,1,0:T(8,128)(2,1)} %all-to-all-done.basis_any), custom_call_target="tpu_custom_call" | custom-call | flops 524288000 | bytes 4915200 | tf_op jit(solution)/shard_map/spectral_parts/pallas_call | solution.py:271
  90.0 32.5 %all_to_all.15.in_ref = bf16[32,104,128]{2,1,0:T(8,128)(2,1)S(1)} all-to-all(bf16[32,104,128]{2,1,0:T(8,128)(2,1)S(1)} %spectral_parts.1), channel_id=1, replica_groups=mesh['x'=4,'zp'=2,'zq'=2,'wave'=8,'lev'=2] {'x','zp','zq','lev'}, dimensions={0} | all-to-all | bytes 1703936 | tf_op jit(solution)/shard_map/all_to_all | solution.py:362
  122.5 1.5 %finish.1 = f32[2560,80]{1,0:T(8,128)} custom-call(bf16[32,104,128]{2,1,0:T(8,128)(2,1)S(1)} %all_to_all.15.in_ref), custom_call_target="tpu_custom_call" | custom-call | flops 425984 | bytes 2162688 | tf_op jit(solution)/shard_map/finish/pallas_call | solution.py:317
  (30 shorter events, 0.1 us)
Async XLA Ops:
  4.6 6.9 %copy-start.7 = (s32[8]{0:T(128)S(1)}, s32[8]{0:T(128)}, u32[]{:S(2)}) copy-start(s32[8]{0:T(128)} %constant.94.clone) | copy-start | bytes 100
  4.6 6.9 %copy-start.8 = (s32[8]{0:T(128)S(1)}, s32[8]{0:T(128)}, u32[]{:S(2)}) copy-start(s32[8]{0:T(128)} %constant.95.clone) | copy-start | bytes 100
  4.7 6.9 %copy-start = (bf16[32,80,320]{2,1,0:T(8,128)(2,1)S(1)}, bf16[32,80,320]{2,1,0:T(8,128)(2,1)}, u32[]{:S(2)}) copy-start(bf16[32,80,320]{2,1,0:T(8,128)(2,1)} %param.10) | copy-start | bytes 4915204
  4.7 6.9 %copy-start.2 = (f32[8,128]{1,0:T(8,128)S(1)}, f32[8,128]{1,0:T(8,128)}, u32[]{:S(2)}) copy-start(f32[8,128]{1,0:T(8,128)} %get-tuple-element.25._) | copy-start | bytes 12292
  4.7 6.9 %copy-start.3 = (f32[32]{0:T(128)S(1)}, f32[32]{0:T(128)}, u32[]{:S(2)}) copy-start(f32[32]{0:T(128)} %rate_ref.1) | copy-start | bytes 388
  4.7 15.0 %copy-start.4 = (s32[640]{0:T(1024)S(1)}, s32[640]{0:T(1024)}, u32[]{:S(2)}) copy-start(s32[640]{0:T(1024)} %param.14) | copy-start | bytes 7684
  4.7 53.1 %all-to-all-start = ((bf16[8,5,80,640]{3,2,1,0:T(8,128)(2,1)}), bf16[8,5,80,640]{3,2,1,0:T(8,128)(2,1)}, u32[]{:S(2)}, u32[]{:S(2)}) async-start(bf16[8,5,80,640]{3,2,1,0:T(8,128)(2,1)} %get-tuple-element.42), calls=%async_computation | async-start | bytes 8192000 | tf_op jit(solution)/shard_map/all_to_all | solution.py:352
  11.6 9.1 %copy-start.5 = (s32[8]{0:T(128)S(1)}, s32[8]{0:T(128)}, u32[]{:S(2)}) copy-start(s32[8]{0:T(128)} %constant.96.clone) | copy-start | bytes 100
  11.6 9.1 %copy-start.6 = (s32[8]{0:T(128)S(1)}, s32[8]{0:T(128)}, u32[]{:S(2)}) copy-start(s32[8]{0:T(128)} %constant.97.clone) | copy-start | bytes 100
  11.6 1.5 %copy-start.1 = (bf16[32,80,320]{2,1,0:T(8,128)(2,1)S(1)}, bf16[32,80,320]{2,1,0:T(8,128)(2,1)}, u32[]{:S(2)}) copy-start(bf16[32,80,320]{2,1,0:T(8,128)(2,1)} %param.11) | copy-start | bytes 4915204
  15.6 6.6 %collective-permute-start = (bf16[2,80,640]{2,1,0:T(8,128)(2,1)}, bf16[2,80,640]{2,1,0:T(8,128)(2,1)S(1)}, u32[]{:S(2)}, u32[]{:S(2)}) collective-permute-start(bf16[2,80,640]{2,1,0:T(8,128)(2,1)} %get-tuple-element.27), channel_id=1, source_target_pairs={{0,2},{2,0},{4,6},{6,4},{8,10},{10,8},{12,14},{14,12},{1,3},{3,1},... | collective-permute-start | bytes 614408 | tf_op jit(solution)/shard_map/ppermute | solution.py:346
  15.6 9.6 %collective-permute-start.1 = (bf16[2,80,640]{2,1,0:T(8,128)(2,1)S(1)}, bf16[2,80,640]{2,1,0:T(8,128)(2,1)S(1)}, u32[]{:S(2)}, u32[]{:S(2)}) collective-permute-start(bf16[2,80,640]{2,1,0:T(8,128)(2,1)S(1)} %get-tuple-element.28), channel_id=1, source_target_pairs={{0,4},{2,14},{4,0},{6,10},{8,12},{10,6},{12,8},{14,2},{1,5},{3,15}... | collective-permute-start | bytes 614408 | tf_op jit(solution)/shard_map/ppermute | solution.py:346
  16.7 11.9 %collective-permute-start.2 = (bf16[2,80,640]{2,1,0:T(8,128)(2,1)S(1)}, bf16[2,80,640]{2,1,0:T(8,128)(2,1)S(1)}, u32[]{:S(2)}, u32[]{:S(2)}) collective-permute-start(bf16[2,80,640]{2,1,0:T(8,128)(2,1)S(1)} %get-tuple-element.29), channel_id=1, source_target_pairs={{0,12},{2,6},{4,8},{6,2},{8,4},{10,14},{12,0},{14,10},{1,13},{3,7}... | collective-permute-start | bytes 614408 | tf_op jit(solution)/shard_map/ppermute | solution.py:346
  18.9 11.1 %collective-permute-start.3 = (bf16[2,80,640]{2,1,0:T(8,128)(2,1)S(1)}, bf16[2,80,640]{2,1,0:T(8,128)(2,1)S(1)}, u32[]{:S(2)}, u32[]{:S(2)}) collective-permute-start(bf16[2,80,640]{2,1,0:T(8,128)(2,1)S(1)} %get-tuple-element.30), channel_id=1, source_target_pairs={{0,8},{2,10},{4,12},{6,14},{8,0},{10,2},{12,4},{14,6},{1,9},{3,11}... | collective-permute-start | bytes 614408 | tf_op jit(solution)/shard_map/ppermute | solution.py:346
  19.7 12.0 %collective-permute-start.4 = (bf16[2,80,640]{2,1,0:T(8,128)(2,1)S(1)}, bf16[2,80,640]{2,1,0:T(8,128)(2,1)S(1)}, u32[]{:S(2)}, u32[]{:S(2)}) collective-permute-start(bf16[2,80,640]{2,1,0:T(8,128)(2,1)S(1)} %get-tuple-element.31), channel_id=1, source_target_pairs={{0,6},{2,12},{4,2},{6,8},{8,14},{10,4},{12,10},{14,0},{1,7},{3,13}... | collective-permute-start | bytes 614408 | tf_op jit(solution)/shard_map/ppermute | solution.py:346
  22.2 14.2 %collective-permute-start.5 = (bf16[2,80,640]{2,1,0:T(8,128)(2,1)S(1)}, bf16[2,80,640]{2,1,0:T(8,128)(2,1)S(1)}, u32[]{:S(2)}, u32[]{:S(2)}) collective-permute-start(bf16[2,80,640]{2,1,0:T(8,128)(2,1)S(1)} %get-tuple-element.32), channel_id=1, source_target_pairs={{0,14},{2,4},{4,10},{6,0},{8,6},{10,12},{12,2},{14,8},{1,15},{3,5}... | collective-permute-start | bytes 614408 | tf_op jit(solution)/shard_map/ppermute | solution.py:346
  25.2 13.5 %collective-permute-start.6 = (bf16[2,80,640]{2,1,0:T(8,128)(2,1)S(1)}, bf16[2,80,640]{2,1,0:T(8,128)(2,1)S(1)}, u32[]{:S(2)}, u32[]{:S(2)}) collective-permute-start(bf16[2,80,640]{2,1,0:T(8,128)(2,1)S(1)} %get-tuple-element.33), channel_id=1, source_target_pairs={{0,10},{2,8},{4,14},{6,12},{8,2},{10,0},{12,6},{14,4},{1,11},{3,9}... | collective-permute-start | bytes 614408 | tf_op jit(solution)/shard_map/ppermute | solution.py:346
  41.3 4.3 %collective-permute-start.7 = (bf16[80,640]{1,0:T(8,128)(2,1)S(1)}, bf16[80,640]{1,0:T(8,128)(2,1)S(1)}, u32[]{:S(2)}, u32[]{:S(2)}) collective-permute-start(bf16[80,640]{1,0:T(8,128)(2,1)S(1)} %get-tuple-element.35), channel_id=1, source_target_pairs={{0,2},{2,0},{4,6},{6,4},{8,10},{10,8},{12,14},{14,12},{1,3},{3,1},... | collective-permute-start | bytes 307208 | tf_op jit(solution)/shard_map/ppermute | solution.py:346
  41.5 7.1 %collective-permute-start.8 = (bf16[80,640]{1,0:T(8,128)(2,1)S(1)}, bf16[80,640]{1,0:T(8,128)(2,1)S(1)}, u32[]{:S(2)}, u32[]{:S(2)}) collective-permute-start(bf16[80,640]{1,0:T(8,128)(2,1)S(1)} %get-tuple-element.36), channel_id=1, source_target_pairs={{0,4},{2,14},{4,0},{6,10},{8,12},{10,6},{12,8},{14,2},{1,5},{3,15}... | collective-permute-start | bytes 307208 | tf_op jit(solution)/shard_map/ppermute | solution.py:346
  41.5 7.1 %collective-permute-start.9 = (bf16[80,640]{1,0:T(8,128)(2,1)S(1)}, bf16[80,640]{1,0:T(8,128)(2,1)S(1)}, u32[]{:S(2)}, u32[]{:S(2)}) collective-permute-start(bf16[80,640]{1,0:T(8,128)(2,1)S(1)} %get-tuple-element.37), channel_id=1, source_target_pairs={{0,12},{2,6},{4,8},{6,2},{8,4},{10,14},{12,0},{14,10},{1,13},{3,7}... | collective-permute-start | bytes 307208 | tf_op jit(solution)/shard_map/ppermute | solution.py:346
  42.9 7.3 %collective-permute-start.10 = (bf16[80,640]{1,0:T(8,128)(2,1)S(1)}, bf16[80,640]{1,0:T(8,128)(2,1)S(1)}, u32[]{:S(2)}, u32[]{:S(2)}) collective-permute-start(bf16[80,640]{1,0:T(8,128)(2,1)S(1)} %get-tuple-element.38), channel_id=1, source_target_pairs={{0,8},{2,10},{4,12},{6,14},{8,0},{10,2},{12,4},{14,6},{1,9},{3,11}... | collective-permute-start | bytes 307208 | tf_op jit(solution)/shard_map/ppermute | solution.py:346
  45.6 5.8 %collective-permute-start.11 = (bf16[80,640]{1,0:T(8,128)(2,1)S(1)}, bf16[80,640]{1,0:T(8,128)(2,1)S(1)}, u32[]{:S(2)}, u32[]{:S(2)}) collective-permute-start(bf16[80,640]{1,0:T(8,128)(2,1)S(1)} %get-tuple-element.39), channel_id=1, source_target_pairs={{0,6},{2,12},{4,2},{6,8},{8,14},{10,4},{12,10},{14,0},{1,7},{3,13}... | collective-permute-start | bytes 307208 | tf_op jit(solution)/shard_map/ppermute | solution.py:346
  45.6 6.0 %collective-permute-start.12 = (bf16[80,640]{1,0:T(8,128)(2,1)S(1)}, bf16[80,640]{1,0:T(8,128)(2,1)S(1)}, u32[]{:S(2)}, u32[]{:S(2)}) collective-permute-start(bf16[80,640]{1,0:T(8,128)(2,1)S(1)} %get-tuple-element.40), channel_id=1, source_target_pairs={{0,14},{2,4},{4,10},{6,0},{8,6},{10,12},{12,2},{14,8},{1,15},{3,5}... | collective-permute-start | bytes 307208 | tf_op jit(solution)/shard_map/ppermute | solution.py:346
  48.6 6.2 %collective-permute-start.13 = (bf16[80,640]{1,0:T(8,128)(2,1)S(1)}, bf16[80,640]{1,0:T(8,128)(2,1)S(1)}, u32[]{:S(2)}, u32[]{:S(2)}) collective-permute-start(bf16[80,640]{1,0:T(8,128)(2,1)S(1)} %get-tuple-element.41), channel_id=1, source_target_pairs={{0,10},{2,8},{4,14},{6,12},{8,2},{10,0},{12,6},{14,4},{1,11},{3,9}... | collective-permute-start | bytes 307208 | tf_op jit(solution)/shard_map/ppermute | solution.py:346
  57.8 29.0 %all-to-all-start.1 = ((bf16[16,5,8,640]{3,2,1,0:T(8,128)(2,1)}), bf16[16,5,8,640]{3,2,1,0:T(8,128)(2,1)S(1)}, u32[]{:S(2)}, u32[]{:S(2)}) async-start(bf16[16,5,8,640]{3,2,1,0:T(8,128)(2,1)} %turn.1), calls=%async_computation.1 | async-start | bytes 1638400 | tf_op jit(solution)/shard_map/all_to_all | solution.py:357

commit v9 on v8

--- a/solution.py
+++ b/solution.py
@@ -198,7 +198,7 @@
     )(waves, *blocks)
 
 
-def spectral_kernel(slot_ref, four_ref, head_ref, basis_any, out_ref, basis, left, total, sems):
+def spectral_kernel(four_ref, head_ref, basis_any, out_ref, basis, left, total, sems):
     steps, _, lats, degs = basis.shape
     deg_dev = degs // 16
     head = head_ref.shape[1]
@@ -227,13 +227,11 @@
             blocks = basis[b]
         else:
             blocks = head_ref[:, b]
-        value = jnp.dot(
+        return jnp.dot(
             left[...].astype(jnp.bfloat16),
             blocks.reshape(8 * lats, degs),
             preferred_element_type=jnp.float32,
         )
-        degree = lax.broadcasted_iota(jnp.int32, value.shape, 1)
-        return jnp.where(degree >= slot_ref[b], value, 0.0)
 
     for k in range(2):
         even, odd = summed(2 * k), summed(2 * k + 1)
@@ -265,12 +263,12 @@
         )
 
 
-def spectral_parts(slots, fourier, head, basis):
+def spectral_parts(fourier, head, basis):
     _, steps, lats, degs = basis.shape
-    vmem, smem = pl.BlockSpec(memory_space=pltpu.VMEM), pl.BlockSpec(memory_space=pltpu.SMEM)
+    vmem = pl.BlockSpec(memory_space=pltpu.VMEM)
     return pl.pallas_call(
         spectral_kernel,
-        in_specs=[smem, vmem, vmem, pl.BlockSpec(memory_space=pl.ANY)],
+        in_specs=[vmem, vmem, pl.BlockSpec(memory_space=pl.ANY)],
         out_shape=jax.ShapeDtypeStruct((32, 104, 128), jnp.bfloat16),
         scratch_shapes=[
             pltpu.VMEM((steps, 8, lats, degs), jnp.bfloat16),
@@ -281,10 +279,10 @@
         compiler_params=params(16),
         cost_estimate=cost(5 * 2 * 128 * 8 * lats * degs, 2 * basis.size + 2 * fourier.size),
         name="spectral_parts",
-    )(slots, fourier, head, basis)
-
-
-def finish_kernel(in_ref, out_hbm, rows, out_ref, sems):
+    )(fourier, head, basis)
+
+
+def finish_kernel(start_ref, slot_ref, in_ref, out_hbm, rows, out_ref, sems):
     depth = in_ref.shape[1]
     for x in range(4):
         for zq in range(2):
@@ -293,6 +291,8 @@
                 second = in_ref[8 * x + 4 + 2 * zq + lev].astype(jnp.float32)
                 rows[pl.ds((8 * lev + 2 * x + zq) * depth, depth), :] = first + second
     low = lax.broadcasted_iota(jnp.int32, (16, 128), 1) < 64
+    slots = out_ref.shape[1]
+    margin = lax.broadcasted_iota(jnp.int32, (128, slots), 0) // 64 + start_ref[0] - slot_ref[...]
     copies = []
     for n in range(0, 40, 2):
         parts = []
@@ -302,7 +302,8 @@
             parts.append(jnp.where(low, one, pltpu.roll(two, 64, 1)))
             parts.append(jnp.where(low, pltpu.roll(one, 64, 1), two))
         parts.append(rows[pl.ds(80 + n // 2, 16, stride=depth), :])
-        out_ref[pl.ds(64 * n, 128), :] = jnp.concatenate(parts, 0).T
+        value = jnp.concatenate(parts, 0).T
+        out_ref[pl.ds(64 * n, 128), :] = jnp.where(margin + n >= 0, value, 0.0)
         if n % 10 == 8:
             piece = pl.ds(64 * (n - 8), 640)
             copies.append(
@@ -313,10 +314,11 @@
         copy.wait()
 
 
-def finish(received):
+def finish(start, slots, received):
     return pl.pallas_call(
         finish_kernel,
-        in_specs=[pl.BlockSpec(memory_space=pltpu.VMEM)],
+        in_specs=[pl.BlockSpec(memory_space=pltpu.SMEM)]
+        + [pl.BlockSpec(memory_space=pltpu.VMEM)] * 2,
         out_specs=pl.BlockSpec(memory_space=pltpu.HBM),
         out_shape=jax.ShapeDtypeStruct((40 * 64, 80), jnp.float32),
         scratch_shapes=[
@@ -327,7 +329,7 @@
         compiler_params=params(12),
         cost_estimate=cost(received.size, 2 * received.size + 4 * 40 * 64 * 128),
         name="finish",
-    )(received)
+    )(start, slots, received)
 
 
 def local(out_grad, grid_state, tend_rate, legendre_basis, wave_slot):
@@ -356,11 +358,12 @@
     fourier, basis = lax.optimization_barrier((turn(source, blocks), basis))
     fourier = lax.all_to_all(fourier, ("x", "zq", "lev"), 0, 0, tiled=True)
 
-    first = wave * slot_dev + 8 * lev + 2 * x + zq
-    slots = jnp.take(wave_slot, first + 16 * jnp.arange(slot_dev // 16, dtype=jnp.int32))
-    parts = spectral_parts(slots, fourier, basis[:, :2], basis)
+    parts = spectral_parts(fourier, basis[:, :2], basis)
     parts = lax.all_to_all(parts, ("x", "zp", "zq", "lev"), 0, 0, tiled=True)
-    return finish(parts).reshape(degs // 16, 2, 32, slot_dev)
+    deg_dev = degs // 16
+    start = (4 * x + 2 * lax.axis_index("zp") + zq).astype(jnp.int32)[None] * deg_dev
+    slots = lax.dynamic_slice_in_dim(wave_slot, wave * slot_dev, slot_dev)[None]
+    return finish(start, slots, parts).reshape(deg_dev, 2, 32, slot_dev)
 
 
 def solution(mesh):

time: 125 us -> 125 us (level)
  blocking collectives: 32.5 us -> 0 us
  waiting for transfers between devices: 33.7 us -> 57.3 us
  starting transfers between devices: 32.2 us -> 41.9 us
    all_to_all x1 -> x0, blocking collectives: 32.5 us -> none  [local(): parts = lax.all_to_all(parts, ('x', 'zp', 'zq', 'lev'), 0, 0, tiled=True)]
    all_to_all x0 -> x1, waiting for transfers between devices: none -> 22.9 us  [local(): parts = lax.all_to_all(parts, ('x', 'zp', 'zq', 'lev'), 0, 0, tiled=True)]
    all_to_all x0 -> x1, starting transfers between devices: none -> 9.72 us  [local(): parts = lax.all_to_all(parts, ('x', 'zp', 'zq', 'lev'), 0, 0, tiled=True)]
  transfers between devices with their start and end apart: 16 -> 17, of which waited for: 10 -> 11; matrix products, arithmetic and copies ran while one was open for 4% -> 4% of each run, Pallas kernels for 7% -> 7%
where the time goes in v9:
time: 125 us
  waiting for transfers between devices  57.3 us (46%)
  starting transfers between devices  41.9 us (34%)
  Pallas kernels  18.6 us (15%)
  local copies, waits for them, and re-layouts  4.18 us (3%)
  other arithmetic  2.36 us (2%)
    all_to_all x1, waiting for transfers between devices, local(): parts = lax.all_to_all(parts, ('x', 'zp', 'zq', 'lev'), 0, 0, tiled=True)  22.9 us
    all_to_all x1, waiting for transfers between devices, local(): fourier = lax.all_to_all(fourier, ('x', 'zq', 'lev'), 0, 0, tiled=True)  17.2 us
    ppermute x14, waiting for transfers between devices, swapped(): lax.ppermute(blocks[k], 'wave', [(w, w ^ TO[w % 2][k]) for w in range(8)])  16.4 us
    ppermute x14, starting transfers between devices, swapped(): lax.ppermute(blocks[k], 'wave', [(w, w ^ TO[w % 2][k]) for w in range(8)])  15.1 us
    all_to_all x1, starting transfers between devices, local(): fourier = lax.all_to_all(fourier, ('x', 'zq', 'lev'), 0, 0, tiled=True)  10.3 us
    all_to_all x1, starting transfers between devices, local(): parts = lax.all_to_all(parts, ('x', 'zp', 'zq', 'lev'), 0, 0, tiled=True)  9.72 us
    all_to_all x1, starting transfers between devices, local(): basis = lax.all_to_all(basis, ('x', 'zq'), 0, 0, tiled=True)  6.86 us
    pallas_call x1, Pallas kernels, basis_blocks(): pl.pallas_call(basis_kernel, in_specs=[pl.BlockSpec(memory_space=pltpu.SM...  4.58 us
  transfers between devices with their start and end apart: 17, of which 11 were waited for; matrix products, arithmetic and copies ran while one was open for 4% of the time, Pallas kernels for 7%

profile of v9, /device:TPU:2, one launch (start us, length us, event | category | flops | bytes accessed | tf_op | source)
XLA Modules:
  0.0 124.8 jit_solution(470965694360560357)
XLA Ops:
  0.0 4.6 %basis_blocks.1 = (bf16[8,5,80,640]{3,2,1,0:T(8,128)(2,1)}, f32[8,128]{1,0:T(8,128)}) custom-call(s32[1]{0:T(128)} %bitcast.4.lev_ref, bf16[80,10,8,640]{3,2,1,0:T(8,128)(2,1)} %bitcast.10), custom_call_target="tpu_custom_call" | custom-call | bytes 8192000 | tf_op jit(solution)/shard_map/basis_blocks/pallas_call | solution.py:56
  4.6 0.0 copy-start.7
  4.6 0.0 copy-start.8
  4.6 0.0 copy-start
  4.6 0.0 copy-start.2
  4.7 0.0 copy-start.4
  4.7 6.9 %all-to-all-start = ((bf16[8,5,80,640]{3,2,1,0:T(8,128)(2,1)}), bf16[8,5,80,640]{3,2,1,0:T(8,128)(2,1)}, u32[]{:S(2)}, u32[]{:S(2)}) async-start(bf16[8,5,80,640]{3,2,1,0:T(8,128)(2,1)} %get-tuple-element.42), calls=%async_computation | async-start | bytes 8192000 | tf_op jit(solution)/shard_map/all_to_all | solution.py:354
  11.6 1.5 %copy-done.1 = bf16[32,80,320]{2,1,0:T(8,128)(2,1)S(1)} copy-done((bf16[32,80,320]{2,1,0:T(8,128)(2,1)S(1)}, bf16[32,80,320]{2,1,0:T(8,128)(2,1)}, u32[]{:S(2)}) %copy-start.1) | copy-done | bytes 1638424
  13.1 2.4 %gradient.1 = (bf16[2,80,640]{2,1,0:T(8,128)(2,1)S(1)}, bf16[2,80,640]{2,1,0:T(8,128)(2,1)}, bf16[2,80,640]{2,1,0:T(8,128)(2,1)S(1)}, bf16[2,80,640]{2,1,0:T(8,1...) custom-call(s32[8]{0:T(128)S(1)} %get-tuple-element.46.wave_ref, ...), custom_call_target="tpu_custom_call" | custom-call | flops 4915200 | bytes 4915200 | tf_op jit(solution)/shard_map/gradient/pallas_call | solution.py:90
  15.6 1.0 collective-permute-start.1
  16.6 2.2 %collective-permute-start.2 = (bf16[2,80,640]{2,1,0:T(8,128)(2,1)S(1)}, bf16[2,80,640]{2,1,0:T(8,128)(2,1)S(1)}, u32[]{:S(2)}, u32[]{:S(2)}) collective-permute-start(bf16[2,80,640]{2,1,0:T(8,128)(2,1)S(1)} %get-tuple-element.29), channel_id=1, source_target_pairs={{0,12},{2,6},{4,8},{6,2},{8,4},{10,14},{12,0},{14,10},{1,13},{3,7}... | collective-permute-start | bytes 614408 | tf_op jit(solution)/shard_map/ppermute | solution.py:348
  18.8 0.9 collective-permute-start.3
  19.7 0.1 reshape.44
  19.8 0.6 gather_fusion
  20.3 0.1 mul.73
  20.4 0.1 broadcast_in_dim.13
  20.5 0.1 add.69
  20.6 1.3 %fusion.4 = (f32[64,1280]{1,0:T(8,128)S(1)}, f32[64,1280]{1,0:T(8,128)S(1)}) fusion(s32[1280]{0:T(1024)S(1)} %add.69, s32[1280]{0:T(1024)S(1)} %mul.73), kind=kLoop, calls=%fused_computation.7 | loop fusion | flops 819200 | bytes 665600 | tf_op jit(solution)/shard_map/sin | solution.py:118
  22.0 0.1 broadcast_add_fusion
  22.1 0.1 add.67
  22.1 3.0 %collective-permute-start.5 = (bf16[2,80,640]{2,1,0:T(8,128)(2,1)S(1)}, bf16[2,80,640]{2,1,0:T(8,128)(2,1)S(1)}, u32[]{:S(2)}, u32[]{:S(2)}) collective-permute-start(bf16[2,80,640]{2,1,0:T(8,128)(2,1)S(1)} %get-tuple-element.32), channel_id=1, source_target_pairs={{0,14},{2,4},{4,10},{6,0},{8,6},{10,12},{12,2},{14,8},{1,15},{3,5}... | collective-permute-start | bytes 614408 | tf_op jit(solution)/shard_map/ppermute | solution.py:348
  25.2 0.7 collective-permute-start.6
  25.9 0.9 sine_multiply_fusion
  26.8 1.7 %wave_table.1.table_ref = bf16[5,2560,256]{2,1,0:T(8,128)(2,1)S(1)} custom-call(f32[40,1280]{1,0:T(8,128)S(1)} %get-tuple-element.52.coarse_cos, f32[40,1280]{1,0:T(8,128)S(1)} %get-tuple-element.51.coarse_sin, f32[64,1280]{1,0:T(8,128)S(1)} %get-tuple-element.50.fine_cos, f32[64,1280]{1,0:T(8,128)S(1)} %get-tuple-element.49.fine_sin), custom_call_target="tpu_custom_call" | custom-call | flops 9830400 | bytes 6553600 | tf_op jit(solution)/shard_map/wave_table/pallas_call | solution.py:126
  28.5 1.4 %collective-permute-done.3.refs_4_ = bf16[2,80,640]{2,1,0:T(8,128)(2,1)S(1)} collective-permute-done((bf16[2,80,640]{2,1,0:T(8,128)(2,1)S(1)}, bf16[2,80,640]{2,1,0:T(8,128)(2,1)S(1)}, u32[]{:S(2)}, u32[]{:S(2)}) %collective-permute-start.3) | collective-permute-done | bytes 204832 | tf_op jit(solution)/shard_map/ppermute | solution.py:348
  29.9 1.8 %collective-permute-done.4.refs_5_ = bf16[2,80,640]{2,1,0:T(8,128)(2,1)S(1)} collective-permute-done((bf16[2,80,640]{2,1,0:T(8,128)(2,1)S(1)}, bf16[2,80,640]{2,1,0:T(8,128)(2,1)S(1)}, u32[]{:S(2)}, u32[]{:S(2)}) %collective-permute-start.4) | collective-permute-done | bytes 204832 | tf_op jit(solution)/shard_map/ppermute | solution.py:348
  31.7 4.5 %collective-permute-done.5.refs_6_ = bf16[2,80,640]{2,1,0:T(8,128)(2,1)S(1)} collective-permute-done((bf16[2,80,640]{2,1,0:T(8,128)(2,1)S(1)}, bf16[2,80,640]{2,1,0:T(8,128)(2,1)S(1)}, u32[]{:S(2)}, u32[]{:S(2)}) %collective-permute-start.5) | collective-permute-done | bytes 204832 | tf_op jit(solution)/shard_map/ppermute | solution.py:348
  36.3 2.4 %collective-permute-done.6.refs_7_ = bf16[2,80,640]{2,1,0:T(8,128)(2,1)S(1)} collective-permute-done((bf16[2,80,640]{2,1,0:T(8,128)(2,1)S(1)}, bf16[2,80,640]{2,1,0:T(8,128)(2,1)S(1)}, u32[]{:S(2)}, u32[]{:S(2)}) %collective-permute-start.6) | collective-permute-done | bytes 204832 | tf_op jit(solution)/shard_map/ppermute | solution.py:348
  38.7 2.6 %fourier_rows.1 = (bf16[80,640]{1,0:T(8,128)(2,1)S(1)}, bf16[80,640]{1,0:T(8,128)(2,1)S(1)}, bf16[80,640]{1,0:T(8,128)(2,1)S(1)}, bf16[80,640]{1,0:T(8,128)(2,1)...) custom-call(bf16[5,2560,256]{2,1,0:T(8,128)(2,1)S(1)} %wave_table.1., ...), custom_call_target="tpu_custom_call" | custom-call | flops 2097152000 | bytes 6553600 | tf_op jit(solution)/shard_map/fourier_rows/pallas_call | solution.py:161
  41.3 0.2 collective-permute-start.7
  41.5 0.0 collective-permute-start.8
  41.5 1.4 %collective-permute-start.9 = (bf16[80,640]{1,0:T(8,128)(2,1)S(1)}, bf16[80,640]{1,0:T(8,128)(2,1)S(1)}, u32[]{:S(2)}, u32[]{:S(2)}) collective-permute-start(bf16[80,640]{1,0:T(8,128)(2,1)S(1)} %get-tuple-element.37), channel_id=1, source_target_pairs={{0,12},{2,6},{4,8},{6,2},{8,4},{10,14},{12,0},{14,10},{1,13},{3,7}... | collective-permute-start | bytes 307208 | tf_op jit(solution)/shard_map/ppermute | solution.py:348
  42.9 2.7 %collective-permute-start.10 = (bf16[80,640]{1,0:T(8,128)(2,1)S(1)}, bf16[80,640]{1,0:T(8,128)(2,1)S(1)}, u32[]{:S(2)}, u32[]{:S(2)}) collective-permute-start(bf16[80,640]{1,0:T(8,128)(2,1)S(1)} %get-tuple-element.38), channel_id=1, source_target_pairs={{0,8},{2,10},{4,12},{6,14},{8,0},{10,2},{12,4},{14,6},{1,9},{3,11}... | collective-permute-start | bytes 307208 | tf_op jit(solution)/shard_map/ppermute | solution.py:348
  45.6 3.0 %collective-permute-start.12 = (bf16[80,640]{1,0:T(8,128)(2,1)S(1)}, bf16[80,640]{1,0:T(8,128)(2,1)S(1)}, u32[]{:S(2)}, u32[]{:S(2)}) collective-permute-start(bf16[80,640]{1,0:T(8,128)(2,1)S(1)} %get-tuple-element.40), channel_id=1, source_target_pairs={{0,14},{2,4},{4,10},{6,0},{8,6},{10,12},{12,2},{14,8},{1,15},{3,5}... | collective-permute-start | bytes 307208 | tf_op jit(solution)/shard_map/ppermute | solution.py:348
  48.5 1.6 %collective-permute-done.10.refs_4_ = bf16[80,640]{1,0:T(8,128)(2,1)S(1)} collective-permute-done((bf16[80,640]{1,0:T(8,128)(2,1)S(1)}, bf16[80,640]{1,0:T(8,128)(2,1)S(1)}, u32[]{:S(2)}, u32[]{:S(2)}) %collective-permute-start.10) | collective-permute-done | bytes 102432 | tf_op jit(solution)/shard_map/ppermute | solution.py:348
  50.2 1.2 collective-permute-done.11.refs_5_
  51.3 0.2 collective-permute-done.12.refs_6_
  51.6 3.2 %collective-permute-done.13.refs_7_ = bf16[80,640]{1,0:T(8,128)(2,1)S(1)} collective-permute-done((bf16[80,640]{1,0:T(8,128)(2,1)S(1)}, bf16[80,640]{1,0:T(8,128)(2,1)S(1)}, u32[]{:S(2)}, u32[]{:S(2)}) %collective-permute-start.13) | collective-permute-done | bytes 102432 | tf_op jit(solution)/shard_map/ppermute | solution.py:348
  54.7 2.1 %turn.1 = bf16[16,5,8,640]{3,2,1,0:T(8,128)(2,1)} custom-call(s32[8]{0:T(128)S(1)} %get-tuple-element.48.wave_ref, bf16[80,640]{1,0:T(8,128)(2,1)S(1)} %get-tuple-element.34.refs_0_, bf16[80,640]{1,0:T(8,128)(2,1)S(1)} %collective-permute-done.7.refs_1_, bf16[80,640]{1,0:T(8,128)(2,1)S(1)} %collective-permute-done.8.refs_2_, ...), custom_call_target="tpu_custom_call" | custom-call | bytes 1638400 | tf_op jit(solution)/shard_map/turn/pallas_call | solution.py:190
  56.8 0.9 all-to-all-done.basis_any
  57.7 10.3 %all-to-all-start.1 = ((bf16[16,5,8,640]{3,2,1,0:T(8,128)(2,1)}), bf16[16,5,8,640]{3,2,1,0:T(8,128)(2,1)S(1)}, u32[]{:S(2)}, u32[]{:S(2)}) async-start(bf16[16,5,8,640]{3,2,1,0:T(8,128)(2,1)} %turn.1), calls=%async_computation.1 | async-start | bytes 1638400 | tf_op jit(solution)/shard_map/all_to_all | solution.py:359
  68.0 1.6 %slice.3.head_ref = bf16[8,2,80,640]{3,2,1,0:T(8,128)(2,1)S(1)} slice(bf16[8,5,80,640]{3,2,1,0:T(8,128)(2,1)} %all-to-all-done.basis_any), slice={[0:8], [0:2], [0:80], [0:640]} | slice | bytes 3276800 | tf_op jit(solution)/shard_map/slice | solution.py:361
  69.6 17.2 %all-to-all-done.1.four_ref = bf16[16,5,8,640]{3,2,1,0:T(8,128)(2,1)S(1)} async-done(((bf16[16,5,8,640]{3,2,1,0:T(8,128)(2,1)}), bf16[16,5,8,640]{3,2,1,0:T(8,128)(2,1)S(1)}, u32[]{:S(2)}, u32[]{:S(2)}) %all-to-all-start.1) | async-done | bytes 819232 | tf_op jit(solution)/shard_map/all_to_all | solution.py:359
  86.7 3.7 %spectral_parts.1 = bf16[32,104,128]{2,1,0:T(8,128)(2,1)} custom-call(bf16[16,5,8,640]{3,2,1,0:T(8,128)(2,1)S(1)} %all-to-all-done.1.four_ref, bf16[8,2,80,640]{3,2,1,0:T(8,128)(2,1)S(1)} %slice.3.head_ref, bf16[8,5,80,640]{3,2,1,0:T(8,128)(2,1)} %all-to-all-done.basis_any), custom_call_target="tpu_custom_call" | custom-call | flops 524288000 | bytes 4915200 | tf_op jit(solution)/shard_map/spectral_parts/pallas_call | solution.py:269
  90.5 9.7 %all-to-all-start.2 = ((bf16[32,104,128]{2,1,0:T(8,128)(2,1)}), bf16[32,104,128]{2,1,0:T(8,128)(2,1)S(1)}, u32[]{:S(2)}, u32[]{:S(2)}) async-start(bf16[32,104,128]{2,1,0:T(8,128)(2,1)} %spectral_parts.1), calls=%async_computation.2 | async-start | bytes 1703936 | tf_op jit(solution)/shard_map/all_to_all | solution.py:362
  100.2 0.1 dynamic-slice_bitcast_fusion.slot_ref
  100.3 22.9 %all-to-all-done.2.in_ref = bf16[32,104,128]{2,1,0:T(8,128)(2,1)S(1)} async-done(((bf16[32,104,128]{2,1,0:T(8,128)(2,1)}), bf16[32,104,128]{2,1,0:T(8,128)(2,1)S(1)}, u32[]{:S(2)}, u32[]{:S(2)}) %all-to-all-start.2) | async-done | bytes 852000 | tf_op jit(solution)/shard_map/all_to_all | solution.py:362
  123.1 1.5 %finish.1 = f32[2560,80]{1,0:T(8,128)} custom-call(s32[1]{0:T(128)} %bitcast.start_ref, s32[1,80]{1,0:T(1,128)S(1)} %dynamic-slice_bitcast_fusion.slot_ref, bf16[32,104,128]{2,1,0:T(8,128)(2,1)S(1)} %all-to-all-done.2.in_ref), custom_call_target="tpu_custom_call" | custom-call | flops 425984 | bytes 2162688 | tf_op jit(solution)/shard_map/finish/pallas_call | solution.py:318
  (28 shorter events, 0.1 us)
Async XLA Ops:
  4.6 6.9 %copy-start.7 = (s32[8]{0:T(128)S(1)}, s32[8]{0:T(128)}, u32[]{:S(2)}) copy-start(s32[8]{0:T(128)} %constant.87.clone) | copy-start | bytes 100
  4.6 6.9 %copy-start.8 = (s32[8]{0:T(128)S(1)}, s32[8]{0:T(128)}, u32[]{:S(2)}) copy-start(s32[8]{0:T(128)} %constant.88.clone) | copy-start | bytes 100
  4.6 6.9 %copy-start = (bf16[32,80,320]{2,1,0:T(8,128)(2,1)S(1)}, bf16[32,80,320]{2,1,0:T(8,128)(2,1)}, u32[]{:S(2)}) copy-start(bf16[32,80,320]{2,1,0:T(8,128)(2,1)} %param.10) | copy-start | bytes 4915204
  4.6 6.9 %copy-start.2 = (f32[8,128]{1,0:T(8,128)S(1)}, f32[8,128]{1,0:T(8,128)}, u32[]{:S(2)}) copy-start(f32[8,128]{1,0:T(8,128)} %get-tuple-element.25._) | copy-start | bytes 12292
  4.6 6.9 %copy-start.3 = (f32[32]{0:T(128)S(1)}, f32[32]{0:T(128)}, u32[]{:S(2)}) copy-start(f32[32]{0:T(128)} %rate_ref.1) | copy-start | bytes 388
  4.7 15.0 %copy-start.4 = (s32[640]{0:T(1024)S(1)}, s32[640]{0:T(1024)}, u32[]{:S(2)}) copy-start(s32[640]{0:T(1024)} %param.14) | copy-start | bytes 7684
  4.7 53.1 %all-to-all-start = ((bf16[8,5,80,640]{3,2,1,0:T(8,128)(2,1)}), bf16[8,5,80,640]{3,2,1,0:T(8,128)(2,1)}, u32[]{:S(2)}, u32[]{:S(2)}) async-start(bf16[8,5,80,640]{3,2,1,0:T(8,128)(2,1)} %get-tuple-element.42), calls=%async_computation | async-start | bytes 8192000 | tf_op jit(solution)/shard_map/all_to_all | solution.py:354
  11.5 9.1 %copy-start.5 = (s32[8]{0:T(128)S(1)}, s32[8]{0:T(128)}, u32[]{:S(2)}) copy-start(s32[8]{0:T(128)} %constant.89.clone) | copy-start | bytes 100
  11.5 9.1 %copy-start.6 = (s32[8]{0:T(128)S(1)}, s32[8]{0:T(128)}, u32[]{:S(2)}) copy-start(s32[8]{0:T(128)} %constant.90.clone) | copy-start | bytes 100
  11.6 1.5 %copy-start.1 = (bf16[32,80,320]{2,1,0:T(8,128)(2,1)S(1)}, bf16[32,80,320]{2,1,0:T(8,128)(2,1)}, u32[]{:S(2)}) copy-start(bf16[32,80,320]{2,1,0:T(8,128)(2,1)} %param.11) | copy-start | bytes 4915204
  15.6 6.6 %collective-permute-start = (bf16[2,80,640]{2,1,0:T(8,128)(2,1)}, bf16[2,80,640]{2,1,0:T(8,128)(2,1)S(1)}, u32[]{:S(2)}, u32[]{:S(2)}) collective-permute-start(bf16[2,80,640]{2,1,0:T(8,128)(2,1)} %get-tuple-element.27), channel_id=1, source_target_pairs={{0,2},{2,0},{4,6},{6,4},{8,10},{10,8},{12,14},{14,12},{1,3},{3,1},... | collective-permute-start | bytes 614408 | tf_op jit(solution)/shard_map/ppermute | solution.py:348
  15.6 9.6 %collective-permute-start.1 = (bf16[2,80,640]{2,1,0:T(8,128)(2,1)S(1)}, bf16[2,80,640]{2,1,0:T(8,128)(2,1)S(1)}, u32[]{:S(2)}, u32[]{:S(2)}) collective-permute-start(bf16[2,80,640]{2,1,0:T(8,128)(2,1)S(1)} %get-tuple-element.28), channel_id=1, source_target_pairs={{0,4},{2,14},{4,0},{6,10},{8,12},{10,6},{12,8},{14,2},{1,5},{3,15}... | collective-permute-start | bytes 614408 | tf_op jit(solution)/shard_map/ppermute | solution.py:348
  16.6 11.9 %collective-permute-start.2 = (bf16[2,80,640]{2,1,0:T(8,128)(2,1)S(1)}, bf16[2,80,640]{2,1,0:T(8,128)(2,1)S(1)}, u32[]{:S(2)}, u32[]{:S(2)}) collective-permute-start(bf16[2,80,640]{2,1,0:T(8,128)(2,1)S(1)} %get-tuple-element.29), channel_id=1, source_target_pairs={{0,12},{2,6},{4,8},{6,2},{8,4},{10,14},{12,0},{14,10},{1,13},{3,7}... | collective-permute-start | bytes 614408 | tf_op jit(solution)/shard_map/ppermute | solution.py:348
  18.8 11.1 %collective-permute-start.3 = (bf16[2,80,640]{2,1,0:T(8,128)(2,1)S(1)}, bf16[2,80,640]{2,1,0:T(8,128)(2,1)S(1)}, u32[]{:S(2)}, u32[]{:S(2)}) collective-permute-start(bf16[2,80,640]{2,1,0:T(8,128)(2,1)S(1)} %get-tuple-element.30), channel_id=1, source_target_pairs={{0,8},{2,10},{4,12},{6,14},{8,0},{10,2},{12,4},{14,6},{1,9},{3,11}... | collective-permute-start | bytes 614408 | tf_op jit(solution)/shard_map/ppermute | solution.py:348
  19.7 12.1 %collective-permute-start.4 = (bf16[2,80,640]{2,1,0:T(8,128)(2,1)S(1)}, bf16[2,80,640]{2,1,0:T(8,128)(2,1)S(1)}, u32[]{:S(2)}, u32[]{:S(2)}) collective-permute-start(bf16[2,80,640]{2,1,0:T(8,128)(2,1)S(1)} %get-tuple-element.31), channel_id=1, source_target_pairs={{0,6},{2,12},{4,2},{6,8},{8,14},{10,4},{12,10},{14,0},{1,7},{3,13}... | collective-permute-start | bytes 614408 | tf_op jit(solution)/shard_map/ppermute | solution.py:348
  22.1 14.1 %collective-permute-start.5 = (bf16[2,80,640]{2,1,0:T(8,128)(2,1)S(1)}, bf16[2,80,640]{2,1,0:T(8,128)(2,1)S(1)}, u32[]{:S(2)}, u32[]{:S(2)}) collective-permute-start(bf16[2,80,640]{2,1,0:T(8,128)(2,1)S(1)} %get-tuple-element.32), channel_id=1, source_target_pairs={{0,14},{2,4},{4,10},{6,0},{8,6},{10,12},{12,2},{14,8},{1,15},{3,5}... | collective-permute-start | bytes 614408 | tf_op jit(solution)/shard_map/ppermute | solution.py:348
  25.2 13.5 %collective-permute-start.6 = (bf16[2,80,640]{2,1,0:T(8,128)(2,1)S(1)}, bf16[2,80,640]{2,1,0:T(8,128)(2,1)S(1)}, u32[]{:S(2)}, u32[]{:S(2)}) collective-permute-start(bf16[2,80,640]{2,1,0:T(8,128)(2,1)S(1)} %get-tuple-element.33), channel_id=1, source_target_pairs={{0,10},{2,8},{4,14},{6,12},{8,2},{10,0},{12,6},{14,4},{1,11},{3,9}... | collective-permute-start | bytes 614408 | tf_op jit(solution)/shard_map/ppermute | solution.py:348
  41.3 4.3 %collective-permute-start.7 = (bf16[80,640]{1,0:T(8,128)(2,1)S(1)}, bf16[80,640]{1,0:T(8,128)(2,1)S(1)}, u32[]{:S(2)}, u32[]{:S(2)}) collective-permute-start(bf16[80,640]{1,0:T(8,128)(2,1)S(1)} %get-tuple-element.35), channel_id=1, source_target_pairs={{0,2},{2,0},{4,6},{6,4},{8,10},{10,8},{12,14},{14,12},{1,3},{3,1},... | collective-permute-start | bytes 307208 | tf_op jit(solution)/shard_map/ppermute | solution.py:348
  41.5 7.1 %collective-permute-start.8 = (bf16[80,640]{1,0:T(8,128)(2,1)S(1)}, bf16[80,640]{1,0:T(8,128)(2,1)S(1)}, u32[]{:S(2)}, u32[]{:S(2)}) collective-permute-start(bf16[80,640]{1,0:T(8,128)(2,1)S(1)} %get-tuple-element.36), channel_id=1, source_target_pairs={{0,4},{2,14},{4,0},{6,10},{8,12},{10,6},{12,8},{14,2},{1,5},{3,15}... | collective-permute-start | bytes 307208 | tf_op jit(solution)/shard_map/ppermute | solution.py:348
  41.5 7.1 %collective-permute-start.9 = (bf16[80,640]{1,0:T(8,128)(2,1)S(1)}, bf16[80,640]{1,0:T(8,128)(2,1)S(1)}, u32[]{:S(2)}, u32[]{:S(2)}) collective-permute-start(bf16[80,640]{1,0:T(8,128)(2,1)S(1)} %get-tuple-element.37), channel_id=1, source_target_pairs={{0,12},{2,6},{4,8},{6,2},{8,4},{10,14},{12,0},{14,10},{1,13},{3,7}... | collective-permute-start | bytes 307208 | tf_op jit(solution)/shard_map/ppermute | solution.py:348
  42.9 7.3 %collective-permute-start.10 = (bf16[80,640]{1,0:T(8,128)(2,1)S(1)}, bf16[80,640]{1,0:T(8,128)(2,1)S(1)}, u32[]{:S(2)}, u32[]{:S(2)}) collective-permute-start(bf16[80,640]{1,0:T(8,128)(2,1)S(1)} %get-tuple-element.38), channel_id=1, source_target_pairs={{0,8},{2,10},{4,12},{6,14},{8,0},{10,2},{12,4},{14,6},{1,9},{3,11}... | collective-permute-start | bytes 307208 | tf_op jit(solution)/shard_map/ppermute | solution.py:348
  45.6 5.8 %collective-permute-start.11 = (bf16[80,640]{1,0:T(8,128)(2,1)S(1)}, bf16[80,640]{1,0:T(8,128)(2,1)S(1)}, u32[]{:S(2)}, u32[]{:S(2)}) collective-permute-start(bf16[80,640]{1,0:T(8,128)(2,1)S(1)} %get-tuple-element.39), channel_id=1, source_target_pairs={{0,6},{2,12},{4,2},{6,8},{8,14},{10,4},{12,10},{14,0},{1,7},{3,13}... | collective-permute-start | bytes 307208 | tf_op jit(solution)/shard_map/ppermute | solution.py:348
  45.6 6.0 %collective-permute-start.12 = (bf16[80,640]{1,0:T(8,128)(2,1)S(1)}, bf16[80,640]{1,0:T(8,128)(2,1)S(1)}, u32[]{:S(2)}, u32[]{:S(2)}) collective-permute-start(bf16[80,640]{1,0:T(8,128)(2,1)S(1)} %get-tuple-element.40), channel_id=1, source_target_pairs={{0,14},{2,4},{4,10},{6,0},{8,6},{10,12},{12,2},{14,8},{1,15},{3,5}... | collective-permute-start | bytes 307208 | tf_op jit(solution)/shard_map/ppermute | solution.py:348
  48.5 6.2 %collective-permute-start.13 = (bf16[80,640]{1,0:T(8,128)(2,1)S(1)}, bf16[80,640]{1,0:T(8,128)(2,1)S(1)}, u32[]{:S(2)}, u32[]{:S(2)}) collective-permute-start(bf16[80,640]{1,0:T(8,128)(2,1)S(1)} %get-tuple-element.41), channel_id=1, source_target_pairs={{0,10},{2,8},{4,14},{6,12},{8,2},{10,0},{12,6},{14,4},{1,11},{3,9}... | collective-permute-start | bytes 307208 | tf_op jit(solution)/shard_map/ppermute | solution.py:348
  57.7 29.0 %all-to-all-start.1 = ((bf16[16,5,8,640]{3,2,1,0:T(8,128)(2,1)}), bf16[16,5,8,640]{3,2,1,0:T(8,128)(2,1)S(1)}, u32[]{:S(2)}, u32[]{:S(2)}) async-start(bf16[16,5,8,640]{3,2,1,0:T(8,128)(2,1)} %turn.1), calls=%async_computation.1 | async-start | bytes 1638400 | tf_op jit(solution)/shard_map/all_to_all | solution.py:359
  90.5 32.7 %all-to-all-start.2 = ((bf16[32,104,128]{2,1,0:T(8,128)(2,1)}), bf16[32,104,128]{2,1,0:T(8,128)(2,1)S(1)}, u32[]{:S(2)}, u32[]{:S(2)}) async-start(bf16[32,104,128]{2,1,0:T(8,128)(2,1)} %spectral_parts.1), calls=%async_computation.2 | async-start | bytes 1703936 | tf_op jit(solution)/shard_map/all_to_all | solution.py:362

commit v10 on v8

--- a/solution.py
+++ b/solution.py
@@ -191,7 +191,7 @@
         turn_kernel,
         in_specs=[pl.BlockSpec(memory_space=pltpu.SMEM)] + [vmem] * 8,
         out_shape=jax.ShapeDtypeStruct((16, slots // 16, 8, width), jnp.bfloat16),
-        scratch_shapes=[pltpu.VMEM((width // 128, 8 * slots, 128), jnp.float32)],
+        scratch_shapes=[pltpu.VMEM((width // 128, 9 * slots, 128), jnp.float32)],
         compiler_params=params(12),
         cost_estimate=cost(0, 32 * blocks[0].size),
         name="turn",
@@ -244,7 +244,7 @@
                 out_ref[2 * a + lev, pl.ds(k * deg_dev, deg_dev)] = both[
                     a * deg_dev : (a + 1) * deg_dev
                 ].astype(jnp.bfloat16)
-    total[...] = summed(4).T
+    total[pl.ds(0, degs), :] = summed(4).T
     half = deg_dev // 2
     even = total[pl.ds(0, degs // 2, stride=2), :]
     odd = total[pl.ds(1, degs // 2, stride=2), :]
@@ -275,7 +275,7 @@
         scratch_shapes=[
             pltpu.VMEM((steps, 8, lats, degs), jnp.bfloat16),
             pltpu.VMEM((128, 8 * lats), jnp.float32),
-            pltpu.VMEM((degs, 128), jnp.float32),
+            pltpu.VMEM((degs + 8, 128), jnp.float32),
             pltpu.SemaphoreType.DMA((steps, 2)),
         ],
         compiler_params=params(16),
@@ -320,7 +320,7 @@
         out_specs=pl.BlockSpec(memory_space=pltpu.HBM),
         out_shape=jax.ShapeDtypeStruct((40 * 64, 80), jnp.float32),
         scratch_shapes=[
-            pltpu.VMEM((16 * received.shape[1], 128), jnp.float32),
+            pltpu.VMEM((17 * received.shape[1], 128), jnp.float32),
             pltpu.VMEM((40 * 64, 80), jnp.float32),
             pltpu.SemaphoreType.DMA((4,)),
         ],
@@ -358,7 +358,7 @@
 
     first = wave * slot_dev + 8 * lev + 2 * x + zq
     slots = jnp.take(wave_slot, first + 16 * jnp.arange(slot_dev // 16, dtype=jnp.int32))
-    parts = spectral_parts(slots, fourier, basis[:, :2], basis)
+    parts = spectral_parts(slots, fourier, basis[:, :3], basis)
     parts = lax.all_to_all(parts, ("x", "zp", "zq", "lev"), 0, 0, tiled=True)
     return finish(parts).reshape(degs // 16, 2, 32, slot_dev)
 

time: 125 us -> 124 us (level)
  transfers between devices with their start and end apart: 16 -> 16, of which waited for: 10 -> 10; matrix products, arithmetic and copies ran while one was open for 4% -> 5% of each run, Pallas kernels for 7% -> 7%
where the time goes in v10:
time: 124 us
  waiting for transfers between devices  33.4 us (27%)
  blocking collectives  32.5 us (26%)
  starting transfers between devices  32.2 us (26%)
  Pallas kernels  18.1 us (15%)
  local copies, waits for them, and re-layouts  5.07 us (4%)
  other arithmetic  2.39 us (2%)
    all_to_all x1, blocking collectives, local(): parts = lax.all_to_all(parts, ('x', 'zp', 'zq', 'lev'), 0, 0, tiled=True)  32.5 us
    ppermute x14, waiting for transfers between devices, swapped(): lax.ppermute(blocks[k], 'wave', [(w, w ^ TO[w % 2][k]) for w in range(8)])  16.4 us
    all_to_all x1, waiting for transfers between devices, local(): fourier = lax.all_to_all(fourier, ('x', 'zq', 'lev'), 0, 0, tiled=True)  16.2 us
    ppermute x14, starting transfers between devices, swapped(): lax.ppermute(blocks[k], 'wave', [(w, w ^ TO[w % 2][k]) for w in range(8)])  15.1 us
    all_to_all x1, starting transfers between devices, local(): fourier = lax.all_to_all(fourier, ('x', 'zq', 'lev'), 0, 0, tiled=True)  10.3 us
    all_to_all x1, starting transfers between devices, local(): basis = lax.all_to_all(basis, ('x', 'zq'), 0, 0, tiled=True)  6.84 us
    pallas_call x1, Pallas kernels, basis_blocks(): pl.pallas_call(basis_kernel, in_specs=[pl.BlockSpec(memory_space=pltpu.SM...  4.63 us
    pallas_call x1, Pallas kernels, spectral_parts(): pl.pallas_call(spectral_kernel, in_specs=[smem, vmem, vmem, pl.BlockSpec(...  3.17 us
  transfers between devices with their start and end apart: 16, of which 10 were waited for; matrix products, arithmetic and copies ran while one was open for 5% of the time, Pallas kernels for 7%

profile of v10, /device:TPU:2, one launch (start us, length us, event | category | flops | bytes accessed | tf_op | source)
XLA Modules:
  0.0 124.1 jit_solution(5368210382922715238)
XLA Ops:
  0.0 4.6 %basis_blocks.1 = (bf16[8,5,80,640]{3,2,1,0:T(8,128)(2,1)}, f32[8,128]{1,0:T(8,128)}) custom-call(s32[1]{0:T(128)} %bitcast.3.lev_ref, bf16[80,10,8,640]{3,2,1,0:T(8,128)(2,1)} %bitcast.9), custom_call_target="tpu_custom_call" | custom-call | bytes 8192000 | tf_op jit(solution)/shard_map/basis_blocks/pallas_call | solution.py:56
  4.6 0.0 copy-start.7
  4.6 0.0 copy-start.8
  4.7 0.0 copy-start
  4.7 0.0 copy-start.2
  4.7 0.0 copy-start.3
  4.7 0.0 copy-start.4
  4.7 6.8 %all-to-all-start = ((bf16[8,5,80,640]{3,2,1,0:T(8,128)(2,1)}), bf16[8,5,80,640]{3,2,1,0:T(8,128)(2,1)}, u32[]{:S(2)}, u32[]{:S(2)}) async-start(bf16[8,5,80,640]{3,2,1,0:T(8,128)(2,1)} %get-tuple-element.42), calls=%async_computation | async-start | bytes 8192000 | tf_op jit(solution)/shard_map/all_to_all | solution.py:352
  11.6 0.0 copy-start.1
  11.6 1.5 %copy-done.1 = bf16[32,80,320]{2,1,0:T(8,128)(2,1)S(1)} copy-done((bf16[32,80,320]{2,1,0:T(8,128)(2,1)S(1)}, bf16[32,80,320]{2,1,0:T(8,128)(2,1)}, u32[]{:S(2)}) %copy-start.1) | copy-done | bytes 1638424
  13.2 2.4 %gradient.1 = (bf16[2,80,640]{2,1,0:T(8,128)(2,1)S(1)}, bf16[2,80,640]{2,1,0:T(8,128)(2,1)}, bf16[2,80,640]{2,1,0:T(8,128)(2,1)S(1)}, bf16[2,80,640]{2,1,0:T(8,1...) custom-call(s32[8]{0:T(128)S(1)} %get-tuple-element.46.wave_ref, ...), custom_call_target="tpu_custom_call" | custom-call | flops 4915200 | bytes 4915200 | tf_op jit(solution)/shard_map/gradient/pallas_call | solution.py:90
  15.6 1.1 collective-permute-start.1
  16.7 2.2 %collective-permute-start.2 = (bf16[2,80,640]{2,1,0:T(8,128)(2,1)S(1)}, bf16[2,80,640]{2,1,0:T(8,128)(2,1)S(1)}, u32[]{:S(2)}, u32[]{:S(2)}) collective-permute-start(bf16[2,80,640]{2,1,0:T(8,128)(2,1)S(1)} %get-tuple-element.29), channel_id=1, source_target_pairs={{0,12},{2,6},{4,8},{6,2},{8,4},{10,14},{12,0},{14,10},{1,13},{3,7}... | collective-permute-start | bytes 614408 | tf_op jit(solution)/shard_map/ppermute | solution.py:346
  18.9 0.9 collective-permute-start.3
  19.7 0.1 reshape.66
  19.8 0.6 gather_fusion.1
  20.4 0.1 mul.86
  20.5 0.1 broadcast_in_dim.11
  20.5 0.1 add.109
  20.7 1.3 %fusion.4 = (f32[64,1280]{1,0:T(8,128)S(1)}, f32[64,1280]{1,0:T(8,128)S(1)}) fusion(s32[1280]{0:T(1024)S(1)} %add.109, s32[1280]{0:T(1024)S(1)} %mul.86), kind=kLoop, calls=%fused_computation.8 | loop fusion | flops 819200 | bytes 665600 | tf_op jit(solution)/shard_map/sin | solution.py:118
  22.0 0.1 broadcast_add_fusion
  22.1 0.1 add.107
  22.2 3.0 %collective-permute-start.5 = (bf16[2,80,640]{2,1,0:T(8,128)(2,1)S(1)}, bf16[2,80,640]{2,1,0:T(8,128)(2,1)S(1)}, u32[]{:S(2)}, u32[]{:S(2)}) collective-permute-start(bf16[2,80,640]{2,1,0:T(8,128)(2,1)S(1)} %get-tuple-element.32), channel_id=1, source_target_pairs={{0,14},{2,4},{4,10},{6,0},{8,6},{10,12},{12,2},{14,8},{1,15},{3,5}... | collective-permute-start | bytes 614408 | tf_op jit(solution)/shard_map/ppermute | solution.py:346
  25.2 0.7 collective-permute-start.6
  25.9 0.9 sine_multiply_fusion
  26.8 1.7 %wave_table.1.table_ref = bf16[5,2560,256]{2,1,0:T(8,128)(2,1)S(1)} custom-call(f32[40,1280]{1,0:T(8,128)S(1)} %get-tuple-element.52.coarse_cos, f32[40,1280]{1,0:T(8,128)S(1)} %get-tuple-element.51.coarse_sin, f32[64,1280]{1,0:T(8,128)S(1)} %get-tuple-element.50.fine_cos, f32[64,1280]{1,0:T(8,128)S(1)} %get-tuple-element.49.fine_sin), custom_call_target="tpu_custom_call" | custom-call | flops 9830400 | bytes 6553600 | tf_op jit(solution)/shard_map/wave_table/pallas_call | solution.py:126
  28.6 1.4 %collective-permute-done.3.refs_4_ = bf16[2,80,640]{2,1,0:T(8,128)(2,1)S(1)} collective-permute-done((bf16[2,80,640]{2,1,0:T(8,128)(2,1)S(1)}, bf16[2,80,640]{2,1,0:T(8,128)(2,1)S(1)}, u32[]{:S(2)}, u32[]{:S(2)}) %collective-permute-start.3) | collective-permute-done | bytes 204832 | tf_op jit(solution)/shard_map/ppermute | solution.py:346
  30.0 1.7 %collective-permute-done.4.refs_5_ = bf16[2,80,640]{2,1,0:T(8,128)(2,1)S(1)} collective-permute-done((bf16[2,80,640]{2,1,0:T(8,128)(2,1)S(1)}, bf16[2,80,640]{2,1,0:T(8,128)(2,1)S(1)}, u32[]{:S(2)}, u32[]{:S(2)}) %collective-permute-start.4) | collective-permute-done | bytes 204832 | tf_op jit(solution)/shard_map/ppermute | solution.py:346
  31.7 4.6 %collective-permute-done.5.refs_6_ = bf16[2,80,640]{2,1,0:T(8,128)(2,1)S(1)} collective-permute-done((bf16[2,80,640]{2,1,0:T(8,128)(2,1)S(1)}, bf16[2,80,640]{2,1,0:T(8,128)(2,1)S(1)}, u32[]{:S(2)}, u32[]{:S(2)}) %collective-permute-start.5) | collective-permute-done | bytes 204832 | tf_op jit(solution)/shard_map/ppermute | solution.py:346
  36.3 2.4 %collective-permute-done.6.refs_7_ = bf16[2,80,640]{2,1,0:T(8,128)(2,1)S(1)} collective-permute-done((bf16[2,80,640]{2,1,0:T(8,128)(2,1)S(1)}, bf16[2,80,640]{2,1,0:T(8,128)(2,1)S(1)}, u32[]{:S(2)}, u32[]{:S(2)}) %collective-permute-start.6) | collective-permute-done | bytes 204832 | tf_op jit(solution)/shard_map/ppermute | solution.py:346
  38.7 2.6 %fourier_rows.1 = (bf16[80,640]{1,0:T(8,128)(2,1)S(1)}, bf16[80,640]{1,0:T(8,128)(2,1)S(1)}, bf16[80,640]{1,0:T(8,128)(2,1)S(1)}, bf16[80,640]{1,0:T(8,128)(2,1)...) custom-call(bf16[5,2560,256]{2,1,0:T(8,128)(2,1)S(1)} %wave_table.1., ...), custom_call_target="tpu_custom_call" | custom-call | flops 2097152000 | bytes 6553600 | tf_op jit(solution)/shard_map/fourier_rows/pallas_call | solution.py:161
  41.3 0.2 collective-permute-start.7
  41.5 1.4 %collective-permute-start.9 = (bf16[80,640]{1,0:T(8,128)(2,1)S(1)}, bf16[80,640]{1,0:T(8,128)(2,1)S(1)}, u32[]{:S(2)}, u32[]{:S(2)}) collective-permute-start(bf16[80,640]{1,0:T(8,128)(2,1)S(1)} %get-tuple-element.37), channel_id=1, source_target_pairs={{0,12},{2,6},{4,8},{6,2},{8,4},{10,14},{12,0},{14,10},{1,13},{3,7}... | collective-permute-start | bytes 307208 | tf_op jit(solution)/shard_map/ppermute | solution.py:346
  42.9 2.7 %collective-permute-start.10 = (bf16[80,640]{1,0:T(8,128)(2,1)S(1)}, bf16[80,640]{1,0:T(8,128)(2,1)S(1)}, u32[]{:S(2)}, u32[]{:S(2)}) collective-permute-start(bf16[80,640]{1,0:T(8,128)(2,1)S(1)} %get-tuple-element.38), channel_id=1, source_target_pairs={{0,8},{2,10},{4,12},{6,14},{8,0},{10,2},{12,4},{14,6},{1,9},{3,11}... | collective-permute-start | bytes 307208 | tf_op jit(solution)/shard_map/ppermute | solution.py:346
  45.6 3.0 %collective-permute-start.12 = (bf16[80,640]{1,0:T(8,128)(2,1)S(1)}, bf16[80,640]{1,0:T(8,128)(2,1)S(1)}, u32[]{:S(2)}, u32[]{:S(2)}) collective-permute-start(bf16[80,640]{1,0:T(8,128)(2,1)S(1)} %get-tuple-element.40), channel_id=1, source_target_pairs={{0,14},{2,4},{4,10},{6,0},{8,6},{10,12},{12,2},{14,8},{1,15},{3,5}... | collective-permute-start | bytes 307208 | tf_op jit(solution)/shard_map/ppermute | solution.py:346
  48.6 1.6 %collective-permute-done.10.refs_4_ = bf16[80,640]{1,0:T(8,128)(2,1)S(1)} collective-permute-done((bf16[80,640]{1,0:T(8,128)(2,1)S(1)}, bf16[80,640]{1,0:T(8,128)(2,1)S(1)}, u32[]{:S(2)}, u32[]{:S(2)}) %collective-permute-start.10) | collective-permute-done | bytes 102432 | tf_op jit(solution)/shard_map/ppermute | solution.py:346
  50.2 1.2 collective-permute-done.11.refs_5_
  51.4 0.2 collective-permute-done.12.refs_6_
  51.6 3.1 %collective-permute-done.13.refs_7_ = bf16[80,640]{1,0:T(8,128)(2,1)S(1)} collective-permute-done((bf16[80,640]{1,0:T(8,128)(2,1)S(1)}, bf16[80,640]{1,0:T(8,128)(2,1)S(1)}, u32[]{:S(2)}, u32[]{:S(2)}) %collective-permute-start.13) | collective-permute-done | bytes 102432 | tf_op jit(solution)/shard_map/ppermute | solution.py:346
  54.8 2.1 %turn.1 = bf16[16,5,8,640]{3,2,1,0:T(8,128)(2,1)} custom-call(s32[8]{0:T(128)S(1)} %get-tuple-element.48.wave_ref, bf16[80,640]{1,0:T(8,128)(2,1)S(1)} %get-tuple-element.34.refs_0_, bf16[80,640]{1,0:T(8,128)(2,1)S(1)} %collective-permute-done.7.refs_1_, bf16[80,640]{1,0:T(8,128)(2,1)S(1)} %collective-permute-done.8.refs_2_, ...), custom_call_target="tpu_custom_call" | custom-call | bytes 1638400 | tf_op jit(solution)/shard_map/turn/pallas_call | solution.py:190
  56.9 0.9 all-to-all-done.basis_any
  57.8 10.3 %all-to-all-start.1 = ((bf16[16,5,8,640]{3,2,1,0:T(8,128)(2,1)}), bf16[16,5,8,640]{3,2,1,0:T(8,128)(2,1)S(1)}, u32[]{:S(2)}, u32[]{:S(2)}) async-start(bf16[16,5,8,640]{3,2,1,0:T(8,128)(2,1)} %turn.1), calls=%async_computation.1 | async-start | bytes 1638400 | tf_op jit(solution)/shard_map/all_to_all | solution.py:357
  68.0 0.6 gather_fusion
  68.7 1.9 %slice.3.head_ref = bf16[8,3,80,640]{3,2,1,0:T(8,128)(2,1)S(1)} slice(bf16[8,5,80,640]{3,2,1,0:T(8,128)(2,1)} %all-to-all-done.basis_any), slice={[0:8], [0:3], [0:80], [0:640]} | slice | bytes 4915200 | tf_op jit(solution)/shard_map/slice | solution.py:361
  70.6 16.2 %all-to-all-done.1.four_ref = bf16[16,5,8,640]{3,2,1,0:T(8,128)(2,1)S(1)} async-done(((bf16[16,5,8,640]{3,2,1,0:T(8,128)(2,1)}), bf16[16,5,8,640]{3,2,1,0:T(8,128)(2,1)S(1)}, u32[]{:S(2)}, u32[]{:S(2)}) %all-to-all-start.1) | async-done | bytes 819232 | tf_op jit(solution)/shard_map/all_to_all | solution.py:357
  86.8 3.2 %spectral_parts.1 = bf16[32,104,128]{2,1,0:T(8,128)(2,1)S(1)} custom-call(s32[5]{0:T(128)S(1)} %and_select_fusion.slot_ref, bf16[16,5,8,640]{3,2,1,0:T(8,128)(2,1)S(1)} %all-to-all-done.1.four_ref, bf16[8,3,80,640]{3,2,1,0:T(8,128)(2,1)S(1)} %slice.3.head_ref, bf16[8,5,80,640]{3,2,1,0:T(8,128)(2,1)} %all-to-all-done.basis_any), custom_call_target="tpu_custom_call" | custom-call | flops 524288000 | bytes 4915200 | tf_op jit(solution)/shard_map/spectral_parts/pallas_call | solution.py:271
  90.0 32.5 %all_to_all.15.in_ref = bf16[32,104,128]{2,1,0:T(8,128)(2,1)S(1)} all-to-all(bf16[32,104,128]{2,1,0:T(8,128)(2,1)S(1)} %spectral_parts.1), channel_id=1, replica_groups=mesh['x'=4,'zp'=2,'zq'=2,'wave'=8,'lev'=2] {'x','zp','zq','lev'}, dimensions={0} | all-to-all | bytes 1703936 | tf_op jit(solution)/shard_map/all_to_all | solution.py:362
  122.4 1.5 %finish.1 = f32[2560,80]{1,0:T(8,128)} custom-call(bf16[32,104,128]{2,1,0:T(8,128)(2,1)S(1)} %all_to_all.15.in_ref), custom_call_target="tpu_custom_call" | custom-call | flops 425984 | bytes 2162688 | tf_op jit(solution)/shard_map/finish/pallas_call | solution.py:317
  (30 shorter events, 0.1 us)
Async XLA Ops:
  4.6 6.9 %copy-start.7 = (s32[8]{0:T(128)S(1)}, s32[8]{0:T(128)}, u32[]{:S(2)}) copy-start(s32[8]{0:T(128)} %constant.94.clone) | copy-start | bytes 100
  4.6 6.9 %copy-start.8 = (s32[8]{0:T(128)S(1)}, s32[8]{0:T(128)}, u32[]{:S(2)}) copy-start(s32[8]{0:T(128)} %constant.95.clone) | copy-start | bytes 100
  4.7 6.9 %copy-start = (bf16[32,80,320]{2,1,0:T(8,128)(2,1)S(1)}, bf16[32,80,320]{2,1,0:T(8,128)(2,1)}, u32[]{:S(2)}) copy-start(bf16[32,80,320]{2,1,0:T(8,128)(2,1)} %param.10) | copy-start | bytes 4915204
  4.7 6.9 %copy-start.2 = (f32[8,128]{1,0:T(8,128)S(1)}, f32[8,128]{1,0:T(8,128)}, u32[]{:S(2)}) copy-start(f32[8,128]{1,0:T(8,128)} %get-tuple-element.25._) | copy-start | bytes 12292
  4.7 6.9 %copy-start.3 = (f32[32]{0:T(128)S(1)}, f32[32]{0:T(128)}, u32[]{:S(2)}) copy-start(f32[32]{0:T(128)} %rate_ref.1) | copy-start | bytes 388
  4.7 15.0 %copy-start.4 = (s32[640]{0:T(1024)S(1)}, s32[640]{0:T(1024)}, u32[]{:S(2)}) copy-start(s32[640]{0:T(1024)} %param.14) | copy-start | bytes 7684
  4.7 53.1 %all-to-all-start = ((bf16[8,5,80,640]{3,2,1,0:T(8,128)(2,1)}), bf16[8,5,80,640]{3,2,1,0:T(8,128)(2,1)}, u32[]{:S(2)}, u32[]{:S(2)}) async-start(bf16[8,5,80,640]{3,2,1,0:T(8,128)(2,1)} %get-tuple-element.42), calls=%async_computation | async-start | bytes 8192000 | tf_op jit(solution)/shard_map/all_to_all | solution.py:352
  11.6 9.1 %copy-start.5 = (s32[8]{0:T(128)S(1)}, s32[8]{0:T(128)}, u32[]{:S(2)}) copy-start(s32[8]{0:T(128)} %constant.96.clone) | copy-start | bytes 100
  11.6 9.1 %copy-start.6 = (s32[8]{0:T(128)S(1)}, s32[8]{0:T(128)}, u32[]{:S(2)}) copy-start(s32[8]{0:T(128)} %constant.97.clone) | copy-start | bytes 100
  11.6 1.5 %copy-start.1 = (bf16[32,80,320]{2,1,0:T(8,128)(2,1)S(1)}, bf16[32,80,320]{2,1,0:T(8,128)(2,1)}, u32[]{:S(2)}) copy-start(bf16[32,80,320]{2,1,0:T(8,128)(2,1)} %param.11) | copy-start | bytes 4915204
  15.6 6.6 %collective-permute-start = (bf16[2,80,640]{2,1,0:T(8,128)(2,1)}, bf16[2,80,640]{2,1,0:T(8,128)(2,1)S(1)}, u32[]{:S(2)}, u32[]{:S(2)}) collective-permute-start(bf16[2,80,640]{2,1,0:T(8,128)(2,1)} %get-tuple-element.27), channel_id=1, source_target_pairs={{0,2},{2,0},{4,6},{6,4},{8,10},{10,8},{12,14},{14,12},{1,3},{3,1},... | collective-permute-start | bytes 614408 | tf_op jit(solution)/shard_map/ppermute | solution.py:346
  15.6 9.6 %collective-permute-start.1 = (bf16[2,80,640]{2,1,0:T(8,128)(2,1)S(1)}, bf16[2,80,640]{2,1,0:T(8,128)(2,1)S(1)}, u32[]{:S(2)}, u32[]{:S(2)}) collective-permute-start(bf16[2,80,640]{2,1,0:T(8,128)(2,1)S(1)} %get-tuple-element.28), channel_id=1, source_target_pairs={{0,4},{2,14},{4,0},{6,10},{8,12},{10,6},{12,8},{14,2},{1,5},{3,15}... | collective-permute-start | bytes 614408 | tf_op jit(solution)/shard_map/ppermute | solution.py:346
  16.7 11.9 %collective-permute-start.2 = (bf16[2,80,640]{2,1,0:T(8,128)(2,1)S(1)}, bf16[2,80,640]{2,1,0:T(8,128)(2,1)S(1)}, u32[]{:S(2)}, u32[]{:S(2)}) collective-permute-start(bf16[2,80,640]{2,1,0:T(8,128)(2,1)S(1)} %get-tuple-element.29), channel_id=1, source_target_pairs={{0,12},{2,6},{4,8},{6,2},{8,4},{10,14},{12,0},{14,10},{1,13},{3,7}... | collective-permute-start | bytes 614408 | tf_op jit(solution)/shard_map/ppermute | solution.py:346
  18.9 11.1 %collective-permute-start.3 = (bf16[2,80,640]{2,1,0:T(8,128)(2,1)S(1)}, bf16[2,80,640]{2,1,0:T(8,128)(2,1)S(1)}, u32[]{:S(2)}, u32[]{:S(2)}) collective-permute-start(bf16[2,80,640]{2,1,0:T(8,128)(2,1)S(1)} %get-tuple-element.30), channel_id=1, source_target_pairs={{0,8},{2,10},{4,12},{6,14},{8,0},{10,2},{12,4},{14,6},{1,9},{3,11}... | collective-permute-start | bytes 614408 | tf_op jit(solution)/shard_map/ppermute | solution.py:346
  19.7 12.0 %collective-permute-start.4 = (bf16[2,80,640]{2,1,0:T(8,128)(2,1)S(1)}, bf16[2,80,640]{2,1,0:T(8,128)(2,1)S(1)}, u32[]{:S(2)}, u32[]{:S(2)}) collective-permute-start(bf16[2,80,640]{2,1,0:T(8,128)(2,1)S(1)} %get-tuple-element.31), channel_id=1, source_target_pairs={{0,6},{2,12},{4,2},{6,8},{8,14},{10,4},{12,10},{14,0},{1,7},{3,13}... | collective-permute-start | bytes 614408 | tf_op jit(solution)/shard_map/ppermute | solution.py:346
  22.2 14.2 %collective-permute-start.5 = (bf16[2,80,640]{2,1,0:T(8,128)(2,1)S(1)}, bf16[2,80,640]{2,1,0:T(8,128)(2,1)S(1)}, u32[]{:S(2)}, u32[]{:S(2)}) collective-permute-start(bf16[2,80,640]{2,1,0:T(8,128)(2,1)S(1)} %get-tuple-element.32), channel_id=1, source_target_pairs={{0,14},{2,4},{4,10},{6,0},{8,6},{10,12},{12,2},{14,8},{1,15},{3,5}... | collective-permute-start | bytes 614408 | tf_op jit(solution)/shard_map/ppermute | solution.py:346
  25.2 13.5 %collective-permute-start.6 = (bf16[2,80,640]{2,1,0:T(8,128)(2,1)S(1)}, bf16[2,80,640]{2,1,0:T(8,128)(2,1)S(1)}, u32[]{:S(2)}, u32[]{:S(2)}) collective-permute-start(bf16[2,80,640]{2,1,0:T(8,128)(2,1)S(1)} %get-tuple-element.33), channel_id=1, source_target_pairs={{0,10},{2,8},{4,14},{6,12},{8,2},{10,0},{12,6},{14,4},{1,11},{3,9}... | collective-permute-start | bytes 614408 | tf_op jit(solution)/shard_map/ppermute | solution.py:346
  41.3 4.3 %collective-permute-start.7 = (bf16[80,640]{1,0:T(8,128)(2,1)S(1)}, bf16[80,640]{1,0:T(8,128)(2,1)S(1)}, u32[]{:S(2)}, u32[]{:S(2)}) collective-permute-start(bf16[80,640]{1,0:T(8,128)(2,1)S(1)} %get-tuple-element.35), channel_id=1, source_target_pairs={{0,2},{2,0},{4,6},{6,4},{8,10},{10,8},{12,14},{14,12},{1,3},{3,1},... | collective-permute-start | bytes 307208 | tf_op jit(solution)/shard_map/ppermute | solution.py:346
  41.5 7.1 %collective-permute-start.8 = (bf16[80,640]{1,0:T(8,128)(2,1)S(1)}, bf16[80,640]{1,0:T(8,128)(2,1)S(1)}, u32[]{:S(2)}, u32[]{:S(2)}) collective-permute-start(bf16[80,640]{1,0:T(8,128)(2,1)S(1)} %get-tuple-element.36), channel_id=1, source_target_pairs={{0,4},{2,14},{4,0},{6,10},{8,12},{10,6},{12,8},{14,2},{1,5},{3,15}... | collective-permute-start | bytes 307208 | tf_op jit(solution)/shard_map/ppermute | solution.py:346
  41.5 7.1 %collective-permute-start.9 = (bf16[80,640]{1,0:T(8,128)(2,1)S(1)}, bf16[80,640]{1,0:T(8,128)(2,1)S(1)}, u32[]{:S(2)}, u32[]{:S(2)}) collective-permute-start(bf16[80,640]{1,0:T(8,128)(2,1)S(1)} %get-tuple-element.37), channel_id=1, source_target_pairs={{0,12},{2,6},{4,8},{6,2},{8,4},{10,14},{12,0},{14,10},{1,13},{3,7}... | collective-permute-start | bytes 307208 | tf_op jit(solution)/shard_map/ppermute | solution.py:346
  42.9 7.3 %collective-permute-start.10 = (bf16[80,640]{1,0:T(8,128)(2,1)S(1)}, bf16[80,640]{1,0:T(8,128)(2,1)S(1)}, u32[]{:S(2)}, u32[]{:S(2)}) collective-permute-start(bf16[80,640]{1,0:T(8,128)(2,1)S(1)} %get-tuple-element.38), channel_id=1, source_target_pairs={{0,8},{2,10},{4,12},{6,14},{8,0},{10,2},{12,4},{14,6},{1,9},{3,11}... | collective-permute-start | bytes 307208 | tf_op jit(solution)/shard_map/ppermute | solution.py:346
  45.6 5.8 %collective-permute-start.11 = (bf16[80,640]{1,0:T(8,128)(2,1)S(1)}, bf16[80,640]{1,0:T(8,128)(2,1)S(1)}, u32[]{:S(2)}, u32[]{:S(2)}) collective-permute-start(bf16[80,640]{1,0:T(8,128)(2,1)S(1)} %get-tuple-element.39), channel_id=1, source_target_pairs={{0,6},{2,12},{4,2},{6,8},{8,14},{10,4},{12,10},{14,0},{1,7},{3,13}... | collective-permute-start | bytes 307208 | tf_op jit(solution)/shard_map/ppermute | solution.py:346
  45.6 6.0 %collective-permute-start.12 = (bf16[80,640]{1,0:T(8,128)(2,1)S(1)}, bf16[80,640]{1,0:T(8,128)(2,1)S(1)}, u32[]{:S(2)}, u32[]{:S(2)}) collective-permute-start(bf16[80,640]{1,0:T(8,128)(2,1)S(1)} %get-tuple-element.40), channel_id=1, source_target_pairs={{0,14},{2,4},{4,10},{6,0},{8,6},{10,12},{12,2},{14,8},{1,15},{3,5}... | collective-permute-start | bytes 307208 | tf_op jit(solution)/shard_map/ppermute | solution.py:346
  48.6 6.2 %collective-permute-start.13 = (bf16[80,640]{1,0:T(8,128)(2,1)S(1)}, bf16[80,640]{1,0:T(8,128)(2,1)S(1)}, u32[]{:S(2)}, u32[]{:S(2)}) collective-permute-start(bf16[80,640]{1,0:T(8,128)(2,1)S(1)} %get-tuple-element.41), channel_id=1, source_target_pairs={{0,10},{2,8},{4,14},{6,12},{8,2},{10,0},{12,6},{14,4},{1,11},{3,9}... | collective-permute-start | bytes 307208 | tf_op jit(solution)/shard_map/ppermute | solution.py:346
  57.8 29.0 %all-to-all-start.1 = ((bf16[16,5,8,640]{3,2,1,0:T(8,128)(2,1)}), bf16[16,5,8,640]{3,2,1,0:T(8,128)(2,1)S(1)}, u32[]{:S(2)}, u32[]{:S(2)}) async-start(bf16[16,5,8,640]{3,2,1,0:T(8,128)(2,1)} %turn.1), calls=%async_computation.1 | async-start | bytes 1638400 | tf_op jit(solution)/shard_map/all_to_all | solution.py:357

commit v11 on v10

--- a/solution.py
+++ b/solution.py
@@ -67,7 +67,7 @@
             pltpu.SemaphoreType.DMA((steps,)),
             pltpu.SemaphoreType.DMA((steps,)),
         ],
-        compiler_params=params(60),
+        compiler_params=params(63),
         cost_estimate=cost(0, 2 * lats * slots * degs),
         name="basis_blocks",
     )(lev, basis.reshape(lats, slots // 8, 8, degs))
@@ -351,7 +351,8 @@
     grads = gradient(to, tend_rate, out_grad, grid_state, token)
     basis = lax.all_to_all(basis, ("x", "zq"), 0, 0, tiled=True)
     grads = swapped(grads)
-    table = wave_table(wave_slot.reshape(8, slot_dev)[to], source, lons, 64)
+    slots, grads[1] = lax.optimization_barrier((wave_slot.reshape(8, slot_dev)[to], grads[1]))
+    table = wave_table(slots, source, lons, 64)
     blocks = swapped(fourier_rows(table, grads))
     fourier, basis = lax.optimization_barrier((turn(source, blocks), basis))
     fourier = lax.all_to_all(fourier, ("x", "zq", "lev"), 0, 0, tiled=True)

time: 124 us -> 124 us (level)
  no operation moved by 1% of the time
where the time goes in v11:
time: 124 us
  waiting for transfers between devices  33.1 us (27%)
  starting transfers between devices  32.5 us (26%)
  blocking collectives  32.5 us (26%)
  Pallas kernels  18.1 us (15%)
  local copies, waits for them, and re-layouts  5.08 us (4%)
  other arithmetic  2.39 us (2%)
    all_to_all x1, blocking collectives, local(): parts = lax.all_to_all(parts, ('x', 'zp', 'zq', 'lev'), 0, 0, tiled=True)  32.5 us
    all_to_all x1, waiting for transfers between devices, local(): fourier = lax.all_to_all(fourier, ('x', 'zq', 'lev'), 0, 0, tiled=True)  16.2 us
    ppermute x14, waiting for transfers between devices, swapped(): lax.ppermute(blocks[k], 'wave', [(w, w ^ TO[w % 2][k]) for w in range(8)])  16.1 us
    ppermute x14, starting transfers between devices, swapped(): lax.ppermute(blocks[k], 'wave', [(w, w ^ TO[w % 2][k]) for w in range(8)])  15.4 us
    all_to_all x1, starting transfers between devices, local(): fourier = lax.all_to_all(fourier, ('x', 'zq', 'lev'), 0, 0, tiled=True)  10.3 us
    all_to_all x1, starting transfers between devices, local(): basis = lax.all_to_all(basis, ('x', 'zq'), 0, 0, tiled=True)  6.84 us
    pallas_call x1, Pallas kernels, basis_blocks(): pl.pallas_call(basis_kernel, in_specs=[pl.BlockSpec(memory_space=pltpu.SM...  4.63 us
    pallas_call x1, Pallas kernels, spectral_parts(): pl.pallas_call(spectral_kernel, in_specs=[smem, vmem, vmem, pl.BlockSpec(...  3.18 us
  transfers between devices with their start and end apart: 16, of which 10 were waited for; matrix products, arithmetic and copies ran while one was open for 5% of the time, Pallas kernels for 7%

profile of v11, /device:TPU:2, one launch (start us, length us, event | category | flops | bytes accessed | tf_op | source)
XLA Modules:
  0.0 124.1 jit_solution(6036492863230780367)
XLA Ops:
  0.0 4.6 %basis_blocks.1 = (bf16[8,5,80,640]{3,2,1,0:T(8,128)(2,1)}, f32[8,128]{1,0:T(8,128)}) custom-call(s32[1]{0:T(128)} %bitcast.3.lev_ref, bf16[80,10,8,640]{3,2,1,0:T(8,128)(2,1)} %bitcast.9), custom_call_target="tpu_custom_call" | custom-call | bytes 8192000 | tf_op jit(solution)/shard_map/basis_blocks/pallas_call | solution.py:56
  4.6 0.0 copy-start.7
  4.6 0.0 copy-start.8
  4.7 0.0 copy-start
  4.7 0.0 copy-start.5
  4.7 0.0 copy-start.6
  4.7 0.0 copy-start.4
  4.7 6.8 %all-to-all-start = ((bf16[8,5,80,640]{3,2,1,0:T(8,128)(2,1)}), bf16[8,5,80,640]{3,2,1,0:T(8,128)(2,1)}, u32[]{:S(2)}, u32[]{:S(2)}) async-start(bf16[8,5,80,640]{3,2,1,0:T(8,128)(2,1)} %get-tuple-element.46), calls=%async_computation | async-start | bytes 8192000 | tf_op jit(solution)/shard_map/all_to_all | solution.py:352
  11.6 0.0 copy-start.1
  11.6 1.5 %copy-done.1 = bf16[32,80,320]{2,1,0:T(8,128)(2,1)S(1)} copy-done((bf16[32,80,320]{2,1,0:T(8,128)(2,1)S(1)}, bf16[32,80,320]{2,1,0:T(8,128)(2,1)}, u32[]{:S(2)}) %copy-start.1) | copy-done | bytes 1638424
  13.2 2.4 %gradient.1 = (bf16[2,80,640]{2,1,0:T(8,128)(2,1)S(1)}, bf16[2,80,640]{2,1,0:T(8,128)(2,1)}, bf16[2,80,640]{2,1,0:T(8,128)(2,1)S(1)}, bf16[2,80,640]{2,1,0:T(8,1...) custom-call(s32[8]{0:T(128)S(1)} %get-tuple-element.50.wave_ref, ...), custom_call_target="tpu_custom_call" | custom-call | flops 4915200 | bytes 4915200 | tf_op jit(solution)/shard_map/gradient/pallas_call | solution.py:90
  15.6 1.1 collective-permute-start.1
  16.7 2.2 %collective-permute-start.2 = (bf16[2,80,640]{2,1,0:T(8,128)(2,1)S(1)}, bf16[2,80,640]{2,1,0:T(8,128)(2,1)S(1)}, u32[]{:S(2)}, u32[]{:S(2)}) collective-permute-start(bf16[2,80,640]{2,1,0:T(8,128)(2,1)S(1)} %get-tuple-element.33), channel_id=1, source_target_pairs={{0,12},{2,6},{4,8},{6,2},{8,4},{10,14},{12,0},{14,10},{1,13},{3,7}... | collective-permute-start | bytes 614408 | tf_op jit(solution)/shard_map/ppermute | solution.py:346
  18.9 0.9 collective-permute-start.3
  19.8 0.1 broadcast_add_fusion
  19.8 0.1 add.107
  19.9 0.1 reshape.66
  20.0 0.1 broadcast_in_dim.12
  20.1 0.1 add.109
  20.2 0.6 gather_fusion.1
  20.7 3.0 %collective-permute-start.5 = (bf16[2,80,640]{2,1,0:T(8,128)(2,1)S(1)}, bf16[2,80,640]{2,1,0:T(8,128)(2,1)S(1)}, u32[]{:S(2)}, u32[]{:S(2)}) collective-permute-start(bf16[2,80,640]{2,1,0:T(8,128)(2,1)S(1)} %get-tuple-element.36), channel_id=1, source_target_pairs={{0,14},{2,4},{4,10},{6,0},{8,6},{10,12},{12,2},{14,8},{1,15},{3,5}... | collective-permute-start | bytes 614408 | tf_op jit(solution)/shard_map/ppermute | solution.py:346
  23.8 0.1 mul.86
  23.8 1.3 %fusion.4 = (f32[64,1280]{1,0:T(8,128)S(1)}, f32[64,1280]{1,0:T(8,128)S(1)}) fusion(s32[1280]{0:T(1024)S(1)} %add.109, s32[1280]{0:T(1024)S(1)} %mul.86), kind=kLoop, calls=%fused_computation.8 | loop fusion | flops 819200 | bytes 665600 | tf_op jit(solution)/shard_map/sin | solution.py:118
  25.2 1.0 collective-permute-start.6
  26.2 0.9 sine_multiply_fusion
  27.1 1.7 %wave_table.1.table_ref = bf16[5,2560,256]{2,1,0:T(8,128)(2,1)S(1)} custom-call(f32[40,1280]{1,0:T(8,128)S(1)} %get-tuple-element.56.coarse_cos, f32[40,1280]{1,0:T(8,128)S(1)} %get-tuple-element.55.coarse_sin, f32[64,1280]{1,0:T(8,128)S(1)} %get-tuple-element.54.fine_cos, f32[64,1280]{1,0:T(8,128)S(1)} %get-tuple-element.53.fine_sin), custom_call_target="tpu_custom_call" | custom-call | flops 9830400 | bytes 6553600 | tf_op jit(solution)/shard_map/wave_table/pallas_call | solution.py:126
  28.9 1.2 collective-permute-done.3.refs_4_
  30.0 1.7 %collective-permute-done.4.refs_5_ = bf16[2,80,640]{2,1,0:T(8,128)(2,1)S(1)} collective-permute-done((bf16[2,80,640]{2,1,0:T(8,128)(2,1)S(1)}, bf16[2,80,640]{2,1,0:T(8,128)(2,1)S(1)}, u32[]{:S(2)}, u32[]{:S(2)}) %collective-permute-start.4) | collective-permute-done | bytes 204832 | tf_op jit(solution)/shard_map/ppermute | solution.py:346
  31.8 4.6 %collective-permute-done.5.refs_6_ = bf16[2,80,640]{2,1,0:T(8,128)(2,1)S(1)} collective-permute-done((bf16[2,80,640]{2,1,0:T(8,128)(2,1)S(1)}, bf16[2,80,640]{2,1,0:T(8,128)(2,1)S(1)}, u32[]{:S(2)}, u32[]{:S(2)}) %collective-permute-start.5) | collective-permute-done | bytes 204832 | tf_op jit(solution)/shard_map/ppermute | solution.py:346
  36.3 2.4 %collective-permute-done.6.refs_7_ = bf16[2,80,640]{2,1,0:T(8,128)(2,1)S(1)} collective-permute-done((bf16[2,80,640]{2,1,0:T(8,128)(2,1)S(1)}, bf16[2,80,640]{2,1,0:T(8,128)(2,1)S(1)}, u32[]{:S(2)}, u32[]{:S(2)}) %collective-permute-start.6) | collective-permute-done | bytes 204832 | tf_op jit(solution)/shard_map/ppermute | solution.py:346
  38.7 2.6 %fourier_rows.1 = (bf16[80,640]{1,0:T(8,128)(2,1)S(1)}, bf16[80,640]{1,0:T(8,128)(2,1)S(1)}, bf16[80,640]{1,0:T(8,128)(2,1)S(1)}, bf16[80,640]{1,0:T(8,128)(2,1)...) custom-call(bf16[5,2560,256]{2,1,0:T(8,128)(2,1)S(1)} %wave_table.1., ...), custom_call_target="tpu_custom_call" | custom-call | flops 2097152000 | bytes 6553600 | tf_op jit(solution)/shard_map/fourier_rows/pallas_call | solution.py:161
  41.3 0.2 collective-permute-start.7
  41.5 1.4 %collective-permute-start.9 = (bf16[80,640]{1,0:T(8,128)(2,1)S(1)}, bf16[80,640]{1,0:T(8,128)(2,1)S(1)}, u32[]{:S(2)}, u32[]{:S(2)}) collective-permute-start(bf16[80,640]{1,0:T(8,128)(2,1)S(1)} %get-tuple-element.41), channel_id=1, source_target_pairs={{0,12},{2,6},{4,8},{6,2},{8,4},{10,14},{12,0},{14,10},{1,13},{3,7}... | collective-permute-start | bytes 307208 | tf_op jit(solution)/shard_map/ppermute | solution.py:346
  42.9 2.7 %collective-permute-start.10 = (bf16[80,640]{1,0:T(8,128)(2,1)S(1)}, bf16[80,640]{1,0:T(8,128)(2,1)S(1)}, u32[]{:S(2)}, u32[]{:S(2)}) collective-permute-start(bf16[80,640]{1,0:T(8,128)(2,1)S(1)} %get-tuple-element.42), channel_id=1, source_target_pairs={{0,8},{2,10},{4,12},{6,14},{8,0},{10,2},{12,4},{14,6},{1,9},{3,11}... | collective-permute-start | bytes 307208 | tf_op jit(solution)/shard_map/ppermute | solution.py:346
  45.6 3.0 %collective-permute-start.12 = (bf16[80,640]{1,0:T(8,128)(2,1)S(1)}, bf16[80,640]{1,0:T(8,128)(2,1)S(1)}, u32[]{:S(2)}, u32[]{:S(2)}) collective-permute-start(bf16[80,640]{1,0:T(8,128)(2,1)S(1)} %get-tuple-element.44), channel_id=1, source_target_pairs={{0,14},{2,4},{4,10},{6,0},{8,6},{10,12},{12,2},{14,8},{1,15},{3,5}... | collective-permute-start | bytes 307208 | tf_op jit(solution)/shard_map/ppermute | solution.py:346
  48.6 1.6 %collective-permute-done.10.refs_4_ = bf16[80,640]{1,0:T(8,128)(2,1)S(1)} collective-permute-done((bf16[80,640]{1,0:T(8,128)(2,1)S(1)}, bf16[80,640]{1,0:T(8,128)(2,1)S(1)}, u32[]{:S(2)}, u32[]{:S(2)}) %collective-permute-start.10) | collective-permute-done | bytes 102432 | tf_op jit(solution)/shard_map/ppermute | solution.py:346
  50.2 1.2 collective-permute-done.11.refs_5_
  51.4 0.2 collective-permute-done.12.refs_6_
  51.7 3.2 %collective-permute-done.13.refs_7_ = bf16[80,640]{1,0:T(8,128)(2,1)S(1)} collective-permute-done((bf16[80,640]{1,0:T(8,128)(2,1)S(1)}, bf16[80,640]{1,0:T(8,128)(2,1)S(1)}, u32[]{:S(2)}, u32[]{:S(2)}) %collective-permute-start.13) | collective-permute-done | bytes 102432 | tf_op jit(solution)/shard_map/ppermute | solution.py:346
  54.8 2.1 %turn.1 = bf16[16,5,8,640]{3,2,1,0:T(8,128)(2,1)} custom-call(s32[8]{0:T(128)S(1)} %get-tuple-element.52.wave_ref, bf16[80,640]{1,0:T(8,128)(2,1)S(1)} %get-tuple-element.38.refs_0_, bf16[80,640]{1,0:T(8,128)(2,1)S(1)} %collective-permute-done.7.refs_1_, bf16[80,640]{1,0:T(8,128)(2,1)S(1)} %collective-permute-done.8.refs_2_, ...), custom_call_target="tpu_custom_call" | custom-call | bytes 1638400 | tf_op jit(solution)/shard_map/turn/pallas_call | solution.py:190
  56.9 0.9 all-to-all-done.basis_any
  57.8 10.3 %all-to-all-start.1 = ((bf16[16,5,8,640]{3,2,1,0:T(8,128)(2,1)}), bf16[16,5,8,640]{3,2,1,0:T(8,128)(2,1)S(1)}, u32[]{:S(2)}, u32[]{:S(2)}) async-start(bf16[16,5,8,640]{3,2,1,0:T(8,128)(2,1)} %turn.1), calls=%async_computation.1 | async-start | bytes 1638400 | tf_op jit(solution)/shard_map/all_to_all | solution.py:358
  68.1 0.6 gather_fusion
  68.7 1.9 %slice.3.head_ref = bf16[8,3,80,640]{3,2,1,0:T(8,128)(2,1)S(1)} slice(bf16[8,5,80,640]{3,2,1,0:T(8,128)(2,1)} %all-to-all-done.basis_any), slice={[0:8], [0:3], [0:80], [0:640]} | slice | bytes 4915200 | tf_op jit(solution)/shard_map/slice | solution.py:362
  70.6 16.2 %all-to-all-done.1.four_ref = bf16[16,5,8,640]{3,2,1,0:T(8,128)(2,1)S(1)} async-done(((bf16[16,5,8,640]{3,2,1,0:T(8,128)(2,1)}), bf16[16,5,8,640]{3,2,1,0:T(8,128)(2,1)S(1)}, u32[]{:S(2)}, u32[]{:S(2)}) %all-to-all-start.1) | async-done | bytes 819232 | tf_op jit(solution)/shard_map/all_to_all | solution.py:358
  86.8 3.2 %spectral_parts.1 = bf16[32,104,128]{2,1,0:T(8,128)(2,1)S(1)} custom-call(s32[5]{0:T(128)S(1)} %and_select_fusion.slot_ref, bf16[16,5,8,640]{3,2,1,0:T(8,128)(2,1)S(1)} %all-to-all-done.1.four_ref, bf16[8,3,80,640]{3,2,1,0:T(8,128)(2,1)S(1)} %slice.3.head_ref, bf16[8,5,80,640]{3,2,1,0:T(8,128)(2,1)} %all-to-all-done.basis_any), custom_call_target="tpu_custom_call" | custom-call | flops 524288000 | bytes 4915200 | tf_op jit(solution)/shard_map/spectral_parts/pallas_call | solution.py:271
  90.0 32.5 %all_to_all.15.in_ref = bf16[32,104,128]{2,1,0:T(8,128)(2,1)S(1)} all-to-all(bf16[32,104,128]{2,1,0:T(8,128)(2,1)S(1)} %spectral_parts.1), channel_id=1, replica_groups=mesh['x'=4,'zp'=2,'zq'=2,'wave'=8,'lev'=2] {'x','zp','zq','lev'}, dimensions={0} | all-to-all | bytes 1703936 | tf_op jit(solution)/shard_map/all_to_all | solution.py:363
  122.5 1.5 %finish.1 = f32[2560,80]{1,0:T(8,128)} custom-call(bf16[32,104,128]{2,1,0:T(8,128)(2,1)S(1)} %all_to_all.15.in_ref), custom_call_target="tpu_custom_call" | custom-call | flops 425984 | bytes 2162688 | tf_op jit(solution)/shard_map/finish/pallas_call | solution.py:317
  (30 shorter events, 0.1 us)
Async XLA Ops:
  4.6 6.9 %copy-start.7 = (s32[8]{0:T(128)S(1)}, s32[8]{0:T(128)}, u32[]{:S(2)}) copy-start(s32[8]{0:T(128)} %constant.95.clone) | copy-start | bytes 100
  4.6 6.9 %copy-start.8 = (s32[8]{0:T(128)S(1)}, s32[8]{0:T(128)}, u32[]{:S(2)}) copy-start(s32[8]{0:T(128)} %constant.94.clone) | copy-start | bytes 100
  4.7 6.9 %copy-start = (bf16[32,80,320]{2,1,0:T(8,128)(2,1)S(1)}, bf16[32,80,320]{2,1,0:T(8,128)(2,1)}, u32[]{:S(2)}) copy-start(bf16[32,80,320]{2,1,0:T(8,128)(2,1)} %param.10) | copy-start | bytes 4915204
  4.7 6.9 %copy-start.2 = (f32[8,128]{1,0:T(8,128)S(1)}, f32[8,128]{1,0:T(8,128)}, u32[]{:S(2)}) copy-start(f32[8,128]{1,0:T(8,128)} %get-tuple-element.27._) | copy-start | bytes 12292
  4.7 6.9 %copy-start.3 = (f32[32]{0:T(128)S(1)}, f32[32]{0:T(128)}, u32[]{:S(2)}) copy-start(f32[32]{0:T(128)} %rate_ref.1) | copy-start | bytes 388
  4.7 15.0 %copy-start.5 = (s32[8]{0:T(128)S(1)}, s32[8]{0:T(128)}, u32[]{:S(2)}) copy-start(s32[8]{0:T(128)} %constant.97.clone) | copy-start | bytes 100
  4.7 15.0 %copy-start.6 = (s32[8]{0:T(128)S(1)}, s32[8]{0:T(128)}, u32[]{:S(2)}) copy-start(s32[8]{0:T(128)} %constant.96.clone) | copy-start | bytes 100
  4.7 15.2 %copy-start.4 = (s32[640]{0:T(1024)S(1)}, s32[640]{0:T(1024)}, u32[]{:S(2)}) copy-start(s32[640]{0:T(1024)} %param.14) | copy-start | bytes 7684
  4.7 53.1 %all-to-all-start = ((bf16[8,5,80,640]{3,2,1,0:T(8,128)(2,1)}), bf16[8,5,80,640]{3,2,1,0:T(8,128)(2,1)}, u32[]{:S(2)}, u32[]{:S(2)}) async-start(bf16[8,5,80,640]{3,2,1,0:T(8,128)(2,1)} %get-tuple-element.46), calls=%async_computation | async-start | bytes 8192000 | tf_op jit(solution)/shard_map/all_to_all | solution.py:352
  11.6 1.5 %copy-start.1 = (bf16[32,80,320]{2,1,0:T(8,128)(2,1)S(1)}, bf16[32,80,320]{2,1,0:T(8,128)(2,1)}, u32[]{:S(2)}) copy-start(bf16[32,80,320]{2,1,0:T(8,128)(2,1)} %param.11) | copy-start | bytes 4915204
  15.6 5.1 %collective-permute-start = (bf16[2,80,640]{2,1,0:T(8,128)(2,1)}, bf16[2,80,640]{2,1,0:T(8,128)(2,1)S(1)}, u32[]{:S(2)}, u32[]{:S(2)}) collective-permute-start(bf16[2,80,640]{2,1,0:T(8,128)(2,1)} %get-tuple-element.28), channel_id=1, source_target_pairs={{0,2},{2,0},{4,6},{6,4},{8,10},{10,8},{12,14},{14,12},{1,3},{3,1},... | collective-permute-start | bytes 614408 | tf_op jit(solution)/shard_map/ppermute | solution.py:346
  15.6 9.6 %collective-permute-start.1 = (bf16[2,80,640]{2,1,0:T(8,128)(2,1)S(1)}, bf16[2,80,640]{2,1,0:T(8,128)(2,1)S(1)}, u32[]{:S(2)}, u32[]{:S(2)}) collective-permute-start(bf16[2,80,640]{2,1,0:T(8,128)(2,1)S(1)} %get-tuple-element.32), channel_id=1, source_target_pairs={{0,4},{2,14},{4,0},{6,10},{8,12},{10,6},{12,8},{14,2},{1,5},{3,15}... | collective-permute-start | bytes 614408 | tf_op jit(solution)/shard_map/ppermute | solution.py:346
  16.7 12.2 %collective-permute-start.2 = (bf16[2,80,640]{2,1,0:T(8,128)(2,1)S(1)}, bf16[2,80,640]{2,1,0:T(8,128)(2,1)S(1)}, u32[]{:S(2)}, u32[]{:S(2)}) collective-permute-start(bf16[2,80,640]{2,1,0:T(8,128)(2,1)S(1)} %get-tuple-element.33), channel_id=1, source_target_pairs={{0,12},{2,6},{4,8},{6,2},{8,4},{10,14},{12,0},{14,10},{1,13},{3,7}... | collective-permute-start | bytes 614408 | tf_op jit(solution)/shard_map/ppermute | solution.py:346
  18.9 11.1 %collective-permute-start.3 = (bf16[2,80,640]{2,1,0:T(8,128)(2,1)S(1)}, bf16[2,80,640]{2,1,0:T(8,128)(2,1)S(1)}, u32[]{:S(2)}, u32[]{:S(2)}) collective-permute-start(bf16[2,80,640]{2,1,0:T(8,128)(2,1)S(1)} %get-tuple-element.34), channel_id=1, source_target_pairs={{0,8},{2,10},{4,12},{6,14},{8,0},{10,2},{12,4},{14,6},{1,9},{3,11}... | collective-permute-start | bytes 614408 | tf_op jit(solution)/shard_map/ppermute | solution.py:346
  19.7 12.0 %collective-permute-start.4 = (bf16[2,80,640]{2,1,0:T(8,128)(2,1)S(1)}, bf16[2,80,640]{2,1,0:T(8,128)(2,1)S(1)}, u32[]{:S(2)}, u32[]{:S(2)}) collective-permute-start(bf16[2,80,640]{2,1,0:T(8,128)(2,1)S(1)} %get-tuple-element.35), channel_id=1, source_target_pairs={{0,6},{2,12},{4,2},{6,8},{8,14},{10,4},{12,10},{14,0},{1,7},{3,13}... | collective-permute-start | bytes 614408 | tf_op jit(solution)/shard_map/ppermute | solution.py:346
  20.7 15.6 %collective-permute-start.5 = (bf16[2,80,640]{2,1,0:T(8,128)(2,1)S(1)}, bf16[2,80,640]{2,1,0:T(8,128)(2,1)S(1)}, u32[]{:S(2)}, u32[]{:S(2)}) collective-permute-start(bf16[2,80,640]{2,1,0:T(8,128)(2,1)S(1)} %get-tuple-element.36), channel_id=1, source_target_pairs={{0,14},{2,4},{4,10},{6,0},{8,6},{10,12},{12,2},{14,8},{1,15},{3,5}... | collective-permute-start | bytes 614408 | tf_op jit(solution)/shard_map/ppermute | solution.py:346
  25.2 13.5 %collective-permute-start.6 = (bf16[2,80,640]{2,1,0:T(8,128)(2,1)S(1)}, bf16[2,80,640]{2,1,0:T(8,128)(2,1)S(1)}, u32[]{:S(2)}, u32[]{:S(2)}) collective-permute-start(bf16[2,80,640]{2,1,0:T(8,128)(2,1)S(1)} %get-tuple-element.37), channel_id=1, source_target_pairs={{0,10},{2,8},{4,14},{6,12},{8,2},{10,0},{12,6},{14,4},{1,11},{3,9}... | collective-permute-start | bytes 614408 | tf_op jit(solution)/shard_map/ppermute | solution.py:346
  41.3 4.3 %collective-permute-start.7 = (bf16[80,640]{1,0:T(8,128)(2,1)S(1)}, bf16[80,640]{1,0:T(8,128)(2,1)S(1)}, u32[]{:S(2)}, u32[]{:S(2)}) collective-permute-start(bf16[80,640]{1,0:T(8,128)(2,1)S(1)} %get-tuple-element.39), channel_id=1, source_target_pairs={{0,2},{2,0},{4,6},{6,4},{8,10},{10,8},{12,14},{14,12},{1,3},{3,1},... | collective-permute-start | bytes 307208 | tf_op jit(solution)/shard_map/ppermute | solution.py:346
  41.5 7.1 %collective-permute-start.8 = (bf16[80,640]{1,0:T(8,128)(2,1)S(1)}, bf16[80,640]{1,0:T(8,128)(2,1)S(1)}, u32[]{:S(2)}, u32[]{:S(2)}) collective-permute-start(bf16[80,640]{1,0:T(8,128)(2,1)S(1)} %get-tuple-element.40), channel_id=1, source_target_pairs={{0,4},{2,14},{4,0},{6,10},{8,12},{10,6},{12,8},{14,2},{1,5},{3,15}... | collective-permute-start | bytes 307208 | tf_op jit(solution)/shard_map/ppermute | solution.py:346
  41.5 7.1 %collective-permute-start.9 = (bf16[80,640]{1,0:T(8,128)(2,1)S(1)}, bf16[80,640]{1,0:T(8,128)(2,1)S(1)}, u32[]{:S(2)}, u32[]{:S(2)}) collective-permute-start(bf16[80,640]{1,0:T(8,128)(2,1)S(1)} %get-tuple-element.41), channel_id=1, source_target_pairs={{0,12},{2,6},{4,8},{6,2},{8,4},{10,14},{12,0},{14,10},{1,13},{3,7}... | collective-permute-start | bytes 307208 | tf_op jit(solution)/shard_map/ppermute | solution.py:346
  42.9 7.3 %collective-permute-start.10 = (bf16[80,640]{1,0:T(8,128)(2,1)S(1)}, bf16[80,640]{1,0:T(8,128)(2,1)S(1)}, u32[]{:S(2)}, u32[]{:S(2)}) collective-permute-start(bf16[80,640]{1,0:T(8,128)(2,1)S(1)} %get-tuple-element.42), channel_id=1, source_target_pairs={{0,8},{2,10},{4,12},{6,14},{8,0},{10,2},{12,4},{14,6},{1,9},{3,11}... | collective-permute-start | bytes 307208 | tf_op jit(solution)/shard_map/ppermute | solution.py:346
  45.6 5.8 %collective-permute-start.11 = (bf16[80,640]{1,0:T(8,128)(2,1)S(1)}, bf16[80,640]{1,0:T(8,128)(2,1)S(1)}, u32[]{:S(2)}, u32[]{:S(2)}) collective-permute-start(bf16[80,640]{1,0:T(8,128)(2,1)S(1)} %get-tuple-element.43), channel_id=1, source_target_pairs={{0,6},{2,12},{4,2},{6,8},{8,14},{10,4},{12,10},{14,0},{1,7},{3,13}... | collective-permute-start | bytes 307208 | tf_op jit(solution)/shard_map/ppermute | solution.py:346
  45.6 6.0 %collective-permute-start.12 = (bf16[80,640]{1,0:T(8,128)(2,1)S(1)}, bf16[80,640]{1,0:T(8,128)(2,1)S(1)}, u32[]{:S(2)}, u32[]{:S(2)}) collective-permute-start(bf16[80,640]{1,0:T(8,128)(2,1)S(1)} %get-tuple-element.44), channel_id=1, source_target_pairs={{0,14},{2,4},{4,10},{6,0},{8,6},{10,12},{12,2},{14,8},{1,15},{3,5}... | collective-permute-start | bytes 307208 | tf_op jit(solution)/shard_map/ppermute | solution.py:346
  48.6 6.2 %collective-permute-start.13 = (bf16[80,640]{1,0:T(8,128)(2,1)S(1)}, bf16[80,640]{1,0:T(8,128)(2,1)S(1)}, u32[]{:S(2)}, u32[]{:S(2)}) collective-permute-start(bf16[80,640]{1,0:T(8,128)(2,1)S(1)} %get-tuple-element.45), channel_id=1, source_target_pairs={{0,10},{2,8},{4,14},{6,12},{8,2},{10,0},{12,6},{14,4},{1,11},{3,9}... | collective-permute-start | bytes 307208 | tf_op jit(solution)/shard_map/ppermute | solution.py:346
  57.8 29.0 %all-to-all-start.1 = ((bf16[16,5,8,640]{3,2,1,0:T(8,128)(2,1)}), bf16[16,5,8,640]{3,2,1,0:T(8,128)(2,1)S(1)}, u32[]{:S(2)}, u32[]{:S(2)}) async-start(bf16[16,5,8,640]{3,2,1,0:T(8,128)(2,1)} %turn.1), calls=%async_computation.1 | async-start | bytes 1638400 | tf_op jit(solution)/shard_map/all_to_all | solution.py:358

commit v12 on v11

--- a/solution.py
+++ b/solution.py
@@ -20,11 +20,13 @@
 
 
 def basis_kernel(lev_ref, basis_hbm, out_hbm, token_ref, in_buf, out_buf, in_sems, out_sems):
-    steps, lats, _, degs = in_buf.shape
+    pieces, lats, steps, _, degs = in_buf.shape
     lev = lev_ref[0]
     reads = [
-        pltpu.make_async_copy(basis_hbm.at[:, 2 * b + lev], in_buf.at[b], in_sems.at[b])
-        for b in range(steps)
+        pltpu.make_async_copy(
+            basis_hbm.at[pl.ds(lats * g, lats), :, lev], in_buf.at[g], in_sems.at[g]
+        )
+        for g in range(pieces)
     ]
     for read in reads:
         read.start()
@@ -33,18 +35,18 @@
     swap = (col == row % 16 * 8 + row // 16).astype(jnp.bfloat16)
     token_ref[...] = jnp.zeros_like(token_ref)
     writes = []
-    for b in range(steps):
-        reads[b].wait()
-        lanes = 384
-        for g in range(lats // 16):
-            part = slice(16 * g, 16 * g + 16)
-            block = in_buf[b, part, :, :lanes].astype(jnp.float32).reshape(128, lanes)
+    for g in range(pieces):
+        reads[g].wait()
+        for b in range(steps):
+            block = in_buf[g, :, b].astype(jnp.float32).reshape(128, degs)
             turned = jnp.dot(swap, block.astype(jnp.bfloat16), preferred_element_type=jnp.float32)
-            out_buf[b, :, part, :lanes] = turned.astype(jnp.bfloat16).reshape(8, 16, lanes)
-            other = jnp.swapaxes(in_buf[b, part, :, lanes:].astype(jnp.float32), 0, 1)
-            out_buf[b, :, part, lanes:] = other.astype(jnp.bfloat16)
-        writes.append(pltpu.make_async_copy(out_buf.at[b], out_hbm.at[:, b], out_sems.at[b]))
-        writes[b].start()
+            out_buf[g, :, b] = turned.astype(jnp.bfloat16).reshape(8, lats, degs)
+        writes.append(
+            pltpu.make_async_copy(
+                out_buf.at[g], out_hbm.at[:, :, pl.ds(lats * g, lats)], out_sems.at[g]
+            )
+        )
+        writes[g].start()
     for write in writes:
         write.wait()
 
@@ -62,15 +64,15 @@
             jax.ShapeDtypeStruct((8, 128), jnp.float32),
         ],
         scratch_shapes=[
-            pltpu.VMEM((steps, lats, 8, degs), jnp.bfloat16),
-            pltpu.VMEM((steps, 8, lats, degs), jnp.bfloat16),
-            pltpu.SemaphoreType.DMA((steps,)),
-            pltpu.SemaphoreType.DMA((steps,)),
+            pltpu.VMEM((lats // 16, 16, steps, 8, degs), jnp.bfloat16),
+            pltpu.VMEM((lats // 16, 8, steps, 16, degs), jnp.bfloat16),
+            pltpu.SemaphoreType.DMA((lats // 16,)),
+            pltpu.SemaphoreType.DMA((lats // 16,)),
         ],
         compiler_params=params(63),
         cost_estimate=cost(0, 2 * lats * slots * degs),
         name="basis_blocks",
-    )(lev, basis.reshape(lats, slots // 8, 8, degs))
+    )(lev, basis.reshape(lats, steps, 2, 8, degs))
 
 
 def grad_kernel(wave_ref, rate_ref, grad_ref, state_ref, _, *outs):

time: 124 us -> 124 us (level)
  no operation moved by 1% of the time
where the time goes in v12:
time: 124 us
  waiting for transfers between devices  33.1 us (27%)
  starting transfers between devices  32.5 us (26%)
  blocking collectives  32.5 us (26%)
  Pallas kernels  18.1 us (15%)
  local copies, waits for them, and re-layouts  5.08 us (4%)
  other arithmetic  2.39 us (2%)
    all_to_all x1, blocking collectives, local(): parts = lax.all_to_all(parts, ('x', 'zp', 'zq', 'lev'), 0, 0, tiled=True)  32.5 us
    all_to_all x1, waiting for transfers between devices, local(): fourier = lax.all_to_all(fourier, ('x', 'zq', 'lev'), 0, 0, tiled=True)  16.2 us
    ppermute x14, waiting for transfers between devices, swapped(): lax.ppermute(blocks[k], 'wave', [(w, w ^ TO[w % 2][k]) for w in range(8)])  16.1 us
    ppermute x14, starting transfers between devices, swapped(): lax.ppermute(blocks[k], 'wave', [(w, w ^ TO[w % 2][k]) for w in range(8)])  15.4 us
    all_to_all x1, starting transfers between devices, local(): fourier = lax.all_to_all(fourier, ('x', 'zq', 'lev'), 0, 0, tiled=True)  10.2 us
    all_to_all x1, starting transfers between devices, local(): basis = lax.all_to_all(basis, ('x', 'zq'), 0, 0, tiled=True)  6.84 us
    pallas_call x1, Pallas kernels, basis_blocks(): pl.pallas_call(basis_kernel, in_specs=[pl.BlockSpec(memory_space=pltpu.SM...  4.59 us
    pallas_call x1, Pallas kernels, spectral_parts(): pl.pallas_call(spectral_kernel, in_specs=[smem, vmem, vmem, pl.BlockSpec(...  3.17 us
  transfers between devices with their start and end apart: 16, of which 10 were waited for; matrix products, arithmetic and copies ran while one was open for 5% of the time, Pallas kernels for 7%

profile of v12, /device:TPU:2, one launch (start us, length us, event | category | flops | bytes accessed | tf_op | source)
XLA Modules:
  0.0 124.0 jit_solution(12577355643966109498)
XLA Ops:
  0.0 4.6 %basis_blocks.1 = (bf16[8,5,80,640]{3,2,1,0:T(8,128)(2,1)}, f32[8,128]{1,0:T(8,128)}) custom-call(s32[1]{0:T(128)} %bitcast.3.lev_ref, bf16[80,5,2,8,640]{4,3,2,1,0:T(8,128)(2,1)} %bitcast.9), custom_call_target="tpu_custom_call" | custom-call | bytes 8192000 | tf_op jit(solution)/shard_map/basis_blocks/pallas_call | solution.py:58
  4.6 0.0 copy-start.7
  4.6 0.0 copy-start.8
  4.6 0.0 copy-start
  4.6 0.0 copy-start.2
  4.7 0.0 copy-start.5
  4.7 0.0 copy-start.6
  4.7 0.0 copy-start.4
  4.7 6.8 %all-to-all-start = ((bf16[8,5,80,640]{3,2,1,0:T(8,128)(2,1)}), bf16[8,5,80,640]{3,2,1,0:T(8,128)(2,1)}, u32[]{:S(2)}, u32[]{:S(2)}) async-start(bf16[8,5,80,640]{3,2,1,0:T(8,128)(2,1)} %get-tuple-element.46), calls=%async_computation | async-start | bytes 8192000 | tf_op jit(solution)/shard_map/all_to_all | solution.py:354
  11.6 1.5 %copy-done.1 = bf16[32,80,320]{2,1,0:T(8,128)(2,1)S(1)} copy-done((bf16[32,80,320]{2,1,0:T(8,128)(2,1)S(1)}, bf16[32,80,320]{2,1,0:T(8,128)(2,1)}, u32[]{:S(2)}) %copy-start.1) | copy-done | bytes 1638424
  13.1 2.4 %gradient.1 = (bf16[2,80,640]{2,1,0:T(8,128)(2,1)S(1)}, bf16[2,80,640]{2,1,0:T(8,128)(2,1)}, bf16[2,80,640]{2,1,0:T(8,128)(2,1)S(1)}, bf16[2,80,640]{2,1,0:T(8,1...) custom-call(s32[8]{0:T(128)S(1)} %get-tuple-element.50.wave_ref, ...), custom_call_target="tpu_custom_call" | custom-call | flops 4915200 | bytes 4915200 | tf_op jit(solution)/shard_map/gradient/pallas_call | solution.py:92
  15.6 1.1 collective-permute-start.1
  16.7 2.2 %collective-permute-start.2 = (bf16[2,80,640]{2,1,0:T(8,128)(2,1)S(1)}, bf16[2,80,640]{2,1,0:T(8,128)(2,1)S(1)}, u32[]{:S(2)}, u32[]{:S(2)}) collective-permute-start(bf16[2,80,640]{2,1,0:T(8,128)(2,1)S(1)} %get-tuple-element.33), channel_id=1, source_target_pairs={{0,12},{2,6},{4,8},{6,2},{8,4},{10,14},{12,0},{14,10},{1,13},{3,7}... | collective-permute-start | bytes 614408 | tf_op jit(solution)/shard_map/ppermute | solution.py:348
  18.9 0.8 collective-permute-start.3
  19.7 0.1 broadcast_add_fusion
  19.8 0.1 add.107
  19.9 0.1 reshape.66
  20.0 0.1 broadcast_in_dim.12
  20.0 0.1 add.109
  20.1 0.6 gather_fusion.1
  20.7 3.0 %collective-permute-start.5 = (bf16[2,80,640]{2,1,0:T(8,128)(2,1)S(1)}, bf16[2,80,640]{2,1,0:T(8,128)(2,1)S(1)}, u32[]{:S(2)}, u32[]{:S(2)}) collective-permute-start(bf16[2,80,640]{2,1,0:T(8,128)(2,1)S(1)} %get-tuple-element.36), channel_id=1, source_target_pairs={{0,14},{2,4},{4,10},{6,0},{8,6},{10,12},{12,2},{14,8},{1,15},{3,5}... | collective-permute-start | bytes 614408 | tf_op jit(solution)/shard_map/ppermute | solution.py:348
  23.7 0.1 mul.86
  23.8 1.3 %fusion.4 = (f32[64,1280]{1,0:T(8,128)S(1)}, f32[64,1280]{1,0:T(8,128)S(1)}) fusion(s32[1280]{0:T(1024)S(1)} %add.109, s32[1280]{0:T(1024)S(1)} %mul.86), kind=kLoop, calls=%fused_computation.8 | loop fusion | flops 819200 | bytes 665600 | tf_op jit(solution)/shard_map/sin | solution.py:120
  25.2 1.0 collective-permute-start.6
  26.2 0.9 sine_multiply_fusion
  27.1 1.7 %wave_table.1.table_ref = bf16[5,2560,256]{2,1,0:T(8,128)(2,1)S(1)} custom-call(f32[40,1280]{1,0:T(8,128)S(1)} %get-tuple-element.56.coarse_cos, f32[40,1280]{1,0:T(8,128)S(1)} %get-tuple-element.55.coarse_sin, f32[64,1280]{1,0:T(8,128)S(1)} %get-tuple-element.54.fine_cos, f32[64,1280]{1,0:T(8,128)S(1)} %get-tuple-element.53.fine_sin), custom_call_target="tpu_custom_call" | custom-call | flops 9830400 | bytes 6553600 | tf_op jit(solution)/shard_map/wave_table/pallas_call | solution.py:128
  28.8 1.1 collective-permute-done.3.refs_4_
  30.0 1.7 %collective-permute-done.4.refs_5_ = bf16[2,80,640]{2,1,0:T(8,128)(2,1)S(1)} collective-permute-done((bf16[2,80,640]{2,1,0:T(8,128)(2,1)S(1)}, bf16[2,80,640]{2,1,0:T(8,128)(2,1)S(1)}, u32[]{:S(2)}, u32[]{:S(2)}) %collective-permute-start.4) | collective-permute-done | bytes 204832 | tf_op jit(solution)/shard_map/ppermute | solution.py:348
  31.7 4.6 %collective-permute-done.5.refs_6_ = bf16[2,80,640]{2,1,0:T(8,128)(2,1)S(1)} collective-permute-done((bf16[2,80,640]{2,1,0:T(8,128)(2,1)S(1)}, bf16[2,80,640]{2,1,0:T(8,128)(2,1)S(1)}, u32[]{:S(2)}, u32[]{:S(2)}) %collective-permute-start.5) | collective-permute-done | bytes 204832 | tf_op jit(solution)/shard_map/ppermute | solution.py:348
  36.3 2.4 %collective-permute-done.6.refs_7_ = bf16[2,80,640]{2,1,0:T(8,128)(2,1)S(1)} collective-permute-done((bf16[2,80,640]{2,1,0:T(8,128)(2,1)S(1)}, bf16[2,80,640]{2,1,0:T(8,128)(2,1)S(1)}, u32[]{:S(2)}, u32[]{:S(2)}) %collective-permute-start.6) | collective-permute-done | bytes 204832 | tf_op jit(solution)/shard_map/ppermute | solution.py:348
  38.7 2.6 %fourier_rows.1 = (bf16[80,640]{1,0:T(8,128)(2,1)S(1)}, bf16[80,640]{1,0:T(8,128)(2,1)S(1)}, bf16[80,640]{1,0:T(8,128)(2,1)S(1)}, bf16[80,640]{1,0:T(8,128)(2,1)...) custom-call(bf16[5,2560,256]{2,1,0:T(8,128)(2,1)S(1)} %wave_table.1., ...), custom_call_target="tpu_custom_call" | custom-call | flops 2097152000 | bytes 6553600 | tf_op jit(solution)/shard_map/fourier_rows/pallas_call | solution.py:163
  41.3 0.2 collective-permute-start.7
  41.5 1.4 %collective-permute-start.9 = (bf16[80,640]{1,0:T(8,128)(2,1)S(1)}, bf16[80,640]{1,0:T(8,128)(2,1)S(1)}, u32[]{:S(2)}, u32[]{:S(2)}) collective-permute-start(bf16[80,640]{1,0:T(8,128)(2,1)S(1)} %get-tuple-element.41), channel_id=1, source_target_pairs={{0,12},{2,6},{4,8},{6,2},{8,4},{10,14},{12,0},{14,10},{1,13},{3,7}... | collective-permute-start | bytes 307208 | tf_op jit(solution)/shard_map/ppermute | solution.py:348
  42.9 2.7 %collective-permute-start.10 = (bf16[80,640]{1,0:T(8,128)(2,1)S(1)}, bf16[80,640]{1,0:T(8,128)(2,1)S(1)}, u32[]{:S(2)}, u32[]{:S(2)}) collective-permute-start(bf16[80,640]{1,0:T(8,128)(2,1)S(1)} %get-tuple-element.42), channel_id=1, source_target_pairs={{0,8},{2,10},{4,12},{6,14},{8,0},{10,2},{12,4},{14,6},{1,9},{3,11}... | collective-permute-start | bytes 307208 | tf_op jit(solution)/shard_map/ppermute | solution.py:348
  45.6 3.0 %collective-permute-start.12 = (bf16[80,640]{1,0:T(8,128)(2,1)S(1)}, bf16[80,640]{1,0:T(8,128)(2,1)S(1)}, u32[]{:S(2)}, u32[]{:S(2)}) collective-permute-start(bf16[80,640]{1,0:T(8,128)(2,1)S(1)} %get-tuple-element.44), channel_id=1, source_target_pairs={{0,14},{2,4},{4,10},{6,0},{8,6},{10,12},{12,2},{14,8},{1,15},{3,5}... | collective-permute-start | bytes 307208 | tf_op jit(solution)/shard_map/ppermute | solution.py:348
  48.5 1.7 %collective-permute-done.10.refs_4_ = bf16[80,640]{1,0:T(8,128)(2,1)S(1)} collective-permute-done((bf16[80,640]{1,0:T(8,128)(2,1)S(1)}, bf16[80,640]{1,0:T(8,128)(2,1)S(1)}, u32[]{:S(2)}, u32[]{:S(2)}) %collective-permute-start.10) | collective-permute-done | bytes 102432 | tf_op jit(solution)/shard_map/ppermute | solution.py:348
  50.2 1.2 collective-permute-done.11.refs_5_
  51.4 0.2 collective-permute-done.12.refs_6_
  51.6 3.2 %collective-permute-done.13.refs_7_ = bf16[80,640]{1,0:T(8,128)(2,1)S(1)} collective-permute-done((bf16[80,640]{1,0:T(8,128)(2,1)S(1)}, bf16[80,640]{1,0:T(8,128)(2,1)S(1)}, u32[]{:S(2)}, u32[]{:S(2)}) %collective-permute-start.13) | collective-permute-done | bytes 102432 | tf_op jit(solution)/shard_map/ppermute | solution.py:348
  54.8 2.1 %turn.1 = bf16[16,5,8,640]{3,2,1,0:T(8,128)(2,1)} custom-call(s32[8]{0:T(128)S(1)} %get-tuple-element.52.wave_ref, bf16[80,640]{1,0:T(8,128)(2,1)S(1)} %get-tuple-element.38.refs_0_, bf16[80,640]{1,0:T(8,128)(2,1)S(1)} %collective-permute-done.7.refs_1_, bf16[80,640]{1,0:T(8,128)(2,1)S(1)} %collective-permute-done.8.refs_2_, ...), custom_call_target="tpu_custom_call" | custom-call | bytes 1638400 | tf_op jit(solution)/shard_map/turn/pallas_call | solution.py:192
  56.9 0.9 all-to-all-done.basis_any
  57.8 10.2 %all-to-all-start.1 = ((bf16[16,5,8,640]{3,2,1,0:T(8,128)(2,1)}), bf16[16,5,8,640]{3,2,1,0:T(8,128)(2,1)S(1)}, u32[]{:S(2)}, u32[]{:S(2)}) async-start(bf16[16,5,8,640]{3,2,1,0:T(8,128)(2,1)} %turn.1), calls=%async_computation.1 | async-start | bytes 1638400 | tf_op jit(solution)/shard_map/all_to_all | solution.py:360
  68.0 0.6 gather_fusion
  68.7 1.9 %slice.3.head_ref = bf16[8,3,80,640]{3,2,1,0:T(8,128)(2,1)S(1)} slice(bf16[8,5,80,640]{3,2,1,0:T(8,128)(2,1)} %all-to-all-done.basis_any), slice={[0:8], [0:3], [0:80], [0:640]} | slice | bytes 4915200 | tf_op jit(solution)/shard_map/slice | solution.py:364
  70.6 16.2 %all-to-all-done.1.four_ref = bf16[16,5,8,640]{3,2,1,0:T(8,128)(2,1)S(1)} async-done(((bf16[16,5,8,640]{3,2,1,0:T(8,128)(2,1)}), bf16[16,5,8,640]{3,2,1,0:T(8,128)(2,1)S(1)}, u32[]{:S(2)}, u32[]{:S(2)}) %all-to-all-start.1) | async-done | bytes 819232 | tf_op jit(solution)/shard_map/all_to_all | solution.py:360
  86.8 3.2 %spectral_parts.1 = bf16[32,104,128]{2,1,0:T(8,128)(2,1)S(1)} custom-call(s32[5]{0:T(128)S(1)} %and_select_fusion.slot_ref, bf16[16,5,8,640]{3,2,1,0:T(8,128)(2,1)S(1)} %all-to-all-done.1.four_ref, bf16[8,3,80,640]{3,2,1,0:T(8,128)(2,1)S(1)} %slice.3.head_ref, bf16[8,5,80,640]{3,2,1,0:T(8,128)(2,1)} %all-to-all-done.basis_any), custom_call_target="tpu_custom_call" | custom-call | flops 524288000 | bytes 4915200 | tf_op jit(solution)/shard_map/spectral_parts/pallas_call | solution.py:273
  89.9 32.5 %all_to_all.15.in_ref = bf16[32,104,128]{2,1,0:T(8,128)(2,1)S(1)} all-to-all(bf16[32,104,128]{2,1,0:T(8,128)(2,1)S(1)} %spectral_parts.1), channel_id=1, replica_groups=mesh['x'=4,'zp'=2,'zq'=2,'wave'=8,'lev'=2] {'x','zp','zq','lev'}, dimensions={0} | all-to-all | bytes 1703936 | tf_op jit(solution)/shard_map/all_to_all | solution.py:365
  122.4 1.5 %finish.1 = f32[2560,80]{1,0:T(8,128)} custom-call(bf16[32,104,128]{2,1,0:T(8,128)(2,1)S(1)} %all_to_all.15.in_ref), custom_call_target="tpu_custom_call" | custom-call | flops 425984 | bytes 2162688 | tf_op jit(solution)/shard_map/finish/pallas_call | solution.py:319
  (30 shorter events, 0.1 us)
Async XLA Ops:
  4.6 6.9 %copy-start.7 = (s32[8]{0:T(128)S(1)}, s32[8]{0:T(128)}, u32[]{:S(2)}) copy-start(s32[8]{0:T(128)} %constant.95.clone) | copy-start | bytes 100
  4.6 6.9 %copy-start.8 = (s32[8]{0:T(128)S(1)}, s32[8]{0:T(128)}, u32[]{:S(2)}) copy-start(s32[8]{0:T(128)} %constant.94.clone) | copy-start | bytes 100
  4.6 6.9 %copy-start = (bf16[32,80,320]{2,1,0:T(8,128)(2,1)S(1)}, bf16[32,80,320]{2,1,0:T(8,128)(2,1)}, u32[]{:S(2)}) copy-start(bf16[32,80,320]{2,1,0:T(8,128)(2,1)} %param.10) | copy-start | bytes 4915204
  4.6 6.9 %copy-start.2 = (f32[8,128]{1,0:T(8,128)S(1)}, f32[8,128]{1,0:T(8,128)}, u32[]{:S(2)}) copy-start(f32[8,128]{1,0:T(8,128)} %get-tuple-element.27._) | copy-start | bytes 12292
  4.6 6.9 %copy-start.3 = (f32[32]{0:T(128)S(1)}, f32[32]{0:T(128)}, u32[]{:S(2)}) copy-start(f32[32]{0:T(128)} %rate_ref.1) | copy-start | bytes 388
  4.7 15.0 %copy-start.5 = (s32[8]{0:T(128)S(1)}, s32[8]{0:T(128)}, u32[]{:S(2)}) copy-start(s32[8]{0:T(128)} %constant.97.clone) | copy-start | bytes 100
  4.7 15.0 %copy-start.6 = (s32[8]{0:T(128)S(1)}, s32[8]{0:T(128)}, u32[]{:S(2)}) copy-start(s32[8]{0:T(128)} %constant.96.clone) | copy-start | bytes 100
  4.7 15.2 %copy-start.4 = (s32[640]{0:T(1024)S(1)}, s32[640]{0:T(1024)}, u32[]{:S(2)}) copy-start(s32[640]{0:T(1024)} %param.14) | copy-start | bytes 7684
  4.7 53.1 %all-to-all-start = ((bf16[8,5,80,640]{3,2,1,0:T(8,128)(2,1)}), bf16[8,5,80,640]{3,2,1,0:T(8,128)(2,1)}, u32[]{:S(2)}, u32[]{:S(2)}) async-start(bf16[8,5,80,640]{3,2,1,0:T(8,128)(2,1)} %get-tuple-element.46), calls=%async_computation | async-start | bytes 8192000 | tf_op jit(solution)/shard_map/all_to_all | solution.py:354
  11.6 1.5 %copy-start.1 = (bf16[32,80,320]{2,1,0:T(8,128)(2,1)S(1)}, bf16[32,80,320]{2,1,0:T(8,128)(2,1)}, u32[]{:S(2)}) copy-start(bf16[32,80,320]{2,1,0:T(8,128)(2,1)} %param.11) | copy-start | bytes 4915204
  15.6 5.1 %collective-permute-start = (bf16[2,80,640]{2,1,0:T(8,128)(2,1)}, bf16[2,80,640]{2,1,0:T(8,128)(2,1)S(1)}, u32[]{:S(2)}, u32[]{:S(2)}) collective-permute-start(bf16[2,80,640]{2,1,0:T(8,128)(2,1)} %get-tuple-element.28), channel_id=1, source_target_pairs={{0,2},{2,0},{4,6},{6,4},{8,10},{10,8},{12,14},{14,12},{1,3},{3,1},... | collective-permute-start | bytes 614408 | tf_op jit(solution)/shard_map/ppermute | solution.py:348
  15.6 9.6 %collective-permute-start.1 = (bf16[2,80,640]{2,1,0:T(8,128)(2,1)S(1)}, bf16[2,80,640]{2,1,0:T(8,128)(2,1)S(1)}, u32[]{:S(2)}, u32[]{:S(2)}) collective-permute-start(bf16[2,80,640]{2,1,0:T(8,128)(2,1)S(1)} %get-tuple-element.32), channel_id=1, source_target_pairs={{0,4},{2,14},{4,0},{6,10},{8,12},{10,6},{12,8},{14,2},{1,5},{3,15}... | collective-permute-start | bytes 614408 | tf_op jit(solution)/shard_map/ppermute | solution.py:348
  16.7 12.2 %collective-permute-start.2 = (bf16[2,80,640]{2,1,0:T(8,128)(2,1)S(1)}, bf16[2,80,640]{2,1,0:T(8,128)(2,1)S(1)}, u32[]{:S(2)}, u32[]{:S(2)}) collective-permute-start(bf16[2,80,640]{2,1,0:T(8,128)(2,1)S(1)} %get-tuple-element.33), channel_id=1, source_target_pairs={{0,12},{2,6},{4,8},{6,2},{8,4},{10,14},{12,0},{14,10},{1,13},{3,7}... | collective-permute-start | bytes 614408 | tf_op jit(solution)/shard_map/ppermute | solution.py:348
  18.9 11.1 %collective-permute-start.3 = (bf16[2,80,640]{2,1,0:T(8,128)(2,1)S(1)}, bf16[2,80,640]{2,1,0:T(8,128)(2,1)S(1)}, u32[]{:S(2)}, u32[]{:S(2)}) collective-permute-start(bf16[2,80,640]{2,1,0:T(8,128)(2,1)S(1)} %get-tuple-element.34), channel_id=1, source_target_pairs={{0,8},{2,10},{4,12},{6,14},{8,0},{10,2},{12,4},{14,6},{1,9},{3,11}... | collective-permute-start | bytes 614408 | tf_op jit(solution)/shard_map/ppermute | solution.py:348
  19.7 12.0 %collective-permute-start.4 = (bf16[2,80,640]{2,1,0:T(8,128)(2,1)S(1)}, bf16[2,80,640]{2,1,0:T(8,128)(2,1)S(1)}, u32[]{:S(2)}, u32[]{:S(2)}) collective-permute-start(bf16[2,80,640]{2,1,0:T(8,128)(2,1)S(1)} %get-tuple-element.35), channel_id=1, source_target_pairs={{0,6},{2,12},{4,2},{6,8},{8,14},{10,4},{12,10},{14,0},{1,7},{3,13}... | collective-permute-start | bytes 614408 | tf_op jit(solution)/shard_map/ppermute | solution.py:348
  20.7 15.6 %collective-permute-start.5 = (bf16[2,80,640]{2,1,0:T(8,128)(2,1)S(1)}, bf16[2,80,640]{2,1,0:T(8,128)(2,1)S(1)}, u32[]{:S(2)}, u32[]{:S(2)}) collective-permute-start(bf16[2,80,640]{2,1,0:T(8,128)(2,1)S(1)} %get-tuple-element.36), channel_id=1, source_target_pairs={{0,14},{2,4},{4,10},{6,0},{8,6},{10,12},{12,2},{14,8},{1,15},{3,5}... | collective-permute-start | bytes 614408 | tf_op jit(solution)/shard_map/ppermute | solution.py:348
  25.2 13.5 %collective-permute-start.6 = (bf16[2,80,640]{2,1,0:T(8,128)(2,1)S(1)}, bf16[2,80,640]{2,1,0:T(8,128)(2,1)S(1)}, u32[]{:S(2)}, u32[]{:S(2)}) collective-permute-start(bf16[2,80,640]{2,1,0:T(8,128)(2,1)S(1)} %get-tuple-element.37), channel_id=1, source_target_pairs={{0,10},{2,8},{4,14},{6,12},{8,2},{10,0},{12,6},{14,4},{1,11},{3,9}... | collective-permute-start | bytes 614408 | tf_op jit(solution)/shard_map/ppermute | solution.py:348
  41.3 4.3 %collective-permute-start.7 = (bf16[80,640]{1,0:T(8,128)(2,1)S(1)}, bf16[80,640]{1,0:T(8,128)(2,1)S(1)}, u32[]{:S(2)}, u32[]{:S(2)}) collective-permute-start(bf16[80,640]{1,0:T(8,128)(2,1)S(1)} %get-tuple-element.39), channel_id=1, source_target_pairs={{0,2},{2,0},{4,6},{6,4},{8,10},{10,8},{12,14},{14,12},{1,3},{3,1},... | collective-permute-start | bytes 307208 | tf_op jit(solution)/shard_map/ppermute | solution.py:348
  41.5 7.1 %collective-permute-start.8 = (bf16[80,640]{1,0:T(8,128)(2,1)S(1)}, bf16[80,640]{1,0:T(8,128)(2,1)S(1)}, u32[]{:S(2)}, u32[]{:S(2)}) collective-permute-start(bf16[80,640]{1,0:T(8,128)(2,1)S(1)} %get-tuple-element.40), channel_id=1, source_target_pairs={{0,4},{2,14},{4,0},{6,10},{8,12},{10,6},{12,8},{14,2},{1,5},{3,15}... | collective-permute-start | bytes 307208 | tf_op jit(solution)/shard_map/ppermute | solution.py:348
  41.5 7.1 %collective-permute-start.9 = (bf16[80,640]{1,0:T(8,128)(2,1)S(1)}, bf16[80,640]{1,0:T(8,128)(2,1)S(1)}, u32[]{:S(2)}, u32[]{:S(2)}) collective-permute-start(bf16[80,640]{1,0:T(8,128)(2,1)S(1)} %get-tuple-element.41), channel_id=1, source_target_pairs={{0,12},{2,6},{4,8},{6,2},{8,4},{10,14},{12,0},{14,10},{1,13},{3,7}... | collective-permute-start | bytes 307208 | tf_op jit(solution)/shard_map/ppermute | solution.py:348
  42.9 7.3 %collective-permute-start.10 = (bf16[80,640]{1,0:T(8,128)(2,1)S(1)}, bf16[80,640]{1,0:T(8,128)(2,1)S(1)}, u32[]{:S(2)}, u32[]{:S(2)}) collective-permute-start(bf16[80,640]{1,0:T(8,128)(2,1)S(1)} %get-tuple-element.42), channel_id=1, source_target_pairs={{0,8},{2,10},{4,12},{6,14},{8,0},{10,2},{12,4},{14,6},{1,9},{3,11}... | collective-permute-start | bytes 307208 | tf_op jit(solution)/shard_map/ppermute | solution.py:348
  45.6 5.8 %collective-permute-start.11 = (bf16[80,640]{1,0:T(8,128)(2,1)S(1)}, bf16[80,640]{1,0:T(8,128)(2,1)S(1)}, u32[]{:S(2)}, u32[]{:S(2)}) collective-permute-start(bf16[80,640]{1,0:T(8,128)(2,1)S(1)} %get-tuple-element.43), channel_id=1, source_target_pairs={{0,6},{2,12},{4,2},{6,8},{8,14},{10,4},{12,10},{14,0},{1,7},{3,13}... | collective-permute-start | bytes 307208 | tf_op jit(solution)/shard_map/ppermute | solution.py:348
  45.6 6.0 %collective-permute-start.12 = (bf16[80,640]{1,0:T(8,128)(2,1)S(1)}, bf16[80,640]{1,0:T(8,128)(2,1)S(1)}, u32[]{:S(2)}, u32[]{:S(2)}) collective-permute-start(bf16[80,640]{1,0:T(8,128)(2,1)S(1)} %get-tuple-element.44), channel_id=1, source_target_pairs={{0,14},{2,4},{4,10},{6,0},{8,6},{10,12},{12,2},{14,8},{1,15},{3,5}... | collective-permute-start | bytes 307208 | tf_op jit(solution)/shard_map/ppermute | solution.py:348
  48.5 6.2 %collective-permute-start.13 = (bf16[80,640]{1,0:T(8,128)(2,1)S(1)}, bf16[80,640]{1,0:T(8,128)(2,1)S(1)}, u32[]{:S(2)}, u32[]{:S(2)}) collective-permute-start(bf16[80,640]{1,0:T(8,128)(2,1)S(1)} %get-tuple-element.45), channel_id=1, source_target_pairs={{0,10},{2,8},{4,14},{6,12},{8,2},{10,0},{12,6},{14,4},{1,11},{3,9}... | collective-permute-start | bytes 307208 | tf_op jit(solution)/shard_map/ppermute | solution.py:348
  57.8 29.0 %all-to-all-start.1 = ((bf16[16,5,8,640]{3,2,1,0:T(8,128)(2,1)}), bf16[16,5,8,640]{3,2,1,0:T(8,128)(2,1)S(1)}, u32[]{:S(2)}, u32[]{:S(2)}) async-start(bf16[16,5,8,640]{3,2,1,0:T(8,128)(2,1)} %turn.1), calls=%async_computation.1 | async-start | bytes 1638400 | tf_op jit(solution)/shard_map/all_to_all | solution.py:360

commit v13 on v11

--- a/solution.py
+++ b/solution.py
@@ -217,10 +217,11 @@
         for q in range(8):
             for lev in range(2):
                 block = four_ref[2 * q + lev, b].astype(jnp.float32)
-                for seg in range(8):
-                    left[pl.ds(64 * lev + 8 * seg, 8), pl.ds(q * lats, lats)] = block[
-                        :, seg * lats : (seg + 1) * lats
-                    ]
+                for seg in range(0, 8, 2):
+                    pair = [block[:, i * lats : (i + 1) * lats] for i in (seg, seg + 1)]
+                    left[pl.ds(64 * lev + 8 * seg, 16), pl.ds(q * lats, lats)] = jnp.concatenate(
+                        pair, 0
+                    ).astype(jnp.bfloat16)
         if b >= head:
             for copy in copies[b - head]:
                 copy.wait()
@@ -228,7 +229,7 @@
         else:
             blocks = head_ref[:, b]
         value = jnp.dot(
-            left[...].astype(jnp.bfloat16),
+            left[...],
             blocks.reshape(8 * lats, degs),
             preferred_element_type=jnp.float32,
         )
@@ -274,7 +275,7 @@
         out_shape=jax.ShapeDtypeStruct((32, 104, 128), jnp.bfloat16),
         scratch_shapes=[
             pltpu.VMEM((steps, 8, lats, degs), jnp.bfloat16),
-            pltpu.VMEM((128, 8 * lats), jnp.float32),
+            pltpu.VMEM((128, 8 * lats), jnp.bfloat16),
             pltpu.VMEM((degs + 8, 128), jnp.float32),
             pltpu.SemaphoreType.DMA((steps, 2)),
         ],
@@ -286,22 +287,23 @@
 
 def finish_kernel(in_ref, out_hbm, rows, out_ref, sems):
     depth = in_ref.shape[1]
+    step = depth + 1
     for x in range(4):
         for zq in range(2):
             for lev in range(2):
                 first = in_ref[8 * x + 2 * zq + lev].astype(jnp.float32)
                 second = in_ref[8 * x + 4 + 2 * zq + lev].astype(jnp.float32)
-                rows[pl.ds((8 * lev + 2 * x + zq) * depth, depth), :] = first + second
+                rows[pl.ds((8 * lev + 2 * x + zq) * step, depth), :] = first + second
     low = lax.broadcasted_iota(jnp.int32, (16, 128), 1) < 64
     copies = []
     for n in range(0, 40, 2):
         parts = []
         for k in range(2):
-            one = rows[pl.ds(40 * k + n, 16, stride=depth), :]
-            two = rows[pl.ds(40 * k + n + 1, 16, stride=depth), :]
+            one = rows[pl.ds(40 * k + n, 16, stride=step), :]
+            two = rows[pl.ds(40 * k + n + 1, 16, stride=step), :]
             parts.append(jnp.where(low, one, pltpu.roll(two, 64, 1)))
             parts.append(jnp.where(low, pltpu.roll(one, 64, 1), two))
-        parts.append(rows[pl.ds(80 + n // 2, 16, stride=depth), :])
+        parts.append(rows[pl.ds(80 + n // 2, 16, stride=step), :])
         out_ref[pl.ds(64 * n, 128), :] = jnp.concatenate(parts, 0).T
         if n % 10 == 8:
             piece = pl.ds(64 * (n - 8), 640)
@@ -320,7 +322,7 @@
         out_specs=pl.BlockSpec(memory_space=pltpu.HBM),
         out_shape=jax.ShapeDtypeStruct((40 * 64, 80), jnp.float32),
         scratch_shapes=[
-            pltpu.VMEM((17 * received.shape[1], 128), jnp.float32),
+            pltpu.VMEM((17 * received.shape[1] + 24, 128), jnp.float32),
             pltpu.VMEM((40 * 64, 80), jnp.float32),
             pltpu.SemaphoreType.DMA((4,)),
         ],

time: 124 us -> 128 us (1.032)
  Pallas kernels: 18.1 us -> 22.2 us
    pallas_call x1, Pallas kernels: 3.18 us -> 7.24 us  [spectral_parts(): pl.pallas_call(spectral_kernel, in_specs=[smem, vmem, vmem, pl.BlockSpec(...]
where the time goes in v13:
time: 128 us
  waiting for transfers between devices  33.1 us (26%)
  starting transfers between devices  32.5 us (25%)
  blocking collectives  32.5 us (25%)
  Pallas kernels  22.2 us (17%)
  local copies, waits for them, and re-layouts  5.08 us (4%)
  other arithmetic  2.39 us (2%)
    all_to_all x1, blocking collectives, local(): parts = lax.all_to_all(parts, ('x', 'zp', 'zq', 'lev'), 0, 0, tiled=True)  32.5 us
    all_to_all x1, waiting for transfers between devices, local(): fourier = lax.all_to_all(fourier, ('x', 'zq', 'lev'), 0, 0, tiled=True)  16.2 us
    ppermute x14, waiting for transfers between devices, swapped(): lax.ppermute(blocks[k], 'wave', [(w, w ^ TO[w % 2][k]) for w in range(8)])  16.1 us
    ppermute x14, starting transfers between devices, swapped(): lax.ppermute(blocks[k], 'wave', [(w, w ^ TO[w % 2][k]) for w in range(8)])  15.4 us
    all_to_all x1, starting transfers between devices, local(): fourier = lax.all_to_all(fourier, ('x', 'zq', 'lev'), 0, 0, tiled=True)  10.3 us
    pallas_call x1, Pallas kernels, spectral_parts(): pl.pallas_call(spectral_kernel, in_specs=[smem, vmem, vmem, pl.BlockSpec(...  7.24 us
    all_to_all x1, starting transfers between devices, local(): basis = lax.all_to_all(basis, ('x', 'zq'), 0, 0, tiled=True)  6.84 us
    pallas_call x1, Pallas kernels, basis_blocks(): pl.pallas_call(basis_kernel, in_specs=[pl.BlockSpec(memory_space=pltpu.SM...  4.63 us
  transfers between devices with their start and end apart: 16, of which 10 were waited for; matrix products, arithmetic and copies ran while one was open for 5% of the time, Pallas kernels for 7%

profile of v13, /device:TPU:2, one launch (start us, length us, event | category | flops | bytes accessed | tf_op | source)
XLA Modules:
  0.0 128.1 jit_solution(4783523854551169220)
XLA Ops:
  0.0 4.6 %basis_blocks.1 = (bf16[8,5,80,640]{3,2,1,0:T(8,128)(2,1)}, f32[8,128]{1,0:T(8,128)}) custom-call(s32[1]{0:T(128)} %bitcast.3.lev_ref, bf16[80,10,8,640]{3,2,1,0:T(8,128)(2,1)} %bitcast.9), custom_call_target="tpu_custom_call" | custom-call | bytes 8192000 | tf_op jit(solution)/shard_map/basis_blocks/pallas_call | solution.py:56
  4.6 0.0 copy-start.7
  4.6 0.0 copy-start.8
  4.7 0.0 copy-start
  4.7 0.0 copy-start.3
  4.7 0.0 copy-start.5
  4.7 0.0 copy-start.6
  4.7 6.8 %all-to-all-start = ((bf16[8,5,80,640]{3,2,1,0:T(8,128)(2,1)}), bf16[8,5,80,640]{3,2,1,0:T(8,128)(2,1)}, u32[]{:S(2)}, u32[]{:S(2)}) async-start(bf16[8,5,80,640]{3,2,1,0:T(8,128)(2,1)} %get-tuple-element.46), calls=%async_computation | async-start | bytes 8192000 | tf_op jit(solution)/shard_map/all_to_all | solution.py:354
  11.6 0.0 copy-start.1
  11.6 1.5 %copy-done.1 = bf16[32,80,320]{2,1,0:T(8,128)(2,1)S(1)} copy-done((bf16[32,80,320]{2,1,0:T(8,128)(2,1)S(1)}, bf16[32,80,320]{2,1,0:T(8,128)(2,1)}, u32[]{:S(2)}) %copy-start.1) | copy-done | bytes 1638424
  13.2 2.4 %gradient.1 = (bf16[2,80,640]{2,1,0:T(8,128)(2,1)S(1)}, bf16[2,80,640]{2,1,0:T(8,128)(2,1)}, bf16[2,80,640]{2,1,0:T(8,128)(2,1)S(1)}, bf16[2,80,640]{2,1,0:T(8,1...) custom-call(s32[8]{0:T(128)S(1)} %get-tuple-element.50.wave_ref, ...), custom_call_target="tpu_custom_call" | custom-call | flops 4915200 | bytes 4915200 | tf_op jit(solution)/shard_map/gradient/pallas_call | solution.py:90
  15.6 1.1 collective-permute-start.1
  16.7 2.2 %collective-permute-start.2 = (bf16[2,80,640]{2,1,0:T(8,128)(2,1)S(1)}, bf16[2,80,640]{2,1,0:T(8,128)(2,1)S(1)}, u32[]{:S(2)}, u32[]{:S(2)}) collective-permute-start(bf16[2,80,640]{2,1,0:T(8,128)(2,1)S(1)} %get-tuple-element.33), channel_id=1, source_target_pairs={{0,12},{2,6},{4,8},{6,2},{8,4},{10,14},{12,0},{14,10},{1,13},{3,7}... | collective-permute-start | bytes 614408 | tf_op jit(solution)/shard_map/ppermute | solution.py:348
  18.9 0.9 collective-permute-start.3
  19.8 0.1 broadcast_add_fusion
  19.8 0.1 add.107
  19.9 0.1 reshape.66
  20.0 0.1 broadcast_in_dim.12
  20.1 0.1 add.109
  20.2 0.6 gather_fusion.1
  20.7 3.0 %collective-permute-start.5 = (bf16[2,80,640]{2,1,0:T(8,128)(2,1)S(1)}, bf16[2,80,640]{2,1,0:T(8,128)(2,1)S(1)}, u32[]{:S(2)}, u32[]{:S(2)}) collective-permute-start(bf16[2,80,640]{2,1,0:T(8,128)(2,1)S(1)} %get-tuple-element.36), channel_id=1, source_target_pairs={{0,14},{2,4},{4,10},{6,0},{8,6},{10,12},{12,2},{14,8},{1,15},{3,5}... | collective-permute-start | bytes 614408 | tf_op jit(solution)/shard_map/ppermute | solution.py:348
  23.8 0.1 mul.86
  23.8 1.3 %fusion.4 = (f32[64,1280]{1,0:T(8,128)S(1)}, f32[64,1280]{1,0:T(8,128)S(1)}) fusion(s32[1280]{0:T(1024)S(1)} %add.109, s32[1280]{0:T(1024)S(1)} %mul.86), kind=kLoop, calls=%fused_computation.8 | loop fusion | flops 819200 | bytes 665600 | tf_op jit(solution)/shard_map/sin | solution.py:118
  25.2 1.0 collective-permute-start.6
  26.2 0.9 sine_multiply_fusion
  27.1 1.7 %wave_table.1.table_ref = bf16[5,2560,256]{2,1,0:T(8,128)(2,1)S(1)} custom-call(f32[40,1280]{1,0:T(8,128)S(1)} %get-tuple-element.56.coarse_cos, f32[40,1280]{1,0:T(8,128)S(1)} %get-tuple-element.55.coarse_sin, f32[64,1280]{1,0:T(8,128)S(1)} %get-tuple-element.54.fine_cos, f32[64,1280]{1,0:T(8,128)S(1)} %get-tuple-element.53.fine_sin), custom_call_target="tpu_custom_call" | custom-call | flops 9830400 | bytes 6553600 | tf_op jit(solution)/shard_map/wave_table/pallas_call | solution.py:126
  28.9 1.2 collective-permute-done.3.refs_4_
  30.0 1.7 %collective-permute-done.4.refs_5_ = bf16[2,80,640]{2,1,0:T(8,128)(2,1)S(1)} collective-permute-done((bf16[2,80,640]{2,1,0:T(8,128)(2,1)S(1)}, bf16[2,80,640]{2,1,0:T(8,128)(2,1)S(1)}, u32[]{:S(2)}, u32[]{:S(2)}) %collective-permute-start.4) | collective-permute-done | bytes 204832 | tf_op jit(solution)/shard_map/ppermute | solution.py:348
  31.8 4.6 %collective-permute-done.5.refs_6_ = bf16[2,80,640]{2,1,0:T(8,128)(2,1)S(1)} collective-permute-done((bf16[2,80,640]{2,1,0:T(8,128)(2,1)S(1)}, bf16[2,80,640]{2,1,0:T(8,128)(2,1)S(1)}, u32[]{:S(2)}, u32[]{:S(2)}) %collective-permute-start.5) | collective-permute-done | bytes 204832 | tf_op jit(solution)/shard_map/ppermute | solution.py:348
  36.3 2.4 %collective-permute-done.6.refs_7_ = bf16[2,80,640]{2,1,0:T(8,128)(2,1)S(1)} collective-permute-done((bf16[2,80,640]{2,1,0:T(8,128)(2,1)S(1)}, bf16[2,80,640]{2,1,0:T(8,128)(2,1)S(1)}, u32[]{:S(2)}, u32[]{:S(2)}) %collective-permute-start.6) | collective-permute-done | bytes 204832 | tf_op jit(solution)/shard_map/ppermute | solution.py:348
  38.7 2.6 %fourier_rows.1 = (bf16[80,640]{1,0:T(8,128)(2,1)S(1)}, bf16[80,640]{1,0:T(8,128)(2,1)S(1)}, bf16[80,640]{1,0:T(8,128)(2,1)S(1)}, bf16[80,640]{1,0:T(8,128)(2,1)...) custom-call(bf16[5,2560,256]{2,1,0:T(8,128)(2,1)S(1)} %wave_table.1., ...), custom_call_target="tpu_custom_call" | custom-call | flops 2097152000 | bytes 6553600 | tf_op jit(solution)/shard_map/fourier_rows/pallas_call | solution.py:161
  41.3 0.2 collective-permute-start.7
  41.5 1.4 %collective-permute-start.9 = (bf16[80,640]{1,0:T(8,128)(2,1)S(1)}, bf16[80,640]{1,0:T(8,128)(2,1)S(1)}, u32[]{:S(2)}, u32[]{:S(2)}) collective-permute-start(bf16[80,640]{1,0:T(8,128)(2,1)S(1)} %get-tuple-element.41), channel_id=1, source_target_pairs={{0,12},{2,6},{4,8},{6,2},{8,4},{10,14},{12,0},{14,10},{1,13},{3,7}... | collective-permute-start | bytes 307208 | tf_op jit(solution)/shard_map/ppermute | solution.py:348
  42.9 2.7 %collective-permute-start.10 = (bf16[80,640]{1,0:T(8,128)(2,1)S(1)}, bf16[80,640]{1,0:T(8,128)(2,1)S(1)}, u32[]{:S(2)}, u32[]{:S(2)}) collective-permute-start(bf16[80,640]{1,0:T(8,128)(2,1)S(1)} %get-tuple-element.42), channel_id=1, source_target_pairs={{0,8},{2,10},{4,12},{6,14},{8,0},{10,2},{12,4},{14,6},{1,9},{3,11}... | collective-permute-start | bytes 307208 | tf_op jit(solution)/shard_map/ppermute | solution.py:348
  45.6 3.0 %collective-permute-start.12 = (bf16[80,640]{1,0:T(8,128)(2,1)S(1)}, bf16[80,640]{1,0:T(8,128)(2,1)S(1)}, u32[]{:S(2)}, u32[]{:S(2)}) collective-permute-start(bf16[80,640]{1,0:T(8,128)(2,1)S(1)} %get-tuple-element.44), channel_id=1, source_target_pairs={{0,14},{2,4},{4,10},{6,0},{8,6},{10,12},{12,2},{14,8},{1,15},{3,5}... | collective-permute-start | bytes 307208 | tf_op jit(solution)/shard_map/ppermute | solution.py:348
  48.6 1.6 %collective-permute-done.10.refs_4_ = bf16[80,640]{1,0:T(8,128)(2,1)S(1)} collective-permute-done((bf16[80,640]{1,0:T(8,128)(2,1)S(1)}, bf16[80,640]{1,0:T(8,128)(2,1)S(1)}, u32[]{:S(2)}, u32[]{:S(2)}) %collective-permute-start.10) | collective-permute-done | bytes 102432 | tf_op jit(solution)/shard_map/ppermute | solution.py:348
  50.2 1.2 collective-permute-done.11.refs_5_
  51.4 0.2 collective-permute-done.12.refs_6_
  51.7 3.2 %collective-permute-done.13.refs_7_ = bf16[80,640]{1,0:T(8,128)(2,1)S(1)} collective-permute-done((bf16[80,640]{1,0:T(8,128)(2,1)S(1)}, bf16[80,640]{1,0:T(8,128)(2,1)S(1)}, u32[]{:S(2)}, u32[]{:S(2)}) %collective-permute-start.13) | collective-permute-done | bytes 102432 | tf_op jit(solution)/shard_map/ppermute | solution.py:348
  54.8 2.1 %turn.1 = bf16[16,5,8,640]{3,2,1,0:T(8,128)(2,1)} custom-call(s32[8]{0:T(128)S(1)} %get-tuple-element.52.wave_ref, bf16[80,640]{1,0:T(8,128)(2,1)S(1)} %get-tuple-element.38.refs_0_, bf16[80,640]{1,0:T(8,128)(2,1)S(1)} %collective-permute-done.7.refs_1_, bf16[80,640]{1,0:T(8,128)(2,1)S(1)} %collective-permute-done.8.refs_2_, ...), custom_call_target="tpu_custom_call" | custom-call | bytes 1638400 | tf_op jit(solution)/shard_map/turn/pallas_call | solution.py:190
  56.9 0.9 all-to-all-done.basis_any
  57.8 10.3 %all-to-all-start.1 = ((bf16[16,5,8,640]{3,2,1,0:T(8,128)(2,1)}), bf16[16,5,8,640]{3,2,1,0:T(8,128)(2,1)S(1)}, u32[]{:S(2)}, u32[]{:S(2)}) async-start(bf16[16,5,8,640]{3,2,1,0:T(8,128)(2,1)} %turn.1), calls=%async_computation.1 | async-start | bytes 1638400 | tf_op jit(solution)/shard_map/all_to_all | solution.py:360
  68.1 0.6 gather_fusion
  68.7 1.9 %slice.3.head_ref = bf16[8,3,80,640]{3,2,1,0:T(8,128)(2,1)S(1)} slice(bf16[8,5,80,640]{3,2,1,0:T(8,128)(2,1)} %all-to-all-done.basis_any), slice={[0:8], [0:3], [0:80], [0:640]} | slice | bytes 4915200 | tf_op jit(solution)/shard_map/slice | solution.py:364
  70.6 16.2 %all-to-all-done.1.four_ref = bf16[16,5,8,640]{3,2,1,0:T(8,128)(2,1)S(1)} async-done(((bf16[16,5,8,640]{3,2,1,0:T(8,128)(2,1)}), bf16[16,5,8,640]{3,2,1,0:T(8,128)(2,1)S(1)}, u32[]{:S(2)}, u32[]{:S(2)}) %all-to-all-start.1) | async-done | bytes 819232 | tf_op jit(solution)/shard_map/all_to_all | solution.py:360
  86.8 7.2 %spectral_parts.1 = bf16[32,104,128]{2,1,0:T(8,128)(2,1)S(1)} custom-call(s32[5]{0:T(128)S(1)} %and_select_fusion.slot_ref, bf16[16,5,8,640]{3,2,1,0:T(8,128)(2,1)S(1)} %all-to-all-done.1.four_ref, bf16[8,3,80,640]{3,2,1,0:T(8,128)(2,1)S(1)} %slice.3.head_ref, bf16[8,5,80,640]{3,2,1,0:T(8,128)(2,1)} %all-to-all-done.basis_any), custom_call_target="tpu_custom_call" | custom-call | flops 524288000 | bytes 4915200 | tf_op jit(solution)/shard_map/spectral_parts/pallas_call | solution.py:272
  94.0 32.5 %all_to_all.15.in_ref = bf16[32,104,128]{2,1,0:T(8,128)(2,1)S(1)} all-to-all(bf16[32,104,128]{2,1,0:T(8,128)(2,1)S(1)} %spectral_parts.1), channel_id=1, replica_groups=mesh['x'=4,'zp'=2,'zq'=2,'wave'=8,'lev'=2] {'x','zp','zq','lev'}, dimensions={0} | all-to-all | bytes 1703936 | tf_op jit(solution)/shard_map/all_to_all | solution.py:365
  126.5 1.5 %finish.1 = f32[2560,80]{1,0:T(8,128)} custom-call(bf16[32,104,128]{2,1,0:T(8,128)(2,1)S(1)} %all_to_all.15.in_ref), custom_call_target="tpu_custom_call" | custom-call | flops 425984 | bytes 2162688 | tf_op jit(solution)/shard_map/finish/pallas_call | solution.py:319
  (30 shorter events, 0.1 us)
Async XLA Ops:
  4.6 6.9 %copy-start.7 = (s32[8]{0:T(128)S(1)}, s32[8]{0:T(128)}, u32[]{:S(2)}) copy-start(s32[8]{0:T(128)} %constant.95.clone) | copy-start | bytes 100
  4.6 6.9 %copy-start.8 = (s32[8]{0:T(128)S(1)}, s32[8]{0:T(128)}, u32[]{:S(2)}) copy-start(s32[8]{0:T(128)} %constant.94.clone) | copy-start | bytes 100
  4.7 6.9 %copy-start = (bf16[32,80,320]{2,1,0:T(8,128)(2,1)S(1)}, bf16[32,80,320]{2,1,0:T(8,128)(2,1)}, u32[]{:S(2)}) copy-start(bf16[32,80,320]{2,1,0:T(8,128)(2,1)} %param.10) | copy-start | bytes 4915204
  4.7 6.9 %copy-start.2 = (f32[8,128]{1,0:T(8,128)S(1)}, f32[8,128]{1,0:T(8,128)}, u32[]{:S(2)}) copy-start(f32[8,128]{1,0:T(8,128)} %get-tuple-element.27._) | copy-start | bytes 12292
  4.7 6.9 %copy-start.3 = (f32[32]{0:T(128)S(1)}, f32[32]{0:T(128)}, u32[]{:S(2)}) copy-start(f32[32]{0:T(128)} %rate_ref.1) | copy-start | bytes 388
  4.7 15.0 %copy-start.5 = (s32[8]{0:T(128)S(1)}, s32[8]{0:T(128)}, u32[]{:S(2)}) copy-start(s32[8]{0:T(128)} %constant.97.clone) | copy-start | bytes 100
  4.7 15.0 %copy-start.6 = (s32[8]{0:T(128)S(1)}, s32[8]{0:T(128)}, u32[]{:S(2)}) copy-start(s32[8]{0:T(128)} %constant.96.clone) | copy-start | bytes 100
  4.7 15.2 %copy-start.4 = (s32[640]{0:T(1024)S(1)}, s32[640]{0:T(1024)}, u32[]{:S(2)}) copy-start(s32[640]{0:T(1024)} %param.14) | copy-start | bytes 7684
  4.7 53.1 %all-to-all-start = ((bf16[8,5,80,640]{3,2,1,0:T(8,128)(2,1)}), bf16[8,5,80,640]{3,2,1,0:T(8,128)(2,1)}, u32[]{:S(2)}, u32[]{:S(2)}) async-start(bf16[8,5,80,640]{3,2,1,0:T(8,128)(2,1)} %get-tuple-element.46), calls=%async_computation | async-start | bytes 8192000 | tf_op jit(solution)/shard_map/all_to_all | solution.py:354
  11.6 1.5 %copy-start.1 = (bf16[32,80,320]{2,1,0:T(8,128)(2,1)S(1)}, bf16[32,80,320]{2,1,0:T(8,128)(2,1)}, u32[]{:S(2)}) copy-start(bf16[32,80,320]{2,1,0:T(8,128)(2,1)} %param.11) | copy-start | bytes 4915204
  15.6 5.1 %collective-permute-start = (bf16[2,80,640]{2,1,0:T(8,128)(2,1)}, bf16[2,80,640]{2,1,0:T(8,128)(2,1)S(1)}, u32[]{:S(2)}, u32[]{:S(2)}) collective-permute-start(bf16[2,80,640]{2,1,0:T(8,128)(2,1)} %get-tuple-element.28), channel_id=1, source_target_pairs={{0,2},{2,0},{4,6},{6,4},{8,10},{10,8},{12,14},{14,12},{1,3},{3,1},... | collective-permute-start | bytes 614408 | tf_op jit(solution)/shard_map/ppermute | solution.py:348
  15.6 9.6 %collective-permute-start.1 = (bf16[2,80,640]{2,1,0:T(8,128)(2,1)S(1)}, bf16[2,80,640]{2,1,0:T(8,128)(2,1)S(1)}, u32[]{:S(2)}, u32[]{:S(2)}) collective-permute-start(bf16[2,80,640]{2,1,0:T(8,128)(2,1)S(1)} %get-tuple-element.32), channel_id=1, source_target_pairs={{0,4},{2,14},{4,0},{6,10},{8,12},{10,6},{12,8},{14,2},{1,5},{3,15}... | collective-permute-start | bytes 614408 | tf_op jit(solution)/shard_map/ppermute | solution.py:348
  16.7 12.2 %collective-permute-start.2 = (bf16[2,80,640]{2,1,0:T(8,128)(2,1)S(1)}, bf16[2,80,640]{2,1,0:T(8,128)(2,1)S(1)}, u32[]{:S(2)}, u32[]{:S(2)}) collective-permute-start(bf16[2,80,640]{2,1,0:T(8,128)(2,1)S(1)} %get-tuple-element.33), channel_id=1, source_target_pairs={{0,12},{2,6},{4,8},{6,2},{8,4},{10,14},{12,0},{14,10},{1,13},{3,7}... | collective-permute-start | bytes 614408 | tf_op jit(solution)/shard_map/ppermute | solution.py:348
  18.9 11.1 %collective-permute-start.3 = (bf16[2,80,640]{2,1,0:T(8,128)(2,1)S(1)}, bf16[2,80,640]{2,1,0:T(8,128)(2,1)S(1)}, u32[]{:S(2)}, u32[]{:S(2)}) collective-permute-start(bf16[2,80,640]{2,1,0:T(8,128)(2,1)S(1)} %get-tuple-element.34), channel_id=1, source_target_pairs={{0,8},{2,10},{4,12},{6,14},{8,0},{10,2},{12,4},{14,6},{1,9},{3,11}... | collective-permute-start | bytes 614408 | tf_op jit(solution)/shard_map/ppermute | solution.py:348
  19.7 12.0 %collective-permute-start.4 = (bf16[2,80,640]{2,1,0:T(8,128)(2,1)S(1)}, bf16[2,80,640]{2,1,0:T(8,128)(2,1)S(1)}, u32[]{:S(2)}, u32[]{:S(2)}) collective-permute-start(bf16[2,80,640]{2,1,0:T(8,128)(2,1)S(1)} %get-tuple-element.35), channel_id=1, source_target_pairs={{0,6},{2,12},{4,2},{6,8},{8,14},{10,4},{12,10},{14,0},{1,7},{3,13}... | collective-permute-start | bytes 614408 | tf_op jit(solution)/shard_map/ppermute | solution.py:348
  20.7 15.6 %collective-permute-start.5 = (bf16[2,80,640]{2,1,0:T(8,128)(2,1)S(1)}, bf16[2,80,640]{2,1,0:T(8,128)(2,1)S(1)}, u32[]{:S(2)}, u32[]{:S(2)}) collective-permute-start(bf16[2,80,640]{2,1,0:T(8,128)(2,1)S(1)} %get-tuple-element.36), channel_id=1, source_target_pairs={{0,14},{2,4},{4,10},{6,0},{8,6},{10,12},{12,2},{14,8},{1,15},{3,5}... | collective-permute-start | bytes 614408 | tf_op jit(solution)/shard_map/ppermute | solution.py:348
  25.2 13.5 %collective-permute-start.6 = (bf16[2,80,640]{2,1,0:T(8,128)(2,1)S(1)}, bf16[2,80,640]{2,1,0:T(8,128)(2,1)S(1)}, u32[]{:S(2)}, u32[]{:S(2)}) collective-permute-start(bf16[2,80,640]{2,1,0:T(8,128)(2,1)S(1)} %get-tuple-element.37), channel_id=1, source_target_pairs={{0,10},{2,8},{4,14},{6,12},{8,2},{10,0},{12,6},{14,4},{1,11},{3,9}... | collective-permute-start | bytes 614408 | tf_op jit(solution)/shard_map/ppermute | solution.py:348
  41.3 4.3 %collective-permute-start.7 = (bf16[80,640]{1,0:T(8,128)(2,1)S(1)}, bf16[80,640]{1,0:T(8,128)(2,1)S(1)}, u32[]{:S(2)}, u32[]{:S(2)}) collective-permute-start(bf16[80,640]{1,0:T(8,128)(2,1)S(1)} %get-tuple-element.39), channel_id=1, source_target_pairs={{0,2},{2,0},{4,6},{6,4},{8,10},{10,8},{12,14},{14,12},{1,3},{3,1},... | collective-permute-start | bytes 307208 | tf_op jit(solution)/shard_map/ppermute | solution.py:348
  41.5 7.1 %collective-permute-start.8 = (bf16[80,640]{1,0:T(8,128)(2,1)S(1)}, bf16[80,640]{1,0:T(8,128)(2,1)S(1)}, u32[]{:S(2)}, u32[]{:S(2)}) collective-permute-start(bf16[80,640]{1,0:T(8,128)(2,1)S(1)} %get-tuple-element.40), channel_id=1, source_target_pairs={{0,4},{2,14},{4,0},{6,10},{8,12},{10,6},{12,8},{14,2},{1,5},{3,15}... | collective-permute-start | bytes 307208 | tf_op jit(solution)/shard_map/ppermute | solution.py:348
  41.5 7.1 %collective-permute-start.9 = (bf16[80,640]{1,0:T(8,128)(2,1)S(1)}, bf16[80,640]{1,0:T(8,128)(2,1)S(1)}, u32[]{:S(2)}, u32[]{:S(2)}) collective-permute-start(bf16[80,640]{1,0:T(8,128)(2,1)S(1)} %get-tuple-element.41), channel_id=1, source_target_pairs={{0,12},{2,6},{4,8},{6,2},{8,4},{10,14},{12,0},{14,10},{1,13},{3,7}... | collective-permute-start | bytes 307208 | tf_op jit(solution)/shard_map/ppermute | solution.py:348
  42.9 7.3 %collective-permute-start.10 = (bf16[80,640]{1,0:T(8,128)(2,1)S(1)}, bf16[80,640]{1,0:T(8,128)(2,1)S(1)}, u32[]{:S(2)}, u32[]{:S(2)}) collective-permute-start(bf16[80,640]{1,0:T(8,128)(2,1)S(1)} %get-tuple-element.42), channel_id=1, source_target_pairs={{0,8},{2,10},{4,12},{6,14},{8,0},{10,2},{12,4},{14,6},{1,9},{3,11}... | collective-permute-start | bytes 307208 | tf_op jit(solution)/shard_map/ppermute | solution.py:348
  45.6 5.8 %collective-permute-start.11 = (bf16[80,640]{1,0:T(8,128)(2,1)S(1)}, bf16[80,640]{1,0:T(8,128)(2,1)S(1)}, u32[]{:S(2)}, u32[]{:S(2)}) collective-permute-start(bf16[80,640]{1,0:T(8,128)(2,1)S(1)} %get-tuple-element.43), channel_id=1, source_target_pairs={{0,6},{2,12},{4,2},{6,8},{8,14},{10,4},{12,10},{14,0},{1,7},{3,13}... | collective-permute-start | bytes 307208 | tf_op jit(solution)/shard_map/ppermute | solution.py:348
  45.6 6.0 %collective-permute-start.12 = (bf16[80,640]{1,0:T(8,128)(2,1)S(1)}, bf16[80,640]{1,0:T(8,128)(2,1)S(1)}, u32[]{:S(2)}, u32[]{:S(2)}) collective-permute-start(bf16[80,640]{1,0:T(8,128)(2,1)S(1)} %get-tuple-element.44), channel_id=1, source_target_pairs={{0,14},{2,4},{4,10},{6,0},{8,6},{10,12},{12,2},{14,8},{1,15},{3,5}... | collective-permute-start | bytes 307208 | tf_op jit(solution)/shard_map/ppermute | solution.py:348
  48.6 6.2 %collective-permute-start.13 = (bf16[80,640]{1,0:T(8,128)(2,1)S(1)}, bf16[80,640]{1,0:T(8,128)(2,1)S(1)}, u32[]{:S(2)}, u32[]{:S(2)}) collective-permute-start(bf16[80,640]{1,0:T(8,128)(2,1)S(1)} %get-tuple-element.45), channel_id=1, source_target_pairs={{0,10},{2,8},{4,14},{6,12},{8,2},{10,0},{12,6},{14,4},{1,11},{3,9}... | collective-permute-start | bytes 307208 | tf_op jit(solution)/shard_map/ppermute | solution.py:348
  57.8 29.0 %all-to-all-start.1 = ((bf16[16,5,8,640]{3,2,1,0:T(8,128)(2,1)}), bf16[16,5,8,640]{3,2,1,0:T(8,128)(2,1)S(1)}, u32[]{:S(2)}, u32[]{:S(2)}) async-start(bf16[16,5,8,640]{3,2,1,0:T(8,128)(2,1)} %turn.1), calls=%async_computation.1 | async-start | bytes 1638400 | tf_op jit(solution)/shard_map/all_to_all | solution.py:360

commit v14 on v11

--- a/solution.py
+++ b/solution.py
@@ -218,7 +218,7 @@
             for lev in range(2):
                 block = four_ref[2 * q + lev, b].astype(jnp.float32)
                 for seg in range(8):
-                    left[pl.ds(64 * lev + 8 * seg, 8), pl.ds(q * lats, lats)] = block[
+                    left[b, pl.ds(64 * lev + 8 * seg, 8), pl.ds(q * lats, lats)] = block[
                         :, seg * lats : (seg + 1) * lats
                     ]
         if b >= head:
@@ -228,7 +228,7 @@
         else:
             blocks = head_ref[:, b]
         value = jnp.dot(
-            left[...].astype(jnp.bfloat16),
+            left[b].astype(jnp.bfloat16),
             blocks.reshape(8 * lats, degs),
             preferred_element_type=jnp.float32,
         )
@@ -274,7 +274,7 @@
         out_shape=jax.ShapeDtypeStruct((32, 104, 128), jnp.bfloat16),
         scratch_shapes=[
             pltpu.VMEM((steps, 8, lats, degs), jnp.bfloat16),
-            pltpu.VMEM((128, 8 * lats), jnp.float32),
+            pltpu.VMEM((steps, 128, 8 * lats), jnp.float32),
             pltpu.VMEM((degs + 8, 128), jnp.float32),
             pltpu.SemaphoreType.DMA((steps, 2)),
         ],

time: 124 us -> 124 us (level)
  no operation moved by 1% of the time
where the time goes in v14:
time: 124 us
  waiting for transfers between devices  33.1 us (27%)
  starting transfers between devices  32.5 us (26%)
  blocking collectives  32.5 us (26%)
  Pallas kernels  18 us (15%)
  local copies, waits for them, and re-layouts  5.08 us (4%)
  other arithmetic  2.39 us (2%)
    all_to_all x1, blocking collectives, local(): parts = lax.all_to_all(parts, ('x', 'zp', 'zq', 'lev'), 0, 0, tiled=True)  32.5 us
    all_to_all x1, waiting for transfers between devices, local(): fourier = lax.all_to_all(fourier, ('x', 'zq', 'lev'), 0, 0, tiled=True)  16.2 us
    ppermute x14, waiting for transfers between devices, swapped(): lax.ppermute(blocks[k], 'wave', [(w, w ^ TO[w % 2][k]) for w in range(8)])  16.1 us
    ppermute x14, starting transfers between devices, swapped(): lax.ppermute(blocks[k], 'wave', [(w, w ^ TO[w % 2][k]) for w in range(8)])  15.4 us
    all_to_all x1, starting transfers between devices, local(): fourier = lax.all_to_all(fourier, ('x', 'zq', 'lev'), 0, 0, tiled=True)  10.3 us
    all_to_all x1, starting transfers between devices, local(): basis = lax.all_to_all(basis, ('x', 'zq'), 0, 0, tiled=True)  6.84 us
    pallas_call x1, Pallas kernels, basis_blocks(): pl.pallas_call(basis_kernel, in_specs=[pl.BlockSpec(memory_space=pltpu.SM...  4.63 us
    pallas_call x1, Pallas kernels, spectral_parts(): pl.pallas_call(spectral_kernel, in_specs=[smem, vmem, vmem, pl.BlockSpec(...  3.06 us
  transfers between devices with their start and end apart: 16, of which 10 were waited for; matrix products, arithmetic and copies ran while one was open for 5% of the time, Pallas kernels for 7%

profile of v14, /device:TPU:2, one launch (start us, length us, event | category | flops | bytes accessed | tf_op | source)
XLA Modules:
  0.0 124.0 jit_solution(6809017521072673447)
XLA Ops:
  0.0 4.6 %basis_blocks.1 = (bf16[8,5,80,640]{3,2,1,0:T(8,128)(2,1)}, f32[8,128]{1,0:T(8,128)}) custom-call(s32[1]{0:T(128)} %bitcast.3.lev_ref, bf16[80,10,8,640]{3,2,1,0:T(8,128)(2,1)} %bitcast.9), custom_call_target="tpu_custom_call" | custom-call | bytes 8192000 | tf_op jit(solution)/shard_map/basis_blocks/pallas_call | solution.py:56
  4.6 0.0 copy-start.7
  4.6 0.0 copy-start.8
  4.7 0.0 copy-start
  4.7 0.0 copy-start.2
  4.7 0.0 copy-start.3
  4.7 0.0 copy-start.5
  4.7 0.0 copy-start.6
  4.7 6.8 %all-to-all-start = ((bf16[8,5,80,640]{3,2,1,0:T(8,128)(2,1)}), bf16[8,5,80,640]{3,2,1,0:T(8,128)(2,1)}, u32[]{:S(2)}, u32[]{:S(2)}) async-start(bf16[8,5,80,640]{3,2,1,0:T(8,128)(2,1)} %get-tuple-element.46), calls=%async_computation | async-start | bytes 8192000 | tf_op jit(solution)/shard_map/all_to_all | solution.py:352
  11.6 1.5 %copy-done.1 = bf16[32,80,320]{2,1,0:T(8,128)(2,1)S(1)} copy-done((bf16[32,80,320]{2,1,0:T(8,128)(2,1)S(1)}, bf16[32,80,320]{2,1,0:T(8,128)(2,1)}, u32[]{:S(2)}) %copy-start.1) | copy-done | bytes 1638424
  13.2 2.4 %gradient.1 = (bf16[2,80,640]{2,1,0:T(8,128)(2,1)S(1)}, bf16[2,80,640]{2,1,0:T(8,128)(2,1)}, bf16[2,80,640]{2,1,0:T(8,128)(2,1)S(1)}, bf16[2,80,640]{2,1,0:T(8,1...) custom-call(s32[8]{0:T(128)S(1)} %get-tuple-element.50.wave_ref, ...), custom_call_target="tpu_custom_call" | custom-call | flops 4915200 | bytes 4915200 | tf_op jit(solution)/shard_map/gradient/pallas_call | solution.py:90
  15.6 1.1 collective-permute-start.1
  16.7 2.2 %collective-permute-start.2 = (bf16[2,80,640]{2,1,0:T(8,128)(2,1)S(1)}, bf16[2,80,640]{2,1,0:T(8,128)(2,1)S(1)}, u32[]{:S(2)}, u32[]{:S(2)}) collective-permute-start(bf16[2,80,640]{2,1,0:T(8,128)(2,1)S(1)} %get-tuple-element.33), channel_id=1, source_target_pairs={{0,12},{2,6},{4,8},{6,2},{8,4},{10,14},{12,0},{14,10},{1,13},{3,7}... | collective-permute-start | bytes 614408 | tf_op jit(solution)/shard_map/ppermute | solution.py:346
  18.9 0.9 collective-permute-start.3
  19.8 0.1 broadcast_add_fusion
  19.8 0.1 add.107
  19.9 0.1 reshape.66
  20.0 0.1 broadcast_in_dim.12
  20.1 0.1 add.109
  20.2 0.6 gather_fusion.1
  20.7 3.0 %collective-permute-start.5 = (bf16[2,80,640]{2,1,0:T(8,128)(2,1)S(1)}, bf16[2,80,640]{2,1,0:T(8,128)(2,1)S(1)}, u32[]{:S(2)}, u32[]{:S(2)}) collective-permute-start(bf16[2,80,640]{2,1,0:T(8,128)(2,1)S(1)} %get-tuple-element.36), channel_id=1, source_target_pairs={{0,14},{2,4},{4,10},{6,0},{8,6},{10,12},{12,2},{14,8},{1,15},{3,5}... | collective-permute-start | bytes 614408 | tf_op jit(solution)/shard_map/ppermute | solution.py:346
  23.8 0.1 mul.86
  23.8 1.3 %fusion.4 = (f32[64,1280]{1,0:T(8,128)S(1)}, f32[64,1280]{1,0:T(8,128)S(1)}) fusion(s32[1280]{0:T(1024)S(1)} %add.109, s32[1280]{0:T(1024)S(1)} %mul.86), kind=kLoop, calls=%fused_computation.8 | loop fusion | flops 819200 | bytes 665600 | tf_op jit(solution)/shard_map/sin | solution.py:118
  25.2 1.0 collective-permute-start.6
  26.2 0.9 sine_multiply_fusion
  27.1 1.7 %wave_table.1.table_ref = bf16[5,2560,256]{2,1,0:T(8,128)(2,1)S(1)} custom-call(f32[40,1280]{1,0:T(8,128)S(1)} %get-tuple-element.56.coarse_cos, f32[40,1280]{1,0:T(8,128)S(1)} %get-tuple-element.55.coarse_sin, f32[64,1280]{1,0:T(8,128)S(1)} %get-tuple-element.54.fine_cos, f32[64,1280]{1,0:T(8,128)S(1)} %get-tuple-element.53.fine_sin), custom_call_target="tpu_custom_call" | custom-call | flops 9830400 | bytes 6553600 | tf_op jit(solution)/shard_map/wave_table/pallas_call | solution.py:126
  28.9 1.2 collective-permute-done.3.refs_4_
  30.0 1.7 %collective-permute-done.4.refs_5_ = bf16[2,80,640]{2,1,0:T(8,128)(2,1)S(1)} collective-permute-done((bf16[2,80,640]{2,1,0:T(8,128)(2,1)S(1)}, bf16[2,80,640]{2,1,0:T(8,128)(2,1)S(1)}, u32[]{:S(2)}, u32[]{:S(2)}) %collective-permute-start.4) | collective-permute-done | bytes 204832 | tf_op jit(solution)/shard_map/ppermute | solution.py:346
  31.8 4.6 %collective-permute-done.5.refs_6_ = bf16[2,80,640]{2,1,0:T(8,128)(2,1)S(1)} collective-permute-done((bf16[2,80,640]{2,1,0:T(8,128)(2,1)S(1)}, bf16[2,80,640]{2,1,0:T(8,128)(2,1)S(1)}, u32[]{:S(2)}, u32[]{:S(2)}) %collective-permute-start.5) | collective-permute-done | bytes 204832 | tf_op jit(solution)/shard_map/ppermute | solution.py:346
  36.3 2.4 %collective-permute-done.6.refs_7_ = bf16[2,80,640]{2,1,0:T(8,128)(2,1)S(1)} collective-permute-done((bf16[2,80,640]{2,1,0:T(8,128)(2,1)S(1)}, bf16[2,80,640]{2,1,0:T(8,128)(2,1)S(1)}, u32[]{:S(2)}, u32[]{:S(2)}) %collective-permute-start.6) | collective-permute-done | bytes 204832 | tf_op jit(solution)/shard_map/ppermute | solution.py:346
  38.7 2.6 %fourier_rows.1 = (bf16[80,640]{1,0:T(8,128)(2,1)S(1)}, bf16[80,640]{1,0:T(8,128)(2,1)S(1)}, bf16[80,640]{1,0:T(8,128)(2,1)S(1)}, bf16[80,640]{1,0:T(8,128)(2,1)...) custom-call(bf16[5,2560,256]{2,1,0:T(8,128)(2,1)S(1)} %wave_table.1., ...), custom_call_target="tpu_custom_call" | custom-call | flops 2097152000 | bytes 6553600 | tf_op jit(solution)/shard_map/fourier_rows/pallas_call | solution.py:161
  41.3 0.2 collective-permute-start.7
  41.5 1.4 %collective-permute-start.9 = (bf16[80,640]{1,0:T(8,128)(2,1)S(1)}, bf16[80,640]{1,0:T(8,128)(2,1)S(1)}, u32[]{:S(2)}, u32[]{:S(2)}) collective-permute-start(bf16[80,640]{1,0:T(8,128)(2,1)S(1)} %get-tuple-element.41), channel_id=1, source_target_pairs={{0,12},{2,6},{4,8},{6,2},{8,4},{10,14},{12,0},{14,10},{1,13},{3,7}... | collective-permute-start | bytes 307208 | tf_op jit(solution)/shard_map/ppermute | solution.py:346
  42.9 2.7 %collective-permute-start.10 = (bf16[80,640]{1,0:T(8,128)(2,1)S(1)}, bf16[80,640]{1,0:T(8,128)(2,1)S(1)}, u32[]{:S(2)}, u32[]{:S(2)}) collective-permute-start(bf16[80,640]{1,0:T(8,128)(2,1)S(1)} %get-tuple-element.42), channel_id=1, source_target_pairs={{0,8},{2,10},{4,12},{6,14},{8,0},{10,2},{12,4},{14,6},{1,9},{3,11}... | collective-permute-start | bytes 307208 | tf_op jit(solution)/shard_map/ppermute | solution.py:346
  45.6 3.0 %collective-permute-start.12 = (bf16[80,640]{1,0:T(8,128)(2,1)S(1)}, bf16[80,640]{1,0:T(8,128)(2,1)S(1)}, u32[]{:S(2)}, u32[]{:S(2)}) collective-permute-start(bf16[80,640]{1,0:T(8,128)(2,1)S(1)} %get-tuple-element.44), channel_id=1, source_target_pairs={{0,14},{2,4},{4,10},{6,0},{8,6},{10,12},{12,2},{14,8},{1,15},{3,5}... | collective-permute-start | bytes 307208 | tf_op jit(solution)/shard_map/ppermute | solution.py:346
  48.6 1.6 %collective-permute-done.10.refs_4_ = bf16[80,640]{1,0:T(8,128)(2,1)S(1)} collective-permute-done((bf16[80,640]{1,0:T(8,128)(2,1)S(1)}, bf16[80,640]{1,0:T(8,128)(2,1)S(1)}, u32[]{:S(2)}, u32[]{:S(2)}) %collective-permute-start.10) | collective-permute-done | bytes 102432 | tf_op jit(solution)/shard_map/ppermute | solution.py:346
  50.2 1.2 collective-permute-done.11.refs_5_
  51.4 0.2 collective-permute-done.12.refs_6_
  51.7 3.2 %collective-permute-done.13.refs_7_ = bf16[80,640]{1,0:T(8,128)(2,1)S(1)} collective-permute-done((bf16[80,640]{1,0:T(8,128)(2,1)S(1)}, bf16[80,640]{1,0:T(8,128)(2,1)S(1)}, u32[]{:S(2)}, u32[]{:S(2)}) %collective-permute-start.13) | collective-permute-done | bytes 102432 | tf_op jit(solution)/shard_map/ppermute | solution.py:346
  54.8 2.1 %turn.1 = bf16[16,5,8,640]{3,2,1,0:T(8,128)(2,1)} custom-call(s32[8]{0:T(128)S(1)} %get-tuple-element.52.wave_ref, bf16[80,640]{1,0:T(8,128)(2,1)S(1)} %get-tuple-element.38.refs_0_, bf16[80,640]{1,0:T(8,128)(2,1)S(1)} %collective-permute-done.7.refs_1_, bf16[80,640]{1,0:T(8,128)(2,1)S(1)} %collective-permute-done.8.refs_2_, ...), custom_call_target="tpu_custom_call" | custom-call | bytes 1638400 | tf_op jit(solution)/shard_map/turn/pallas_call | solution.py:190
  56.9 0.9 all-to-all-done.basis_any
  57.8 10.3 %all-to-all-start.1 = ((bf16[16,5,8,640]{3,2,1,0:T(8,128)(2,1)}), bf16[16,5,8,640]{3,2,1,0:T(8,128)(2,1)S(1)}, u32[]{:S(2)}, u32[]{:S(2)}) async-start(bf16[16,5,8,640]{3,2,1,0:T(8,128)(2,1)} %turn.1), calls=%async_computation.1 | async-start | bytes 1638400 | tf_op jit(solution)/shard_map/all_to_all | solution.py:358
  68.1 0.6 gather_fusion
  68.7 1.9 %slice.3.head_ref = bf16[8,3,80,640]{3,2,1,0:T(8,128)(2,1)S(1)} slice(bf16[8,5,80,640]{3,2,1,0:T(8,128)(2,1)} %all-to-all-done.basis_any), slice={[0:8], [0:3], [0:80], [0:640]} | slice | bytes 4915200 | tf_op jit(solution)/shard_map/slice | solution.py:362
  70.6 16.2 %all-to-all-done.1.four_ref = bf16[16,5,8,640]{3,2,1,0:T(8,128)(2,1)S(1)} async-done(((bf16[16,5,8,640]{3,2,1,0:T(8,128)(2,1)}), bf16[16,5,8,640]{3,2,1,0:T(8,128)(2,1)S(1)}, u32[]{:S(2)}, u32[]{:S(2)}) %all-to-all-start.1) | async-done | bytes 819232 | tf_op jit(solution)/shard_map/all_to_all | solution.py:358
  86.8 3.1 %spectral_parts.1 = bf16[32,104,128]{2,1,0:T(8,128)(2,1)S(1)} custom-call(s32[5]{0:T(128)S(1)} %and_select_fusion.slot_ref, bf16[16,5,8,640]{3,2,1,0:T(8,128)(2,1)S(1)} %all-to-all-done.1.four_ref, bf16[8,3,80,640]{3,2,1,0:T(8,128)(2,1)S(1)} %slice.3.head_ref, bf16[8,5,80,640]{3,2,1,0:T(8,128)(2,1)} %all-to-all-done.basis_any), custom_call_target="tpu_custom_call" | custom-call | flops 524288000 | bytes 4915200 | tf_op jit(solution)/shard_map/spectral_parts/pallas_call | solution.py:271
  89.9 32.5 %all_to_all.15.in_ref = bf16[32,104,128]{2,1,0:T(8,128)(2,1)S(1)} all-to-all(bf16[32,104,128]{2,1,0:T(8,128)(2,1)S(1)} %spectral_parts.1), channel_id=1, replica_groups=mesh['x'=4,'zp'=2,'zq'=2,'wave'=8,'lev'=2] {'x','zp','zq','lev'}, dimensions={0} | all-to-all | bytes 1703936 | tf_op jit(solution)/shard_map/all_to_all | solution.py:363
  122.3 1.5 %finish.1 = f32[2560,80]{1,0:T(8,128)} custom-call(bf16[32,104,128]{2,1,0:T(8,128)(2,1)S(1)} %all_to_all.15.in_ref), custom_call_target="tpu_custom_call" | custom-call | flops 425984 | bytes 2162688 | tf_op jit(solution)/shard_map/finish/pallas_call | solution.py:317
  (30 shorter events, 0.1 us)
Async XLA Ops:
  4.6 6.9 %copy-start.7 = (s32[8]{0:T(128)S(1)}, s32[8]{0:T(128)}, u32[]{:S(2)}) copy-start(s32[8]{0:T(128)} %constant.95.clone) | copy-start | bytes 100
  4.6 6.9 %copy-start.8 = (s32[8]{0:T(128)S(1)}, s32[8]{0:T(128)}, u32[]{:S(2)}) copy-start(s32[8]{0:T(128)} %constant.94.clone) | copy-start | bytes 100
  4.7 6.9 %copy-start = (bf16[32,80,320]{2,1,0:T(8,128)(2,1)S(1)}, bf16[32,80,320]{2,1,0:T(8,128)(2,1)}, u32[]{:S(2)}) copy-start(bf16[32,80,320]{2,1,0:T(8,128)(2,1)} %param.10) | copy-start | bytes 4915204
  4.7 6.9 %copy-start.2 = (f32[8,128]{1,0:T(8,128)S(1)}, f32[8,128]{1,0:T(8,128)}, u32[]{:S(2)}) copy-start(f32[8,128]{1,0:T(8,128)} %get-tuple-element.27._) | copy-start | bytes 12292
  4.7 6.9 %copy-start.3 = (f32[32]{0:T(128)S(1)}, f32[32]{0:T(128)}, u32[]{:S(2)}) copy-start(f32[32]{0:T(128)} %rate_ref.1) | copy-start | bytes 388
  4.7 15.0 %copy-start.5 = (s32[8]{0:T(128)S(1)}, s32[8]{0:T(128)}, u32[]{:S(2)}) copy-start(s32[8]{0:T(128)} %constant.97.clone) | copy-start | bytes 100
  4.7 15.0 %copy-start.6 = (s32[8]{0:T(128)S(1)}, s32[8]{0:T(128)}, u32[]{:S(2)}) copy-start(s32[8]{0:T(128)} %constant.96.clone) | copy-start | bytes 100
  4.7 15.2 %copy-start.4 = (s32[640]{0:T(1024)S(1)}, s32[640]{0:T(1024)}, u32[]{:S(2)}) copy-start(s32[640]{0:T(1024)} %param.14) | copy-start | bytes 7684
  4.7 53.1 %all-to-all-start = ((bf16[8,5,80,640]{3,2,1,0:T(8,128)(2,1)}), bf16[8,5,80,640]{3,2,1,0:T(8,128)(2,1)}, u32[]{:S(2)}, u32[]{:S(2)}) async-start(bf16[8,5,80,640]{3,2,1,0:T(8,128)(2,1)} %get-tuple-element.46), calls=%async_computation | async-start | bytes 8192000 | tf_op jit(solution)/shard_map/all_to_all | solution.py:352
  11.6 1.5 %copy-start.1 = (bf16[32,80,320]{2,1,0:T(8,128)(2,1)S(1)}, bf16[32,80,320]{2,1,0:T(8,128)(2,1)}, u32[]{:S(2)}) copy-start(bf16[32,80,320]{2,1,0:T(8,128)(2,1)} %param.11) | copy-start | bytes 4915204
  15.6 5.1 %collective-permute-start = (bf16[2,80,640]{2,1,0:T(8,128)(2,1)}, bf16[2,80,640]{2,1,0:T(8,128)(2,1)S(1)}, u32[]{:S(2)}, u32[]{:S(2)}) collective-permute-start(bf16[2,80,640]{2,1,0:T(8,128)(2,1)} %get-tuple-element.28), channel_id=1, source_target_pairs={{0,2},{2,0},{4,6},{6,4},{8,10},{10,8},{12,14},{14,12},{1,3},{3,1},... | collective-permute-start | bytes 614408 | tf_op jit(solution)/shard_map/ppermute | solution.py:346
  15.6 9.6 %collective-permute-start.1 = (bf16[2,80,640]{2,1,0:T(8,128)(2,1)S(1)}, bf16[2,80,640]{2,1,0:T(8,128)(2,1)S(1)}, u32[]{:S(2)}, u32[]{:S(2)}) collective-permute-start(bf16[2,80,640]{2,1,0:T(8,128)(2,1)S(1)} %get-tuple-element.32), channel_id=1, source_target_pairs={{0,4},{2,14},{4,0},{6,10},{8,12},{10,6},{12,8},{14,2},{1,5},{3,15}... | collective-permute-start | bytes 614408 | tf_op jit(solution)/shard_map/ppermute | solution.py:346
  16.7 12.2 %collective-permute-start.2 = (bf16[2,80,640]{2,1,0:T(8,128)(2,1)S(1)}, bf16[2,80,640]{2,1,0:T(8,128)(2,1)S(1)}, u32[]{:S(2)}, u32[]{:S(2)}) collective-permute-start(bf16[2,80,640]{2,1,0:T(8,128)(2,1)S(1)} %get-tuple-element.33), channel_id=1, source_target_pairs={{0,12},{2,6},{4,8},{6,2},{8,4},{10,14},{12,0},{14,10},{1,13},{3,7}... | collective-permute-start | bytes 614408 | tf_op jit(solution)/shard_map/ppermute | solution.py:346
  18.9 11.1 %collective-permute-start.3 = (bf16[2,80,640]{2,1,0:T(8,128)(2,1)S(1)}, bf16[2,80,640]{2,1,0:T(8,128)(2,1)S(1)}, u32[]{:S(2)}, u32[]{:S(2)}) collective-permute-start(bf16[2,80,640]{2,1,0:T(8,128)(2,1)S(1)} %get-tuple-element.34), channel_id=1, source_target_pairs={{0,8},{2,10},{4,12},{6,14},{8,0},{10,2},{12,4},{14,6},{1,9},{3,11}... | collective-permute-start | bytes 614408 | tf_op jit(solution)/shard_map/ppermute | solution.py:346
  19.7 12.0 %collective-permute-start.4 = (bf16[2,80,640]{2,1,0:T(8,128)(2,1)S(1)}, bf16[2,80,640]{2,1,0:T(8,128)(2,1)S(1)}, u32[]{:S(2)}, u32[]{:S(2)}) collective-permute-start(bf16[2,80,640]{2,1,0:T(8,128)(2,1)S(1)} %get-tuple-element.35), channel_id=1, source_target_pairs={{0,6},{2,12},{4,2},{6,8},{8,14},{10,4},{12,10},{14,0},{1,7},{3,13}... | collective-permute-start | bytes 614408 | tf_op jit(solution)/shard_map/ppermute | solution.py:346
  20.7 15.6 %collective-permute-start.5 = (bf16[2,80,640]{2,1,0:T(8,128)(2,1)S(1)}, bf16[2,80,640]{2,1,0:T(8,128)(2,1)S(1)}, u32[]{:S(2)}, u32[]{:S(2)}) collective-permute-start(bf16[2,80,640]{2,1,0:T(8,128)(2,1)S(1)} %get-tuple-element.36), channel_id=1, source_target_pairs={{0,14},{2,4},{4,10},{6,0},{8,6},{10,12},{12,2},{14,8},{1,15},{3,5}... | collective-permute-start | bytes 614408 | tf_op jit(solution)/shard_map/ppermute | solution.py:346
  25.2 13.5 %collective-permute-start.6 = (bf16[2,80,640]{2,1,0:T(8,128)(2,1)S(1)}, bf16[2,80,640]{2,1,0:T(8,128)(2,1)S(1)}, u32[]{:S(2)}, u32[]{:S(2)}) collective-permute-start(bf16[2,80,640]{2,1,0:T(8,128)(2,1)S(1)} %get-tuple-element.37), channel_id=1, source_target_pairs={{0,10},{2,8},{4,14},{6,12},{8,2},{10,0},{12,6},{14,4},{1,11},{3,9}... | collective-permute-start | bytes 614408 | tf_op jit(solution)/shard_map/ppermute | solution.py:346
  41.3 4.3 %collective-permute-start.7 = (bf16[80,640]{1,0:T(8,128)(2,1)S(1)}, bf16[80,640]{1,0:T(8,128)(2,1)S(1)}, u32[]{:S(2)}, u32[]{:S(2)}) collective-permute-start(bf16[80,640]{1,0:T(8,128)(2,1)S(1)} %get-tuple-element.39), channel_id=1, source_target_pairs={{0,2},{2,0},{4,6},{6,4},{8,10},{10,8},{12,14},{14,12},{1,3},{3,1},... | collective-permute-start | bytes 307208 | tf_op jit(solution)/shard_map/ppermute | solution.py:346
  41.5 7.1 %collective-permute-start.8 = (bf16[80,640]{1,0:T(8,128)(2,1)S(1)}, bf16[80,640]{1,0:T(8,128)(2,1)S(1)}, u32[]{:S(2)}, u32[]{:S(2)}) collective-permute-start(bf16[80,640]{1,0:T(8,128)(2,1)S(1)} %get-tuple-element.40), channel_id=1, source_target_pairs={{0,4},{2,14},{4,0},{6,10},{8,12},{10,6},{12,8},{14,2},{1,5},{3,15}... | collective-permute-start | bytes 307208 | tf_op jit(solution)/shard_map/ppermute | solution.py:346
  41.5 7.1 %collective-permute-start.9 = (bf16[80,640]{1,0:T(8,128)(2,1)S(1)}, bf16[80,640]{1,0:T(8,128)(2,1)S(1)}, u32[]{:S(2)}, u32[]{:S(2)}) collective-permute-start(bf16[80,640]{1,0:T(8,128)(2,1)S(1)} %get-tuple-element.41), channel_id=1, source_target_pairs={{0,12},{2,6},{4,8},{6,2},{8,4},{10,14},{12,0},{14,10},{1,13},{3,7}... | collective-permute-start | bytes 307208 | tf_op jit(solution)/shard_map/ppermute | solution.py:346
  42.9 7.3 %collective-permute-start.10 = (bf16[80,640]{1,0:T(8,128)(2,1)S(1)}, bf16[80,640]{1,0:T(8,128)(2,1)S(1)}, u32[]{:S(2)}, u32[]{:S(2)}) collective-permute-start(bf16[80,640]{1,0:T(8,128)(2,1)S(1)} %get-tuple-element.42), channel_id=1, source_target_pairs={{0,8},{2,10},{4,12},{6,14},{8,0},{10,2},{12,4},{14,6},{1,9},{3,11}... | collective-permute-start | bytes 307208 | tf_op jit(solution)/shard_map/ppermute | solution.py:346
  45.6 5.8 %collective-permute-start.11 = (bf16[80,640]{1,0:T(8,128)(2,1)S(1)}, bf16[80,640]{1,0:T(8,128)(2,1)S(1)}, u32[]{:S(2)}, u32[]{:S(2)}) collective-permute-start(bf16[80,640]{1,0:T(8,128)(2,1)S(1)} %get-tuple-element.43), channel_id=1, source_target_pairs={{0,6},{2,12},{4,2},{6,8},{8,14},{10,4},{12,10},{14,0},{1,7},{3,13}... | collective-permute-start | bytes 307208 | tf_op jit(solution)/shard_map/ppermute | solution.py:346
  45.6 6.0 %collective-permute-start.12 = (bf16[80,640]{1,0:T(8,128)(2,1)S(1)}, bf16[80,640]{1,0:T(8,128)(2,1)S(1)}, u32[]{:S(2)}, u32[]{:S(2)}) collective-permute-start(bf16[80,640]{1,0:T(8,128)(2,1)S(1)} %get-tuple-element.44), channel_id=1, source_target_pairs={{0,14},{2,4},{4,10},{6,0},{8,6},{10,12},{12,2},{14,8},{1,15},{3,5}... | collective-permute-start | bytes 307208 | tf_op jit(solution)/shard_map/ppermute | solution.py:346
  48.6 6.2 %collective-permute-start.13 = (bf16[80,640]{1,0:T(8,128)(2,1)S(1)}, bf16[80,640]{1,0:T(8,128)(2,1)S(1)}, u32[]{:S(2)}, u32[]{:S(2)}) collective-permute-start(bf16[80,640]{1,0:T(8,128)(2,1)S(1)} %get-tuple-element.45), channel_id=1, source_target_pairs={{0,10},{2,8},{4,14},{6,12},{8,2},{10,0},{12,6},{14,4},{1,11},{3,9}... | collective-permute-start | bytes 307208 | tf_op jit(solution)/shard_map/ppermute | solution.py:346
  57.8 29.0 %all-to-all-start.1 = ((bf16[16,5,8,640]{3,2,1,0:T(8,128)(2,1)}), bf16[16,5,8,640]{3,2,1,0:T(8,128)(2,1)S(1)}, u32[]{:S(2)}, u32[]{:S(2)}) async-start(bf16[16,5,8,640]{3,2,1,0:T(8,128)(2,1)} %turn.1), calls=%async_computation.1 | async-start | bytes 1638400 | tf_op jit(solution)/shard_map/all_to_all | solution.py:358
